TPU v7x, 32 devices: a whole 2x2x4 slice. The times are simulated.
32 devices in a mesh: freq: 16 (over z, x, core), mz: 2 (over y).
Axes of the slice: x: 2, y: 2, z: 4, core: 2. Of those that a mesh axis runs over, the one named last changes fastest.
Arguments:
- intensity: bfloat16 [8, 6144, 4096], P(None, 'freq', 'mz'), may hold values from -6 to 6
- elution: float32 [6144, 64], P(('freq', 'mz')), may hold values from -6 to 6
- loadings: float32 [8, 64], replicated, may hold values from 0.0005 to 0.01
- shifts: int32 [8, 64], replicated, may hold values from 0 to 255
- bin_weight: float32 [6144], replicated, may hold values from 0.25 to 4
Outputs:
- spectral: float32 [64, 4096], P(None, ('mz', 'freq'))
All inputs are finite; a program needn't handle non-finite values.
Results may differ from a plain program's by a relative error of at most 0.0003.
Values may be sent and summed in bfloat16 or wider, within the bound.
No kernel may reach another device: no remote copies, remote signals or barrier semaphores. Data moves between devices by JAX's collectives and lax.ppermute only.
A program may use at most 64 MiB of HBM per device.

v0:
```python
import functools
import math

import jax
import jax.numpy as jnp
import numpy as np
from jax import lax
from jax.experimental import pallas as pl
from jax.experimental.pallas import tpu as pltpu
from jax.sharding import PartitionSpec as P

PRECISE = lax.Precision.HIGHEST
LANES = 128
REACH = 256
MIB = 1024 * 1024


def f32_dot(a, b, dims=(((1,), (0,)), ((), ()))):
    return lax.dot_general(a, b, dims, precision=PRECISE, preferred_element_type=jnp.float32)


def two_terms(x):
    high = x.astype(jnp.bfloat16)
    low = (x - high.astype(jnp.float32)).astype(jnp.bfloat16)
    return high, low


def vmem(count):
    return [pl.BlockSpec(memory_space=pltpu.VMEM)] * count


def pack_kernel(x_ref, o_ref):
    x = x_ref[...]
    components, rows = x.shape
    pad = -rows % LANES
    if pad:
        x = jnp.concatenate([x, jnp.zeros((components, pad), x.dtype)], axis=1)
    high, low = two_terms(x.T[:rows])
    o_ref[...] = jnp.concatenate([high, low], axis=1)


def pack(elution):
    rows, components = elution.shape
    return pl.pallas_call(
        pack_kernel,
        out_shape=jax.ShapeDtypeStruct((rows, 2 * components), jnp.bfloat16),
        in_specs=vmem(1),
        out_specs=vmem(1)[0],
        compiler_params=pltpu.CompilerParams(vmem_limit_bytes=8 * MIB),
        name="pack_elution",
    )(elution.T)


def circulant_kernel(w_ref, lane_ref, twid_ref, row_ref, u_ref):
    rows = w_ref.shape[1]
    w = w_ref[...]
    over_lanes = (((0,), (0,)), ((), ()))
    a_re = f32_dot(w, lane_ref[0], over_lanes)
    a_im = -f32_dot(w, lane_ref[1], over_lanes)
    b_re = a_re * twid_ref[0] + a_im * twid_ref[1]
    b_im = a_im * twid_ref[0] - a_re * twid_ref[1]
    c = f32_dot(row_ref[0], b_re) + f32_dot(row_ref[1], b_im)
    sub = lax.broadcasted_iota(jnp.int32, (LANES, LANES), 0)
    lane = lax.broadcasted_iota(jnp.int32, (LANES, LANES), 1)

    def turned(row):
        return pltpu.roll(jnp.broadcast_to(c[row : row + 1], (LANES, LANES)), 0, 1, stride=1, stride_axis=0)

    before = turned(rows - 1)
    for row in range(rows):
        now = turned(row)
        high, low = two_terms(jnp.where(lane >= sub, now, before))
        u_ref[0:LANES, row * LANES : (row + 1) * LANES] = high
        u_ref[LANES:, row * LANES : (row + 1) * LANES] = low
        before = now


def circulant(bin_weight):
    length = bin_weight.shape[0]
    rows = length // LANES

    def tables(a, b, period):
        angle = 2.0 * math.pi / period * ((a[:, None] * b[None, :]) % period)
        return np.stack([np.cos(angle), np.sin(angle)])

    lane_ids, row_ids = np.arange(LANES), np.arange(rows)
    lane_table = tables(lane_ids, lane_ids, LANES).astype(np.float32)
    twid_table = tables(row_ids, lane_ids, length).astype(np.float32)
    row_table = (tables(row_ids, row_ids, rows) / length).astype(np.float32)
    return pl.pallas_call(
        circulant_kernel,
        out_shape=jax.ShapeDtypeStruct((2 * LANES, length), jnp.bfloat16),
        in_specs=vmem(4),
        out_specs=vmem(1)[0],
        compiler_params=pltpu.CompilerParams(vmem_limit_bytes=16 * MIB),
        cost_estimate=pl.CostEstimate(flops=2_000_000_000, bytes_accessed=4 * MIB, transcendentals=0),
        name="circulant_block",
    )(bin_weight.reshape(LANES, rows), lane_table, twid_table, row_table)


def model_kernel(places, planes, *refs):
    u_ref, g_ref, wide = refs[-3:]
    length = u_ref.shape[1]
    components = g_ref.shape[0]
    freq_rank = lax.axis_index("freq")
    if planes:
        own_ref, came_ref = refs[:2]
        mz_rank = lax.axis_index("mz")
        freq_count = 2 * own_ref.shape[0]
        rows = own_ref.shape[1]
        empty = jnp.zeros((rows, LANES), jnp.bfloat16)
        for block in range(-1, freq_count + 1):
            apart = lax.bitwise_xor((freq_rank + block) & (freq_count - 1), freq_rank)
            ref = came_ref if block % 2 else own_ref
            values = ref[pl.ds(block_place(apart, freq_count), 1)][0]
            for here, half in ((values, mz_rank), (empty, 1 - mz_rank)):
                to = pl.multiple_of(2 * REACH + (2 * block + half) * rows, 64)
                wide[pl.ds(to, rows), 0:LANES] = here
                wide[pl.ds(pl.multiple_of(to - LANES, 64), rows), LANES:] = here
    else:
        own_ref = refs[0]
        step = own_ref.shape[1]
        steps = length // step
        bin_count = length // lax.axis_size("freq")
        first = lax.rem(freq_rank * bin_count + length - REACH, length) // step

        def bring(j, carry):
            values = own_ref[pl.ds(lax.rem(first + j, steps), 1)][0]
            to = pl.multiple_of(REACH + j * step, step)
            wide[pl.ds(to, step), 0:LANES] = values
            wide[pl.ds(pl.multiple_of(to - LANES, step), step), LANES:] = values
            return carry

        lax.fori_loop(0, (wide.shape[0] - REACH) // step, bring, 0)
    for a in range(0, places, 2):
        at = REACH + a * LANES
        made = jnp.dot(u_ref[...], wide[at : at + length, :], preferred_element_type=jnp.float32)
        made = made[:LANES] + made[LANES:]
        for half in range(min(2, places - a)):
            piece = made[:, half * LANES : (half + 1) * LANES].T
            g_ref[:, (a + half) * LANES : (a + half + 1) * LANES] = piece[:components] + piece[components:]


def block_place(apart, freq_count):
    return (apart >> 2) + ((apart >> 1) & 1) * (freq_count // 4)


def partial_model(gathered, u, bin_count, components):
    length = u.shape[1]
    places = -(-(bin_count + REACH) // LANES)
    planes = len(gathered) == 2
    wide_rows = 2 * REACH + length + bin_count if planes else REACH + length + 2 * LANES * ((places - 1) // 2)
    return pl.pallas_call(
        functools.partial(model_kernel, places, planes),
        out_shape=jax.ShapeDtypeStruct((components, places * LANES), jnp.float32),
        in_specs=vmem(len(gathered) + 1),
        out_specs=vmem(1)[0],
        scratch_shapes=[pltpu.VMEM((wide_rows, 2 * LANES), jnp.bfloat16)],
        compiler_params=pltpu.CompilerParams(vmem_limit_bytes=24 * MIB),
        cost_estimate=pl.CostEstimate(flops=2_000_000_000, bytes_accessed=4 * MIB, transcendentals=0),
        name="partial_model",
    )(*gathered, u)


def product_kernel(parts, planes, *refs):
    i_ref = refs[0]
    g_refs = refs[1 : 1 + parts]
    if planes:
        mine_ref, came_ref, near_ref, far_ref, amp_ref, lag_ref, keep_ref, send_ref = refs[1 + parts : 9 + parts]
    else:
        own_ref, amp_ref, lag_ref, num_ref, gram_ref = refs[1 + parts : 6 + parts]
    window, terms, held, sems = refs[-4:]
    run_count, bin_count, local_mz = i_ref.shape
    components = amp_ref.shape[1]
    chunks = sems.shape[0]
    chunk = local_mz // chunks
    copies = []
    for n in range(chunks):
        part = pl.ds(n * chunk, chunk)
        copies.append(pltpu.make_async_copy(i_ref.at[:, :, part], held.at[:, :, part], sems.at[n]))
        copies[-1].start()

    freq_rank = lax.axis_index("freq")
    if planes:
        mz_rank = lax.axis_index("mz")
        freq_count = 2 * came_ref.shape[0]
        rows = mine_ref.shape[0]
        apart = lax.bitwise_xor((freq_rank - 1) & (freq_count - 1), freq_rank)
        before = came_ref[pl.ds(block_place(apart, freq_count), 1)][0]
        skip = bin_count - REACH
        for block, half, values in (
            (0, mz_rank, before),
            (0, 1 - mz_rank, far_ref[...]),
            (1, mz_rank, mine_ref[...]),
            (1, 1 - mz_rank, near_ref[...]),
        ):
            window[pl.ds(pl.multiple_of((2 * block + half) * rows, 64), rows), :] = values
    else:
        step = own_ref.shape[1]
        steps = own_ref.shape[0]
        first = lax.rem(freq_rank * bin_count + steps * step - REACH, steps * step) // step
        skip = 0
        for j in range(window.shape[0] // step):
            window[j * step : (j + 1) * step, :] = own_ref[pl.ds(lax.rem(first + j, steps), 1)][0]
    g = g_refs[0][...]
    for ref in g_refs[1:]:
        g = g + ref[...]
    pieces = []
    for a in range(g.shape[1] // LANES):
        piece = window[skip + a * LANES : skip + (a + 1) * LANES, :].astype(jnp.float32).T
        pieces.append(piece[:components] + piece[components:])
    base = jnp.concatenate([g, jnp.concatenate(pieces, axis=1)], axis=0)
    span = -(-bin_count // LANES) * LANES
    amps, lags = amp_ref[...].T, lag_ref[...].T
    for k in range(run_count):
        lag = lags[:, k : k + 1]
        left = REACH - 1 - jnp.concatenate([lag, lag], axis=0)
        y = base
        for bit in (7, 6, 5, 4, 3, 2, 1, 0):
            move = 1 << bit
            y = jnp.where((left & move) != 0, pltpu.roll(y, y.shape[1] - move, 1), y)
            if move == LANES:
                y = y[:, : span + LANES]
        y = pltpu.roll(y, y.shape[1] - 1, 1)[:, :bin_count]
        amp = amps[:, k : k + 1]
        high, low = two_terms(y * jnp.concatenate([amp, amp], axis=0))
        part = slice(k * bin_count, (k + 1) * bin_count)
        terms[0:components, part] = high[:components]
        terms[components : 2 * components, part] = low[:components]
        terms[2 * components : 3 * components, part] = high[components:]
        terms[3 * components :, part] = low[components:]
    gram = lax.dot_general(
        terms[0 : 2 * components, :],
        terms[2 * components :, :],
        (((1,), (1,)), ((), ())),
        preferred_element_type=jnp.float32,
    )
    gram = gram[:components] + gram[components:]
    gram = gram[:, :components] + gram[:, components:]
    if planes:
        half = components // 2
        gram = jnp.concatenate([gram[:half], gram[half:]], axis=1)
        keep_ref[chunks * components :, :] = gram
        send_ref[chunks * components :, :] = gram
    else:
        gram_ref[...] = gram

    for n in range(chunks):
        copies[n].wait()
        data = held[:, :, n * chunk : (n + 1) * chunk].reshape(run_count * bin_count, chunk)
        made = jnp.dot(terms[0 : 2 * components, :], data, preferred_element_type=jnp.float32)
        made = made[:components] + made[components:]
        if planes:
            core = freq_rank & 1
            place = block_place(lax.bitwise_xor(freq_rank, 2 * n + core), freq_count)
            at = pl.ds(pl.multiple_of(place * components, components), components)
            even, odd = made[:, :LANES], made[:, LANES:]
            keep_ref[at, :] = jnp.where(core == 0, even, odd)
            send_ref[at, :] = jnp.where(core == 0, odd, even)
        else:
            num_ref[:, n * chunk : (n + 1) * chunk] = made


def product(intensity, models, elutions, loadings, shifts):
    run_count, bin_count, local_mz = intensity.shape
    components = loadings.shape[1]
    chunk = 2 * LANES
    chunks = local_mz // chunk
    planes = len(elutions) > 1
    if planes:
        out_shapes = [(chunks * components + components // 2, LANES)] * 2
        window_rows = 2 * bin_count
    else:
        out_shapes = [(components, local_mz), (components, components)]
        window_rows = models[0].shape[1]
    return pl.pallas_call(
        functools.partial(product_kernel, len(models), planes),
        out_shape=tuple(jax.ShapeDtypeStruct(shape, jnp.float32) for shape in out_shapes),
        in_specs=[pl.BlockSpec(memory_space=pl.ANY)] + vmem(len(models) + len(elutions) + 2),
        out_specs=tuple(vmem(2)),
        scratch_shapes=[
            pltpu.VMEM((window_rows, LANES), jnp.bfloat16),
            pltpu.VMEM((4 * components, run_count * bin_count), jnp.bfloat16),
            pltpu.VMEM(intensity.shape, jnp.bfloat16),
            pltpu.SemaphoreType.DMA((chunks,)),
        ],
        compiler_params=pltpu.CompilerParams(vmem_limit_bytes=48 * MIB),
        cost_estimate=pl.CostEstimate(
            flops=8_000_000_000, bytes_accessed=2 * intensity.size, transcendentals=0
        ),
        name="model_products",
    )(intensity, *models, *elutions, loadings, shifts)


def eliminate(gram, right):
    components = gram.shape[0]
    row_id = lax.broadcasted_iota(jnp.int32, (components, 1), 0)
    for j in range(0, components, 2):
        first = jnp.broadcast_to(gram[:, j : j + 1], gram.shape)
        second = jnp.broadcast_to(gram[:, j + 1 : j + 2], gram.shape)
        a, b, d = first[j : j + 1], second[j : j + 1], second[j + 1 : j + 2]
        scale = 1.0 / (a * d - b * b)
        away = (row_id != j) & (row_id != j + 1)
        f1 = jnp.where(away, first * (d * scale) - second * (b * scale), 0.0)
        f2 = jnp.where(away, second * (a * scale) - first * (b * scale), 0.0)
        gram, right = (
            gram - f1 * gram[j : j + 1] - f2 * gram[j + 1 : j + 2],
            right - f1[:, : right.shape[1]] * right[j : j + 1] - f2[:, : right.shape[1]] * right[j + 1 : j + 2],
        )
    lane = lax.broadcasted_iota(jnp.int32, gram.shape, 1)
    even = row_id % 2 == 0

    def across(x):
        return jnp.where(even, pltpu.roll(x, components - 1, 0), pltpu.roll(x, 1, 0))

    own = jnp.sum(jnp.where(lane == row_id, gram, 0.0), axis=1, keepdims=True) + jnp.zeros_like(right)
    off = jnp.sum(jnp.where(lane == (row_id ^ 1), gram, 0.0), axis=1, keepdims=True)
    other = across(own)
    return (other * right - off * across(right)) / (other * own - off * off)


def summed(refs, rows, tail):
    total = refs[0][0:rows] + refs[1][0:rows]
    gram = refs[0][refs[0].shape[0] - tail :] + refs[1][refs[1].shape[0] - tail :]
    for ref in refs[2:]:
        total = total + ref[0:rows]
        gram = gram + ref[ref.shape[0] - tail :]
    return total, gram


def stage_kernel(tail, count, *refs):
    outs = refs[-count:]
    rows = outs[0].shape[0] - tail
    total, gram = summed(refs[:-count], (count + 1) * rows, tail)
    for n, o_ref in enumerate(outs):
        o_ref[0:rows, :] = total[(n + 1) * rows : (n + 2) * rows]
        o_ref[rows:, :] = gram


def solve_planes_kernel(tail, *refs):
    o_ref = refs[-1]
    total, gram = summed(refs[:-1], o_ref.shape[0], tail)
    gram = jnp.concatenate([gram, pltpu.roll(gram, gram.shape[1] // 2, 1)], axis=0)
    o_ref[...] = eliminate(gram, total)


def solve_kernel(g_ref, n_ref, o_ref):
    components = o_ref.shape[0]
    gram = jnp.concatenate([g_ref[...], jnp.zeros((components, LANES - components), jnp.float32)], axis=1)
    o_ref[...] = eliminate(gram, n_ref[...])


def small_call(kernel, out_shape, name, *args, count=1):
    outs = pl.pallas_call(
        kernel,
        out_shape=(jax.ShapeDtypeStruct(out_shape, jnp.float32),) * count,
        in_specs=vmem(len(args)),
        out_specs=tuple(vmem(count)),
        compiler_params=pltpu.CompilerParams(vmem_limit_bytes=8 * MIB),
        name=name,
    )(*args)
    return outs


def swap(x, axes, count, value):
    return lax.ppermute(x, axes, [(i, i ^ value) for i in range(count)])


def on_device(intensity, elution, loadings, shifts, bin_weight):
    freq_count = lax.axis_size("freq")
    mz_count = lax.axis_size("mz")
    components = loadings.shape[1]
    bin_count = intensity.shape[1]
    axes = ("freq", "mz")
    mine = pack(elution)
    own = intensity.shape[2] // freq_count
    planes = (
        own == LANES
        and 2 * components == LANES
        and mz_count == 2
        and freq_count & (freq_count - 1) == 0
        and freq_count >= 8
        and elution.shape[0] % 64 == 0
        and bin_count % LANES == 0
        and bin_count >= REACH
    )
    if not planes:
        gathered = lax.all_gather(mine, axes, axis=0).reshape(-1, math.gcd(bin_count, LANES), LANES)
        g = partial_model((gathered,), circulant(bin_weight), bin_count, components)
        numerator, gram = product(intensity, (g,), (gathered,), loadings, shifts)
        gram = lax.psum(gram, "freq")
        owned = lax.psum_scatter(numerator, "freq", scatter_dimension=1, tiled=True)
        return small_call(solve_kernel, (components, own), "solve", gram, owned)[0]
    z_steps = range(4, freq_count, 4)
    held = jnp.stack([mine] + [swap(mine, "freq", freq_count, step) for step in z_steps])
    held = jnp.concatenate([held, swap(held, "freq", freq_count, 2)], axis=0)
    u = circulant(bin_weight)
    held, u = lax.optimization_barrier((held, u))
    came = swap(held, "freq", freq_count, 1)
    near = swap(mine, "mz", mz_count, 1)
    onward = [
        (f * mz_count + y, (f + 1) % freq_count * mz_count + 1 - y)
        for f in range(freq_count)
        for y in range(mz_count)
    ]
    far = lax.ppermute(mine, axes, onward)
    g = partial_model((held, came), u, bin_count, components)
    models = (g, swap(g, "mz", mz_count, 1))
    keep, send = product(intensity, models, (mine, came, near, far), loadings, shifts)
    tail = components // 2
    quarter = freq_count // 4 * components
    parts = [keep, swap(send, "freq", freq_count, 1)]
    (send,) = small_call(
        functools.partial(stage_kernel, tail, 1), (quarter + tail, LANES), "reduce_stage", *parts
    )
    parts.append(swap(send, "freq", freq_count, 2))
    count = len(z_steps)
    sends = small_call(
        functools.partial(stage_kernel, tail, count), (components + tail, LANES), "reduce_stage", *parts, count=count
    )
    parts += [swap(send, "freq", freq_count, step) for send, step in zip(sends, z_steps)]
    return small_call(functools.partial(solve_planes_kernel, tail), (components, own), "solve", *parts)[0]


def solution(mesh):
    in_specs = (P(None, "freq", "mz"), P(("freq", "mz"), None), P(), P(), P())
    out_specs = P(None, ("mz", "freq"))
    return jax.shard_map(on_device, mesh=mesh, in_specs=in_specs, out_specs=out_specs, check_vma=False)
```

profile of v0, /device:TPU:0, one launch (start us, length us, event | category | flops | bytes accessed | tf_op | source)
XLA Modules:
  0.0 66.3 jit_solution(11169492209124543944)
XLA Ops:
  0.0 0.0 copy-start
  0.0 0.8 %copy-done = f32[192,64]{0,1:T(8,128)S(1)} copy-done((f32[192,64]{0,1:T(8,128)S(1)}, f32[192,64]{0,1:T(8,128)}, u32[]{:S(2)}) %copy-start) | copy-done | bytes 49176
  0.8 0.0 copy-start.1
  0.8 0.0 copy-start.2
  0.8 0.2 pack_elution.1.refs_3_
  1.0 3.1 %collective-permute-start = (bf16[192,128]{1,0:T(8,128)(2,1)S(1)}, bf16[192,128]{1,0:T(8,128)(2,1)S(1)}, u32[]{:S(2)}, u32[]{:S(2)}) collective-permute-start(bf16[192,128]{1,0:T(8,128)(2,1)S(1)} %pack_elution.1.refs_3_), channel_id=1, source_target_pairs={{0,8},{2,10},{4,12},{6,14},{8,0},{10,2},{12,4},{14,6},{16,24},{18,... | collective-permute-start | bytes 147464 | tf_op jit(solution)/shard_map/ppermute | solution.py:366
  4.1 2.6 %collective-permute-start.1 = (bf16[192,128]{1,0:T(8,128)(2,1)S(1)}, bf16[192,128]{1,0:T(8,128)(2,1)S(1)}, u32[]{:S(2)}, u32[]{:S(2)}) collective-permute-start(bf16[192,128]{1,0:T(8,128)(2,1)S(1)} %pack_elution.1.refs_3_), channel_id=1, source_target_pairs={{0,16},{2,18},{4,20},{6,22},{8,24},{10,26},{12,28},{14,30},{16,0},... | collective-permute-start | bytes 147464 | tf_op jit(solution)/shard_map/ppermute | solution.py:366
  6.7 0.0 collective-permute-start.2
  6.7 0.8 %reshape.3.w_ref = f32[128,48]{1,0:T(8,128)S(1)} reshape(f32[6144]{0:T(1024)} %param.12) | data formatting | bytes 49152 | tf_op jit(solution)/shard_map/reshape | solution.py:98
  7.5 0.0 copy-start.3
  7.5 0.9 %copy-done.3 = f32[2,128,128]{2,1,0:T(8,128)S(1)} copy-done((f32[2,128,128]{2,1,0:T(8,128)S(1)}, f32[2,128,128]{2,1,0:T(8,128)}, u32[]{:S(2)}) %copy-start.3) | copy-done | bytes 131096
  8.4 0.0 copy-start.4
  8.4 0.8 %copy-done.4 = f32[2,48,128]{2,1,0:T(8,128)S(1)} copy-done((f32[2,48,128]{2,1,0:T(8,128)S(1)}, f32[2,48,128]{2,1,0:T(8,128)}, u32[]{:S(2)}) %copy-start.4) | copy-done | bytes 49176
  9.2 0.0 copy-start.5
  9.2 0.8 %copy-done.5 = f32[2,48,48]{2,1,0:T(8,128)S(1)} copy-done((f32[2,48,48]{2,1,0:T(8,128)S(1)}, f32[2,48,48]{2,1,0:T(8,128)}, u32[]{:S(2)}) %copy-start.5) | copy-done | bytes 18456
  10.0 1.4 %circulant_block.1.refs_2_ = bf16[256,6144]{1,0:T(8,128)(2,1)S(1)} custom-call(f32[128,48]{1,0:T(8,128)S(1)} %reshape.3.w_ref, f32[2,128,128]{2,1,0:T(8,128)S(1)} %copy-done.3, f32[2,48,128]{2,1,0:T(8,128)S(1)} %copy-done.4, f32[2,48,48]{2,1,0:T(8,128)S(1)} %copy-done.5), custom_call_target="tpu_custom_call" | custom-call | flops 2000000000 | bytes 4194304 | tf_op jit(solution)/shard_map/circulant_block/pallas_call | solution.py:90
  11.5 0.0 collective-permute-done
  11.5 0.0 collective-permute-done.1
  11.5 1.1 %collective-permute-done.2 = bf16[192,128]{1,0:T(8,128)(2,1)S(1)} collective-permute-done((bf16[192,128]{1,0:T(8,128)(2,1)S(1)}, bf16[192,128]{1,0:T(8,128)(2,1)S(1)}, u32[]{:S(2)}, u32[]{:S(2)}) %collective-permute-start.2) | collective-permute-done | bytes 49184 | tf_op jit(solution)/shard_map/ppermute | solution.py:366
  12.6 1.6 %collective-permute-start.3 = (bf16[4,192,128]{2,1,0:T(8,128)(2,1)S(1)}, bf16[4,192,128]{2,1,0:T(8,128)(2,1)S(1)}, u32[]{:S(2)}, u32[]{:S(2)}) collective-permute-start(bf16[4,192,128]{2,1,0:T(8,128)(2,1)S(1)} %pad_maximum_fusion), channel_id=1, source_target_pairs={{0,4},{2,6},{4,0},{6,2},{8,12},{10,14},{12,8},{14,10},{16,20},{18,... | collective-permute-start | bytes 589832 | tf_op jit(solution)/shard_map/ppermute | solution.py:366
  14.2 4.1 %collective-permute-done.3 = bf16[4,192,128]{2,1,0:T(8,128)(2,1)S(1)} collective-permute-done((bf16[4,192,128]{2,1,0:T(8,128)(2,1)S(1)}, bf16[4,192,128]{2,1,0:T(8,128)(2,1)S(1)}, u32[]{:S(2)}, u32[]{:S(2)}) %collective-permute-start.3) | collective-permute-done | bytes 196640 | tf_op jit(solution)/shard_map/ppermute | solution.py:366
  18.4 0.1 collective-permute-start.4
  18.5 1.7 %collective-permute-done.4.refs_1_.refs_4_ = bf16[8,192,128]{2,1,0:T(8,128)(2,1)S(1)} collective-permute-done((bf16[8,192,128]{2,1,0:T(8,128)(2,1)S(1)}, bf16[8,192,128]{2,1,0:T(8,128)(2,1)S(1)}, u32[]{:S(2)}, u32[]{:S(2)}) %collective-permute-start.4) | collective-permute-done | bytes 393248 | tf_op jit(solution)/shard_map/ppermute | solution.py:366
  20.2 3.1 %partial_model.1.refs_1_ = f32[64,640]{1,0:T(8,128)S(1)} custom-call(bf16[8,192,128]{2,1,0:T(8,128)(2,1)S(1)} %constant_dynamic-update-slice_fusion.refs_0_, bf16[8,192,128]{2,1,0:T(8,128)(2,1)S(1)} %collective-permute-done.4.refs_1_.refs_4_, bf16[256,6144]{1,0:T(8,128)(2,1)S(1)} %circulant_block.1.refs_2_), custom_call_target="tpu_custom_call" | custom-call | flops 2000000000 | bytes 4194304 | tf_op jit(solution)/shard_map/partial_model/pallas_call | solution.py:153
  23.3 1.6 %collective-permute-start.5 = (f32[64,640]{1,0:T(8,128)S(1)}, f32[64,640]{1,0:T(8,128)S(1)}, u32[]{:S(2)}, u32[]{:S(2)}) collective-permute-start(f32[64,640]{1,0:T(8,128)S(1)} %partial_model.1.refs_1_), channel_id=1, source_target_pairs={{0,1},{1,0},{2,3},{3,2},{4,5},{5,4},{6,7},{7,6},{8,9},{9,8},{10,11... | collective-permute-start | bytes 491528 | tf_op jit(solution)/shard_map/ppermute | solution.py:366
  24.9 0.5 collective-permute-start.6
  25.4 0.7 %collective-permute-start.7 = (bf16[192,128]{1,0:T(8,128)(2,1)S(1)}, bf16[192,128]{1,0:T(8,128)(2,1)S(1)}, u32[]{:S(2)}, u32[]{:S(2)}) collective-permute-start(bf16[192,128]{1,0:T(8,128)(2,1)S(1)} %pack_elution.1.refs_3_), channel_id=1, source_target_pairs={{0,3},{1,2},{2,5},{3,4},{4,7},{5,6},{6,9},{7,8},{8,11},{9,10},{10,... | collective-permute-start | bytes 147464 | tf_op jit(solution)/shard_map/ppermute | solution.py:406
  26.1 4.6 %collective-permute-done.6.refs_5_ = bf16[192,128]{1,0:T(8,128)(2,1)S(1)} collective-permute-done((bf16[192,128]{1,0:T(8,128)(2,1)S(1)}, bf16[192,128]{1,0:T(8,128)(2,1)S(1)}, u32[]{:S(2)}, u32[]{:S(2)}) %collective-permute-start.6) | collective-permute-done | bytes 49184 | tf_op jit(solution)/shard_map/ppermute | solution.py:366
  30.6 1.8 %collective-permute-done.7.refs_6_ = bf16[192,128]{1,0:T(8,128)(2,1)S(1)} collective-permute-done((bf16[192,128]{1,0:T(8,128)(2,1)S(1)}, bf16[192,128]{1,0:T(8,128)(2,1)S(1)}, u32[]{:S(2)}, u32[]{:S(2)}) %collective-permute-start.7) | collective-permute-done | bytes 49184 | tf_op jit(solution)/shard_map/ppermute | solution.py:406
  32.5 0.0 collective-permute-done.5.refs_2_
  32.5 0.0 copy-done.1
  32.5 0.0 copy-done.2
  32.5 13.9 %model_products.1 = (f32[544,128]{1,0:T(8,128)S(1)}, f32[544,128]{1,0:T(8,128)S(1)}) custom-call(bf16[8,384,2048]{2,1,0:T(8,128)(2,1)} %refs_0_.1, f32[64,640]{1,0:T(8,128)S(1)} %partial_model.1.refs_1_, f32[64,640]{1,0:T(8,128)S(1)} %collective-permute-done.5.refs_2_, bf16[192,128]{1,0:T(8,128)(2,1)S(1)} %pack_elution.1.refs_3_, ...), custom_call_target="tpu_custom_call" | custom-call | flops 8000000000 | bytes 12582912 | tf_op jit(solution)/shard_map/model_products/pallas_call | solution.py:276
  46.4 0.1 collective-permute-start.8
  46.5 1.5 %collective-permute-done.8.refs_1_ = f32[544,128]{1,0:T(8,128)S(1)} collective-permute-done((f32[544,128]{1,0:T(8,128)S(1)}, f32[544,128]{1,0:T(8,128)S(1)}, u32[]{:S(2)}, u32[]{:S(2)}) %collective-permute-start.8) | collective-permute-done | bytes 278560 | tf_op jit(solution)/shard_map/ppermute | solution.py:366
  48.0 0.2 collective-permute-start.9
  48.3 5.7 %collective-permute-done.9.refs_2_ = f32[288,128]{1,0:T(8,128)S(1)} collective-permute-done((f32[288,128]{1,0:T(8,128)S(1)}, f32[288,128]{1,0:T(8,128)S(1)}, u32[]{:S(2)}, u32[]{:S(2)}) %collective-permute-start.9) | collective-permute-done | bytes 147488 | tf_op jit(solution)/shard_map/ppermute | solution.py:366
  54.0 0.1 collective-permute-start.10
  54.1 2.3 %collective-permute-start.11 = (f32[96,128]{1,0:T(8,128)S(1)}, f32[96,128]{1,0:T(8,128)S(1)}, u32[]{:S(2)}, u32[]{:S(2)}) collective-permute-start(f32[96,128]{1,0:T(8,128)S(1)} %get-tuple-element.17), channel_id=1, source_target_pairs={{0,16},{2,18},{4,20},{6,22},{8,24},{10,26},{12,28},{14,30},{16,0},... | collective-permute-start | bytes 147464 | tf_op jit(solution)/shard_map/ppermute | solution.py:366
  56.4 2.0 %collective-permute-start.12 = (f32[96,128]{1,0:T(8,128)S(1)}, f32[96,128]{1,0:T(8,128)S(1)}, u32[]{:S(2)}, u32[]{:S(2)}) collective-permute-start(f32[96,128]{1,0:T(8,128)S(1)} %get-tuple-element.18), channel_id=1, source_target_pairs={{0,24},{2,26},{4,28},{6,30},{8,16},{10,18},{12,20},{14,22},{16,8},... | collective-permute-start | bytes 147464 | tf_op jit(solution)/shard_map/ppermute | solution.py:366
  58.5 0.0 collective-permute-done.10.refs_3_
  58.5 0.9 %collective-permute-done.11.refs_4_ = f32[96,128]{1,0:T(8,128)S(1)} collective-permute-done((f32[96,128]{1,0:T(8,128)S(1)}, f32[96,128]{1,0:T(8,128)S(1)}, u32[]{:S(2)}, u32[]{:S(2)}) %collective-permute-start.11) | collective-permute-done | bytes 49184 | tf_op jit(solution)/shard_map/ppermute | solution.py:366
  59.4 2.9 %collective-permute-done.12.refs_5_ = f32[96,128]{1,0:T(8,128)S(1)} collective-permute-done((f32[96,128]{1,0:T(8,128)S(1)}, f32[96,128]{1,0:T(8,128)S(1)}, u32[]{:S(2)}, u32[]{:S(2)}) %collective-permute-start.12) | collective-permute-done | bytes 49184 | tf_op jit(solution)/shard_map/ppermute | solution.py:366
  62.3 3.9 %solve.1 = f32[64,128]{1,0:T(8,128)} custom-call(f32[544,128]{1,0:T(8,128)S(1)} %get-tuple-element.14.refs_0_, f32[544,128]{1,0:T(8,128)S(1)} %collective-permute-done.8.refs_1_, f32[288,128]{1,0:T(8,128)S(1)} %collective-permute-done.9.refs_2_, f32[96,128]{1,0:T(8,128)S(1)} %collective-permute-done.10.refs_3_, ...), custom_call_target="tpu_custom_call" | custom-call | tf_op jit(solution)/shard_map/solve/pallas_call | solution.py:354
  (8 shorter events, 0.1 us)
Async XLA Ops:
  0.0 0.8 %copy-start = (f32[192,64]{0,1:T(8,128)S(1)}, f32[192,64]{0,1:T(8,128)}, u32[]{:S(2)}) copy-start(f32[192,64]{0,1:T(8,128)} %param.9) | copy-start | bytes 147460
  0.8 31.6 %copy-start.1 = (f32[8,64]{1,0:T(8,128)S(1)}, f32[8,64]{1,0:T(8,128)}, u32[]{:S(2)}) copy-start(f32[8,64]{1,0:T(8,128)} %refs_7_.1) | copy-start | bytes 6148
  0.8 31.6 %copy-start.2 = (s32[8,64]{1,0:T(8,128)S(1)}, s32[8,64]{1,0:T(8,128)}, u32[]{:S(2)}) copy-start(s32[8,64]{1,0:T(8,128)} %refs_8_.1) | copy-start | bytes 6148
  1.0 10.5 %collective-permute-start = (bf16[192,128]{1,0:T(8,128)(2,1)S(1)}, bf16[192,128]{1,0:T(8,128)(2,1)S(1)}, u32[]{:S(2)}, u32[]{:S(2)}) collective-permute-start(bf16[192,128]{1,0:T(8,128)(2,1)S(1)} %pack_elution.1.refs_3_), channel_id=1, source_target_pairs={{0,8},{2,10},{4,12},{6,14},{8,0},{10,2},{12,4},{14,6},{16,24},{18,... | collective-permute-start | bytes 147464 | tf_op jit(solution)/shard_map/ppermute | solution.py:366
  4.1 7.4 %collective-permute-start.1 = (bf16[192,128]{1,0:T(8,128)(2,1)S(1)}, bf16[192,128]{1,0:T(8,128)(2,1)S(1)}, u32[]{:S(2)}, u32[]{:S(2)}) collective-permute-start(bf16[192,128]{1,0:T(8,128)(2,1)S(1)} %pack_elution.1.refs_3_), channel_id=1, source_target_pairs={{0,16},{2,18},{4,20},{6,22},{8,24},{10,26},{12,28},{14,30},{16,0},... | collective-permute-start | bytes 147464 | tf_op jit(solution)/shard_map/ppermute | solution.py:366
  6.7 5.9 %collective-permute-start.2 = (bf16[192,128]{1,0:T(8,128)(2,1)S(1)}, bf16[192,128]{1,0:T(8,128)(2,1)S(1)}, u32[]{:S(2)}, u32[]{:S(2)}) collective-permute-start(bf16[192,128]{1,0:T(8,128)(2,1)S(1)} %pack_elution.1.refs_3_), channel_id=1, source_target_pairs={{0,24},{2,26},{4,28},{6,30},{8,16},{10,18},{12,20},{14,22},{16,8},... | collective-permute-start | bytes 147464 | tf_op jit(solution)/shard_map/ppermute | solution.py:366
  7.5 0.9 %copy-start.3 = (f32[2,128,128]{2,1,0:T(8,128)S(1)}, f32[2,128,128]{2,1,0:T(8,128)}, u32[]{:S(2)}) copy-start(f32[2,128,128]{2,1,0:T(8,128)} %constant.6.clone.lane_ref) | copy-start | bytes 393220
  8.4 0.8 %copy-start.4 = (f32[2,48,128]{2,1,0:T(8,128)S(1)}, f32[2,48,128]{2,1,0:T(8,128)}, u32[]{:S(2)}) copy-start(f32[2,48,128]{2,1,0:T(8,128)} %constant.7.clone.twid_ref) | copy-start | bytes 147460
  9.2 0.8 %copy-start.5 = (f32[2,48,48]{2,1,0:T(8,128)S(1)}, f32[2,48,48]{2,1,0:T(8,128)}, u32[]{:S(2)}) copy-start(f32[2,48,48]{2,1,0:T(8,128)} %constant.8.clone.row_ref) | copy-start | bytes 55300
  12.6 5.7 %collective-permute-start.3 = (bf16[4,192,128]{2,1,0:T(8,128)(2,1)S(1)}, bf16[4,192,128]{2,1,0:T(8,128)(2,1)S(1)}, u32[]{:S(2)}, u32[]{:S(2)}) collective-permute-start(bf16[4,192,128]{2,1,0:T(8,128)(2,1)S(1)} %pad_maximum_fusion), channel_id=1, source_target_pairs={{0,4},{2,6},{4,0},{6,2},{8,12},{10,14},{12,8},{14,10},{16,20},{18,... | collective-permute-start | bytes 589832 | tf_op jit(solution)/shard_map/ppermute | solution.py:366
  18.4 1.8 %collective-permute-start.4 = (bf16[8,192,128]{2,1,0:T(8,128)(2,1)S(1)}, bf16[8,192,128]{2,1,0:T(8,128)(2,1)S(1)}, u32[]{:S(2)}, u32[]{:S(2)}) collective-permute-start(bf16[8,192,128]{2,1,0:T(8,128)(2,1)S(1)} %constant_dynamic-update-slice_fusion.refs_0_), channel_id=1, source_target_pairs={{0,2},{2,0},{4,6},{6,4},{8,10},{10,8},{12,14},{14,12},{16,18},{18,... | collective-permute-start | bytes 1179656 | tf_op jit(solution)/shard_map/ppermute | solution.py:366
  23.3 9.2 %collective-permute-start.5 = (f32[64,640]{1,0:T(8,128)S(1)}, f32[64,640]{1,0:T(8,128)S(1)}, u32[]{:S(2)}, u32[]{:S(2)}) collective-permute-start(f32[64,640]{1,0:T(8,128)S(1)} %partial_model.1.refs_1_), channel_id=1, source_target_pairs={{0,1},{1,0},{2,3},{3,2},{4,5},{5,4},{6,7},{7,6},{8,9},{9,8},{10,11... | collective-permute-start | bytes 491528 | tf_op jit(solution)/shard_map/ppermute | solution.py:366
  24.9 5.8 %collective-permute-start.6 = (bf16[192,128]{1,0:T(8,128)(2,1)S(1)}, bf16[192,128]{1,0:T(8,128)(2,1)S(1)}, u32[]{:S(2)}, u32[]{:S(2)}) collective-permute-start(bf16[192,128]{1,0:T(8,128)(2,1)S(1)} %pack_elution.1.refs_3_), channel_id=1, source_target_pairs={{0,1},{1,0},{2,3},{3,2},{4,5},{5,4},{6,7},{7,6},{8,9},{9,8},{10,11... | collective-permute-start | bytes 147464 | tf_op jit(solution)/shard_map/ppermute | solution.py:366
  25.4 7.1 %collective-permute-start.7 = (bf16[192,128]{1,0:T(8,128)(2,1)S(1)}, bf16[192,128]{1,0:T(8,128)(2,1)S(1)}, u32[]{:S(2)}, u32[]{:S(2)}) collective-permute-start(bf16[192,128]{1,0:T(8,128)(2,1)S(1)} %pack_elution.1.refs_3_), channel_id=1, source_target_pairs={{0,3},{1,2},{2,5},{3,4},{4,7},{5,6},{6,9},{7,8},{8,11},{9,10},{10,... | collective-permute-start | bytes 147464 | tf_op jit(solution)/shard_map/ppermute | solution.py:406
  46.4 1.6 %collective-permute-start.8 = (f32[544,128]{1,0:T(8,128)S(1)}, f32[544,128]{1,0:T(8,128)S(1)}, u32[]{:S(2)}, u32[]{:S(2)}) collective-permute-start(f32[544,128]{1,0:T(8,128)S(1)} %get-tuple-element.15), channel_id=1, source_target_pairs={{0,2},{2,0},{4,6},{6,4},{8,10},{10,8},{12,14},{14,12},{16,18},{18,... | collective-permute-start | bytes 835592 | tf_op jit(solution)/shard_map/ppermute | solution.py:366
  48.0 6.0 %collective-permute-start.9 = (f32[288,128]{1,0:T(8,128)S(1)}, f32[288,128]{1,0:T(8,128)S(1)}, u32[]{:S(2)}, u32[]{:S(2)}) collective-permute-start(f32[288,128]{1,0:T(8,128)S(1)} %reduce_stage.2), channel_id=1, source_target_pairs={{0,4},{2,6},{4,0},{6,2},{8,12},{10,14},{12,8},{14,10},{16,20},{18,... | collective-permute-start | bytes 442376 | tf_op jit(solution)/shard_map/ppermute | solution.py:366
  54.0 4.5 %collective-permute-start.10 = (f32[96,128]{1,0:T(8,128)S(1)}, f32[96,128]{1,0:T(8,128)S(1)}, u32[]{:S(2)}, u32[]{:S(2)}) collective-permute-start(f32[96,128]{1,0:T(8,128)S(1)} %get-tuple-element.16), channel_id=1, source_target_pairs={{0,8},{2,10},{4,12},{6,14},{8,0},{10,2},{12,4},{14,6},{16,24},{18,... | collective-permute-start | bytes 147464 | tf_op jit(solution)/shard_map/ppermute | solution.py:366
  54.1 5.3 %collective-permute-start.11 = (f32[96,128]{1,0:T(8,128)S(1)}, f32[96,128]{1,0:T(8,128)S(1)}, u32[]{:S(2)}, u32[]{:S(2)}) collective-permute-start(f32[96,128]{1,0:T(8,128)S(1)} %get-tuple-element.17), channel_id=1, source_target_pairs={{0,16},{2,18},{4,20},{6,22},{8,24},{10,26},{12,28},{14,30},{16,0},... | collective-permute-start | bytes 147464 | tf_op jit(solution)/shard_map/ppermute | solution.py:366
  56.4 5.9 %collective-permute-start.12 = (f32[96,128]{1,0:T(8,128)S(1)}, f32[96,128]{1,0:T(8,128)S(1)}, u32[]{:S(2)}, u32[]{:S(2)}) collective-permute-start(f32[96,128]{1,0:T(8,128)S(1)} %get-tuple-element.18), channel_id=1, source_target_pairs={{0,24},{2,26},{4,28},{6,30},{8,16},{10,18},{12,20},{14,22},{16,8},... | collective-permute-start | bytes 147464 | tf_op jit(solution)/shard_map/ppermute | solution.py:366
where the time goes:
time: 66.6 us; the launch traced here: 66.3 us
  waiting for transfers between devices  24.4 us (37%)
  Pallas kernels  22.6 us (34%)
  starting transfers between devices  14.9 us (22%)
  local copies, waits for them, and re-layouts  4.22 us (6%)
    ppermute x12, waiting for transfers between devices, swap(): return lax.ppermute(x, axes, [(i, i ^ value) for i in range(count)])  22.6 us
    ppermute x12, starting transfers between devices, swap(): return lax.ppermute(x, axes, [(i, i ^ value) for i in range(count)])  14.2 us
    pallas_call x1, Pallas kernels, product(): pl.pallas_call(functools.partial(product_kernel, len(models), planes), ou...  13.9 us
    pallas_call x3, Pallas kernels, small_call(): pl.pallas_call(kernel, out_shape=(jax.ShapeDtypeStruct(out_shape, jnp.flo...  3.99 us
    unnamed x16, local copies, waits for them, and re-layouts  3.38 us
    pallas_call x1, Pallas kernels, partial_model(): pl.pallas_call(functools.partial(model_kernel, places, planes), out_shape...  3.09 us
    ppermute x1, waiting for transfers between devices, on_device(): far = lax.ppermute(mine, axes, onward)  1.84 us
    pallas_call x1, Pallas kernels, circulant(): pl.pallas_call(circulant_kernel, out_shape=jax.ShapeDtypeStruct((2 * LANE...  1.45 us
  transfers between devices with their start and end apart: 13, of which 9 were waited for; matrix products, arithmetic and copies ran while one was open for 1% of the time, Pallas kernels for 2%

commit v1 on v0

--- a/solution.py
+++ b/solution.py
@@ -51,15 +51,22 @@
     )(elution.T)
 
 
-def circulant_kernel(w_ref, lane_ref, twid_ref, row_ref, u_ref):
+def circulant_kernel(w_ref, table_ref, u_ref):
     rows = w_ref.shape[1]
     w = w_ref[...]
     over_lanes = (((0,), (0,)), ((), ()))
-    a_re = f32_dot(w, lane_ref[0], over_lanes)
-    a_im = -f32_dot(w, lane_ref[1], over_lanes)
-    b_re = a_re * twid_ref[0] + a_im * twid_ref[1]
-    b_im = a_im * twid_ref[0] - a_re * twid_ref[1]
-    c = f32_dot(row_ref[0], b_re) + f32_dot(row_ref[1], b_im)
+
+    def table(at, height, width):
+        return table_ref[at : at + height, :width], table_ref[at + height : at + 2 * height, :width]
+
+    lane_cos, lane_sin = table(0, LANES, LANES)
+    twid_cos, twid_sin = table(2 * LANES, rows, LANES)
+    row_cos, row_sin = table(2 * LANES + 2 * rows, rows, rows)
+    a_re = f32_dot(w, lane_cos, over_lanes)
+    a_im = -f32_dot(w, lane_sin, over_lanes)
+    b_re = a_re * twid_cos + a_im * twid_sin
+    b_im = a_im * twid_cos - a_re * twid_sin
+    c = f32_dot(row_cos, b_re) + f32_dot(row_sin, b_im)
     sub = lax.broadcasted_iota(jnp.int32, (LANES, LANES), 0)
     lane = lax.broadcasted_iota(jnp.int32, (LANES, LANES), 1)
 
@@ -81,21 +88,25 @@
 
     def tables(a, b, period):
         angle = 2.0 * math.pi / period * ((a[:, None] * b[None, :]) % period)
-        return np.stack([np.cos(angle), np.sin(angle)])
+        return np.pad(np.concatenate([np.cos(angle), np.sin(angle)]), ((0, 0), (0, LANES - b.size)))
 
     lane_ids, row_ids = np.arange(LANES), np.arange(rows)
-    lane_table = tables(lane_ids, lane_ids, LANES).astype(np.float32)
-    twid_table = tables(row_ids, lane_ids, length).astype(np.float32)
-    row_table = (tables(row_ids, row_ids, rows) / length).astype(np.float32)
+    table = np.concatenate(
+        [
+            tables(lane_ids, lane_ids, LANES),
+            tables(row_ids, lane_ids, length),
+            tables(row_ids, row_ids, rows) / length,
+        ]
+    ).astype(np.float32)
     return pl.pallas_call(
         circulant_kernel,
         out_shape=jax.ShapeDtypeStruct((2 * LANES, length), jnp.bfloat16),
-        in_specs=vmem(4),
+        in_specs=vmem(2),
         out_specs=vmem(1)[0],
         compiler_params=pltpu.CompilerParams(vmem_limit_bytes=16 * MIB),
         cost_estimate=pl.CostEstimate(flops=2_000_000_000, bytes_accessed=4 * MIB, transcendentals=0),
         name="circulant_block",
-    )(bin_weight.reshape(LANES, rows), lane_table, twid_table, row_table)
+    )(bin_weight.reshape(LANES, rows), table)
 
 
 def model_kernel(places, planes, *refs):
@@ -162,26 +173,37 @@
     )(*gathered, u)
 
 
-def product_kernel(parts, planes, *refs):
-    i_ref = refs[0]
-    g_refs = refs[1 : 1 + parts]
-    if planes:
-        mine_ref, came_ref, near_ref, far_ref, amp_ref, lag_ref, keep_ref, send_ref = refs[1 + parts : 9 + parts]
-    else:
-        own_ref, amp_ref, lag_ref, num_ref, gram_ref = refs[1 + parts : 6 + parts]
-    window, terms, held, sems = refs[-4:]
-    run_count, bin_count, local_mz = i_ref.shape
+def shifted_terms(x, amps, lags, bin_count, terms):
+    components = x.shape[0]
+    out_count = -(-bin_count // LANES)
+    x = pltpu.roll(x, x.shape[1] - 1, 1)
+    height = 16
+    lane = lax.broadcasted_iota(jnp.int32, (height, LANES), 1)
+    for at in range(0, components, height):
+        vectors = [x[at : at + height, v * LANES : (v + 1) * LANES] for v in range(out_count + 2)]
+        for k in range(amps.shape[1]):
+            left = REACH - 1 - jnp.broadcast_to(lags[at : at + height, k : k + 1], lane.shape)
+            amp = jnp.broadcast_to(amps[at : at + height, k : k + 1], lane.shape)
+            source = lane + (left & (LANES - 1))
+            index = source & (LANES - 1)
+            far, same = left >= LANES, source < LANES
+            turned = [jnp.take_along_axis(v, index, axis=1, mode="promise_in_bounds") for v in vectors]
+            turned = [jnp.where(far, turned[v + 1], turned[v]) for v in range(out_count + 1)]
+            for v in range(out_count):
+                high, low = two_terms(amp * jnp.where(same, turned[v], turned[v + 1]))
+                width = min(LANES, bin_count - v * LANES)
+                to = slice(k * bin_count + v * LANES, k * bin_count + v * LANES + width)
+                terms[at : at + height, to] = high[:, :width]
+                terms[components + at : components + at + height, to] = low[:, :width]
+
+
+def elution_kernel(planes, *refs):
+    amp_ref, lag_ref, terms, window = refs[-4:]
     components = amp_ref.shape[1]
-    chunks = sems.shape[0]
-    chunk = local_mz // chunks
-    copies = []
-    for n in range(chunks):
-        part = pl.ds(n * chunk, chunk)
-        copies.append(pltpu.make_async_copy(i_ref.at[:, :, part], held.at[:, :, part], sems.at[n]))
-        copies[-1].start()
-
+    bin_count = terms.shape[1] // amp_ref.shape[0]
     freq_rank = lax.axis_index("freq")
     if planes:
+        mine_ref, came_ref, near_ref, far_ref = refs[:4]
         mz_rank = lax.axis_index("mz")
         freq_count = 2 * came_ref.shape[0]
         rows = mine_ref.shape[0]
@@ -196,63 +218,77 @@
         ):
             window[pl.ds(pl.multiple_of((2 * block + half) * rows, 64), rows), :] = values
     else:
+        own_ref = refs[0]
         step = own_ref.shape[1]
         steps = own_ref.shape[0]
         first = lax.rem(freq_rank * bin_count + steps * step - REACH, steps * step) // step
         skip = 0
         for j in range(window.shape[0] // step):
             window[j * step : (j + 1) * step, :] = own_ref[pl.ds(lax.rem(first + j, steps), 1)][0]
+    pieces = []
+    for at in range(skip, window.shape[0], LANES):
+        piece = window[at : at + LANES, :].astype(jnp.float32).T
+        pieces.append(piece[:components] + piece[components:])
+    shifted_terms(jnp.concatenate(pieces, axis=1), amp_ref[...].T, lag_ref[...].T, bin_count, terms)
+
+
+def elution_terms(elutions, loadings, shifts, bin_count):
+    run_count, components = loadings.shape
+    places = -(-(bin_count + REACH) // LANES)
+    planes = len(elutions) > 1
+    return pl.pallas_call(
+        functools.partial(elution_kernel, planes),
+        out_shape=jax.ShapeDtypeStruct((2 * components, run_count * bin_count), jnp.bfloat16),
+        in_specs=vmem(len(elutions) + 2),
+        out_specs=vmem(1)[0],
+        scratch_shapes=[pltpu.VMEM((2 * bin_count if planes else places * LANES, LANES), jnp.bfloat16)],
+        compiler_params=pltpu.CompilerParams(vmem_limit_bytes=12 * MIB),
+        cost_estimate=pl.CostEstimate(flops=1_000_000_000, bytes_accessed=2 * MIB, transcendentals=0),
+        name="elution_terms",
+    )(*elutions, loadings, shifts)
+
+
+def product_kernel(parts, planes, *refs):
+    i_ref = refs[0]
+    g_refs = refs[1 : 1 + parts]
+    elution_ref, amp_ref, lag_ref, num_ref, other_ref, terms, held, sems = refs[1 + parts :]
+    run_count, bin_count, local_mz = i_ref.shape
+    components = amp_ref.shape[1]
+    chunks = sems.shape[0]
+    chunk = local_mz // chunks
+    copies = []
+    for n in range(chunks):
+        part = pl.ds(n * chunk, chunk)
+        copies.append(pltpu.make_async_copy(i_ref.at[:, :, part], held.at[:, :, part], sems.at[n]))
+        copies[-1].start()
+
     g = g_refs[0][...]
     for ref in g_refs[1:]:
         g = g + ref[...]
-    pieces = []
-    for a in range(g.shape[1] // LANES):
-        piece = window[skip + a * LANES : skip + (a + 1) * LANES, :].astype(jnp.float32).T
-        pieces.append(piece[:components] + piece[components:])
-    base = jnp.concatenate([g, jnp.concatenate(pieces, axis=1)], axis=0)
-    span = -(-bin_count // LANES) * LANES
-    amps, lags = amp_ref[...].T, lag_ref[...].T
-    for k in range(run_count):
-        lag = lags[:, k : k + 1]
-        left = REACH - 1 - jnp.concatenate([lag, lag], axis=0)
-        y = base
-        for bit in (7, 6, 5, 4, 3, 2, 1, 0):
-            move = 1 << bit
-            y = jnp.where((left & move) != 0, pltpu.roll(y, y.shape[1] - move, 1), y)
-            if move == LANES:
-                y = y[:, : span + LANES]
-        y = pltpu.roll(y, y.shape[1] - 1, 1)[:, :bin_count]
-        amp = amps[:, k : k + 1]
-        high, low = two_terms(y * jnp.concatenate([amp, amp], axis=0))
-        part = slice(k * bin_count, (k + 1) * bin_count)
-        terms[0:components, part] = high[:components]
-        terms[components : 2 * components, part] = low[:components]
-        terms[2 * components : 3 * components, part] = high[components:]
-        terms[3 * components :, part] = low[components:]
+    shifted_terms(g, amp_ref[...].T, lag_ref[...].T, bin_count, terms)
     gram = lax.dot_general(
-        terms[0 : 2 * components, :],
-        terms[2 * components :, :],
-        (((1,), (1,)), ((), ())),
-        preferred_element_type=jnp.float32,
+        terms[...], elution_ref[...], (((1,), (1,)), ((), ())), preferred_element_type=jnp.float32
     )
     gram = gram[:components] + gram[components:]
     gram = gram[:, :components] + gram[:, components:]
     if planes:
+        keep_ref, send_ref = num_ref, other_ref
         half = components // 2
         gram = jnp.concatenate([gram[:half], gram[half:]], axis=1)
         keep_ref[chunks * components :, :] = gram
         send_ref[chunks * components :, :] = gram
     else:
-        gram_ref[...] = gram
+        other_ref[...] = gram
 
     for n in range(chunks):
         copies[n].wait()
         data = held[:, :, n * chunk : (n + 1) * chunk].reshape(run_count * bin_count, chunk)
-        made = jnp.dot(terms[0 : 2 * components, :], data, preferred_element_type=jnp.float32)
+        made = jnp.dot(terms[...], data, preferred_element_type=jnp.float32)
         made = made[:components] + made[components:]
         if planes:
+            freq_rank = lax.axis_index("freq")
             core = freq_rank & 1
-            place = block_place(lax.bitwise_xor(freq_rank, 2 * n + core), freq_count)
+            place = block_place(lax.bitwise_xor(freq_rank, 2 * n + core), 2 * chunks)
             at = pl.ds(pl.multiple_of(place * components, components), components)
             even, odd = made[:, :LANES], made[:, LANES:]
             keep_ref[at, :] = jnp.where(core == 0, even, odd)
@@ -261,26 +297,22 @@
             num_ref[:, n * chunk : (n + 1) * chunk] = made
 
 
-def product(intensity, models, elutions, loadings, shifts):
+def product(intensity, models, elution, loadings, shifts, planes):
     run_count, bin_count, local_mz = intensity.shape
     components = loadings.shape[1]
     chunk = 2 * LANES
     chunks = local_mz // chunk
-    planes = len(elutions) > 1
     if planes:
         out_shapes = [(chunks * components + components // 2, LANES)] * 2
-        window_rows = 2 * bin_count
     else:
         out_shapes = [(components, local_mz), (components, components)]
-        window_rows = models[0].shape[1]
     return pl.pallas_call(
         functools.partial(product_kernel, len(models), planes),
         out_shape=tuple(jax.ShapeDtypeStruct(shape, jnp.float32) for shape in out_shapes),
-        in_specs=[pl.BlockSpec(memory_space=pl.ANY)] + vmem(len(models) + len(elutions) + 2),
+        in_specs=[pl.BlockSpec(memory_space=pl.ANY)] + vmem(len(models) + 3),
         out_specs=tuple(vmem(2)),
         scratch_shapes=[
-            pltpu.VMEM((window_rows, LANES), jnp.bfloat16),
-            pltpu.VMEM((4 * components, run_count * bin_count), jnp.bfloat16),
+            pltpu.VMEM((2 * components, run_count * bin_count), jnp.bfloat16),
             pltpu.VMEM(intensity.shape, jnp.bfloat16),
             pltpu.SemaphoreType.DMA((chunks,)),
         ],
@@ -289,7 +321,7 @@
             flops=8_000_000_000, bytes_accessed=2 * intensity.size, transcendentals=0
         ),
         name="model_products",
-    )(intensity, *models, *elutions, loadings, shifts)
+    )(intensity, *models, elution, loadings, shifts)
 
 
 def eliminate(gram, right):
@@ -387,16 +419,11 @@
     if not planes:
         gathered = lax.all_gather(mine, axes, axis=0).reshape(-1, math.gcd(bin_count, LANES), LANES)
         g = partial_model((gathered,), circulant(bin_weight), bin_count, components)
-        numerator, gram = product(intensity, (g,), (gathered,), loadings, shifts)
+        shifted = elution_terms((gathered,), loadings, shifts, bin_count)
+        numerator, gram = product(intensity, (g,), shifted, loadings, shifts, planes)
         gram = lax.psum(gram, "freq")
         owned = lax.psum_scatter(numerator, "freq", scatter_dimension=1, tiled=True)
         return small_call(solve_kernel, (components, own), "solve", gram, owned)[0]
-    z_steps = range(4, freq_count, 4)
-    held = jnp.stack([mine] + [swap(mine, "freq", freq_count, step) for step in z_steps])
-    held = jnp.concatenate([held, swap(held, "freq", freq_count, 2)], axis=0)
-    u = circulant(bin_weight)
-    held, u = lax.optimization_barrier((held, u))
-    came = swap(held, "freq", freq_count, 1)
     near = swap(mine, "mz", mz_count, 1)
     onward = [
         (f * mz_count + y, (f + 1) % freq_count * mz_count + 1 - y)
@@ -404,9 +431,17 @@
         for y in range(mz_count)
     ]
     far = lax.ppermute(mine, axes, onward)
+    z_steps = range(4, freq_count, 4)
+    held = jnp.stack([mine] + [swap(mine, "freq", freq_count, step) for step in z_steps])
+    held, near, far, bin_weight = lax.optimization_barrier((held, near, far, bin_weight))
+    held = jnp.concatenate([held, swap(held, "freq", freq_count, 2)], axis=0)
+    u = circulant(bin_weight)
+    held, u = lax.optimization_barrier((held, u))
+    came = swap(held, "freq", freq_count, 1)
     g = partial_model((held, came), u, bin_count, components)
     models = (g, swap(g, "mz", mz_count, 1))
-    keep, send = product(intensity, models, (mine, came, near, far), loadings, shifts)
+    shifted = elution_terms((mine, came, near, far), loadings, shifts, bin_count)
+    keep, send = product(intensity, models, shifted, loadings, shifts, planes)
     tail = components // 2
     quarter = freq_count // 4 * components
     parts = [keep, swap(send, "freq", freq_count, 1)]

time: 66.6 us -> 59.5 us (0.89)
  Pallas kernels: 22.6 us -> 18.6 us
  local copies, waits for them, and re-layouts: 4.22 us -> 2.6 us
  waiting for transfers between devices: 24.4 us -> 23.3 us
    pallas_call x1, Pallas kernels: 13.9 us -> 7.02 us  [product(): pl.pallas_call(functools.partial(product_kernel, len(models), planes), ou...]
    pallas_call x0 -> x1, Pallas kernels: none -> 2.91 us  [elution_terms(): pl.pallas_call(functools.partial(elution_kernel, planes), out_shape=jax.S...]
    ppermute x12, waiting for transfers between devices: 22.6 us -> 20.5 us  [swap(): return lax.ppermute(x, axes, [(i, i ^ value) for i in range(count)])]
    unnamed x16 -> x8, local copies, waits for them, and re-layouts: 3.38 us -> 1.78 us
    ppermute x1, waiting for transfers between devices: 1.84 us -> 2.73 us  [on_device(): far = lax.ppermute(mine, axes, onward)]
  transfers between devices with their start and end apart: 13 -> 13, of which waited for: 9 -> 9; matrix products, arithmetic and copies ran while one was open for 1% -> 1% of each run, Pallas kernels for 2% -> 7%
where the time goes in v1:
time: 59.5 us; the launch traced here: 59.3 us
  waiting for transfers between devices  23.3 us (39%)
  Pallas kernels  18.6 us (31%)
  starting transfers between devices  14.7 us (25%)
  local copies, waits for them, and re-layouts  2.6 us (4%)
    ppermute x12, waiting for transfers between devices, swap(): return lax.ppermute(x, axes, [(i, i ^ value) for i in range(count)])  20.5 us
    ppermute x12, starting transfers between devices, swap(): return lax.ppermute(x, axes, [(i, i ^ value) for i in range(count)])  14.3 us
    pallas_call x1, Pallas kernels, product(): pl.pallas_call(functools.partial(product_kernel, len(models), planes), ou...  7.02 us
    pallas_call x3, Pallas kernels, small_call(): pl.pallas_call(kernel, out_shape=(jax.ShapeDtypeStruct(out_shape, jnp.flo...  3.99 us
    pallas_call x1, Pallas kernels, partial_model(): pl.pallas_call(functools.partial(model_kernel, places, planes), out_shape...  3.04 us
    pallas_call x1, Pallas kernels, elution_terms(): pl.pallas_call(functools.partial(elution_kernel, planes), out_shape=jax.S...  2.91 us
    ppermute x1, waiting for transfers between devices, on_device(): far = lax.ppermute(mine, axes, onward)  2.73 us
    unnamed x8, local copies, waits for them, and re-layouts  1.78 us
  transfers between devices with their start and end apart: 13, of which 9 were waited for; matrix products, arithmetic and copies ran while one was open for 1% of the time, Pallas kernels for 7%

profile of v1, /device:TPU:0, one launch (start us, length us, event | category | flops | bytes accessed | tf_op | source)
XLA Modules:
  0.0 59.3 jit_solution(10040633959870267254)
XLA Ops:
  0.0 0.0 copy-start
  0.0 0.8 %copy-done = f32[192,64]{0,1:T(8,128)S(1)} copy-done((f32[192,64]{0,1:T(8,128)S(1)}, f32[192,64]{0,1:T(8,128)}, u32[]{:S(2)}) %copy-start) | copy-done | bytes 49176
  0.8 0.0 copy-start.1
  0.8 0.0 copy-start.2
  0.8 0.2 pack_elution.1.refs_0_
  1.0 5.1 %collective-permute-start.2 = (bf16[192,128]{1,0:T(8,128)(2,1)S(1)}, bf16[192,128]{1,0:T(8,128)(2,1)S(1)}, u32[]{:S(2)}, u32[]{:S(2)}) collective-permute-start(bf16[192,128]{1,0:T(8,128)(2,1)S(1)} %pack_elution.1.refs_0_), channel_id=1, source_target_pairs={{0,24},{2,26},{4,28},{6,30},{8,16},{10,18},{12,20},{14,22},{16,8},... | collective-permute-start | bytes 147464 | tf_op jit(solution)/shard_map/ppermute | solution.py:398
  6.1 0.0 collective-permute-start.1
  6.1 0.6 %collective-permute-start = (bf16[192,128]{1,0:T(8,128)(2,1)S(1)}, bf16[192,128]{1,0:T(8,128)(2,1)S(1)}, u32[]{:S(2)}, u32[]{:S(2)}) collective-permute-start(bf16[192,128]{1,0:T(8,128)(2,1)S(1)} %pack_elution.1.refs_0_), channel_id=1, source_target_pairs={{0,8},{2,10},{4,12},{6,14},{8,0},{10,2},{12,4},{14,6},{16,24},{18,... | collective-permute-start | bytes 147464 | tf_op jit(solution)/shard_map/ppermute | solution.py:398
  6.8 0.4 collective-permute-start.4
  7.2 1.3 %collective-permute-start.3 = (bf16[192,128]{1,0:T(8,128)(2,1)S(1)}, bf16[192,128]{1,0:T(8,128)(2,1)S(1)}, u32[]{:S(2)}, u32[]{:S(2)}) collective-permute-start(bf16[192,128]{1,0:T(8,128)(2,1)S(1)} %pack_elution.1.refs_0_), channel_id=1, source_target_pairs={{0,1},{1,0},{2,3},{3,2},{4,5},{5,4},{6,7},{7,6},{8,9},{9,8},{10,11... | collective-permute-start | bytes 147464 | tf_op jit(solution)/shard_map/ppermute | solution.py:398
  8.4 0.0 collective-permute-done.2
  8.4 2.7 %collective-permute-done.1 = bf16[192,128]{1,0:T(8,128)(2,1)S(1)} collective-permute-done((bf16[192,128]{1,0:T(8,128)(2,1)S(1)}, bf16[192,128]{1,0:T(8,128)(2,1)S(1)}, u32[]{:S(2)}, u32[]{:S(2)}) %collective-permute-start.1) | collective-permute-done | bytes 49184 | tf_op jit(solution)/shard_map/ppermute | solution.py:398
  11.1 0.0 collective-permute-done
  11.2 2.7 %collective-permute-done.4.refs_3_ = bf16[192,128]{1,0:T(8,128)(2,1)S(1)} collective-permute-done((bf16[192,128]{1,0:T(8,128)(2,1)S(1)}, bf16[192,128]{1,0:T(8,128)(2,1)S(1)}, u32[]{:S(2)}, u32[]{:S(2)}) %collective-permute-start.4) | collective-permute-done | bytes 49184 | tf_op jit(solution)/shard_map/ppermute | solution.py:433
  13.9 0.0 collective-permute-done.3.refs_2_
  13.9 0.0 collective-permute-start.5
  13.9 0.8 %reshape.3.w_ref = f32[128,48]{1,0:T(8,128)S(1)} reshape(f32[6144]{0:T(1024)} %param.10) | data formatting | bytes 49152 | tf_op jit(solution)/shard_map/reshape | solution.py:109
  14.7 0.0 copy-start.3
  14.7 0.9 %copy-done.3 = f32[448,128]{1,0:T(8,128)S(1)} copy-done((f32[448,128]{1,0:T(8,128)S(1)}, f32[448,128]{1,0:T(8,128)}, u32[]{:S(2)}) %copy-start.3) | copy-done | bytes 229400
  15.7 1.5 %circulant_block.1.refs_2_ = bf16[256,6144]{1,0:T(8,128)(2,1)S(1)} custom-call(f32[128,48]{1,0:T(8,128)S(1)} %reshape.3.w_ref, f32[448,128]{1,0:T(8,128)S(1)} %copy-done.3), custom_call_target="tpu_custom_call" | custom-call | flops 2000000000 | bytes 4194304 | tf_op jit(solution)/shard_map/circulant_block/pallas_call | solution.py:101
  17.1 2.4 %collective-permute-done.5 = bf16[4,192,128]{2,1,0:T(8,128)(2,1)S(1)} collective-permute-done((bf16[4,192,128]{2,1,0:T(8,128)(2,1)S(1)}, bf16[4,192,128]{2,1,0:T(8,128)(2,1)S(1)}, u32[]{:S(2)}, u32[]{:S(2)}) %collective-permute-start.5) | collective-permute-done | bytes 196640 | tf_op jit(solution)/shard_map/ppermute | solution.py:398
  19.6 0.1 collective-permute-start.6
  19.7 1.7 %collective-permute-done.6.refs_1_ = bf16[8,192,128]{2,1,0:T(8,128)(2,1)S(1)} collective-permute-done((bf16[8,192,128]{2,1,0:T(8,128)(2,1)S(1)}, bf16[8,192,128]{2,1,0:T(8,128)(2,1)S(1)}, u32[]{:S(2)}, u32[]{:S(2)}) %collective-permute-start.6) | collective-permute-done | bytes 393248 | tf_op jit(solution)/shard_map/ppermute | solution.py:398
  21.4 3.0 %partial_model.1.refs_1_ = f32[64,640]{1,0:T(8,128)S(1)} custom-call(bf16[8,192,128]{2,1,0:T(8,128)(2,1)S(1)} %pad_maximum_fusion.refs_0_, bf16[8,192,128]{2,1,0:T(8,128)(2,1)S(1)} %collective-permute-done.6.refs_1_, bf16[256,6144]{1,0:T(8,128)(2,1)S(1)} %circulant_block.1.refs_2_), custom_call_target="tpu_custom_call" | custom-call | flops 2000000000 | bytes 4194304 | tf_op jit(solution)/shard_map/partial_model/pallas_call | solution.py:164
  24.4 1.7 %collective-permute-start.7 = (f32[64,640]{1,0:T(8,128)S(1)}, f32[64,640]{1,0:T(8,128)S(1)}, u32[]{:S(2)}, u32[]{:S(2)}) collective-permute-start(f32[64,640]{1,0:T(8,128)S(1)} %partial_model.1.refs_1_), channel_id=1, source_target_pairs={{0,1},{1,0},{2,3},{3,2},{4,5},{5,4},{6,7},{7,6},{8,9},{9,8},{10,11... | collective-permute-start | bytes 491528 | tf_op jit(solution)/shard_map/ppermute | solution.py:398
  26.2 0.0 copy-done.1
  26.2 0.0 copy-done.2
  26.2 2.9 %elution_terms.1.refs_3_ = bf16[128,3072]{1,0:T(8,128)(2,1)S(1)} custom-call(bf16[192,128]{1,0:T(8,128)(2,1)S(1)} %pack_elution.1.refs_0_, bf16[8,192,128]{2,1,0:T(8,128)(2,1)S(1)} %collective-permute-done.6.refs_1_, bf16[192,128]{1,0:T(8,128)(2,1)S(1)} %collective-permute-done.3.refs_2_, bf16[192,128]{1,0:T(8,128)(2,1)S(1)} %collective-permute-done.4.refs_3_, ...), custom_call_target="tpu_custom_call" | custom-call | flops 1000000000 | bytes 2097152 | tf_op jit(solution)/shard_map/elution_terms/pallas_call | solution.py:239
  29.1 1.7 %collective-permute-done.7.refs_2_ = f32[64,640]{1,0:T(8,128)S(1)} collective-permute-done((f32[64,640]{1,0:T(8,128)S(1)}, f32[64,640]{1,0:T(8,128)S(1)}, u32[]{:S(2)}, u32[]{:S(2)}) %collective-permute-start.7) | collective-permute-done | bytes 163872 | tf_op jit(solution)/shard_map/ppermute | solution.py:398
  30.7 7.0 %model_products.1 = (f32[544,128]{1,0:T(8,128)S(1)}, f32[544,128]{1,0:T(8,128)S(1)}) custom-call(bf16[8,384,2048]{2,1,0:T(8,128)(2,1)} %refs_0_.1, f32[64,640]{1,0:T(8,128)S(1)} %partial_model.1.refs_1_, f32[64,640]{1,0:T(8,128)S(1)} %collective-permute-done.7.refs_2_, bf16[128,3072]{1,0:T(8,128)(2,1)S(1)} %elution_terms.1.refs_3_, f32[8,64]{1,0:T(8,128)S(1)} %copy-done.1, ...), custom_call_target="tpu_custom_call" | custom-call | flops 8000000000 | bytes 12582912 | tf_op jit(solution)/shard_map/model_products/pallas_call | solution.py:309
  37.8 0.1 collective-permute-start.8
  37.9 1.5 %collective-permute-done.8.refs_1_ = f32[544,128]{1,0:T(8,128)S(1)} collective-permute-done((f32[544,128]{1,0:T(8,128)S(1)}, f32[544,128]{1,0:T(8,128)S(1)}, u32[]{:S(2)}, u32[]{:S(2)}) %collective-permute-start.8) | collective-permute-done | bytes 278560 | tf_op jit(solution)/shard_map/ppermute | solution.py:398
  39.4 0.9 %collective-permute-start.9 = (f32[288,128]{1,0:T(8,128)S(1)}, f32[288,128]{1,0:T(8,128)S(1)}, u32[]{:S(2)}, u32[]{:S(2)}) collective-permute-start(f32[288,128]{1,0:T(8,128)S(1)} %reduce_stage.2), channel_id=1, source_target_pairs={{0,4},{2,6},{4,0},{6,2},{8,12},{10,14},{12,8},{14,10},{16,20},{18,... | collective-permute-start | bytes 442376 | tf_op jit(solution)/shard_map/ppermute | solution.py:398
  40.4 5.0 %collective-permute-done.9.refs_2_ = f32[288,128]{1,0:T(8,128)S(1)} collective-permute-done((f32[288,128]{1,0:T(8,128)S(1)}, f32[288,128]{1,0:T(8,128)S(1)}, u32[]{:S(2)}, u32[]{:S(2)}) %collective-permute-start.9) | collective-permute-done | bytes 147488 | tf_op jit(solution)/shard_map/ppermute | solution.py:398
  45.4 1.5 %collective-permute-start.10 = (f32[96,128]{1,0:T(8,128)S(1)}, f32[96,128]{1,0:T(8,128)S(1)}, u32[]{:S(2)}, u32[]{:S(2)}) collective-permute-start(f32[96,128]{1,0:T(8,128)S(1)} %get-tuple-element.24), channel_id=1, source_target_pairs={{0,8},{2,10},{4,12},{6,14},{8,0},{10,2},{12,4},{14,6},{16,24},{18,... | collective-permute-start | bytes 147464 | tf_op jit(solution)/shard_map/ppermute | solution.py:398
  46.9 2.6 %collective-permute-start.11 = (f32[96,128]{1,0:T(8,128)S(1)}, f32[96,128]{1,0:T(8,128)S(1)}, u32[]{:S(2)}, u32[]{:S(2)}) collective-permute-start(f32[96,128]{1,0:T(8,128)S(1)} %get-tuple-element.25), channel_id=1, source_target_pairs={{0,16},{2,18},{4,20},{6,22},{8,24},{10,26},{12,28},{14,30},{16,0},... | collective-permute-start | bytes 147464 | tf_op jit(solution)/shard_map/ppermute | solution.py:398
  49.5 0.4 collective-permute-start.12
  49.9 0.0 collective-permute-done.10.refs_3_
  49.9 2.5 %collective-permute-done.11.refs_4_ = f32[96,128]{1,0:T(8,128)S(1)} collective-permute-done((f32[96,128]{1,0:T(8,128)S(1)}, f32[96,128]{1,0:T(8,128)S(1)}, u32[]{:S(2)}, u32[]{:S(2)}) %collective-permute-start.11) | collective-permute-done | bytes 49184 | tf_op jit(solution)/shard_map/ppermute | solution.py:398
  52.4 3.0 %collective-permute-done.12.refs_5_ = f32[96,128]{1,0:T(8,128)S(1)} collective-permute-done((f32[96,128]{1,0:T(8,128)S(1)}, f32[96,128]{1,0:T(8,128)S(1)}, u32[]{:S(2)}, u32[]{:S(2)}) %collective-permute-start.12) | collective-permute-done | bytes 49184 | tf_op jit(solution)/shard_map/ppermute | solution.py:398
  55.3 3.9 %solve.1 = f32[64,128]{1,0:T(8,128)} custom-call(f32[544,128]{1,0:T(8,128)S(1)} %get-tuple-element.22.refs_0_, f32[544,128]{1,0:T(8,128)S(1)} %collective-permute-done.8.refs_1_, f32[288,128]{1,0:T(8,128)S(1)} %collective-permute-done.9.refs_2_, f32[96,128]{1,0:T(8,128)S(1)} %collective-permute-done.10.refs_3_, ...), custom_call_target="tpu_custom_call" | custom-call | tf_op jit(solution)/shard_map/solve/pallas_call | solution.py:386
  (4 shorter events, 0.1 us)
Async XLA Ops:
  0.0 0.8 %copy-start = (f32[192,64]{0,1:T(8,128)S(1)}, f32[192,64]{0,1:T(8,128)}, u32[]{:S(2)}) copy-start(f32[192,64]{0,1:T(8,128)} %param.7) | copy-start | bytes 147460
  0.8 25.3 %copy-start.1 = (f32[8,64]{1,0:T(8,128)S(1)}, f32[8,64]{1,0:T(8,128)}, u32[]{:S(2)}) copy-start(f32[8,64]{1,0:T(8,128)} %refs_4_.3) | copy-start | bytes 6148
  0.8 25.3 %copy-start.2 = (s32[8,64]{1,0:T(8,128)S(1)}, s32[8,64]{1,0:T(8,128)}, u32[]{:S(2)}) copy-start(s32[8,64]{1,0:T(8,128)} %refs_5_.3) | copy-start | bytes 6148
  1.0 7.4 %collective-permute-start.2 = (bf16[192,128]{1,0:T(8,128)(2,1)S(1)}, bf16[192,128]{1,0:T(8,128)(2,1)S(1)}, u32[]{:S(2)}, u32[]{:S(2)}) collective-permute-start(bf16[192,128]{1,0:T(8,128)(2,1)S(1)} %pack_elution.1.refs_0_), channel_id=1, source_target_pairs={{0,24},{2,26},{4,28},{6,30},{8,16},{10,18},{12,20},{14,22},{16,8},... | collective-permute-start | bytes 147464 | tf_op jit(solution)/shard_map/ppermute | solution.py:398
  6.1 5.0 %collective-permute-start.1 = (bf16[192,128]{1,0:T(8,128)(2,1)S(1)}, bf16[192,128]{1,0:T(8,128)(2,1)S(1)}, u32[]{:S(2)}, u32[]{:S(2)}) collective-permute-start(bf16[192,128]{1,0:T(8,128)(2,1)S(1)} %pack_elution.1.refs_0_), channel_id=1, source_target_pairs={{0,16},{2,18},{4,20},{6,22},{8,24},{10,26},{12,28},{14,30},{16,0},... | collective-permute-start | bytes 147464 | tf_op jit(solution)/shard_map/ppermute | solution.py:398
  6.1 5.0 %collective-permute-start = (bf16[192,128]{1,0:T(8,128)(2,1)S(1)}, bf16[192,128]{1,0:T(8,128)(2,1)S(1)}, u32[]{:S(2)}, u32[]{:S(2)}) collective-permute-start(bf16[192,128]{1,0:T(8,128)(2,1)S(1)} %pack_elution.1.refs_0_), channel_id=1, source_target_pairs={{0,8},{2,10},{4,12},{6,14},{8,0},{10,2},{12,4},{14,6},{16,24},{18,... | collective-permute-start | bytes 147464 | tf_op jit(solution)/shard_map/ppermute | solution.py:398
  6.8 7.1 %collective-permute-start.4 = (bf16[192,128]{1,0:T(8,128)(2,1)S(1)}, bf16[192,128]{1,0:T(8,128)(2,1)S(1)}, u32[]{:S(2)}, u32[]{:S(2)}) collective-permute-start(bf16[192,128]{1,0:T(8,128)(2,1)S(1)} %pack_elution.1.refs_0_), channel_id=1, source_target_pairs={{0,3},{1,2},{2,5},{3,4},{4,7},{5,6},{6,9},{7,8},{8,11},{9,10},{10,... | collective-permute-start | bytes 147464 | tf_op jit(solution)/shard_map/ppermute | solution.py:433
  7.2 6.7 %collective-permute-start.3 = (bf16[192,128]{1,0:T(8,128)(2,1)S(1)}, bf16[192,128]{1,0:T(8,128)(2,1)S(1)}, u32[]{:S(2)}, u32[]{:S(2)}) collective-permute-start(bf16[192,128]{1,0:T(8,128)(2,1)S(1)} %pack_elution.1.refs_0_), channel_id=1, source_target_pairs={{0,1},{1,0},{2,3},{3,2},{4,5},{5,4},{6,7},{7,6},{8,9},{9,8},{10,11... | collective-permute-start | bytes 147464 | tf_op jit(solution)/shard_map/ppermute | solution.py:398
  13.9 5.7 %collective-permute-start.5 = (bf16[4,192,128]{2,1,0:T(8,128)(2,1)S(1)}, bf16[4,192,128]{2,1,0:T(8,128)(2,1)S(1)}, u32[]{:S(2)}, u32[]{:S(2)}) collective-permute-start(bf16[4,192,128]{2,1,0:T(8,128)(2,1)S(1)} %pad_maximum_fusion.1), channel_id=1, source_target_pairs={{0,4},{2,6},{4,0},{6,2},{8,12},{10,14},{12,8},{14,10},{16,20},{18,... | collective-permute-start | bytes 589832 | tf_op jit(solution)/shard_map/ppermute | solution.py:398
  14.7 0.9 %copy-start.3 = (f32[448,128]{1,0:T(8,128)S(1)}, f32[448,128]{1,0:T(8,128)}, u32[]{:S(2)}) copy-start(f32[448,128]{1,0:T(8,128)} %constant.2.clone.table_ref) | copy-start | bytes 688132
  19.6 1.8 %collective-permute-start.6 = (bf16[8,192,128]{2,1,0:T(8,128)(2,1)S(1)}, bf16[8,192,128]{2,1,0:T(8,128)(2,1)S(1)}, u32[]{:S(2)}, u32[]{:S(2)}) collective-permute-start(bf16[8,192,128]{2,1,0:T(8,128)(2,1)S(1)} %pad_maximum_fusion.refs_0_), channel_id=1, source_target_pairs={{0,2},{2,0},{4,6},{6,4},{8,10},{10,8},{12,14},{14,12},{16,18},{18,... | collective-permute-start | bytes 1179656 | tf_op jit(solution)/shard_map/ppermute | solution.py:398
  24.4 6.3 %collective-permute-start.7 = (f32[64,640]{1,0:T(8,128)S(1)}, f32[64,640]{1,0:T(8,128)S(1)}, u32[]{:S(2)}, u32[]{:S(2)}) collective-permute-start(f32[64,640]{1,0:T(8,128)S(1)} %partial_model.1.refs_1_), channel_id=1, source_target_pairs={{0,1},{1,0},{2,3},{3,2},{4,5},{5,4},{6,7},{7,6},{8,9},{9,8},{10,11... | collective-permute-start | bytes 491528 | tf_op jit(solution)/shard_map/ppermute | solution.py:398
  37.8 1.6 %collective-permute-start.8 = (f32[544,128]{1,0:T(8,128)S(1)}, f32[544,128]{1,0:T(8,128)S(1)}, u32[]{:S(2)}, u32[]{:S(2)}) collective-permute-start(f32[544,128]{1,0:T(8,128)S(1)} %get-tuple-element.23), channel_id=1, source_target_pairs={{0,2},{2,0},{4,6},{6,4},{8,10},{10,8},{12,14},{14,12},{16,18},{18,... | collective-permute-start | bytes 835592 | tf_op jit(solution)/shard_map/ppermute | solution.py:398
  39.4 6.0 %collective-permute-start.9 = (f32[288,128]{1,0:T(8,128)S(1)}, f32[288,128]{1,0:T(8,128)S(1)}, u32[]{:S(2)}, u32[]{:S(2)}) collective-permute-start(f32[288,128]{1,0:T(8,128)S(1)} %reduce_stage.2), channel_id=1, source_target_pairs={{0,4},{2,6},{4,0},{6,2},{8,12},{10,14},{12,8},{14,10},{16,20},{18,... | collective-permute-start | bytes 442376 | tf_op jit(solution)/shard_map/ppermute | solution.py:398
  45.4 4.5 %collective-permute-start.10 = (f32[96,128]{1,0:T(8,128)S(1)}, f32[96,128]{1,0:T(8,128)S(1)}, u32[]{:S(2)}, u32[]{:S(2)}) collective-permute-start(f32[96,128]{1,0:T(8,128)S(1)} %get-tuple-element.24), channel_id=1, source_target_pairs={{0,8},{2,10},{4,12},{6,14},{8,0},{10,2},{12,4},{14,6},{16,24},{18,... | collective-permute-start | bytes 147464 | tf_op jit(solution)/shard_map/ppermute | solution.py:398
  46.9 5.5 %collective-permute-start.11 = (f32[96,128]{1,0:T(8,128)S(1)}, f32[96,128]{1,0:T(8,128)S(1)}, u32[]{:S(2)}, u32[]{:S(2)}) collective-permute-start(f32[96,128]{1,0:T(8,128)S(1)} %get-tuple-element.25), channel_id=1, source_target_pairs={{0,16},{2,18},{4,20},{6,22},{8,24},{10,26},{12,28},{14,30},{16,0},... | collective-permute-start | bytes 147464 | tf_op jit(solution)/shard_map/ppermute | solution.py:398
  49.5 5.9 %collective-permute-start.12 = (f32[96,128]{1,0:T(8,128)S(1)}, f32[96,128]{1,0:T(8,128)S(1)}, u32[]{:S(2)}, u32[]{:S(2)}) collective-permute-start(f32[96,128]{1,0:T(8,128)S(1)} %get-tuple-element.26), channel_id=1, source_target_pairs={{0,24},{2,26},{4,28},{6,30},{8,16},{10,18},{12,20},{14,22},{16,8},... | collective-permute-start | bytes 147464 | tf_op jit(solution)/shard_map/ppermute | solution.py:398

commit v2 on v1

--- a/solution.py
+++ b/solution.py
@@ -82,8 +82,8 @@
         before = now
 
 
-def circulant(bin_weight):
-    length = bin_weight.shape[0]
+def circulant(weights):
+    length = weights.size
     rows = length // LANES
 
     def tables(a, b, period):
@@ -106,7 +106,7 @@
         compiler_params=pltpu.CompilerParams(vmem_limit_bytes=16 * MIB),
         cost_estimate=pl.CostEstimate(flops=2_000_000_000, bytes_accessed=4 * MIB, transcendentals=0),
         name="circulant_block",
-    )(bin_weight.reshape(LANES, rows), table)
+    )(weights, table)
 
 
 def model_kernel(places, planes, *refs):
@@ -251,17 +251,11 @@
 def product_kernel(parts, planes, *refs):
     i_ref = refs[0]
     g_refs = refs[1 : 1 + parts]
-    elution_ref, amp_ref, lag_ref, num_ref, other_ref, terms, held, sems = refs[1 + parts :]
+    elution_ref, amp_ref, lag_ref, num_ref, other_ref, terms = refs[1 + parts :]
     run_count, bin_count, local_mz = i_ref.shape
     components = amp_ref.shape[1]
-    chunks = sems.shape[0]
-    chunk = local_mz // chunks
-    copies = []
-    for n in range(chunks):
-        part = pl.ds(n * chunk, chunk)
-        copies.append(pltpu.make_async_copy(i_ref.at[:, :, part], held.at[:, :, part], sems.at[n]))
-        copies[-1].start()
-
+    chunk = 2 * LANES
+    chunks = local_mz // chunk
     g = g_refs[0][...]
     for ref in g_refs[1:]:
         g = g + ref[...]
@@ -281,8 +275,7 @@
         other_ref[...] = gram
 
     for n in range(chunks):
-        copies[n].wait()
-        data = held[:, :, n * chunk : (n + 1) * chunk].reshape(run_count * bin_count, chunk)
+        data = i_ref[:, :, n * chunk : (n + 1) * chunk].reshape(run_count * bin_count, chunk)
         made = jnp.dot(terms[...], data, preferred_element_type=jnp.float32)
         made = made[:components] + made[components:]
         if planes:
@@ -309,14 +302,10 @@
     return pl.pallas_call(
         functools.partial(product_kernel, len(models), planes),
         out_shape=tuple(jax.ShapeDtypeStruct(shape, jnp.float32) for shape in out_shapes),
-        in_specs=[pl.BlockSpec(memory_space=pl.ANY)] + vmem(len(models) + 3),
+        in_specs=vmem(len(models) + 4),
         out_specs=tuple(vmem(2)),
-        scratch_shapes=[
-            pltpu.VMEM((2 * components, run_count * bin_count), jnp.bfloat16),
-            pltpu.VMEM(intensity.shape, jnp.bfloat16),
-            pltpu.SemaphoreType.DMA((chunks,)),
-        ],
-        compiler_params=pltpu.CompilerParams(vmem_limit_bytes=48 * MIB),
+        scratch_shapes=[pltpu.VMEM((2 * components, run_count * bin_count), jnp.bfloat16)],
+        compiler_params=pltpu.CompilerParams(vmem_limit_bytes=24 * MIB),
         cost_estimate=pl.CostEstimate(
             flops=8_000_000_000, bytes_accessed=2 * intensity.size, transcendentals=0
         ),
@@ -324,31 +313,44 @@
     )(intensity, *models, elution, loadings, shifts)
 
 
+def inverse2(a, b, d):
+    scale = 1.0 / (a * d - b * b)
+    return d * scale, -b * scale, a * scale
+
+
 def eliminate(gram, right):
     components = gram.shape[0]
-    row_id = lax.broadcasted_iota(jnp.int32, (components, 1), 0)
-    for j in range(0, components, 2):
-        first = jnp.broadcast_to(gram[:, j : j + 1], gram.shape)
-        second = jnp.broadcast_to(gram[:, j + 1 : j + 2], gram.shape)
-        a, b, d = first[j : j + 1], second[j : j + 1], second[j + 1 : j + 2]
-        scale = 1.0 / (a * d - b * b)
-        away = (row_id != j) & (row_id != j + 1)
-        f1 = jnp.where(away, first * (d * scale) - second * (b * scale), 0.0)
-        f2 = jnp.where(away, second * (a * scale) - first * (b * scale), 0.0)
-        gram, right = (
-            gram - f1 * gram[j : j + 1] - f2 * gram[j + 1 : j + 2],
-            right - f1[:, : right.shape[1]] * right[j : j + 1] - f2[:, : right.shape[1]] * right[j + 1 : j + 2],
+    row_id = lax.broadcasted_iota(jnp.int32, gram.shape, 0)
+    for j in range(0, components, 4):
+        columns = [jnp.broadcast_to(gram[:, j + n : j + n + 1], gram.shape) for n in range(4)]
+        pivot = [[columns[n][j + m : j + m + 1] for n in range(4)] for m in range(4)]
+        a00, a01, a11 = inverse2(pivot[0][0], pivot[0][1], pivot[1][1])
+        b00, b01, b10, b11 = pivot[0][2], pivot[0][3], pivot[1][2], pivot[1][3]
+        w00, w01 = a00 * b00 + a01 * b10, a00 * b01 + a01 * b11
+        w10, w11 = a01 * b00 + a11 * b10, a01 * b01 + a11 * b11
+        s00, s01, s11 = inverse2(
+            pivot[2][2] - (b00 * w00 + b10 * w10),
+            pivot[2][3] - (b00 * w01 + b10 * w11),
+            pivot[3][3] - (b01 * w01 + b11 * w11),
         )
-    lane = lax.broadcasted_iota(jnp.int32, gram.shape, 1)
-    even = row_id % 2 == 0
-
-    def across(x):
-        return jnp.where(even, pltpu.roll(x, components - 1, 0), pltpu.roll(x, 1, 0))
-
-    own = jnp.sum(jnp.where(lane == row_id, gram, 0.0), axis=1, keepdims=True) + jnp.zeros_like(right)
-    off = jnp.sum(jnp.where(lane == (row_id ^ 1), gram, 0.0), axis=1, keepdims=True)
-    other = across(own)
-    return (other * right - off * across(right)) / (other * own - off * off)
+        away = (row_id < j) | (row_id >= j + 4)
+        c0, c1, c2, c3 = (
+            jnp.where(away, column, jnp.where(row_id == j + n, -1.0, 0.0)) for n, column in enumerate(columns)
+        )
+        t2, t3 = c2 - c0 * w00 - c1 * w10, c3 - c0 * w01 - c1 * w11
+        f2, f3 = t2 * s00 + t3 * s01, t2 * s01 + t3 * s11
+        f0 = c0 * a00 + c1 * a01 - f2 * w00 - f3 * w01
+        f1 = c0 * a01 + c1 * a11 - f2 * w10 - f3 * w11
+        factors = (f0, f1, f2, f3)
+
+        def reduced(x):
+            out = jnp.where(away[:, : x.shape[1]], x, 0.0)
+            for n, factor in enumerate(factors):
+                out = out - factor[:, : x.shape[1]] * x[j + n : j + n + 1]
+            return out
+
+        gram, right = reduced(gram), reduced(right)
+    return right
 
 
 def summed(refs, rows, tail):
@@ -418,25 +420,26 @@
     )
     if not planes:
         gathered = lax.all_gather(mine, axes, axis=0).reshape(-1, math.gcd(bin_count, LANES), LANES)
-        g = partial_model((gathered,), circulant(bin_weight), bin_count, components)
+        g = partial_model((gathered,), circulant(bin_weight.reshape(LANES, -1)), bin_count, components)
         shifted = elution_terms((gathered,), loadings, shifts, bin_count)
         numerator, gram = product(intensity, (g,), shifted, loadings, shifts, planes)
         gram = lax.psum(gram, "freq")
         owned = lax.psum_scatter(numerator, "freq", scatter_dimension=1, tiled=True)
         return small_call(solve_kernel, (components, own), "solve", gram, owned)[0]
-    near = swap(mine, "mz", mz_count, 1)
+    z_steps = range(4, freq_count, 4)
+    held = jnp.stack([mine] + [swap(mine, "freq", freq_count, step) for step in z_steps])
+    weights = bin_weight.reshape(LANES, -1)
+    held, weights, later = lax.optimization_barrier((held, weights, mine))
+    near = swap(later, "mz", mz_count, 1)
     onward = [
         (f * mz_count + y, (f + 1) % freq_count * mz_count + 1 - y)
         for f in range(freq_count)
         for y in range(mz_count)
     ]
-    far = lax.ppermute(mine, axes, onward)
-    z_steps = range(4, freq_count, 4)
-    held = jnp.stack([mine] + [swap(mine, "freq", freq_count, step) for step in z_steps])
-    held, near, far, bin_weight = lax.optimization_barrier((held, near, far, bin_weight))
+    far = lax.ppermute(later, axes, onward)
     held = jnp.concatenate([held, swap(held, "freq", freq_count, 2)], axis=0)
-    u = circulant(bin_weight)
-    held, u = lax.optimization_barrier((held, u))
+    u = circulant(weights)
+    held, u, near, far = lax.optimization_barrier((held, u, near, far))
     came = swap(held, "freq", freq_count, 1)
     g = partial_model((held, came), u, bin_count, components)
     models = (g, swap(g, "mz", mz_count, 1))

time: 59.5 us -> 52.1 us (0.88)
  Pallas kernels: 18.6 us -> 13.8 us
  waiting for transfers between devices: 23.3 us -> 20.3 us
    pallas_call x1, Pallas kernels: 7.02 us -> 3.14 us  [product(): pl.pallas_call(functools.partial(product_kernel, len(models), planes), ou...]
    ppermute x12, waiting for transfers between devices: 20.5 us -> 17.5 us  [swap(): return lax.ppermute(x, axes, [(i, i ^ value) for i in range(count)])]
    pallas_call x3, Pallas kernels: 3.99 us -> 3.09 us  [small_call(): pl.pallas_call(kernel, out_shape=(jax.ShapeDtypeStruct(out_shape, jnp.flo...]
    ppermute x12, starting transfers between devices: 14.3 us -> 15 us  [swap(): return lax.ppermute(x, axes, [(i, i ^ value) for i in range(count)])]
    unnamed x8 -> x10, local copies, waits for them, and re-layouts: 1.78 us -> 1.79 us
  transfers between devices with their start and end apart: 13 -> 13, of which waited for: 9 -> 10; matrix products, arithmetic and copies ran while one was open for 1% -> 2% of each run, Pallas kernels for 7% -> 8%
where the time goes in v2:
time: 52.1 us; the launch traced here: 51.9 us
  waiting for transfers between devices  20.3 us (39%)
  starting transfers between devices  15 us (29%)
  Pallas kernels  13.8 us (26%)
  local copies, waits for them, and re-layouts  2.6 us (5%)
    ppermute x12, waiting for transfers between devices, swap(): return lax.ppermute(x, axes, [(i, i ^ value) for i in range(count)])  17.5 us
    ppermute x12, starting transfers between devices, swap(): return lax.ppermute(x, axes, [(i, i ^ value) for i in range(count)])  15 us
    pallas_call x1, Pallas kernels, product(): pl.pallas_call(functools.partial(product_kernel, len(models), planes), ou...  3.14 us
    pallas_call x3, Pallas kernels, small_call(): pl.pallas_call(kernel, out_shape=(jax.ShapeDtypeStruct(out_shape, jnp.flo...  3.09 us
    pallas_call x1, Pallas kernels, partial_model(): pl.pallas_call(functools.partial(model_kernel, places, planes), out_shape...  3.04 us
    pallas_call x1, Pallas kernels, elution_terms(): pl.pallas_call(functools.partial(elution_kernel, planes), out_shape=jax.S...  2.91 us
    ppermute x1, waiting for transfers between devices, on_device(): far = lax.ppermute(later, axes, onward)  2.81 us
    unnamed x10, local copies, waits for them, and re-layouts  1.79 us
  transfers between devices with their start and end apart: 13, of which 10 were waited for; matrix products, arithmetic and copies ran while one was open for 2% of the time, Pallas kernels for 8%

profile of v2, /device:TPU:0, one launch (start us, length us, event | category | flops | bytes accessed | tf_op | source)
XLA Modules:
  0.0 51.9 jit_solution(10835022846452440343)
XLA Ops:
  0.0 0.0 copy-start
  0.0 0.8 %copy-done = f32[192,64]{0,1:T(8,128)S(1)} copy-done((f32[192,64]{0,1:T(8,128)S(1)}, f32[192,64]{0,1:T(8,128)}, u32[]{:S(2)}) %copy-start) | copy-done | bytes 49176
  0.8 0.0 copy-start.2
  0.8 0.0 copy-start.3
  0.8 0.2 pack_elution.1.refs_0_
  1.0 5.1 %collective-permute-start.2 = (bf16[192,128]{1,0:T(8,128)(2,1)S(1)}, bf16[192,128]{1,0:T(8,128)(2,1)S(1)}, u32[]{:S(2)}, u32[]{:S(2)}) collective-permute-start(bf16[192,128]{1,0:T(8,128)(2,1)S(1)} %pack_elution.1.refs_0_), channel_id=1, source_target_pairs={{0,24},{2,26},{4,28},{6,30},{8,16},{10,18},{12,20},{14,22},{16,8},... | collective-permute-start | bytes 147464 | tf_op jit(solution)/shard_map/ppermute | solution.py:400
  6.1 0.0 collective-permute-start.1
  6.1 0.6 %collective-permute-start = (bf16[192,128]{1,0:T(8,128)(2,1)S(1)}, bf16[192,128]{1,0:T(8,128)(2,1)S(1)}, u32[]{:S(2)}, u32[]{:S(2)}) collective-permute-start(bf16[192,128]{1,0:T(8,128)(2,1)S(1)} %pack_elution.1.refs_0_), channel_id=1, source_target_pairs={{0,8},{2,10},{4,12},{6,14},{8,0},{10,2},{12,4},{14,6},{16,24},{18,... | collective-permute-start | bytes 147464 | tf_op jit(solution)/shard_map/ppermute | solution.py:400
  6.8 0.8 %reshape.3.w_ref = f32[128,48]{1,0:T(8,128)S(1)} reshape(f32[6144]{0:T(1024)} %param.10) | data formatting | bytes 49152 | tf_op jit(solution)/shard_map/reshape | solution.py:431
  7.6 0.0 copy-start.1
  7.6 0.8 %collective-permute-done.2 = bf16[192,128]{1,0:T(8,128)(2,1)S(1)} collective-permute-done((bf16[192,128]{1,0:T(8,128)(2,1)S(1)}, bf16[192,128]{1,0:T(8,128)(2,1)S(1)}, u32[]{:S(2)}, u32[]{:S(2)}) %collective-permute-start.2) | collective-permute-done | bytes 49184 | tf_op jit(solution)/shard_map/ppermute | solution.py:400
  8.4 2.8 %collective-permute-done.1 = bf16[192,128]{1,0:T(8,128)(2,1)S(1)} collective-permute-done((bf16[192,128]{1,0:T(8,128)(2,1)S(1)}, bf16[192,128]{1,0:T(8,128)(2,1)S(1)}, u32[]{:S(2)}, u32[]{:S(2)}) %collective-permute-start.1) | collective-permute-done | bytes 49184 | tf_op jit(solution)/shard_map/ppermute | solution.py:400
  11.1 0.0 collective-permute-done
  11.2 1.6 %collective-permute-start.3 = (bf16[4,192,128]{2,1,0:T(8,128)(2,1)S(1)}, bf16[4,192,128]{2,1,0:T(8,128)(2,1)S(1)}, u32[]{:S(2)}, u32[]{:S(2)}) collective-permute-start(bf16[4,192,128]{2,1,0:T(8,128)(2,1)S(1)} %pad_maximum_fusion.1), channel_id=1, source_target_pairs={{0,4},{2,6},{4,0},{6,2},{8,12},{10,14},{12,8},{14,10},{16,20},{18,... | collective-permute-start | bytes 589832 | tf_op jit(solution)/shard_map/ppermute | solution.py:400
  12.7 0.0 collective-permute-start.5
  12.7 1.5 %collective-permute-start.4 = (bf16[192,128]{1,0:T(8,128)(2,1)S(1)}, bf16[192,128]{1,0:T(8,128)(2,1)S(1)}, u32[]{:S(2)}, u32[]{:S(2)}) collective-permute-start(bf16[192,128]{1,0:T(8,128)(2,1)S(1)} %pack_elution.1.refs_0_), channel_id=1, source_target_pairs={{0,1},{1,0},{2,3},{3,2},{4,5},{5,4},{6,7},{7,6},{8,9},{9,8},{10,11... | collective-permute-start | bytes 147464 | tf_op jit(solution)/shard_map/ppermute | solution.py:400
  14.2 0.0 copy-start.4
  14.2 0.9 %copy-done.4 = f32[448,128]{1,0:T(8,128)S(1)} copy-done((f32[448,128]{1,0:T(8,128)S(1)}, f32[448,128]{1,0:T(8,128)}, u32[]{:S(2)}) %copy-start.4) | copy-done | bytes 229400
  15.2 1.5 %circulant_block.1.refs_2_ = bf16[256,6144]{1,0:T(8,128)(2,1)S(1)} custom-call(f32[128,48]{1,0:T(8,128)S(1)} %reshape.3.w_ref, f32[448,128]{1,0:T(8,128)S(1)} %copy-done.4), custom_call_target="tpu_custom_call" | custom-call | flops 2000000000 | bytes 4194304 | tf_op jit(solution)/shard_map/circulant_block/pallas_call | solution.py:101
  16.6 0.3 collective-permute-done.3
  17.0 2.8 %collective-permute-done.5.refs_3_ = bf16[192,128]{1,0:T(8,128)(2,1)S(1)} collective-permute-done((bf16[192,128]{1,0:T(8,128)(2,1)S(1)}, bf16[192,128]{1,0:T(8,128)(2,1)S(1)}, u32[]{:S(2)}, u32[]{:S(2)}) %collective-permute-start.5) | collective-permute-done | bytes 49184 | tf_op jit(solution)/shard_map/ppermute | solution.py:439
  19.8 0.0 collective-permute-done.4.refs_2_
  19.8 0.0 collective-permute-start.6
  19.8 1.7 %collective-permute-done.6.refs_1_ = bf16[8,192,128]{2,1,0:T(8,128)(2,1)S(1)} collective-permute-done((bf16[8,192,128]{2,1,0:T(8,128)(2,1)S(1)}, bf16[8,192,128]{2,1,0:T(8,128)(2,1)S(1)}, u32[]{:S(2)}, u32[]{:S(2)}) %collective-permute-start.6) | collective-permute-done | bytes 393248 | tf_op jit(solution)/shard_map/ppermute | solution.py:400
  21.6 3.0 %partial_model.1.refs_1_ = f32[64,640]{1,0:T(8,128)S(1)} custom-call(bf16[8,192,128]{2,1,0:T(8,128)(2,1)S(1)} %pad_maximum_fusion.refs_0_, bf16[8,192,128]{2,1,0:T(8,128)(2,1)S(1)} %collective-permute-done.6.refs_1_, bf16[256,6144]{1,0:T(8,128)(2,1)S(1)} %circulant_block.1.refs_2_), custom_call_target="tpu_custom_call" | custom-call | flops 2000000000 | bytes 4194304 | tf_op jit(solution)/shard_map/partial_model/pallas_call | solution.py:164
  24.6 1.6 %collective-permute-start.7 = (f32[64,640]{1,0:T(8,128)S(1)}, f32[64,640]{1,0:T(8,128)S(1)}, u32[]{:S(2)}, u32[]{:S(2)}) collective-permute-start(f32[64,640]{1,0:T(8,128)S(1)} %partial_model.1.refs_1_), channel_id=1, source_target_pairs={{0,1},{1,0},{2,3},{3,2},{4,5},{5,4},{6,7},{7,6},{8,9},{9,8},{10,11... | collective-permute-start | bytes 491528 | tf_op jit(solution)/shard_map/ppermute | solution.py:400
  26.2 0.0 copy-done.2
  26.2 0.0 copy-done.3
  26.2 2.9 %elution_terms.1.refs_3_ = bf16[128,3072]{1,0:T(8,128)(2,1)S(1)} custom-call(bf16[192,128]{1,0:T(8,128)(2,1)S(1)} %pack_elution.1.refs_0_, bf16[8,192,128]{2,1,0:T(8,128)(2,1)S(1)} %collective-permute-done.6.refs_1_, bf16[192,128]{1,0:T(8,128)(2,1)S(1)} %collective-permute-done.4.refs_2_, bf16[192,128]{1,0:T(8,128)(2,1)S(1)} %collective-permute-done.5.refs_3_, ...), custom_call_target="tpu_custom_call" | custom-call | flops 1000000000 | bytes 2097152 | tf_op jit(solution)/shard_map/elution_terms/pallas_call | solution.py:239
  29.1 1.8 %collective-permute-done.7.refs_2_ = f32[64,640]{1,0:T(8,128)S(1)} collective-permute-done((f32[64,640]{1,0:T(8,128)S(1)}, f32[64,640]{1,0:T(8,128)S(1)}, u32[]{:S(2)}, u32[]{:S(2)}) %collective-permute-start.7) | collective-permute-done | bytes 163872 | tf_op jit(solution)/shard_map/ppermute | solution.py:400
  30.9 0.0 copy-done.1
  30.9 3.1 %model_products.1 = (f32[544,128]{1,0:T(8,128)S(1)}, f32[544,128]{1,0:T(8,128)S(1)}) custom-call(bf16[8,384,2048]{2,1,0:T(8,128)(2,1)S(1)} %copy-done.1, f32[64,640]{1,0:T(8,128)S(1)} %partial_model.1.refs_1_, f32[64,640]{1,0:T(8,128)S(1)} %collective-permute-done.7.refs_2_, bf16[128,3072]{1,0:T(8,128)(2,1)S(1)} %elution_terms.1.refs_3_, ...), custom_call_target="tpu_custom_call" | custom-call | flops 8000000000 | bytes 12582912 | tf_op jit(solution)/shard_map/model_products/pallas_call | solution.py:302
  34.1 0.1 collective-permute-start.8
  34.1 1.5 %collective-permute-done.8.refs_1_ = f32[544,128]{1,0:T(8,128)S(1)} collective-permute-done((f32[544,128]{1,0:T(8,128)S(1)}, f32[544,128]{1,0:T(8,128)S(1)}, u32[]{:S(2)}, u32[]{:S(2)}) %collective-permute-start.8) | collective-permute-done | bytes 278560 | tf_op jit(solution)/shard_map/ppermute | solution.py:400
  35.7 0.1 collective-permute-start.9
  35.8 5.9 %collective-permute-done.9.refs_2_ = f32[288,128]{1,0:T(8,128)S(1)} collective-permute-done((f32[288,128]{1,0:T(8,128)S(1)}, f32[288,128]{1,0:T(8,128)S(1)}, u32[]{:S(2)}, u32[]{:S(2)}) %collective-permute-start.9) | collective-permute-done | bytes 147488 | tf_op jit(solution)/shard_map/ppermute | solution.py:400
  41.7 0.1 collective-permute-start.10
  41.8 1.0 %collective-permute-start.11 = (f32[96,128]{1,0:T(8,128)S(1)}, f32[96,128]{1,0:T(8,128)S(1)}, u32[]{:S(2)}, u32[]{:S(2)}) collective-permute-start(f32[96,128]{1,0:T(8,128)S(1)} %get-tuple-element.27), channel_id=1, source_target_pairs={{0,16},{2,18},{4,20},{6,22},{8,24},{10,26},{12,28},{14,30},{16,0},... | collective-permute-start | bytes 147464 | tf_op jit(solution)/shard_map/ppermute | solution.py:400
  42.7 3.4 %collective-permute-start.12 = (f32[96,128]{1,0:T(8,128)S(1)}, f32[96,128]{1,0:T(8,128)S(1)}, u32[]{:S(2)}, u32[]{:S(2)}) collective-permute-start(f32[96,128]{1,0:T(8,128)S(1)} %get-tuple-element.28), channel_id=1, source_target_pairs={{0,24},{2,26},{4,28},{6,30},{8,16},{10,18},{12,20},{14,22},{16,8},... | collective-permute-start | bytes 147464 | tf_op jit(solution)/shard_map/ppermute | solution.py:400
  46.1 0.0 collective-permute-done.10.refs_3_
  46.1 1.2 %collective-permute-done.11.refs_4_ = f32[96,128]{1,0:T(8,128)S(1)} collective-permute-done((f32[96,128]{1,0:T(8,128)S(1)}, f32[96,128]{1,0:T(8,128)S(1)}, u32[]{:S(2)}, u32[]{:S(2)}) %collective-permute-start.11) | collective-permute-done | bytes 49184 | tf_op jit(solution)/shard_map/ppermute | solution.py:400
  47.3 1.5 %collective-permute-done.12.refs_5_ = f32[96,128]{1,0:T(8,128)S(1)} collective-permute-done((f32[96,128]{1,0:T(8,128)S(1)}, f32[96,128]{1,0:T(8,128)S(1)}, u32[]{:S(2)}, u32[]{:S(2)}) %collective-permute-start.12) | collective-permute-done | bytes 49184 | tf_op jit(solution)/shard_map/ppermute | solution.py:400
  48.8 3.0 %solve.1 = f32[64,128]{1,0:T(8,128)} custom-call(f32[544,128]{1,0:T(8,128)S(1)} %get-tuple-element.24.refs_0_, f32[544,128]{1,0:T(8,128)S(1)} %collective-permute-done.8.refs_1_, f32[288,128]{1,0:T(8,128)S(1)} %collective-permute-done.9.refs_2_, f32[96,128]{1,0:T(8,128)S(1)} %collective-permute-done.10.refs_3_, ...), custom_call_target="tpu_custom_call" | custom-call | tf_op jit(solution)/shard_map/solve/pallas_call | solution.py:388
  (4 shorter events, 0.1 us)
Async XLA Ops:
  0.0 0.8 %copy-start = (f32[192,64]{0,1:T(8,128)S(1)}, f32[192,64]{0,1:T(8,128)}, u32[]{:S(2)}) copy-start(f32[192,64]{0,1:T(8,128)} %param.7) | copy-start | bytes 147460
  0.8 25.4 %copy-start.2 = (f32[8,64]{1,0:T(8,128)S(1)}, f32[8,64]{1,0:T(8,128)}, u32[]{:S(2)}) copy-start(f32[8,64]{1,0:T(8,128)} %refs_4_.3) | copy-start | bytes 6148
  0.8 25.4 %copy-start.3 = (s32[8,64]{1,0:T(8,128)S(1)}, s32[8,64]{1,0:T(8,128)}, u32[]{:S(2)}) copy-start(s32[8,64]{1,0:T(8,128)} %refs_5_.3) | copy-start | bytes 6148
  1.0 7.3 %collective-permute-start.2 = (bf16[192,128]{1,0:T(8,128)(2,1)S(1)}, bf16[192,128]{1,0:T(8,128)(2,1)S(1)}, u32[]{:S(2)}, u32[]{:S(2)}) collective-permute-start(bf16[192,128]{1,0:T(8,128)(2,1)S(1)} %pack_elution.1.refs_0_), channel_id=1, source_target_pairs={{0,24},{2,26},{4,28},{6,30},{8,16},{10,18},{12,20},{14,22},{16,8},... | collective-permute-start | bytes 147464 | tf_op jit(solution)/shard_map/ppermute | solution.py:400
  6.1 5.0 %collective-permute-start.1 = (bf16[192,128]{1,0:T(8,128)(2,1)S(1)}, bf16[192,128]{1,0:T(8,128)(2,1)S(1)}, u32[]{:S(2)}, u32[]{:S(2)}) collective-permute-start(bf16[192,128]{1,0:T(8,128)(2,1)S(1)} %pack_elution.1.refs_0_), channel_id=1, source_target_pairs={{0,16},{2,18},{4,20},{6,22},{8,24},{10,26},{12,28},{14,30},{16,0},... | collective-permute-start | bytes 147464 | tf_op jit(solution)/shard_map/ppermute | solution.py:400
  6.1 5.0 %collective-permute-start = (bf16[192,128]{1,0:T(8,128)(2,1)S(1)}, bf16[192,128]{1,0:T(8,128)(2,1)S(1)}, u32[]{:S(2)}, u32[]{:S(2)}) collective-permute-start(bf16[192,128]{1,0:T(8,128)(2,1)S(1)} %pack_elution.1.refs_0_), channel_id=1, source_target_pairs={{0,8},{2,10},{4,12},{6,14},{8,0},{10,2},{12,4},{14,6},{16,24},{18,... | collective-permute-start | bytes 147464 | tf_op jit(solution)/shard_map/ppermute | solution.py:400
  7.6 23.3 %copy-start.1 = (bf16[8,384,2048]{2,1,0:T(8,128)(2,1)S(1)}, bf16[8,384,2048]{2,1,0:T(8,128)(2,1)}, u32[]{:S(2)}) copy-start(bf16[8,384,2048]{2,1,0:T(8,128)(2,1)} %refs_0_.1) | copy-start | bytes 37748740
  11.2 5.8 %collective-permute-start.3 = (bf16[4,192,128]{2,1,0:T(8,128)(2,1)S(1)}, bf16[4,192,128]{2,1,0:T(8,128)(2,1)S(1)}, u32[]{:S(2)}, u32[]{:S(2)}) collective-permute-start(bf16[4,192,128]{2,1,0:T(8,128)(2,1)S(1)} %pad_maximum_fusion.1), channel_id=1, source_target_pairs={{0,4},{2,6},{4,0},{6,2},{8,12},{10,14},{12,8},{14,10},{16,20},{18,... | collective-permute-start | bytes 589832 | tf_op jit(solution)/shard_map/ppermute | solution.py:400
  12.7 7.1 %collective-permute-start.5 = (bf16[192,128]{1,0:T(8,128)(2,1)S(1)}, bf16[192,128]{1,0:T(8,128)(2,1)S(1)}, u32[]{:S(2)}, u32[]{:S(2)}) collective-permute-start(bf16[192,128]{1,0:T(8,128)(2,1)S(1)} %pack_elution.1.refs_0_), channel_id=1, source_target_pairs={{0,3},{1,2},{2,5},{3,4},{4,7},{5,6},{6,9},{7,8},{8,11},{9,10},{10,... | collective-permute-start | bytes 147464 | tf_op jit(solution)/shard_map/ppermute | solution.py:439
  12.7 7.1 %collective-permute-start.4 = (bf16[192,128]{1,0:T(8,128)(2,1)S(1)}, bf16[192,128]{1,0:T(8,128)(2,1)S(1)}, u32[]{:S(2)}, u32[]{:S(2)}) collective-permute-start(bf16[192,128]{1,0:T(8,128)(2,1)S(1)} %pack_elution.1.refs_0_), channel_id=1, source_target_pairs={{0,1},{1,0},{2,3},{3,2},{4,5},{5,4},{6,7},{7,6},{8,9},{9,8},{10,11... | collective-permute-start | bytes 147464 | tf_op jit(solution)/shard_map/ppermute | solution.py:400
  14.2 0.9 %copy-start.4 = (f32[448,128]{1,0:T(8,128)S(1)}, f32[448,128]{1,0:T(8,128)}, u32[]{:S(2)}) copy-start(f32[448,128]{1,0:T(8,128)} %constant.2.clone.table_ref) | copy-start | bytes 688132
  19.8 1.7 %collective-permute-start.6 = (bf16[8,192,128]{2,1,0:T(8,128)(2,1)S(1)}, bf16[8,192,128]{2,1,0:T(8,128)(2,1)S(1)}, u32[]{:S(2)}, u32[]{:S(2)}) collective-permute-start(bf16[8,192,128]{2,1,0:T(8,128)(2,1)S(1)} %pad_maximum_fusion.refs_0_), channel_id=1, source_target_pairs={{0,2},{2,0},{4,6},{6,4},{8,10},{10,8},{12,14},{14,12},{16,18},{18,... | collective-permute-start | bytes 1179656 | tf_op jit(solution)/shard_map/ppermute | solution.py:400
  24.6 6.3 %collective-permute-start.7 = (f32[64,640]{1,0:T(8,128)S(1)}, f32[64,640]{1,0:T(8,128)S(1)}, u32[]{:S(2)}, u32[]{:S(2)}) collective-permute-start(f32[64,640]{1,0:T(8,128)S(1)} %partial_model.1.refs_1_), channel_id=1, source_target_pairs={{0,1},{1,0},{2,3},{3,2},{4,5},{5,4},{6,7},{7,6},{8,9},{9,8},{10,11... | collective-permute-start | bytes 491528 | tf_op jit(solution)/shard_map/ppermute | solution.py:400
  34.1 1.6 %collective-permute-start.8 = (f32[544,128]{1,0:T(8,128)S(1)}, f32[544,128]{1,0:T(8,128)S(1)}, u32[]{:S(2)}, u32[]{:S(2)}) collective-permute-start(f32[544,128]{1,0:T(8,128)S(1)} %get-tuple-element.25), channel_id=1, source_target_pairs={{0,2},{2,0},{4,6},{6,4},{8,10},{10,8},{12,14},{14,12},{16,18},{18,... | collective-permute-start | bytes 835592 | tf_op jit(solution)/shard_map/ppermute | solution.py:400
  35.7 6.0 %collective-permute-start.9 = (f32[288,128]{1,0:T(8,128)S(1)}, f32[288,128]{1,0:T(8,128)S(1)}, u32[]{:S(2)}, u32[]{:S(2)}) collective-permute-start(f32[288,128]{1,0:T(8,128)S(1)} %reduce_stage.2), channel_id=1, source_target_pairs={{0,4},{2,6},{4,0},{6,2},{8,12},{10,14},{12,8},{14,10},{16,20},{18,... | collective-permute-start | bytes 442376 | tf_op jit(solution)/shard_map/ppermute | solution.py:400
  41.7 4.5 %collective-permute-start.10 = (f32[96,128]{1,0:T(8,128)S(1)}, f32[96,128]{1,0:T(8,128)S(1)}, u32[]{:S(2)}, u32[]{:S(2)}) collective-permute-start(f32[96,128]{1,0:T(8,128)S(1)} %get-tuple-element.26), channel_id=1, source_target_pairs={{0,8},{2,10},{4,12},{6,14},{8,0},{10,2},{12,4},{14,6},{16,24},{18,... | collective-permute-start | bytes 147464 | tf_op jit(solution)/shard_map/ppermute | solution.py:400
  41.8 5.5 %collective-permute-start.11 = (f32[96,128]{1,0:T(8,128)S(1)}, f32[96,128]{1,0:T(8,128)S(1)}, u32[]{:S(2)}, u32[]{:S(2)}) collective-permute-start(f32[96,128]{1,0:T(8,128)S(1)} %get-tuple-element.27), channel_id=1, source_target_pairs={{0,16},{2,18},{4,20},{6,22},{8,24},{10,26},{12,28},{14,30},{16,0},... | collective-permute-start | bytes 147464 | tf_op jit(solution)/shard_map/ppermute | solution.py:400
  42.7 6.1 %collective-permute-start.12 = (f32[96,128]{1,0:T(8,128)S(1)}, f32[96,128]{1,0:T(8,128)S(1)}, u32[]{:S(2)}, u32[]{:S(2)}) collective-permute-start(f32[96,128]{1,0:T(8,128)S(1)} %get-tuple-element.28), channel_id=1, source_target_pairs={{0,24},{2,26},{4,28},{6,30},{8,16},{10,18},{12,20},{14,22},{16,8},... | collective-permute-start | bytes 147464 | tf_op jit(solution)/shard_map/ppermute | solution.py:400

commit v3 on v2

--- a/solution.py
+++ b/solution.py
@@ -353,29 +353,43 @@
     return right
 
 
-def summed(refs, rows, tail):
-    total = refs[0][0:rows] + refs[1][0:rows]
-    gram = refs[0][refs[0].shape[0] - tail :] + refs[1][refs[1].shape[0] - tail :]
-    for ref in refs[2:]:
-        total = total + ref[0:rows]
-        gram = gram + ref[ref.shape[0] - tail :]
-    return total, gram
-
-
-def stage_kernel(tail, count, *refs):
-    outs = refs[-count:]
-    rows = outs[0].shape[0] - tail
-    total, gram = summed(refs[:-count], (count + 1) * rows, tail)
+def total_of(refs, at, rows):
+    total = refs[0][at : at + rows]
+    for ref in refs[1:]:
+        total = total + ref[at : at + rows]
+    return total
+
+
+def halve_kernel(tail, a_ref, b_ref, o_ref, gram_ref):
+    rows = o_ref.shape[0]
+    o_ref[...] = total_of((a_ref, b_ref), rows, rows)
+    gram_ref[...] = total_of((a_ref, b_ref), 2 * rows, tail)
+
+
+def spread_kernel(*refs):
+    ins, outs = refs[:3], refs[3:]
+    rows = outs[0].shape[0]
     for n, o_ref in enumerate(outs):
-        o_ref[0:rows, :] = total[(n + 1) * rows : (n + 2) * rows]
-        o_ref[rows:, :] = gram
-
-
-def solve_planes_kernel(tail, *refs):
+        o_ref[...] = total_of(ins, (n + 1) * rows, rows)
+
+
+def sum_kernel(*refs):
+    refs[-1][...] = total_of(refs[:-1], 0, refs[-1].shape[0])
+
+
+def invert_kernel(*refs):
     o_ref = refs[-1]
-    total, gram = summed(refs[:-1], o_ref.shape[0], tail)
+    gram = total_of(refs[:-1], 0, refs[0].shape[0])
     gram = jnp.concatenate([gram, pltpu.roll(gram, gram.shape[1] // 2, 1)], axis=0)
-    o_ref[...] = eliminate(gram, total)
+    row_id = lax.broadcasted_iota(jnp.int32, gram.shape, 0)
+    eye = jnp.where(row_id == lax.broadcasted_iota(jnp.int32, gram.shape, 1), 1.0, 0.0)
+    o_ref[...] = eliminate(gram, eye)
+
+
+def finish_kernel(inverse_ref, *refs):
+    o_ref = refs[-1]
+    components = o_ref.shape[0]
+    o_ref[...] = f32_dot(inverse_ref[:, :components], total_of(refs[:-1], 0, components))
 
 
 def solve_kernel(g_ref, n_ref, o_ref):
@@ -384,13 +398,14 @@
     o_ref[...] = eliminate(gram, n_ref[...])
 
 
-def small_call(kernel, out_shape, name, *args, count=1):
+def small_call(kernel, shapes, name, *args, flops=1_000_000):
     outs = pl.pallas_call(
         kernel,
-        out_shape=(jax.ShapeDtypeStruct(out_shape, jnp.float32),) * count,
+        out_shape=tuple(jax.ShapeDtypeStruct(shape, jnp.float32) for shape in shapes),
         in_specs=vmem(len(args)),
-        out_specs=tuple(vmem(count)),
+        out_specs=tuple(vmem(len(shapes))),
         compiler_params=pltpu.CompilerParams(vmem_limit_bytes=8 * MIB),
+        cost_estimate=pl.CostEstimate(flops=flops, bytes_accessed=1024, transcendentals=0),
         name=name,
     )(*args)
     return outs
@@ -425,7 +440,7 @@
         numerator, gram = product(intensity, (g,), shifted, loadings, shifts, planes)
         gram = lax.psum(gram, "freq")
         owned = lax.psum_scatter(numerator, "freq", scatter_dimension=1, tiled=True)
-        return small_call(solve_kernel, (components, own), "solve", gram, owned)[0]
+        return small_call(solve_kernel, [(components, own)], "solve", gram, owned)[0]
     z_steps = range(4, freq_count, 4)
     held = jnp.stack([mine] + [swap(mine, "freq", freq_count, step) for step in z_steps])
     weights = bin_weight.reshape(LANES, -1)
@@ -446,18 +461,24 @@
     shifted = elution_terms((mine, came, near, far), loadings, shifts, bin_count)
     keep, send = product(intensity, models, shifted, loadings, shifts, planes)
     tail = components // 2
-    quarter = freq_count // 4 * components
-    parts = [keep, swap(send, "freq", freq_count, 1)]
-    (send,) = small_call(
-        functools.partial(stage_kernel, tail, 1), (quarter + tail, LANES), "reduce_stage", *parts
+    came = swap(send, "freq", freq_count, 1)
+    send, gram = small_call(
+        functools.partial(halve_kernel, tail),
+        [(freq_count // 4 * components, LANES), (tail, LANES)],
+        "reduce_cores",
+        keep,
+        came,
     )
-    parts.append(swap(send, "freq", freq_count, 2))
-    count = len(z_steps)
-    sends = small_call(
-        functools.partial(stage_kernel, tail, count), (components + tail, LANES), "reduce_stage", *parts, count=count
+    across = swap(send, "freq", freq_count, 2)
+    grams = [swap(gram, "freq", freq_count, step) for step in z_steps]
+    (gram,) = small_call(sum_kernel, [(tail, LANES)], "reduce_gram", gram, *grams)
+    gram_across = swap(gram, "freq", freq_count, 2)
+    sends = small_call(spread_kernel, [(components, LANES)] * len(z_steps), "reduce_x", keep, came, across)
+    parts = [swap(part, "freq", freq_count, step) for part, step in zip(sends, z_steps)]
+    (inverse,) = small_call(
+        invert_kernel, [(components, LANES)], "invert_gram", gram, gram_across, flops=3_000_000_000
     )
-    parts += [swap(send, "freq", freq_count, step) for send, step in zip(sends, z_steps)]
-    return small_call(functools.partial(solve_planes_kernel, tail), (components, own), "solve", *parts)[0]
+    return small_call(finish_kernel, [(components, own)], "finish", inverse, keep, came, across, *parts)[0]
 
 
 def solution(mesh):

time: 52.1 us -> 53.7 us (1.031)
  starting transfers between devices: 15 us -> 21 us
  waiting for transfers between devices: 20.3 us -> 15.8 us
    ppermute x12 -> x16, starting transfers between devices: 15 us -> 21 us  [swap(): return lax.ppermute(x, axes, [(i, i ^ value) for i in range(count)])]
    ppermute x12 -> x16, waiting for transfers between devices: 17.5 us -> 13 us  [swap(): return lax.ppermute(x, axes, [(i, i ^ value) for i in range(count)])]
    pallas_call x3 -> x5, Pallas kernels: 3.09 us -> 3.23 us  [small_call(): pl.pallas_call(kernel, out_shape=tuple((jax.ShapeDtypeStruct(shape, jnp.f...]
  transfers between devices with their start and end apart: 13 -> 17, of which waited for: 10 -> 10; matrix products, arithmetic and copies ran while one was open for 2% -> 2% of each run, Pallas kernels for 8% -> 13%
where the time goes in v3:
time: 53.7 us; the launch traced here: 53.5 us
  starting transfers between devices  21 us (39%)
  waiting for transfers between devices  15.8 us (29%)
  Pallas kernels  14 us (26%)
  local copies, waits for them, and re-layouts  2.6 us (5%)
    ppermute x16, starting transfers between devices, swap(): return lax.ppermute(x, axes, [(i, i ^ value) for i in range(count)])  21 us
    ppermute x16, waiting for transfers between devices, swap(): return lax.ppermute(x, axes, [(i, i ^ value) for i in range(count)])  13 us
    pallas_call x5, Pallas kernels, small_call(): pl.pallas_call(kernel, out_shape=tuple((jax.ShapeDtypeStruct(shape, jnp.f...  3.23 us
    pallas_call x1, Pallas kernels, product(): pl.pallas_call(functools.partial(product_kernel, len(models), planes), ou...  3.14 us
    pallas_call x1, Pallas kernels, partial_model(): pl.pallas_call(functools.partial(model_kernel, places, planes), out_shape...  3.04 us
    pallas_call x1, Pallas kernels, elution_terms(): pl.pallas_call(functools.partial(elution_kernel, planes), out_shape=jax.S...  2.91 us
    ppermute x1, waiting for transfers between devices, on_device(): far = lax.ppermute(later, axes, onward)  2.81 us
    unnamed x10, local copies, waits for them, and re-layouts  1.79 us
  transfers between devices with their start and end apart: 17, of which 10 were waited for; matrix products, arithmetic and copies ran while one was open for 2% of the time, Pallas kernels for 13%

profile of v3, /device:TPU:0, one launch (start us, length us, event | category | flops | bytes accessed | tf_op | source)
XLA Modules:
  0.0 53.5 jit_solution(724953930996527273)
XLA Ops:
  0.0 0.0 copy-start
  0.0 0.8 %copy-done = f32[192,64]{0,1:T(8,128)S(1)} copy-done((f32[192,64]{0,1:T(8,128)S(1)}, f32[192,64]{0,1:T(8,128)}, u32[]{:S(2)}) %copy-start) | copy-done | bytes 49176
  0.8 0.0 copy-start.2
  0.8 0.0 copy-start.3
  0.8 0.2 pack_elution.1.refs_0_
  1.0 5.1 %collective-permute-start.2 = (bf16[192,128]{1,0:T(8,128)(2,1)S(1)}, bf16[192,128]{1,0:T(8,128)(2,1)S(1)}, u32[]{:S(2)}, u32[]{:S(2)}) collective-permute-start(bf16[192,128]{1,0:T(8,128)(2,1)S(1)} %pack_elution.1.refs_0_), channel_id=1, source_target_pairs={{0,24},{2,26},{4,28},{6,30},{8,16},{10,18},{12,20},{14,22},{16,8},... | collective-permute-start | bytes 147464 | tf_op jit(solution)/shard_map/ppermute | solution.py:415
  6.1 0.0 collective-permute-start.1
  6.1 0.6 %collective-permute-start = (bf16[192,128]{1,0:T(8,128)(2,1)S(1)}, bf16[192,128]{1,0:T(8,128)(2,1)S(1)}, u32[]{:S(2)}, u32[]{:S(2)}) collective-permute-start(bf16[192,128]{1,0:T(8,128)(2,1)S(1)} %pack_elution.1.refs_0_), channel_id=1, source_target_pairs={{0,8},{2,10},{4,12},{6,14},{8,0},{10,2},{12,4},{14,6},{16,24},{18,... | collective-permute-start | bytes 147464 | tf_op jit(solution)/shard_map/ppermute | solution.py:415
  6.8 0.8 %reshape.3.w_ref = f32[128,48]{1,0:T(8,128)S(1)} reshape(f32[6144]{0:T(1024)} %param.10) | data formatting | bytes 49152 | tf_op jit(solution)/shard_map/reshape | solution.py:446
  7.6 0.0 copy-start.1
  7.6 0.8 %collective-permute-done.2 = bf16[192,128]{1,0:T(8,128)(2,1)S(1)} collective-permute-done((bf16[192,128]{1,0:T(8,128)(2,1)S(1)}, bf16[192,128]{1,0:T(8,128)(2,1)S(1)}, u32[]{:S(2)}, u32[]{:S(2)}) %collective-permute-start.2) | collective-permute-done | bytes 49184 | tf_op jit(solution)/shard_map/ppermute | solution.py:415
  8.4 2.8 %collective-permute-done.1 = bf16[192,128]{1,0:T(8,128)(2,1)S(1)} collective-permute-done((bf16[192,128]{1,0:T(8,128)(2,1)S(1)}, bf16[192,128]{1,0:T(8,128)(2,1)S(1)}, u32[]{:S(2)}, u32[]{:S(2)}) %collective-permute-start.1) | collective-permute-done | bytes 49184 | tf_op jit(solution)/shard_map/ppermute | solution.py:415
  11.1 0.0 collective-permute-done
  11.2 1.6 %collective-permute-start.3 = (bf16[4,192,128]{2,1,0:T(8,128)(2,1)S(1)}, bf16[4,192,128]{2,1,0:T(8,128)(2,1)S(1)}, u32[]{:S(2)}, u32[]{:S(2)}) collective-permute-start(bf16[4,192,128]{2,1,0:T(8,128)(2,1)S(1)} %pad_maximum_fusion.1), channel_id=1, source_target_pairs={{0,4},{2,6},{4,0},{6,2},{8,12},{10,14},{12,8},{14,10},{16,20},{18,... | collective-permute-start | bytes 589832 | tf_op jit(solution)/shard_map/ppermute | solution.py:415
  12.7 0.0 collective-permute-start.5
  12.7 1.5 %collective-permute-start.4 = (bf16[192,128]{1,0:T(8,128)(2,1)S(1)}, bf16[192,128]{1,0:T(8,128)(2,1)S(1)}, u32[]{:S(2)}, u32[]{:S(2)}) collective-permute-start(bf16[192,128]{1,0:T(8,128)(2,1)S(1)} %pack_elution.1.refs_0_), channel_id=1, source_target_pairs={{0,1},{1,0},{2,3},{3,2},{4,5},{5,4},{6,7},{7,6},{8,9},{9,8},{10,11... | collective-permute-start | bytes 147464 | tf_op jit(solution)/shard_map/ppermute | solution.py:415
  14.2 0.0 copy-start.4
  14.2 0.9 %copy-done.4 = f32[448,128]{1,0:T(8,128)S(1)} copy-done((f32[448,128]{1,0:T(8,128)S(1)}, f32[448,128]{1,0:T(8,128)}, u32[]{:S(2)}) %copy-start.4) | copy-done | bytes 229400
  15.2 1.5 %circulant_block.1.refs_2_ = bf16[256,6144]{1,0:T(8,128)(2,1)S(1)} custom-call(f32[128,48]{1,0:T(8,128)S(1)} %reshape.3.w_ref, f32[448,128]{1,0:T(8,128)S(1)} %copy-done.4), custom_call_target="tpu_custom_call" | custom-call | flops 2000000000 | bytes 4194304 | tf_op jit(solution)/shard_map/circulant_block/pallas_call | solution.py:101
  16.6 0.3 collective-permute-done.3
  17.0 2.8 %collective-permute-done.5.refs_3_ = bf16[192,128]{1,0:T(8,128)(2,1)S(1)} collective-permute-done((bf16[192,128]{1,0:T(8,128)(2,1)S(1)}, bf16[192,128]{1,0:T(8,128)(2,1)S(1)}, u32[]{:S(2)}, u32[]{:S(2)}) %collective-permute-start.5) | collective-permute-done | bytes 49184 | tf_op jit(solution)/shard_map/ppermute | solution.py:454
  19.8 0.0 collective-permute-done.4.refs_2_
  19.8 0.0 collective-permute-start.6
  19.8 1.7 %collective-permute-done.6.refs_1_ = bf16[8,192,128]{2,1,0:T(8,128)(2,1)S(1)} collective-permute-done((bf16[8,192,128]{2,1,0:T(8,128)(2,1)S(1)}, bf16[8,192,128]{2,1,0:T(8,128)(2,1)S(1)}, u32[]{:S(2)}, u32[]{:S(2)}) %collective-permute-start.6) | collective-permute-done | bytes 393248 | tf_op jit(solution)/shard_map/ppermute | solution.py:415
  21.6 3.0 %partial_model.1.refs_1_ = f32[64,640]{1,0:T(8,128)S(1)} custom-call(bf16[8,192,128]{2,1,0:T(8,128)(2,1)S(1)} %pad_maximum_fusion.refs_0_, bf16[8,192,128]{2,1,0:T(8,128)(2,1)S(1)} %collective-permute-done.6.refs_1_, bf16[256,6144]{1,0:T(8,128)(2,1)S(1)} %circulant_block.1.refs_2_), custom_call_target="tpu_custom_call" | custom-call | flops 2000000000 | bytes 4194304 | tf_op jit(solution)/shard_map/partial_model/pallas_call | solution.py:164
  24.6 1.6 %collective-permute-start.7 = (f32[64,640]{1,0:T(8,128)S(1)}, f32[64,640]{1,0:T(8,128)S(1)}, u32[]{:S(2)}, u32[]{:S(2)}) collective-permute-start(f32[64,640]{1,0:T(8,128)S(1)} %partial_model.1.refs_1_), channel_id=1, source_target_pairs={{0,1},{1,0},{2,3},{3,2},{4,5},{5,4},{6,7},{7,6},{8,9},{9,8},{10,11... | collective-permute-start | bytes 491528 | tf_op jit(solution)/shard_map/ppermute | solution.py:415
  26.2 0.0 copy-done.2
  26.2 0.0 copy-done.3
  26.2 2.9 %elution_terms.1.refs_3_ = bf16[128,3072]{1,0:T(8,128)(2,1)S(1)} custom-call(bf16[192,128]{1,0:T(8,128)(2,1)S(1)} %pack_elution.1.refs_0_, bf16[8,192,128]{2,1,0:T(8,128)(2,1)S(1)} %collective-permute-done.6.refs_1_, bf16[192,128]{1,0:T(8,128)(2,1)S(1)} %collective-permute-done.4.refs_2_, bf16[192,128]{1,0:T(8,128)(2,1)S(1)} %collective-permute-done.5.refs_3_, ...), custom_call_target="tpu_custom_call" | custom-call | flops 1000000000 | bytes 2097152 | tf_op jit(solution)/shard_map/elution_terms/pallas_call | solution.py:239
  29.1 1.8 %collective-permute-done.7.refs_2_ = f32[64,640]{1,0:T(8,128)S(1)} collective-permute-done((f32[64,640]{1,0:T(8,128)S(1)}, f32[64,640]{1,0:T(8,128)S(1)}, u32[]{:S(2)}, u32[]{:S(2)}) %collective-permute-start.7) | collective-permute-done | bytes 163872 | tf_op jit(solution)/shard_map/ppermute | solution.py:415
  30.9 0.0 copy-done.1
  30.9 3.1 %model_products.1 = (f32[544,128]{1,0:T(8,128)S(1)}, f32[544,128]{1,0:T(8,128)S(1)}) custom-call(bf16[8,384,2048]{2,1,0:T(8,128)(2,1)S(1)} %copy-done.1, f32[64,640]{1,0:T(8,128)S(1)} %partial_model.1.refs_1_, f32[64,640]{1,0:T(8,128)S(1)} %collective-permute-done.7.refs_2_, bf16[128,3072]{1,0:T(8,128)(2,1)S(1)} %elution_terms.1.refs_3_, ...), custom_call_target="tpu_custom_call" | custom-call | flops 8000000000 | bytes 12582912 | tf_op jit(solution)/shard_map/model_products/pallas_call | solution.py:302
  34.1 0.1 collective-permute-start.8
  34.1 1.5 %collective-permute-done.8.b_ref.refs_1_ = f32[544,128]{1,0:T(8,128)S(1)} collective-permute-done((f32[544,128]{1,0:T(8,128)S(1)}, f32[544,128]{1,0:T(8,128)S(1)}, u32[]{:S(2)}, u32[]{:S(2)}) %collective-permute-start.8) | collective-permute-done | bytes 278560 | tf_op jit(solution)/shard_map/ppermute | solution.py:415
  35.7 0.1 collective-permute-start.13
  35.8 2.0 %collective-permute-start.11 = (f32[32,128]{1,0:T(8,128)S(1)}, f32[32,128]{1,0:T(8,128)S(1)}, u32[]{:S(2)}, u32[]{:S(2)}) collective-permute-start(f32[32,128]{1,0:T(8,128)S(1)} %get-tuple-element.28.refs_0_), channel_id=1, source_target_pairs={{0,24},{2,26},{4,28},{6,30},{8,16},{10,18},{12,20},{14,22},{16,8},... | collective-permute-start | bytes 49160 | tf_op jit(solution)/shard_map/ppermute | solution.py:415
  37.8 0.2 collective-permute-start.10
  38.0 2.2 %collective-permute-start.9 = (f32[32,128]{1,0:T(8,128)S(1)}, f32[32,128]{1,0:T(8,128)S(1)}, u32[]{:S(2)}, u32[]{:S(2)}) collective-permute-start(f32[32,128]{1,0:T(8,128)S(1)} %get-tuple-element.28.refs_0_), channel_id=1, source_target_pairs={{0,8},{2,10},{4,12},{6,14},{8,0},{10,2},{12,4},{14,6},{16,24},{18,... | collective-permute-start | bytes 49160 | tf_op jit(solution)/shard_map/ppermute | solution.py:415
  40.2 1.1 %collective-permute-done.11.refs_3_ = f32[32,128]{1,0:T(8,128)S(1)} collective-permute-done((f32[32,128]{1,0:T(8,128)S(1)}, f32[32,128]{1,0:T(8,128)S(1)}, u32[]{:S(2)}, u32[]{:S(2)}) %collective-permute-start.11) | collective-permute-done | bytes 16416 | tf_op jit(solution)/shard_map/ppermute | solution.py:415
  41.4 1.1 %collective-permute-done.10.refs_2_ = f32[32,128]{1,0:T(8,128)S(1)} collective-permute-done((f32[32,128]{1,0:T(8,128)S(1)}, f32[32,128]{1,0:T(8,128)S(1)}, u32[]{:S(2)}, u32[]{:S(2)}) %collective-permute-start.10) | collective-permute-done | bytes 16416 | tf_op jit(solution)/shard_map/ppermute | solution.py:415
  42.5 0.0 collective-permute-done.9.refs_1_
  42.5 1.4 %collective-permute-start.12 = (f32[32,128]{1,0:T(8,128)S(1)}, f32[32,128]{1,0:T(8,128)S(1)}, u32[]{:S(2)}, u32[]{:S(2)}) collective-permute-start(f32[32,128]{1,0:T(8,128)S(1)} %reduce_gram.1.refs_0_), channel_id=1, source_target_pairs={{0,4},{2,6},{4,0},{6,2},{8,12},{10,14},{12,8},{14,10},{16,20},{18,... | collective-permute-start | bytes 49160 | tf_op jit(solution)/shard_map/ppermute | solution.py:415
  43.9 0.0 collective-permute-done.13.refs_2_
  43.9 2.1 %collective-permute-start.14 = (f32[64,128]{1,0:T(8,128)S(1)}, f32[64,128]{1,0:T(8,128)S(1)}, u32[]{:S(2)}, u32[]{:S(2)}) collective-permute-start(f32[64,128]{1,0:T(8,128)S(1)} %get-tuple-element.30), channel_id=1, source_target_pairs={{0,8},{2,10},{4,12},{6,14},{8,0},{10,2},{12,4},{14,6},{16,24},{18,... | collective-permute-start | bytes 98312 | tf_op jit(solution)/shard_map/ppermute | solution.py:415
  46.0 1.0 %collective-permute-start.15 = (f32[64,128]{1,0:T(8,128)S(1)}, f32[64,128]{1,0:T(8,128)S(1)}, u32[]{:S(2)}, u32[]{:S(2)}) collective-permute-start(f32[64,128]{1,0:T(8,128)S(1)} %get-tuple-element.31), channel_id=1, source_target_pairs={{0,16},{2,18},{4,20},{6,22},{8,24},{10,26},{12,28},{14,30},{16,0},... | collective-permute-start | bytes 98312 | tf_op jit(solution)/shard_map/ppermute | solution.py:415
  47.0 1.5 %collective-permute-start.16 = (f32[64,128]{1,0:T(8,128)S(1)}, f32[64,128]{1,0:T(8,128)S(1)}, u32[]{:S(2)}, u32[]{:S(2)}) collective-permute-start(f32[64,128]{1,0:T(8,128)S(1)} %get-tuple-element.32), channel_id=1, source_target_pairs={{0,24},{2,26},{4,28},{6,30},{8,16},{10,18},{12,20},{14,22},{16,8},... | collective-permute-start | bytes 98312 | tf_op jit(solution)/shard_map/ppermute | solution.py:415
  48.5 0.0 collective-permute-done.12.refs_1_
  48.5 2.4 %invert_gram.1.inverse_ref = f32[64,128]{1,0:T(8,128)S(1)} custom-call(f32[32,128]{1,0:T(8,128)S(1)} %reduce_gram.1.refs_0_, f32[32,128]{1,0:T(8,128)S(1)} %collective-permute-done.12.refs_1_), custom_call_target="tpu_custom_call" | custom-call | flops 3000000000 | bytes 1024 | tf_op jit(solution)/shard_map/invert_gram/pallas_call | solution.py:402
  50.9 0.0 collective-permute-done.14.refs_3_
  50.9 0.0 collective-permute-done.15.refs_4_
  50.9 1.8 %collective-permute-done.16.refs_5_ = f32[64,128]{1,0:T(8,128)S(1)} collective-permute-done((f32[64,128]{1,0:T(8,128)S(1)}, f32[64,128]{1,0:T(8,128)S(1)}, u32[]{:S(2)}, u32[]{:S(2)}) %collective-permute-start.16) | collective-permute-done | bytes 32800 | tf_op jit(solution)/shard_map/ppermute | solution.py:415
  52.7 0.8 %finish.1 = f32[64,128]{1,0:T(8,128)} custom-call(f32[64,128]{1,0:T(8,128)S(1)} %invert_gram.1.inverse_ref, f32[544,128]{1,0:T(8,128)S(1)} %get-tuple-element.26.a_ref.refs_0_, f32[544,128]{1,0:T(8,128)S(1)} %collective-permute-done.8.b_ref.refs_1_, f32[256,128]{1,0:T(8,128)S(1)} %collective-permute-done.13.refs_2_, ...), custom_call_target="tpu_custom_call" | custom-call | flops 1000000 | bytes 1024 | tf_op jit(solution)/shard_map/finish/pallas_call | solution.py:402
  (5 shorter events, 0.1 us)
Async XLA Ops:
  0.0 0.8 %copy-start = (f32[192,64]{0,1:T(8,128)S(1)}, f32[192,64]{0,1:T(8,128)}, u32[]{:S(2)}) copy-start(f32[192,64]{0,1:T(8,128)} %param.7) | copy-start | bytes 147460
  0.8 25.4 %copy-start.2 = (f32[8,64]{1,0:T(8,128)S(1)}, f32[8,64]{1,0:T(8,128)}, u32[]{:S(2)}) copy-start(f32[8,64]{1,0:T(8,128)} %refs_4_.3) | copy-start | bytes 6148
  0.8 25.4 %copy-start.3 = (s32[8,64]{1,0:T(8,128)S(1)}, s32[8,64]{1,0:T(8,128)}, u32[]{:S(2)}) copy-start(s32[8,64]{1,0:T(8,128)} %refs_5_.3) | copy-start | bytes 6148
  1.0 7.3 %collective-permute-start.2 = (bf16[192,128]{1,0:T(8,128)(2,1)S(1)}, bf16[192,128]{1,0:T(8,128)(2,1)S(1)}, u32[]{:S(2)}, u32[]{:S(2)}) collective-permute-start(bf16[192,128]{1,0:T(8,128)(2,1)S(1)} %pack_elution.1.refs_0_), channel_id=1, source_target_pairs={{0,24},{2,26},{4,28},{6,30},{8,16},{10,18},{12,20},{14,22},{16,8},... | collective-permute-start | bytes 147464 | tf_op jit(solution)/shard_map/ppermute | solution.py:415
  6.1 5.0 %collective-permute-start.1 = (bf16[192,128]{1,0:T(8,128)(2,1)S(1)}, bf16[192,128]{1,0:T(8,128)(2,1)S(1)}, u32[]{:S(2)}, u32[]{:S(2)}) collective-permute-start(bf16[192,128]{1,0:T(8,128)(2,1)S(1)} %pack_elution.1.refs_0_), channel_id=1, source_target_pairs={{0,16},{2,18},{4,20},{6,22},{8,24},{10,26},{12,28},{14,30},{16,0},... | collective-permute-start | bytes 147464 | tf_op jit(solution)/shard_map/ppermute | solution.py:415
  6.1 5.0 %collective-permute-start = (bf16[192,128]{1,0:T(8,128)(2,1)S(1)}, bf16[192,128]{1,0:T(8,128)(2,1)S(1)}, u32[]{:S(2)}, u32[]{:S(2)}) collective-permute-start(bf16[192,128]{1,0:T(8,128)(2,1)S(1)} %pack_elution.1.refs_0_), channel_id=1, source_target_pairs={{0,8},{2,10},{4,12},{6,14},{8,0},{10,2},{12,4},{14,6},{16,24},{18,... | collective-permute-start | bytes 147464 | tf_op jit(solution)/shard_map/ppermute | solution.py:415
  7.6 23.3 %copy-start.1 = (bf16[8,384,2048]{2,1,0:T(8,128)(2,1)S(1)}, bf16[8,384,2048]{2,1,0:T(8,128)(2,1)}, u32[]{:S(2)}) copy-start(bf16[8,384,2048]{2,1,0:T(8,128)(2,1)} %refs_0_.1) | copy-start | bytes 37748740
  11.2 5.8 %collective-permute-start.3 = (bf16[4,192,128]{2,1,0:T(8,128)(2,1)S(1)}, bf16[4,192,128]{2,1,0:T(8,128)(2,1)S(1)}, u32[]{:S(2)}, u32[]{:S(2)}) collective-permute-start(bf16[4,192,128]{2,1,0:T(8,128)(2,1)S(1)} %pad_maximum_fusion.1), channel_id=1, source_target_pairs={{0,4},{2,6},{4,0},{6,2},{8,12},{10,14},{12,8},{14,10},{16,20},{18,... | collective-permute-start | bytes 589832 | tf_op jit(solution)/shard_map/ppermute | solution.py:415
  12.7 7.1 %collective-permute-start.5 = (bf16[192,128]{1,0:T(8,128)(2,1)S(1)}, bf16[192,128]{1,0:T(8,128)(2,1)S(1)}, u32[]{:S(2)}, u32[]{:S(2)}) collective-permute-start(bf16[192,128]{1,0:T(8,128)(2,1)S(1)} %pack_elution.1.refs_0_), channel_id=1, source_target_pairs={{0,3},{1,2},{2,5},{3,4},{4,7},{5,6},{6,9},{7,8},{8,11},{9,10},{10,... | collective-permute-start | bytes 147464 | tf_op jit(solution)/shard_map/ppermute | solution.py:454
  12.7 7.1 %collective-permute-start.4 = (bf16[192,128]{1,0:T(8,128)(2,1)S(1)}, bf16[192,128]{1,0:T(8,128)(2,1)S(1)}, u32[]{:S(2)}, u32[]{:S(2)}) collective-permute-start(bf16[192,128]{1,0:T(8,128)(2,1)S(1)} %pack_elution.1.refs_0_), channel_id=1, source_target_pairs={{0,1},{1,0},{2,3},{3,2},{4,5},{5,4},{6,7},{7,6},{8,9},{9,8},{10,11... | collective-permute-start | bytes 147464 | tf_op jit(solution)/shard_map/ppermute | solution.py:415
  14.2 0.9 %copy-start.4 = (f32[448,128]{1,0:T(8,128)S(1)}, f32[448,128]{1,0:T(8,128)}, u32[]{:S(2)}) copy-start(f32[448,128]{1,0:T(8,128)} %constant.2.clone.table_ref) | copy-start | bytes 688132
  19.8 1.7 %collective-permute-start.6 = (bf16[8,192,128]{2,1,0:T(8,128)(2,1)S(1)}, bf16[8,192,128]{2,1,0:T(8,128)(2,1)S(1)}, u32[]{:S(2)}, u32[]{:S(2)}) collective-permute-start(bf16[8,192,128]{2,1,0:T(8,128)(2,1)S(1)} %pad_maximum_fusion.refs_0_), channel_id=1, source_target_pairs={{0,2},{2,0},{4,6},{6,4},{8,10},{10,8},{12,14},{14,12},{16,18},{18,... | collective-permute-start | bytes 1179656 | tf_op jit(solution)/shard_map/ppermute | solution.py:415
  24.6 6.3 %collective-permute-start.7 = (f32[64,640]{1,0:T(8,128)S(1)}, f32[64,640]{1,0:T(8,128)S(1)}, u32[]{:S(2)}, u32[]{:S(2)}) collective-permute-start(f32[64,640]{1,0:T(8,128)S(1)} %partial_model.1.refs_1_), channel_id=1, source_target_pairs={{0,1},{1,0},{2,3},{3,2},{4,5},{5,4},{6,7},{7,6},{8,9},{9,8},{10,11... | collective-permute-start | bytes 491528 | tf_op jit(solution)/shard_map/ppermute | solution.py:415
  34.1 1.6 %collective-permute-start.8 = (f32[544,128]{1,0:T(8,128)S(1)}, f32[544,128]{1,0:T(8,128)S(1)}, u32[]{:S(2)}, u32[]{:S(2)}) collective-permute-start(f32[544,128]{1,0:T(8,128)S(1)} %get-tuple-element.27), channel_id=1, source_target_pairs={{0,2},{2,0},{4,6},{6,4},{8,10},{10,8},{12,14},{14,12},{16,18},{18,... | collective-permute-start | bytes 835592 | tf_op jit(solution)/shard_map/ppermute | solution.py:415
  35.7 8.2 %collective-permute-start.13 = (f32[256,128]{1,0:T(8,128)S(1)}, f32[256,128]{1,0:T(8,128)S(1)}, u32[]{:S(2)}, u32[]{:S(2)}) collective-permute-start(f32[256,128]{1,0:T(8,128)S(1)} %get-tuple-element.29), channel_id=1, source_target_pairs={{0,4},{2,6},{4,0},{6,2},{8,12},{10,14},{12,8},{14,10},{16,20},{18,... | collective-permute-start | bytes 393224 | tf_op jit(solution)/shard_map/ppermute | solution.py:415
  35.8 5.6 %collective-permute-start.11 = (f32[32,128]{1,0:T(8,128)S(1)}, f32[32,128]{1,0:T(8,128)S(1)}, u32[]{:S(2)}, u32[]{:S(2)}) collective-permute-start(f32[32,128]{1,0:T(8,128)S(1)} %get-tuple-element.28.refs_0_), channel_id=1, source_target_pairs={{0,24},{2,26},{4,28},{6,30},{8,16},{10,18},{12,20},{14,22},{16,8},... | collective-permute-start | bytes 49160 | tf_op jit(solution)/shard_map/ppermute | solution.py:415
  37.8 4.6 %collective-permute-start.10 = (f32[32,128]{1,0:T(8,128)S(1)}, f32[32,128]{1,0:T(8,128)S(1)}, u32[]{:S(2)}, u32[]{:S(2)}) collective-permute-start(f32[32,128]{1,0:T(8,128)S(1)} %get-tuple-element.28.refs_0_), channel_id=1, source_target_pairs={{0,16},{2,18},{4,20},{6,22},{8,24},{10,26},{12,28},{14,30},{16,0},... | collective-permute-start | bytes 49160 | tf_op jit(solution)/shard_map/ppermute | solution.py:415
  38.0 4.4 %collective-permute-start.9 = (f32[32,128]{1,0:T(8,128)S(1)}, f32[32,128]{1,0:T(8,128)S(1)}, u32[]{:S(2)}, u32[]{:S(2)}) collective-permute-start(f32[32,128]{1,0:T(8,128)S(1)} %get-tuple-element.28.refs_0_), channel_id=1, source_target_pairs={{0,8},{2,10},{4,12},{6,14},{8,0},{10,2},{12,4},{14,6},{16,24},{18,... | collective-permute-start | bytes 49160 | tf_op jit(solution)/shard_map/ppermute | solution.py:415
  42.5 6.0 %collective-permute-start.12 = (f32[32,128]{1,0:T(8,128)S(1)}, f32[32,128]{1,0:T(8,128)S(1)}, u32[]{:S(2)}, u32[]{:S(2)}) collective-permute-start(f32[32,128]{1,0:T(8,128)S(1)} %reduce_gram.1.refs_0_), channel_id=1, source_target_pairs={{0,4},{2,6},{4,0},{6,2},{8,12},{10,14},{12,8},{14,10},{16,20},{18,... | collective-permute-start | bytes 49160 | tf_op jit(solution)/shard_map/ppermute | solution.py:415
  43.9 6.9 %collective-permute-start.14 = (f32[64,128]{1,0:T(8,128)S(1)}, f32[64,128]{1,0:T(8,128)S(1)}, u32[]{:S(2)}, u32[]{:S(2)}) collective-permute-start(f32[64,128]{1,0:T(8,128)S(1)} %get-tuple-element.30), channel_id=1, source_target_pairs={{0,8},{2,10},{4,12},{6,14},{8,0},{10,2},{12,4},{14,6},{16,24},{18,... | collective-permute-start | bytes 98312 | tf_op jit(solution)/shard_map/ppermute | solution.py:415
  46.0 4.9 %collective-permute-start.15 = (f32[64,128]{1,0:T(8,128)S(1)}, f32[64,128]{1,0:T(8,128)S(1)}, u32[]{:S(2)}, u32[]{:S(2)}) collective-permute-start(f32[64,128]{1,0:T(8,128)S(1)} %get-tuple-element.31), channel_id=1, source_target_pairs={{0,16},{2,18},{4,20},{6,22},{8,24},{10,26},{12,28},{14,30},{16,0},... | collective-permute-start | bytes 98312 | tf_op jit(solution)/shard_map/ppermute | solution.py:415
  47.0 5.7 %collective-permute-start.16 = (f32[64,128]{1,0:T(8,128)S(1)}, f32[64,128]{1,0:T(8,128)S(1)}, u32[]{:S(2)}, u32[]{:S(2)}) collective-permute-start(f32[64,128]{1,0:T(8,128)S(1)} %get-tuple-element.32), channel_id=1, source_target_pairs={{0,24},{2,26},{4,28},{6,30},{8,16},{10,18},{12,20},{14,22},{16,8},... | collective-permute-start | bytes 98312 | tf_op jit(solution)/shard_map/ppermute | solution.py:415

commit v4 on v2

--- a/solution.py
+++ b/solution.py
@@ -51,7 +51,7 @@
     )(elution.T)
 
 
-def circulant_kernel(w_ref, table_ref, u_ref):
+def circulant_kernel(turn, w_ref, table_ref, u_ref):
     rows = w_ref.shape[1]
     w = w_ref[...]
     over_lanes = (((0,), (0,)), ((), ()))
@@ -70,6 +70,15 @@
     sub = lax.broadcasted_iota(jnp.int32, (LANES, LANES), 0)
     lane = lax.broadcasted_iota(jnp.int32, (LANES, LANES), 1)
 
+    if turn:
+        part = LANES - turn % LANES
+        near, after = (
+            pltpu.roll(jnp.concatenate([c[n:], c[:n]], axis=0), part % LANES, 1)
+            for n in (turn // LANES, turn // LANES + 1)
+        )
+        moved = jnp.where(lax.broadcasted_iota(jnp.int32, c.shape, 1) < part, near, after)
+        c = jnp.where(lax.axis_index("mz") == 1, moved, c)
+
     def turned(row):
         return pltpu.roll(jnp.broadcast_to(c[row : row + 1], (LANES, LANES)), 0, 1, stride=1, stride_axis=0)
 
@@ -82,7 +91,7 @@
         before = now
 
 
-def circulant(weights):
+def circulant(weights, turn):
     length = weights.size
     rows = length // LANES
 
@@ -99,7 +108,7 @@
         ]
     ).astype(np.float32)
     return pl.pallas_call(
-        circulant_kernel,
+        functools.partial(circulant_kernel, turn),
         out_shape=jax.ShapeDtypeStruct((2 * LANES, length), jnp.bfloat16),
         in_specs=vmem(2),
         out_specs=vmem(1)[0],
@@ -116,33 +125,49 @@
     freq_rank = lax.axis_index("freq")
     if planes:
         own_ref, came_ref = refs[:2]
-        mz_rank = lax.axis_index("mz")
         freq_count = 2 * own_ref.shape[0]
         rows = own_ref.shape[1]
-        empty = jnp.zeros((rows, LANES), jnp.bfloat16)
-        for block in range(-1, freq_count + 1):
+        padded = wide.shape[0] // freq_count
+        for block in range(freq_count):
             apart = lax.bitwise_xor((freq_rank + block) & (freq_count - 1), freq_rank)
             ref = came_ref if block % 2 else own_ref
             values = ref[pl.ds(block_place(apart, freq_count), 1)][0]
-            for here, half in ((values, mz_rank), (empty, 1 - mz_rank)):
-                to = pl.multiple_of(2 * REACH + (2 * block + half) * rows, 64)
-                wide[pl.ds(to, rows), 0:LANES] = here
-                wide[pl.ds(pl.multiple_of(to - LANES, 64), rows), LANES:] = here
-    else:
-        own_ref = refs[0]
-        step = own_ref.shape[1]
-        steps = length // step
-        bin_count = length // lax.axis_size("freq")
-        first = lax.rem(freq_rank * bin_count + length - REACH, length) // step
-
-        def bring(j, carry):
-            values = own_ref[pl.ds(lax.rem(first + j, steps), 1)][0]
-            to = pl.multiple_of(REACH + j * step, step)
-            wide[pl.ds(to, step), 0:LANES] = values
-            wide[pl.ds(pl.multiple_of(to - LANES, step), step), LANES:] = values
-            return carry
-
-        lax.fori_loop(0, (wide.shape[0] - REACH) // step, bring, 0)
+            at, before = block * padded, (block - 1) % freq_count * padded
+            wide[at : at + rows, 0:LANES] = values
+            wide[before : before + rows, LANES:] = values
+            wide[at + rows : at + padded, :] = jnp.zeros((padded - rows, 2 * LANES), jnp.bfloat16)
+        period = length // freq_count // LANES
+        for a in range(min(period, places)):
+            columns = []
+            for block in range(freq_count):
+                first = REACH // LANES + period * block - a
+                for n in range(first, first + padded // LANES):
+                    at = n % (length // LANES) * LANES
+                    columns.append(u_ref[:, at : at + LANES])
+            width = 2 * LANES if a + period < places else LANES
+            made = jnp.dot(
+                jnp.concatenate(columns, axis=1), wide[:, :width], preferred_element_type=jnp.float32
+            )
+            made = made[:LANES] + made[LANES:]
+            for half in range(width // LANES):
+                piece = made[:, half * LANES : (half + 1) * LANES].T
+                to = (a + half * period) * LANES
+                g_ref[:, to : to + LANES] = piece[:components] + piece[components:]
+        return
+    own_ref = refs[0]
+    step = own_ref.shape[1]
+    steps = length // step
+    bin_count = length // lax.axis_size("freq")
+    first = lax.rem(freq_rank * bin_count + length - REACH, length) // step
+
+    def bring(j, carry):
+        values = own_ref[pl.ds(lax.rem(first + j, steps), 1)][0]
+        to = pl.multiple_of(REACH + j * step, step)
+        wide[pl.ds(to, step), 0:LANES] = values
+        wide[pl.ds(pl.multiple_of(to - LANES, step), step), LANES:] = values
+        return carry
+
+    lax.fori_loop(0, (wide.shape[0] - REACH) // step, bring, 0)
     for a in range(0, places, 2):
         at = REACH + a * LANES
         made = jnp.dot(u_ref[...], wide[at : at + length, :], preferred_element_type=jnp.float32)
@@ -160,7 +185,11 @@
     length = u.shape[1]
     places = -(-(bin_count + REACH) // LANES)
     planes = len(gathered) == 2
-    wide_rows = 2 * REACH + length + bin_count if planes else REACH + length + 2 * LANES * ((places - 1) // 2)
+    if planes:
+        own = gathered[0]
+        wide_rows = 2 * own.shape[0] * (-(-own.shape[1] // LANES) * LANES)
+    else:
+        wide_rows = REACH + length + 2 * LANES * ((places - 1) // 2)
     return pl.pallas_call(
         functools.partial(model_kernel, places, planes),
         out_shape=jax.ShapeDtypeStruct((components, places * LANES), jnp.float32),
@@ -197,26 +226,40 @@
                 terms[components + at : components + at + height, to] = low[:, :width]
 
 
+def pair_kernel(mine_ref, came_ref, o_ref):
+    rows = mine_ref.shape[0]
+    freq_count = 2 * came_ref.shape[0]
+    freq_rank = lax.axis_index("freq")
+    apart = lax.bitwise_xor((freq_rank - 1) & (freq_count - 1), freq_rank)
+    o_ref[0:rows, :] = came_ref[pl.ds(block_place(apart, freq_count), 1)][0]
+    o_ref[rows:, :] = mine_ref[...]
+
+
+def window_pair(mine, came):
+    return pl.pallas_call(
+        pair_kernel,
+        out_shape=jax.ShapeDtypeStruct((2 * mine.shape[0], mine.shape[1]), mine.dtype),
+        in_specs=vmem(2),
+        out_specs=vmem(1)[0],
+        compiler_params=pltpu.CompilerParams(vmem_limit_bytes=8 * MIB),
+        name="window_pair",
+    )(mine, came)
+
+
 def elution_kernel(planes, *refs):
     amp_ref, lag_ref, terms, window = refs[-4:]
     components = amp_ref.shape[1]
     bin_count = terms.shape[1] // amp_ref.shape[0]
     freq_rank = lax.axis_index("freq")
     if planes:
-        mine_ref, came_ref, near_ref, far_ref = refs[:4]
+        pair_ref, other_ref = refs[:2]
         mz_rank = lax.axis_index("mz")
-        freq_count = 2 * came_ref.shape[0]
-        rows = mine_ref.shape[0]
-        apart = lax.bitwise_xor((freq_rank - 1) & (freq_count - 1), freq_rank)
-        before = came_ref[pl.ds(block_place(apart, freq_count), 1)][0]
+        rows = pair_ref.shape[0] // 2
         skip = bin_count - REACH
-        for block, half, values in (
-            (0, mz_rank, before),
-            (0, 1 - mz_rank, far_ref[...]),
-            (1, mz_rank, mine_ref[...]),
-            (1, 1 - mz_rank, near_ref[...]),
-        ):
-            window[pl.ds(pl.multiple_of((2 * block + half) * rows, 64), rows), :] = values
+        for ref, half in ((pair_ref, mz_rank), (other_ref, 1 - mz_rank)):
+            for block in range(2):
+                to = pl.multiple_of((2 * block + half) * rows, 64)
+                window[pl.ds(to, rows), :] = ref[block * rows : (block + 1) * rows, :]
     else:
         own_ref = refs[0]
         step = own_ref.shape[1]
@@ -281,7 +324,7 @@
         if planes:
             freq_rank = lax.axis_index("freq")
             core = freq_rank & 1
-            place = block_place(lax.bitwise_xor(freq_rank, 2 * n + core), 2 * chunks)
+            place = n // 2 + ((lax.bitwise_xor(freq_rank, 2 * n) >> 1) & 1) * (chunks // 2)
             at = pl.ds(pl.multiple_of(place * components, components), components)
             even, odd = made[:, :LANES], made[:, LANES:]
             keep_ref[at, :] = jnp.where(core == 0, even, odd)
@@ -353,29 +396,35 @@
     return right
 
 
-def summed(refs, rows, tail):
-    total = refs[0][0:rows] + refs[1][0:rows]
-    gram = refs[0][refs[0].shape[0] - tail :] + refs[1][refs[1].shape[0] - tail :]
-    for ref in refs[2:]:
-        total = total + ref[0:rows]
-        gram = gram + ref[ref.shape[0] - tail :]
-    return total, gram
-
-
-def stage_kernel(tail, count, *refs):
-    outs = refs[-count:]
-    rows = outs[0].shape[0] - tail
-    total, gram = summed(refs[:-count], (count + 1) * rows, tail)
-    for n, o_ref in enumerate(outs):
-        o_ref[0:rows, :] = total[(n + 1) * rows : (n + 2) * rows]
-        o_ref[rows:, :] = gram
-
-
-def solve_planes_kernel(tail, *refs):
-    o_ref = refs[-1]
-    total, gram = summed(refs[:-1], o_ref.shape[0], tail)
+def total_of(refs, at, rows):
+    total = refs[0][at : at + rows]
+    for ref in refs[1:]:
+        total = total + ref[at : at + rows]
+    return total
+
+
+def halve_kernel(tail, a_ref, b_ref, o_ref):
+    rows = o_ref.shape[0] - tail
+    o_ref[...] = total_of((a_ref, b_ref), rows, rows + tail)
+
+
+def spread_kernel(tail, a_ref, b_ref, c_ref, o_ref):
+    rows = o_ref.shape[1] - tail
+    count = o_ref.shape[0]
+    gram = total_of((a_ref, b_ref), 2 * count * rows, tail) + c_ref[count * rows :, :]
+    for n in range(count):
+        o_ref[n, 0:rows, :] = total_of((a_ref, b_ref, c_ref), n * rows, rows)
+        o_ref[n, rows:, :] = gram
+
+
+def solve_planes_kernel(x_ref, o_ref):
+    components = o_ref.shape[0]
+    total = x_ref[0]
+    for n in range(1, x_ref.shape[0]):
+        total = total + x_ref[n]
+    gram = total[components:]
     gram = jnp.concatenate([gram, pltpu.roll(gram, gram.shape[1] // 2, 1)], axis=0)
-    o_ref[...] = eliminate(gram, total)
+    o_ref[...] = eliminate(gram, total[:components])
 
 
 def solve_kernel(g_ref, n_ref, o_ref):
@@ -384,16 +433,15 @@
     o_ref[...] = eliminate(gram, n_ref[...])
 
 
-def small_call(kernel, out_shape, name, *args, count=1):
-    outs = pl.pallas_call(
+def small_call(kernel, shape, name, *args):
+    return pl.pallas_call(
         kernel,
-        out_shape=(jax.ShapeDtypeStruct(out_shape, jnp.float32),) * count,
+        out_shape=jax.ShapeDtypeStruct(shape, jnp.float32),
         in_specs=vmem(len(args)),
-        out_specs=tuple(vmem(count)),
+        out_specs=vmem(1)[0],
         compiler_params=pltpu.CompilerParams(vmem_limit_bytes=8 * MIB),
         name=name,
     )(*args)
-    return outs
 
 
 def swap(x, axes, count, value):
@@ -420,44 +468,40 @@
     )
     if not planes:
         gathered = lax.all_gather(mine, axes, axis=0).reshape(-1, math.gcd(bin_count, LANES), LANES)
-        g = partial_model((gathered,), circulant(bin_weight.reshape(LANES, -1)), bin_count, components)
+        g = partial_model((gathered,), circulant(bin_weight.reshape(LANES, -1), 0), bin_count, components)
         shifted = elution_terms((gathered,), loadings, shifts, bin_count)
         numerator, gram = product(intensity, (g,), shifted, loadings, shifts, planes)
         gram = lax.psum(gram, "freq")
         owned = lax.psum_scatter(numerator, "freq", scatter_dimension=1, tiled=True)
-        return small_call(solve_kernel, (components, own), "solve", gram, owned)[0]
+        return small_call(solve_kernel, (components, own), "solve", gram, owned)
     z_steps = range(4, freq_count, 4)
     held = jnp.stack([mine] + [swap(mine, "freq", freq_count, step) for step in z_steps])
     weights = bin_weight.reshape(LANES, -1)
-    held, weights, later = lax.optimization_barrier((held, weights, mine))
-    near = swap(later, "mz", mz_count, 1)
-    onward = [
-        (f * mz_count + y, (f + 1) % freq_count * mz_count + 1 - y)
-        for f in range(freq_count)
-        for y in range(mz_count)
-    ]
-    far = lax.ppermute(later, axes, onward)
+    held, weights = lax.optimization_barrier((held, weights))
     held = jnp.concatenate([held, swap(held, "freq", freq_count, 2)], axis=0)
-    u = circulant(weights)
-    held, u, near, far = lax.optimization_barrier((held, u, near, far))
+    u = circulant(weights, elution.shape[0])
+    held, u = lax.optimization_barrier((held, u))
     came = swap(held, "freq", freq_count, 1)
+    pair = window_pair(mine, came)
+    other = swap(pair, "mz", mz_count, 1)
     g = partial_model((held, came), u, bin_count, components)
+    g, other = lax.optimization_barrier((g, other))
     models = (g, swap(g, "mz", mz_count, 1))
-    shifted = elution_terms((mine, came, near, far), loadings, shifts, bin_count)
+    shifted = elution_terms((pair, other), loadings, shifts, bin_count)
     keep, send = product(intensity, models, shifted, loadings, shifts, planes)
     tail = components // 2
-    quarter = freq_count // 4 * components
-    parts = [keep, swap(send, "freq", freq_count, 1)]
-    (send,) = small_call(
-        functools.partial(stage_kernel, tail, 1), (quarter + tail, LANES), "reduce_stage", *parts
+    chips = freq_count // 4
+    came = swap(send, "freq", freq_count, 1)
+    send = small_call(
+        functools.partial(halve_kernel, tail), (chips * components + tail, LANES), "reduce_cores", keep, came
     )
-    parts.append(swap(send, "freq", freq_count, 2))
-    count = len(z_steps)
-    sends = small_call(
-        functools.partial(stage_kernel, tail, count), (components + tail, LANES), "reduce_stage", *parts, count=count
+    across = swap(send, "freq", freq_count, 2)
+    send = small_call(
+        functools.partial(spread_kernel, tail), (chips, components + tail, LANES), "reduce_x", keep, came, across
     )
-    parts += [swap(send, "freq", freq_count, step) for send, step in zip(sends, z_steps)]
-    return small_call(functools.partial(solve_planes_kernel, tail), (components, own), "solve", *parts)[0]
+    groups = [[4 * z + chip for z in range(chips)] for chip in range(4)]
+    spread = lax.all_to_all(send, "freq", 0, 0, axis_index_groups=groups)
+    return small_call(solve_planes_kernel, (components, own), "solve", spread)
 
 
 def solution(mesh):

time: 52.1 us -> 53.3 us (1.023)
  blocking collectives: 0 us -> 10.1 us
  waiting for transfers between devices: 20.3 us -> 15.3 us
  starting transfers between devices: 15 us -> 12.1 us
  Pallas kernels: 13.8 us -> 12.7 us
    all_to_all x0 -> x1, blocking collectives: none -> 10.1 us  [on_device(): spread = lax.all_to_all(send, 'freq', 0, 0, axis_index_groups=groups)]
    ppermute x12 -> x9, starting transfers between devices: 15 us -> 12.1 us  [swap(): return lax.ppermute(x, axes, [(i, i ^ value) for i in range(count)])]
    ppermute x1 -> x0, waiting for transfers between devices: 2.81 us -> none  [on_device(): far = lax.ppermute(later, axes, onward)]
    ppermute x12 -> x9, waiting for transfers between devices: 17.5 us -> 15.3 us  [swap(): return lax.ppermute(x, axes, [(i, i ^ value) for i in range(count)])]
    pallas_call x1, Pallas kernels: 3.04 us -> 1.92 us  [partial_model(): pl.pallas_call(functools.partial(model_kernel, places, planes), out_shape...]
    pallas_call x4 -> x5, Pallas kernels: 4.54 us -> 4.63 us  [the longest x3 3.09 us: small_call(): pl.pallas_call(kernel, out_shape=jax.ShapeDtypeStruct(shape, jnp.float32)...]
  transfers between devices with their start and end apart: 13 -> 9, of which waited for: 10 -> 8; matrix products, arithmetic and copies ran while one was open for 2% -> 2% of each run, Pallas kernels for 8% -> 12%
where the time goes in v4:
time: 53.3 us; the launch traced here: 53 us
  waiting for transfers between devices  15.3 us (29%)
  Pallas kernels  12.7 us (24%)
  starting transfers between devices  12.1 us (23%)
  blocking collectives  10.1 us (19%)
  local copies, waits for them, and re-layouts  2.6 us (5%)
    ppermute x9, waiting for transfers between devices, swap(): return lax.ppermute(x, axes, [(i, i ^ value) for i in range(count)])  15.3 us
    ppermute x9, starting transfers between devices, swap(): return lax.ppermute(x, axes, [(i, i ^ value) for i in range(count)])  12.1 us
    all_to_all x1, blocking collectives, on_device(): spread = lax.all_to_all(send, 'freq', 0, 0, axis_index_groups=groups)  10.1 us
    pallas_call x1, Pallas kernels, product(): pl.pallas_call(functools.partial(product_kernel, len(models), planes), ou...  3.14 us
    pallas_call x3, Pallas kernels, small_call(): pl.pallas_call(kernel, out_shape=jax.ShapeDtypeStruct(shape, jnp.float32)...  3.09 us
    pallas_call x1, Pallas kernels, elution_terms(): pl.pallas_call(functools.partial(elution_kernel, planes), out_shape=jax.S...  2.89 us
    pallas_call x1, Pallas kernels, partial_model(): pl.pallas_call(functools.partial(model_kernel, places, planes), out_shape...  1.92 us
    unnamed x10, local copies, waits for them, and re-layouts  1.79 us
  transfers between devices with their start and end apart: 9, of which 8 were waited for; matrix products, arithmetic and copies ran while one was open for 2% of the time, Pallas kernels for 12%

profile of v4, /device:TPU:0, one launch (start us, length us, event | category | flops | bytes accessed | tf_op | source)
XLA Modules:
  0.0 53.0 jit_solution(14817907255565493786)
XLA Ops:
  0.0 0.0 copy-start
  0.0 0.8 %copy-done = f32[192,64]{0,1:T(8,128)S(1)} copy-done((f32[192,64]{0,1:T(8,128)S(1)}, f32[192,64]{0,1:T(8,128)}, u32[]{:S(2)}) %copy-start) | copy-done | bytes 49176
  0.8 0.0 copy-start.2
  0.8 0.0 copy-start.3
  0.8 0.2 pack_elution.1.mine_ref
  1.0 5.1 %collective-permute-start.2 = (bf16[192,128]{1,0:T(8,128)(2,1)S(1)}, bf16[192,128]{1,0:T(8,128)(2,1)S(1)}, u32[]{:S(2)}, u32[]{:S(2)}) collective-permute-start(bf16[192,128]{1,0:T(8,128)(2,1)S(1)} %pack_elution.1.mine_ref), channel_id=1, source_target_pairs={{0,24},{2,26},{4,28},{6,30},{8,16},{10,18},{12,20},{14,22},{16,8},... | collective-permute-start | bytes 147464 | tf_op jit(solution)/shard_map/ppermute | solution.py:448
  6.1 0.0 collective-permute-start.1
  6.1 0.6 %collective-permute-start = (bf16[192,128]{1,0:T(8,128)(2,1)S(1)}, bf16[192,128]{1,0:T(8,128)(2,1)S(1)}, u32[]{:S(2)}, u32[]{:S(2)}) collective-permute-start(bf16[192,128]{1,0:T(8,128)(2,1)S(1)} %pack_elution.1.mine_ref), channel_id=1, source_target_pairs={{0,8},{2,10},{4,12},{6,14},{8,0},{10,2},{12,4},{14,6},{16,24},{18,... | collective-permute-start | bytes 147464 | tf_op jit(solution)/shard_map/ppermute | solution.py:448
  6.8 0.8 %reshape.3.w_ref = f32[128,48]{1,0:T(8,128)S(1)} reshape(f32[6144]{0:T(1024)} %param.10) | data formatting | bytes 49152 | tf_op jit(solution)/shard_map/reshape | solution.py:479
  7.6 0.0 copy-start.1
  7.6 0.8 %collective-permute-done.2 = bf16[192,128]{1,0:T(8,128)(2,1)S(1)} collective-permute-done((bf16[192,128]{1,0:T(8,128)(2,1)S(1)}, bf16[192,128]{1,0:T(8,128)(2,1)S(1)}, u32[]{:S(2)}, u32[]{:S(2)}) %collective-permute-start.2) | collective-permute-done | bytes 49184 | tf_op jit(solution)/shard_map/ppermute | solution.py:448
  8.4 2.8 %collective-permute-done.1 = bf16[192,128]{1,0:T(8,128)(2,1)S(1)} collective-permute-done((bf16[192,128]{1,0:T(8,128)(2,1)S(1)}, bf16[192,128]{1,0:T(8,128)(2,1)S(1)}, u32[]{:S(2)}, u32[]{:S(2)}) %collective-permute-start.1) | collective-permute-done | bytes 49184 | tf_op jit(solution)/shard_map/ppermute | solution.py:448
  11.1 0.0 collective-permute-done
  11.2 1.6 %collective-permute-start.3 = (bf16[4,192,128]{2,1,0:T(8,128)(2,1)S(1)}, bf16[4,192,128]{2,1,0:T(8,128)(2,1)S(1)}, u32[]{:S(2)}, u32[]{:S(2)}) collective-permute-start(bf16[4,192,128]{2,1,0:T(8,128)(2,1)S(1)} %pad_maximum_fusion.1), channel_id=1, source_target_pairs={{0,4},{2,6},{4,0},{6,2},{8,12},{10,14},{12,8},{14,10},{16,20},{18,... | collective-permute-start | bytes 589832 | tf_op jit(solution)/shard_map/ppermute | solution.py:448
  12.7 0.0 copy-start.4
  12.7 0.9 %copy-done.4 = f32[448,128]{1,0:T(8,128)S(1)} copy-done((f32[448,128]{1,0:T(8,128)S(1)}, f32[448,128]{1,0:T(8,128)}, u32[]{:S(2)}) %copy-start.4) | copy-done | bytes 229400
  13.7 1.5 %circulant_block.1.refs_2_ = bf16[256,6144]{1,0:T(8,128)(2,1)S(1)} custom-call(f32[128,48]{1,0:T(8,128)S(1)} %reshape.3.w_ref, f32[448,128]{1,0:T(8,128)S(1)} %copy-done.4), custom_call_target="tpu_custom_call" | custom-call | flops 2000000000 | bytes 4194304 | tf_op jit(solution)/shard_map/circulant_block/pallas_call | solution.py:110
  15.2 1.8 %collective-permute-done.3 = bf16[4,192,128]{2,1,0:T(8,128)(2,1)S(1)} collective-permute-done((bf16[4,192,128]{2,1,0:T(8,128)(2,1)S(1)}, bf16[4,192,128]{2,1,0:T(8,128)(2,1)S(1)}, u32[]{:S(2)}, u32[]{:S(2)}) %collective-permute-start.3) | collective-permute-done | bytes 196640 | tf_op jit(solution)/shard_map/ppermute | solution.py:448
  17.0 0.1 collective-permute-start.4
  17.1 1.7 %collective-permute-done.4.refs_1_.came_ref = bf16[8,192,128]{2,1,0:T(8,128)(2,1)S(1)} collective-permute-done((bf16[8,192,128]{2,1,0:T(8,128)(2,1)S(1)}, bf16[8,192,128]{2,1,0:T(8,128)(2,1)S(1)}, u32[]{:S(2)}, u32[]{:S(2)}) %collective-permute-start.4) | collective-permute-done | bytes 393248 | tf_op jit(solution)/shard_map/ppermute | solution.py:448
  18.8 1.6 %collective-permute-start.5 = (bf16[384,128]{1,0:T(8,128)(2,1)S(1)}, bf16[384,128]{1,0:T(8,128)(2,1)S(1)}, u32[]{:S(2)}, u32[]{:S(2)}) collective-permute-start(bf16[384,128]{1,0:T(8,128)(2,1)S(1)} %window_pair.1.refs_0_), channel_id=1, source_target_pairs={{0,1},{1,0},{2,3},{3,2},{4,5},{5,4},{6,7},{7,6},{8,9},{9,8},{10,11... | collective-permute-start | bytes 294920 | tf_op jit(solution)/shard_map/ppermute | solution.py:448
  20.4 1.9 %partial_model.1.refs_1_ = f32[64,640]{1,0:T(8,128)S(1)} custom-call(bf16[8,192,128]{2,1,0:T(8,128)(2,1)S(1)} %pad_maximum_fusion.refs_0_, bf16[8,192,128]{2,1,0:T(8,128)(2,1)S(1)} %collective-permute-done.4.refs_1_.came_ref, bf16[256,6144]{1,0:T(8,128)(2,1)S(1)} %circulant_block.1.refs_2_), custom_call_target="tpu_custom_call" | custom-call | flops 2000000000 | bytes 4194304 | tf_op jit(solution)/shard_map/partial_model/pallas_call | solution.py:193
  22.3 1.4 %collective-permute-done.5.refs_1_ = bf16[384,128]{1,0:T(8,128)(2,1)S(1)} collective-permute-done((bf16[384,128]{1,0:T(8,128)(2,1)S(1)}, bf16[384,128]{1,0:T(8,128)(2,1)S(1)}, u32[]{:S(2)}, u32[]{:S(2)}) %collective-permute-start.5) | collective-permute-done | bytes 98336 | tf_op jit(solution)/shard_map/ppermute | solution.py:448
  23.7 1.5 %collective-permute-start.6 = (f32[64,640]{1,0:T(8,128)S(1)}, f32[64,640]{1,0:T(8,128)S(1)}, u32[]{:S(2)}, u32[]{:S(2)}) collective-permute-start(f32[64,640]{1,0:T(8,128)S(1)} %partial_model.1.refs_1_), channel_id=1, source_target_pairs={{0,1},{1,0},{2,3},{3,2},{4,5},{5,4},{6,7},{7,6},{8,9},{9,8},{10,11... | collective-permute-start | bytes 491528 | tf_op jit(solution)/shard_map/ppermute | solution.py:448
  25.2 0.0 copy-done.2
  25.2 0.0 copy-done.3
  25.2 2.9 %elution_terms.1.refs_3_ = bf16[128,3072]{1,0:T(8,128)(2,1)S(1)} custom-call(bf16[384,128]{1,0:T(8,128)(2,1)S(1)} %window_pair.1.refs_0_, bf16[384,128]{1,0:T(8,128)(2,1)S(1)} %collective-permute-done.5.refs_1_, f32[8,64]{1,0:T(8,128)S(1)} %copy-done.2, s32[8,64]{1,0:T(8,128)S(1)} %copy-done.3), custom_call_target="tpu_custom_call" | custom-call | flops 1000000000 | bytes 2097152 | tf_op jit(solution)/shard_map/elution_terms/pallas_call | solution.py:282
  28.1 1.0 %collective-permute-done.6.refs_2_ = f32[64,640]{1,0:T(8,128)S(1)} collective-permute-done((f32[64,640]{1,0:T(8,128)S(1)}, f32[64,640]{1,0:T(8,128)S(1)}, u32[]{:S(2)}, u32[]{:S(2)}) %collective-permute-start.6) | collective-permute-done | bytes 163872 | tf_op jit(solution)/shard_map/ppermute | solution.py:448
  29.1 0.0 copy-done.1
  29.1 3.1 %model_products.1 = (f32[544,128]{1,0:T(8,128)S(1)}, f32[544,128]{1,0:T(8,128)S(1)}) custom-call(bf16[8,384,2048]{2,1,0:T(8,128)(2,1)S(1)} %copy-done.1, f32[64,640]{1,0:T(8,128)S(1)} %partial_model.1.refs_1_, f32[64,640]{1,0:T(8,128)S(1)} %collective-permute-done.6.refs_2_, bf16[128,3072]{1,0:T(8,128)(2,1)S(1)} %elution_terms.1.refs_3_, ...), custom_call_target="tpu_custom_call" | custom-call | flops 8000000000 | bytes 12582912 | tf_op jit(solution)/shard_map/model_products/pallas_call | solution.py:345
  32.3 0.1 collective-permute-start.7
  32.3 1.5 %collective-permute-done.7.b_ref = f32[544,128]{1,0:T(8,128)S(1)} collective-permute-done((f32[544,128]{1,0:T(8,128)S(1)}, f32[544,128]{1,0:T(8,128)S(1)}, u32[]{:S(2)}, u32[]{:S(2)}) %collective-permute-start.7) | collective-permute-done | bytes 278560 | tf_op jit(solution)/shard_map/ppermute | solution.py:448
  33.9 1.6 %collective-permute-start.8 = (f32[288,128]{1,0:T(8,128)S(1)}, f32[288,128]{1,0:T(8,128)S(1)}, u32[]{:S(2)}, u32[]{:S(2)}) collective-permute-start(f32[288,128]{1,0:T(8,128)S(1)} %reduce_cores.1), channel_id=1, source_target_pairs={{0,4},{2,6},{4,0},{6,2},{8,12},{10,14},{12,8},{14,10},{16,20},{18,... | collective-permute-start | bytes 442376 | tf_op jit(solution)/shard_map/ppermute | solution.py:448
  35.5 4.4 %collective-permute-done.8.c_ref = f32[288,128]{1,0:T(8,128)S(1)} collective-permute-done((f32[288,128]{1,0:T(8,128)S(1)}, f32[288,128]{1,0:T(8,128)S(1)}, u32[]{:S(2)}, u32[]{:S(2)}) %collective-permute-start.8) | collective-permute-done | bytes 147488 | tf_op jit(solution)/shard_map/ppermute | solution.py:448
  39.9 10.1 %all_to_all.5.x_ref = f32[4,96,128]{2,1,0:T(8,128)S(1)} all-to-all(f32[4,96,128]{2,1,0:T(8,128)S(1)} %reduce_x.1), channel_id=1, replica_groups={{0,8,16,24},{2,10,18,26},{4,12,20,28},{6,14,22,30},{1,9,17,25},{3,11,19..., dimensions={0} | all-to-all | bytes 393216 | tf_op jit(solution)/shard_map/all_to_all | solution.py:503
  49.9 3.0 %solve.1 = f32[64,128]{1,0:T(8,128)} custom-call(f32[4,96,128]{2,1,0:T(8,128)S(1)} %all_to_all.5.x_ref), custom_call_target="tpu_custom_call" | custom-call | tf_op jit(solution)/shard_map/solve/pallas_call | solution.py:437
  (5 shorter events, 0.1 us)
Async XLA Ops:
  0.0 0.8 %copy-start = (f32[192,64]{0,1:T(8,128)S(1)}, f32[192,64]{0,1:T(8,128)}, u32[]{:S(2)}) copy-start(f32[192,64]{0,1:T(8,128)} %param.7) | copy-start | bytes 147460
  0.8 24.4 %copy-start.2 = (f32[8,64]{1,0:T(8,128)S(1)}, f32[8,64]{1,0:T(8,128)}, u32[]{:S(2)}) copy-start(f32[8,64]{1,0:T(8,128)} %refs_4_.1) | copy-start | bytes 6148
  0.8 24.4 %copy-start.3 = (s32[8,64]{1,0:T(8,128)S(1)}, s32[8,64]{1,0:T(8,128)}, u32[]{:S(2)}) copy-start(s32[8,64]{1,0:T(8,128)} %refs_5_.1) | copy-start | bytes 6148
  1.0 7.3 %collective-permute-start.2 = (bf16[192,128]{1,0:T(8,128)(2,1)S(1)}, bf16[192,128]{1,0:T(8,128)(2,1)S(1)}, u32[]{:S(2)}, u32[]{:S(2)}) collective-permute-start(bf16[192,128]{1,0:T(8,128)(2,1)S(1)} %pack_elution.1.mine_ref), channel_id=1, source_target_pairs={{0,24},{2,26},{4,28},{6,30},{8,16},{10,18},{12,20},{14,22},{16,8},... | collective-permute-start | bytes 147464 | tf_op jit(solution)/shard_map/ppermute | solution.py:448
  6.1 5.0 %collective-permute-start.1 = (bf16[192,128]{1,0:T(8,128)(2,1)S(1)}, bf16[192,128]{1,0:T(8,128)(2,1)S(1)}, u32[]{:S(2)}, u32[]{:S(2)}) collective-permute-start(bf16[192,128]{1,0:T(8,128)(2,1)S(1)} %pack_elution.1.mine_ref), channel_id=1, source_target_pairs={{0,16},{2,18},{4,20},{6,22},{8,24},{10,26},{12,28},{14,30},{16,0},... | collective-permute-start | bytes 147464 | tf_op jit(solution)/shard_map/ppermute | solution.py:448
  6.1 5.0 %collective-permute-start = (bf16[192,128]{1,0:T(8,128)(2,1)S(1)}, bf16[192,128]{1,0:T(8,128)(2,1)S(1)}, u32[]{:S(2)}, u32[]{:S(2)}) collective-permute-start(bf16[192,128]{1,0:T(8,128)(2,1)S(1)} %pack_elution.1.mine_ref), channel_id=1, source_target_pairs={{0,8},{2,10},{4,12},{6,14},{8,0},{10,2},{12,4},{14,6},{16,24},{18,... | collective-permute-start | bytes 147464 | tf_op jit(solution)/shard_map/ppermute | solution.py:448
  7.6 21.5 %copy-start.1 = (bf16[8,384,2048]{2,1,0:T(8,128)(2,1)S(1)}, bf16[8,384,2048]{2,1,0:T(8,128)(2,1)}, u32[]{:S(2)}) copy-start(bf16[8,384,2048]{2,1,0:T(8,128)(2,1)} %refs_0_.1) | copy-start | bytes 37748740
  11.2 5.8 %collective-permute-start.3 = (bf16[4,192,128]{2,1,0:T(8,128)(2,1)S(1)}, bf16[4,192,128]{2,1,0:T(8,128)(2,1)S(1)}, u32[]{:S(2)}, u32[]{:S(2)}) collective-permute-start(bf16[4,192,128]{2,1,0:T(8,128)(2,1)S(1)} %pad_maximum_fusion.1), channel_id=1, source_target_pairs={{0,4},{2,6},{4,0},{6,2},{8,12},{10,14},{12,8},{14,10},{16,20},{18,... | collective-permute-start | bytes 589832 | tf_op jit(solution)/shard_map/ppermute | solution.py:448
  12.7 0.9 %copy-start.4 = (f32[448,128]{1,0:T(8,128)S(1)}, f32[448,128]{1,0:T(8,128)}, u32[]{:S(2)}) copy-start(f32[448,128]{1,0:T(8,128)} %constant.2.clone.table_ref) | copy-start | bytes 688132
  17.0 1.8 %collective-permute-start.4 = (bf16[8,192,128]{2,1,0:T(8,128)(2,1)S(1)}, bf16[8,192,128]{2,1,0:T(8,128)(2,1)S(1)}, u32[]{:S(2)}, u32[]{:S(2)}) collective-permute-start(bf16[8,192,128]{2,1,0:T(8,128)(2,1)S(1)} %pad_maximum_fusion.refs_0_), channel_id=1, source_target_pairs={{0,2},{2,0},{4,6},{6,4},{8,10},{10,8},{12,14},{14,12},{16,18},{18,... | collective-permute-start | bytes 1179656 | tf_op jit(solution)/shard_map/ppermute | solution.py:448
  18.8 4.9 %collective-permute-start.5 = (bf16[384,128]{1,0:T(8,128)(2,1)S(1)}, bf16[384,128]{1,0:T(8,128)(2,1)S(1)}, u32[]{:S(2)}, u32[]{:S(2)}) collective-permute-start(bf16[384,128]{1,0:T(8,128)(2,1)S(1)} %window_pair.1.refs_0_), channel_id=1, source_target_pairs={{0,1},{1,0},{2,3},{3,2},{4,5},{5,4},{6,7},{7,6},{8,9},{9,8},{10,11... | collective-permute-start | bytes 294920 | tf_op jit(solution)/shard_map/ppermute | solution.py:448
  23.7 5.4 %collective-permute-start.6 = (f32[64,640]{1,0:T(8,128)S(1)}, f32[64,640]{1,0:T(8,128)S(1)}, u32[]{:S(2)}, u32[]{:S(2)}) collective-permute-start(f32[64,640]{1,0:T(8,128)S(1)} %partial_model.1.refs_1_), channel_id=1, source_target_pairs={{0,1},{1,0},{2,3},{3,2},{4,5},{5,4},{6,7},{7,6},{8,9},{9,8},{10,11... | collective-permute-start | bytes 491528 | tf_op jit(solution)/shard_map/ppermute | solution.py:448
  32.3 1.6 %collective-permute-start.7 = (f32[544,128]{1,0:T(8,128)S(1)}, f32[544,128]{1,0:T(8,128)S(1)}, u32[]{:S(2)}, u32[]{:S(2)}) collective-permute-start(f32[544,128]{1,0:T(8,128)S(1)} %get-tuple-element.20), channel_id=1, source_target_pairs={{0,2},{2,0},{4,6},{6,4},{8,10},{10,8},{12,14},{14,12},{16,18},{18,... | collective-permute-start | bytes 835592 | tf_op jit(solution)/shard_map/ppermute | solution.py:448
  33.9 6.0 %collective-permute-start.8 = (f32[288,128]{1,0:T(8,128)S(1)}, f32[288,128]{1,0:T(8,128)S(1)}, u32[]{:S(2)}, u32[]{:S(2)}) collective-permute-start(f32[288,128]{1,0:T(8,128)S(1)} %reduce_cores.1), channel_id=1, source_target_pairs={{0,4},{2,6},{4,0},{6,2},{8,12},{10,14},{12,8},{14,10},{16,20},{18,... | collective-permute-start | bytes 442376 | tf_op jit(solution)/shard_map/ppermute | solution.py:448

commit v5 on v4

--- a/solution.py
+++ b/solution.py
@@ -324,7 +324,7 @@
         if planes:
             freq_rank = lax.axis_index("freq")
             core = freq_rank & 1
-            place = n // 2 + ((lax.bitwise_xor(freq_rank, 2 * n) >> 1) & 1) * (chunks // 2)
+            place = block_place(lax.bitwise_xor(freq_rank, 2 * n + core), 2 * chunks)
             at = pl.ds(pl.multiple_of(place * components, components), components)
             even, odd = made[:, :LANES], made[:, LANES:]
             keep_ref[at, :] = jnp.where(core == 0, even, odd)
@@ -408,20 +408,19 @@
     o_ref[...] = total_of((a_ref, b_ref), rows, rows + tail)
 
 
-def spread_kernel(tail, a_ref, b_ref, c_ref, o_ref):
-    rows = o_ref.shape[1] - tail
-    count = o_ref.shape[0]
+def spread_kernel(tail, a_ref, b_ref, c_ref, *outs):
+    rows = outs[0].shape[0] - tail
+    count = len(outs)
     gram = total_of((a_ref, b_ref), 2 * count * rows, tail) + c_ref[count * rows :, :]
-    for n in range(count):
-        o_ref[n, 0:rows, :] = total_of((a_ref, b_ref, c_ref), n * rows, rows)
-        o_ref[n, rows:, :] = gram
-
-
-def solve_planes_kernel(x_ref, o_ref):
+    for n, o_ref in enumerate(outs):
+        o_ref[0:rows, :] = total_of((a_ref, b_ref, c_ref), n * rows, rows)
+        o_ref[rows:, :] = gram
+
+
+def solve_planes_kernel(*refs):
+    o_ref = refs[-1]
     components = o_ref.shape[0]
-    total = x_ref[0]
-    for n in range(1, x_ref.shape[0]):
-        total = total + x_ref[n]
+    total = total_of(refs[:-1], 0, refs[0].shape[0])
     gram = total[components:]
     gram = jnp.concatenate([gram, pltpu.roll(gram, gram.shape[1] // 2, 1)], axis=0)
     o_ref[...] = eliminate(gram, total[:components])
@@ -433,12 +432,12 @@
     o_ref[...] = eliminate(gram, n_ref[...])
 
 
-def small_call(kernel, shape, name, *args):
+def small_call(kernel, shape, name, *args, count=1):
     return pl.pallas_call(
         kernel,
-        out_shape=jax.ShapeDtypeStruct(shape, jnp.float32),
+        out_shape=(jax.ShapeDtypeStruct(shape, jnp.float32),) * count,
         in_specs=vmem(len(args)),
-        out_specs=vmem(1)[0],
+        out_specs=tuple(vmem(count)),
         compiler_params=pltpu.CompilerParams(vmem_limit_bytes=8 * MIB),
         name=name,
     )(*args)
@@ -473,7 +472,7 @@
         numerator, gram = product(intensity, (g,), shifted, loadings, shifts, planes)
         gram = lax.psum(gram, "freq")
         owned = lax.psum_scatter(numerator, "freq", scatter_dimension=1, tiled=True)
-        return small_call(solve_kernel, (components, own), "solve", gram, owned)
+        return small_call(solve_kernel, (components, own), "solve", gram, owned)[0]
     z_steps = range(4, freq_count, 4)
     held = jnp.stack([mine] + [swap(mine, "freq", freq_count, step) for step in z_steps])
     weights = bin_weight.reshape(LANES, -1)
@@ -485,23 +484,21 @@
     pair = window_pair(mine, came)
     other = swap(pair, "mz", mz_count, 1)
     g = partial_model((held, came), u, bin_count, components)
-    g, other = lax.optimization_barrier((g, other))
     models = (g, swap(g, "mz", mz_count, 1))
     shifted = elution_terms((pair, other), loadings, shifts, bin_count)
     keep, send = product(intensity, models, shifted, loadings, shifts, planes)
     tail = components // 2
     chips = freq_count // 4
     came = swap(send, "freq", freq_count, 1)
-    send = small_call(
+    (send,) = small_call(
         functools.partial(halve_kernel, tail), (chips * components + tail, LANES), "reduce_cores", keep, came
     )
     across = swap(send, "freq", freq_count, 2)
-    send = small_call(
-        functools.partial(spread_kernel, tail), (chips, components + tail, LANES), "reduce_x", keep, came, across
+    own_part, *sends = small_call(
+        functools.partial(spread_kernel, tail), (components + tail, LANES), "reduce_x", keep, came, across, count=chips
     )
-    groups = [[4 * z + chip for z in range(chips)] for chip in range(4)]
-    spread = lax.all_to_all(send, "freq", 0, 0, axis_index_groups=groups)
-    return small_call(solve_planes_kernel, (components, own), "solve", spread)
+    parts = [swap(send, "freq", freq_count, step) for send, step in zip(sends, z_steps)]
+    return small_call(solve_planes_kernel, (components, own), "solve", own_part, *parts)[0]
 
 
 def solution(mesh):

time: 53.3 us -> 51 us (0.957)
  blocking collectives: 10.1 us -> 0 us
  waiting for transfers between devices: 15.3 us -> 19.6 us
  starting transfers between devices: 12.1 us -> 15.6 us
    all_to_all x1 -> x0, blocking collectives: 10.1 us -> none  [on_device(): spread = lax.all_to_all(send, 'freq', 0, 0, axis_index_groups=groups)]
    ppermute x9 -> x12, waiting for transfers between devices: 15.3 us -> 19.6 us  [swap(): return lax.ppermute(x, axes, [(i, i ^ value) for i in range(count)])]
    ppermute x9 -> x12, starting transfers between devices: 12.1 us -> 15.6 us  [swap(): return lax.ppermute(x, axes, [(i, i ^ value) for i in range(count)])]
  transfers between devices with their start and end apart: 9 -> 12, of which waited for: 8 -> 10; matrix products, arithmetic and copies ran while one was open for 2% -> 2% of each run, Pallas kernels for 12% -> 12%
where the time goes in v5:
time: 51 us; the launch traced here: 50.7 us
  waiting for transfers between devices  19.6 us (38%)
  starting transfers between devices  15.6 us (31%)
  Pallas kernels  12.8 us (25%)
  local copies, waits for them, and re-layouts  2.6 us (5%)
    ppermute x12, waiting for transfers between devices, swap(): return lax.ppermute(x, axes, [(i, i ^ value) for i in range(count)])  19.6 us
    ppermute x12, starting transfers between devices, swap(): return lax.ppermute(x, axes, [(i, i ^ value) for i in range(count)])  15.6 us
    pallas_call x1, Pallas kernels, product(): pl.pallas_call(functools.partial(product_kernel, len(models), planes), ou...  3.15 us
    pallas_call x3, Pallas kernels, small_call(): pl.pallas_call(kernel, out_shape=(jax.ShapeDtypeStruct(shape, jnp.float32...  3.09 us
    pallas_call x1, Pallas kernels, elution_terms(): pl.pallas_call(functools.partial(elution_kernel, planes), out_shape=jax.S...  2.89 us
    pallas_call x1, Pallas kernels, partial_model(): pl.pallas_call(functools.partial(model_kernel, places, planes), out_shape...  1.92 us
    unnamed x10, local copies, waits for them, and re-layouts  1.79 us
    pallas_call x1, Pallas kernels, circulant(): pl.pallas_call(functools.partial(circulant_kernel, turn), out_shape=jax.S...  1.53 us
  transfers between devices with their start and end apart: 12, of which 10 were waited for; matrix products, arithmetic and copies ran while one was open for 2% of the time, Pallas kernels for 12%

profile of v5, /device:TPU:0, one launch (start us, length us, event | category | flops | bytes accessed | tf_op | source)
XLA Modules:
  0.0 50.7 jit_solution(1268146730662406306)
XLA Ops:
  0.0 0.0 copy-start
  0.0 0.8 %copy-done = f32[192,64]{0,1:T(8,128)S(1)} copy-done((f32[192,64]{0,1:T(8,128)S(1)}, f32[192,64]{0,1:T(8,128)}, u32[]{:S(2)}) %copy-start) | copy-done | bytes 49176
  0.8 0.0 copy-start.2
  0.8 0.0 copy-start.3
  0.8 0.2 pack_elution.1.mine_ref
  1.0 5.1 %collective-permute-start.2 = (bf16[192,128]{1,0:T(8,128)(2,1)S(1)}, bf16[192,128]{1,0:T(8,128)(2,1)S(1)}, u32[]{:S(2)}, u32[]{:S(2)}) collective-permute-start(bf16[192,128]{1,0:T(8,128)(2,1)S(1)} %pack_elution.1.mine_ref), channel_id=1, source_target_pairs={{0,24},{2,26},{4,28},{6,30},{8,16},{10,18},{12,20},{14,22},{16,8},... | collective-permute-start | bytes 147464 | tf_op jit(solution)/shard_map/ppermute | solution.py:447
  6.1 0.0 collective-permute-start.1
  6.1 0.6 %collective-permute-start = (bf16[192,128]{1,0:T(8,128)(2,1)S(1)}, bf16[192,128]{1,0:T(8,128)(2,1)S(1)}, u32[]{:S(2)}, u32[]{:S(2)}) collective-permute-start(bf16[192,128]{1,0:T(8,128)(2,1)S(1)} %pack_elution.1.mine_ref), channel_id=1, source_target_pairs={{0,8},{2,10},{4,12},{6,14},{8,0},{10,2},{12,4},{14,6},{16,24},{18,... | collective-permute-start | bytes 147464 | tf_op jit(solution)/shard_map/ppermute | solution.py:447
  6.8 0.8 %reshape.3.w_ref = f32[128,48]{1,0:T(8,128)S(1)} reshape(f32[6144]{0:T(1024)} %param.10) | data formatting | bytes 49152 | tf_op jit(solution)/shard_map/reshape | solution.py:478
  7.6 0.0 copy-start.1
  7.6 0.8 %collective-permute-done.2 = bf16[192,128]{1,0:T(8,128)(2,1)S(1)} collective-permute-done((bf16[192,128]{1,0:T(8,128)(2,1)S(1)}, bf16[192,128]{1,0:T(8,128)(2,1)S(1)}, u32[]{:S(2)}, u32[]{:S(2)}) %collective-permute-start.2) | collective-permute-done | bytes 49184 | tf_op jit(solution)/shard_map/ppermute | solution.py:447
  8.4 2.8 %collective-permute-done.1 = bf16[192,128]{1,0:T(8,128)(2,1)S(1)} collective-permute-done((bf16[192,128]{1,0:T(8,128)(2,1)S(1)}, bf16[192,128]{1,0:T(8,128)(2,1)S(1)}, u32[]{:S(2)}, u32[]{:S(2)}) %collective-permute-start.1) | collective-permute-done | bytes 49184 | tf_op jit(solution)/shard_map/ppermute | solution.py:447
  11.1 0.0 collective-permute-done
  11.2 1.6 %collective-permute-start.3 = (bf16[4,192,128]{2,1,0:T(8,128)(2,1)S(1)}, bf16[4,192,128]{2,1,0:T(8,128)(2,1)S(1)}, u32[]{:S(2)}, u32[]{:S(2)}) collective-permute-start(bf16[4,192,128]{2,1,0:T(8,128)(2,1)S(1)} %pad_maximum_fusion.1), channel_id=1, source_target_pairs={{0,4},{2,6},{4,0},{6,2},{8,12},{10,14},{12,8},{14,10},{16,20},{18,... | collective-permute-start | bytes 589832 | tf_op jit(solution)/shard_map/ppermute | solution.py:447
  12.7 0.0 copy-start.4
  12.7 0.9 %copy-done.4 = f32[448,128]{1,0:T(8,128)S(1)} copy-done((f32[448,128]{1,0:T(8,128)S(1)}, f32[448,128]{1,0:T(8,128)}, u32[]{:S(2)}) %copy-start.4) | copy-done | bytes 229400
  13.7 1.5 %circulant_block.1.refs_2_ = bf16[256,6144]{1,0:T(8,128)(2,1)S(1)} custom-call(f32[128,48]{1,0:T(8,128)S(1)} %reshape.3.w_ref, f32[448,128]{1,0:T(8,128)S(1)} %copy-done.4), custom_call_target="tpu_custom_call" | custom-call | flops 2000000000 | bytes 4194304 | tf_op jit(solution)/shard_map/circulant_block/pallas_call | solution.py:110
  15.2 1.8 %collective-permute-done.3 = bf16[4,192,128]{2,1,0:T(8,128)(2,1)S(1)} collective-permute-done((bf16[4,192,128]{2,1,0:T(8,128)(2,1)S(1)}, bf16[4,192,128]{2,1,0:T(8,128)(2,1)S(1)}, u32[]{:S(2)}, u32[]{:S(2)}) %collective-permute-start.3) | collective-permute-done | bytes 196640 | tf_op jit(solution)/shard_map/ppermute | solution.py:447
  17.0 0.1 collective-permute-start.4
  17.1 1.7 %collective-permute-done.4.refs_1_.came_ref = bf16[8,192,128]{2,1,0:T(8,128)(2,1)S(1)} collective-permute-done((bf16[8,192,128]{2,1,0:T(8,128)(2,1)S(1)}, bf16[8,192,128]{2,1,0:T(8,128)(2,1)S(1)}, u32[]{:S(2)}, u32[]{:S(2)}) %collective-permute-start.4) | collective-permute-done | bytes 393248 | tf_op jit(solution)/shard_map/ppermute | solution.py:447
  18.8 1.6 %collective-permute-start.6 = (bf16[384,128]{1,0:T(8,128)(2,1)S(1)}, bf16[384,128]{1,0:T(8,128)(2,1)S(1)}, u32[]{:S(2)}, u32[]{:S(2)}) collective-permute-start(bf16[384,128]{1,0:T(8,128)(2,1)S(1)} %window_pair.1.refs_0_), channel_id=1, source_target_pairs={{0,1},{1,0},{2,3},{3,2},{4,5},{5,4},{6,7},{7,6},{8,9},{9,8},{10,11... | collective-permute-start | bytes 294920 | tf_op jit(solution)/shard_map/ppermute | solution.py:447
  20.4 1.9 %partial_model.1.refs_1_ = f32[64,640]{1,0:T(8,128)S(1)} custom-call(bf16[8,192,128]{2,1,0:T(8,128)(2,1)S(1)} %pad_maximum_fusion.refs_0_, bf16[8,192,128]{2,1,0:T(8,128)(2,1)S(1)} %collective-permute-done.4.refs_1_.came_ref, bf16[256,6144]{1,0:T(8,128)(2,1)S(1)} %circulant_block.1.refs_2_), custom_call_target="tpu_custom_call" | custom-call | flops 2000000000 | bytes 4194304 | tf_op jit(solution)/shard_map/partial_model/pallas_call | solution.py:193
  22.3 0.6 %collective-permute-start.5 = (f32[64,640]{1,0:T(8,128)S(1)}, f32[64,640]{1,0:T(8,128)S(1)}, u32[]{:S(2)}, u32[]{:S(2)}) collective-permute-start(f32[64,640]{1,0:T(8,128)S(1)} %partial_model.1.refs_1_), channel_id=1, source_target_pairs={{0,1},{1,0},{2,3},{3,2},{4,5},{5,4},{6,7},{7,6},{8,9},{9,8},{10,11... | collective-permute-start | bytes 491528 | tf_op jit(solution)/shard_map/ppermute | solution.py:447
  22.9 0.8 %collective-permute-done.6.refs_1_ = bf16[384,128]{1,0:T(8,128)(2,1)S(1)} collective-permute-done((bf16[384,128]{1,0:T(8,128)(2,1)S(1)}, bf16[384,128]{1,0:T(8,128)(2,1)S(1)}, u32[]{:S(2)}, u32[]{:S(2)}) %collective-permute-start.6) | collective-permute-done | bytes 98336 | tf_op jit(solution)/shard_map/ppermute | solution.py:447
  23.7 0.0 copy-done.2
  23.7 0.0 copy-done.3
  23.7 2.9 %elution_terms.1.refs_3_ = bf16[128,3072]{1,0:T(8,128)(2,1)S(1)} custom-call(bf16[384,128]{1,0:T(8,128)(2,1)S(1)} %window_pair.1.refs_0_, bf16[384,128]{1,0:T(8,128)(2,1)S(1)} %collective-permute-done.6.refs_1_, f32[8,64]{1,0:T(8,128)S(1)} %copy-done.2, s32[8,64]{1,0:T(8,128)S(1)} %copy-done.3), custom_call_target="tpu_custom_call" | custom-call | flops 1000000000 | bytes 2097152 | tf_op jit(solution)/shard_map/elution_terms/pallas_call | solution.py:282
  26.6 1.7 %collective-permute-done.5.refs_2_ = f32[64,640]{1,0:T(8,128)S(1)} collective-permute-done((f32[64,640]{1,0:T(8,128)S(1)}, f32[64,640]{1,0:T(8,128)S(1)}, u32[]{:S(2)}, u32[]{:S(2)}) %collective-permute-start.5) | collective-permute-done | bytes 163872 | tf_op jit(solution)/shard_map/ppermute | solution.py:447
  28.3 0.0 copy-done.1
  28.3 3.1 %model_products.1 = (f32[544,128]{1,0:T(8,128)S(1)}, f32[544,128]{1,0:T(8,128)S(1)}) custom-call(bf16[8,384,2048]{2,1,0:T(8,128)(2,1)S(1)} %copy-done.1, f32[64,640]{1,0:T(8,128)S(1)} %partial_model.1.refs_1_, f32[64,640]{1,0:T(8,128)S(1)} %collective-permute-done.5.refs_2_, bf16[128,3072]{1,0:T(8,128)(2,1)S(1)} %elution_terms.1.refs_3_, ...), custom_call_target="tpu_custom_call" | custom-call | flops 8000000000 | bytes 12582912 | tf_op jit(solution)/shard_map/model_products/pallas_call | solution.py:345
  31.5 0.1 collective-permute-start.7
  31.6 1.5 %collective-permute-done.7.b_ref = f32[544,128]{1,0:T(8,128)S(1)} collective-permute-done((f32[544,128]{1,0:T(8,128)S(1)}, f32[544,128]{1,0:T(8,128)S(1)}, u32[]{:S(2)}, u32[]{:S(2)}) %collective-permute-start.7) | collective-permute-done | bytes 278560 | tf_op jit(solution)/shard_map/ppermute | solution.py:447
  33.1 1.6 %collective-permute-start.8 = (f32[288,128]{1,0:T(8,128)S(1)}, f32[288,128]{1,0:T(8,128)S(1)}, u32[]{:S(2)}, u32[]{:S(2)}) collective-permute-start(f32[288,128]{1,0:T(8,128)S(1)} %reduce_cores.1), channel_id=1, source_target_pairs={{0,4},{2,6},{4,0},{6,2},{8,12},{10,14},{12,8},{14,10},{16,20},{18,... | collective-permute-start | bytes 442376 | tf_op jit(solution)/shard_map/ppermute | solution.py:447
  34.7 4.4 %collective-permute-done.8.c_ref = f32[288,128]{1,0:T(8,128)S(1)} collective-permute-done((f32[288,128]{1,0:T(8,128)S(1)}, f32[288,128]{1,0:T(8,128)S(1)}, u32[]{:S(2)}, u32[]{:S(2)}) %collective-permute-start.8) | collective-permute-done | bytes 147488 | tf_op jit(solution)/shard_map/ppermute | solution.py:447
  39.1 0.8 %collective-permute-start.9 = (f32[96,128]{1,0:T(8,128)S(1)}, f32[96,128]{1,0:T(8,128)S(1)}, u32[]{:S(2)}, u32[]{:S(2)}) collective-permute-start(f32[96,128]{1,0:T(8,128)S(1)} %get-tuple-element.22), channel_id=1, source_target_pairs={{0,8},{2,10},{4,12},{6,14},{8,0},{10,2},{12,4},{14,6},{16,24},{18,... | collective-permute-start | bytes 147464 | tf_op jit(solution)/shard_map/ppermute | solution.py:447
  39.9 1.9 %collective-permute-start.10 = (f32[96,128]{1,0:T(8,128)S(1)}, f32[96,128]{1,0:T(8,128)S(1)}, u32[]{:S(2)}, u32[]{:S(2)}) collective-permute-start(f32[96,128]{1,0:T(8,128)S(1)} %get-tuple-element.23), channel_id=1, source_target_pairs={{0,16},{2,18},{4,20},{6,22},{8,24},{10,26},{12,28},{14,30},{16,0},... | collective-permute-start | bytes 147464 | tf_op jit(solution)/shard_map/ppermute | solution.py:447
  41.8 1.8 %collective-permute-start.11 = (f32[96,128]{1,0:T(8,128)S(1)}, f32[96,128]{1,0:T(8,128)S(1)}, u32[]{:S(2)}, u32[]{:S(2)}) collective-permute-start(f32[96,128]{1,0:T(8,128)S(1)} %get-tuple-element.24), channel_id=1, source_target_pairs={{0,24},{2,26},{4,28},{6,30},{8,16},{10,18},{12,20},{14,22},{16,8},... | collective-permute-start | bytes 147464 | tf_op jit(solution)/shard_map/ppermute | solution.py:447
  43.6 0.0 collective-permute-done.9.refs_1_
  43.6 1.4 %collective-permute-done.10.refs_2_ = f32[96,128]{1,0:T(8,128)S(1)} collective-permute-done((f32[96,128]{1,0:T(8,128)S(1)}, f32[96,128]{1,0:T(8,128)S(1)}, u32[]{:S(2)}, u32[]{:S(2)}) %collective-permute-start.10) | collective-permute-done | bytes 49184 | tf_op jit(solution)/shard_map/ppermute | solution.py:447
  45.0 2.7 %collective-permute-done.11.refs_3_ = f32[96,128]{1,0:T(8,128)S(1)} collective-permute-done((f32[96,128]{1,0:T(8,128)S(1)}, f32[96,128]{1,0:T(8,128)S(1)}, u32[]{:S(2)}, u32[]{:S(2)}) %collective-permute-start.11) | collective-permute-done | bytes 49184 | tf_op jit(solution)/shard_map/ppermute | solution.py:447
  47.7 3.0 %solve.1 = f32[64,128]{1,0:T(8,128)} custom-call(f32[96,128]{1,0:T(8,128)S(1)} %get-tuple-element.21.refs_0_, f32[96,128]{1,0:T(8,128)S(1)} %collective-permute-done.9.refs_1_, f32[96,128]{1,0:T(8,128)S(1)} %collective-permute-done.10.refs_2_, f32[96,128]{1,0:T(8,128)S(1)} %collective-permute-done.11.refs_3_), custom_call_target="tpu_custom_call" | custom-call | tf_op jit(solution)/shard_map/solve/pallas_call | solution.py:436
  (5 shorter events, 0.1 us)
Async XLA Ops:
  0.0 0.8 %copy-start = (f32[192,64]{0,1:T(8,128)S(1)}, f32[192,64]{0,1:T(8,128)}, u32[]{:S(2)}) copy-start(f32[192,64]{0,1:T(8,128)} %param.7) | copy-start | bytes 147460
  0.8 22.9 %copy-start.2 = (f32[8,64]{1,0:T(8,128)S(1)}, f32[8,64]{1,0:T(8,128)}, u32[]{:S(2)}) copy-start(f32[8,64]{1,0:T(8,128)} %refs_4_.1) | copy-start | bytes 6148
  0.8 22.9 %copy-start.3 = (s32[8,64]{1,0:T(8,128)S(1)}, s32[8,64]{1,0:T(8,128)}, u32[]{:S(2)}) copy-start(s32[8,64]{1,0:T(8,128)} %refs_5_.1) | copy-start | bytes 6148
  1.0 7.3 %collective-permute-start.2 = (bf16[192,128]{1,0:T(8,128)(2,1)S(1)}, bf16[192,128]{1,0:T(8,128)(2,1)S(1)}, u32[]{:S(2)}, u32[]{:S(2)}) collective-permute-start(bf16[192,128]{1,0:T(8,128)(2,1)S(1)} %pack_elution.1.mine_ref), channel_id=1, source_target_pairs={{0,24},{2,26},{4,28},{6,30},{8,16},{10,18},{12,20},{14,22},{16,8},... | collective-permute-start | bytes 147464 | tf_op jit(solution)/shard_map/ppermute | solution.py:447
  6.1 5.0 %collective-permute-start.1 = (bf16[192,128]{1,0:T(8,128)(2,1)S(1)}, bf16[192,128]{1,0:T(8,128)(2,1)S(1)}, u32[]{:S(2)}, u32[]{:S(2)}) collective-permute-start(bf16[192,128]{1,0:T(8,128)(2,1)S(1)} %pack_elution.1.mine_ref), channel_id=1, source_target_pairs={{0,16},{2,18},{4,20},{6,22},{8,24},{10,26},{12,28},{14,30},{16,0},... | collective-permute-start | bytes 147464 | tf_op jit(solution)/shard_map/ppermute | solution.py:447
  6.1 5.0 %collective-permute-start = (bf16[192,128]{1,0:T(8,128)(2,1)S(1)}, bf16[192,128]{1,0:T(8,128)(2,1)S(1)}, u32[]{:S(2)}, u32[]{:S(2)}) collective-permute-start(bf16[192,128]{1,0:T(8,128)(2,1)S(1)} %pack_elution.1.mine_ref), channel_id=1, source_target_pairs={{0,8},{2,10},{4,12},{6,14},{8,0},{10,2},{12,4},{14,6},{16,24},{18,... | collective-permute-start | bytes 147464 | tf_op jit(solution)/shard_map/ppermute | solution.py:447
  7.6 20.8 %copy-start.1 = (bf16[8,384,2048]{2,1,0:T(8,128)(2,1)S(1)}, bf16[8,384,2048]{2,1,0:T(8,128)(2,1)}, u32[]{:S(2)}) copy-start(bf16[8,384,2048]{2,1,0:T(8,128)(2,1)} %refs_0_.1) | copy-start | bytes 37748740
  11.2 5.8 %collective-permute-start.3 = (bf16[4,192,128]{2,1,0:T(8,128)(2,1)S(1)}, bf16[4,192,128]{2,1,0:T(8,128)(2,1)S(1)}, u32[]{:S(2)}, u32[]{:S(2)}) collective-permute-start(bf16[4,192,128]{2,1,0:T(8,128)(2,1)S(1)} %pad_maximum_fusion.1), channel_id=1, source_target_pairs={{0,4},{2,6},{4,0},{6,2},{8,12},{10,14},{12,8},{14,10},{16,20},{18,... | collective-permute-start | bytes 589832 | tf_op jit(solution)/shard_map/ppermute | solution.py:447
  12.7 0.9 %copy-start.4 = (f32[448,128]{1,0:T(8,128)S(1)}, f32[448,128]{1,0:T(8,128)}, u32[]{:S(2)}) copy-start(f32[448,128]{1,0:T(8,128)} %constant.2.clone.table_ref) | copy-start | bytes 688132
  17.0 1.8 %collective-permute-start.4 = (bf16[8,192,128]{2,1,0:T(8,128)(2,1)S(1)}, bf16[8,192,128]{2,1,0:T(8,128)(2,1)S(1)}, u32[]{:S(2)}, u32[]{:S(2)}) collective-permute-start(bf16[8,192,128]{2,1,0:T(8,128)(2,1)S(1)} %pad_maximum_fusion.refs_0_), channel_id=1, source_target_pairs={{0,2},{2,0},{4,6},{6,4},{8,10},{10,8},{12,14},{14,12},{16,18},{18,... | collective-permute-start | bytes 1179656 | tf_op jit(solution)/shard_map/ppermute | solution.py:447
  18.8 4.9 %collective-permute-start.6 = (bf16[384,128]{1,0:T(8,128)(2,1)S(1)}, bf16[384,128]{1,0:T(8,128)(2,1)S(1)}, u32[]{:S(2)}, u32[]{:S(2)}) collective-permute-start(bf16[384,128]{1,0:T(8,128)(2,1)S(1)} %window_pair.1.refs_0_), channel_id=1, source_target_pairs={{0,1},{1,0},{2,3},{3,2},{4,5},{5,4},{6,7},{7,6},{8,9},{9,8},{10,11... | collective-permute-start | bytes 294920 | tf_op jit(solution)/shard_map/ppermute | solution.py:447
  22.3 6.0 %collective-permute-start.5 = (f32[64,640]{1,0:T(8,128)S(1)}, f32[64,640]{1,0:T(8,128)S(1)}, u32[]{:S(2)}, u32[]{:S(2)}) collective-permute-start(f32[64,640]{1,0:T(8,128)S(1)} %partial_model.1.refs_1_), channel_id=1, source_target_pairs={{0,1},{1,0},{2,3},{3,2},{4,5},{5,4},{6,7},{7,6},{8,9},{9,8},{10,11... | collective-permute-start | bytes 491528 | tf_op jit(solution)/shard_map/ppermute | solution.py:447
  31.5 1.6 %collective-permute-start.7 = (f32[544,128]{1,0:T(8,128)S(1)}, f32[544,128]{1,0:T(8,128)S(1)}, u32[]{:S(2)}, u32[]{:S(2)}) collective-permute-start(f32[544,128]{1,0:T(8,128)S(1)} %get-tuple-element.20), channel_id=1, source_target_pairs={{0,2},{2,0},{4,6},{6,4},{8,10},{10,8},{12,14},{14,12},{16,18},{18,... | collective-permute-start | bytes 835592 | tf_op jit(solution)/shard_map/ppermute | solution.py:447
  33.1 6.0 %collective-permute-start.8 = (f32[288,128]{1,0:T(8,128)S(1)}, f32[288,128]{1,0:T(8,128)S(1)}, u32[]{:S(2)}, u32[]{:S(2)}) collective-permute-start(f32[288,128]{1,0:T(8,128)S(1)} %reduce_cores.1), channel_id=1, source_target_pairs={{0,4},{2,6},{4,0},{6,2},{8,12},{10,14},{12,8},{14,10},{16,20},{18,... | collective-permute-start | bytes 442376 | tf_op jit(solution)/shard_map/ppermute | solution.py:447
  39.1 4.5 %collective-permute-start.9 = (f32[96,128]{1,0:T(8,128)S(1)}, f32[96,128]{1,0:T(8,128)S(1)}, u32[]{:S(2)}, u32[]{:S(2)}) collective-permute-start(f32[96,128]{1,0:T(8,128)S(1)} %get-tuple-element.22), channel_id=1, source_target_pairs={{0,8},{2,10},{4,12},{6,14},{8,0},{10,2},{12,4},{14,6},{16,24},{18,... | collective-permute-start | bytes 147464 | tf_op jit(solution)/shard_map/ppermute | solution.py:447
  39.9 5.1 %collective-permute-start.10 = (f32[96,128]{1,0:T(8,128)S(1)}, f32[96,128]{1,0:T(8,128)S(1)}, u32[]{:S(2)}, u32[]{:S(2)}) collective-permute-start(f32[96,128]{1,0:T(8,128)S(1)} %get-tuple-element.23), channel_id=1, source_target_pairs={{0,16},{2,18},{4,20},{6,22},{8,24},{10,26},{12,28},{14,30},{16,0},... | collective-permute-start | bytes 147464 | tf_op jit(solution)/shard_map/ppermute | solution.py:447
  41.8 5.9 %collective-permute-start.11 = (f32[96,128]{1,0:T(8,128)S(1)}, f32[96,128]{1,0:T(8,128)S(1)}, u32[]{:S(2)}, u32[]{:S(2)}) collective-permute-start(f32[96,128]{1,0:T(8,128)S(1)} %get-tuple-element.24), channel_id=1, source_target_pairs={{0,24},{2,26},{4,28},{6,30},{8,16},{10,18},{12,20},{14,22},{16,8},... | collective-permute-start | bytes 147464 | tf_op jit(solution)/shard_map/ppermute | solution.py:447

commit v6 on v5

--- a/solution.py
+++ b/solution.py
@@ -13,6 +13,7 @@
 LANES = 128
 REACH = 256
 MIB = 1024 * 1024
+FULL = 32767.0
 
 
 def f32_dot(a, b, dims=(((1,), (0,)), ((), ()))):
@@ -48,6 +49,49 @@
         out_specs=vmem(1)[0],
         compiler_params=pltpu.CompilerParams(vmem_limit_bytes=8 * MIB),
         name="pack_elution",
+    )(elution.T)
+
+
+def encode_kernel(x_ref, o_ref):
+    components, rows = x_ref.shape
+    half = rows // 2
+    x = x_ref[...]
+    pad = -rows % LANES
+    x = jnp.concatenate([x, jnp.zeros((components, pad), x.dtype)], axis=1).T[:rows]
+    peak = jnp.maximum(jnp.max(jnp.abs(x), axis=0, keepdims=True), 1e-30)
+    level = jnp.floor(256.0 / math.log(2.0) * jnp.log(peak)) + 1.0
+    x = x * (FULL / scale_of(level))
+    x = jnp.clip(jnp.floor(x + 0.5), -FULL, FULL).astype(jnp.int32).astype(jnp.int16)
+    o_ref[0:half, :] = jnp.concatenate([x[:half], x[half:]], axis=1)
+    level = jnp.broadcast_to(level, (16, components)).astype(jnp.int32).astype(jnp.int16)
+    o_ref[half:, :] = jnp.concatenate([level, level], axis=1)
+
+
+def scale_of(level):
+    return jnp.exp(math.log(2.0) / 256.0 * level)
+
+
+def decoded(x):
+    half = x.shape[0] - 16
+    x = x.astype(jnp.int32).astype(jnp.float32)
+    x = x[:half] * (scale_of(x[half : half + 1]) * (1.0 / FULL))
+    high = x.astype(jnp.bfloat16).astype(jnp.float32)
+    low = x - high
+    left = lax.broadcasted_iota(jnp.int32, x.shape, 1) < LANES // 2
+    top = jnp.where(left, high, pltpu.roll(low, LANES // 2, 1))
+    bottom = jnp.where(left, pltpu.roll(high, LANES // 2, 1), low)
+    return jnp.concatenate([top, bottom], axis=0).astype(jnp.bfloat16)
+
+
+def encode(elution):
+    rows, components = elution.shape
+    return pl.pallas_call(
+        encode_kernel,
+        out_shape=jax.ShapeDtypeStruct((rows // 2 + 16, 2 * components), jnp.int16),
+        in_specs=vmem(1),
+        out_specs=vmem(1)[0],
+        compiler_params=pltpu.CompilerParams(vmem_limit_bytes=8 * MIB),
+        name="encode_elution",
     )(elution.T)
 
 
@@ -126,12 +170,12 @@
     if planes:
         own_ref, came_ref = refs[:2]
         freq_count = 2 * own_ref.shape[0]
-        rows = own_ref.shape[1]
+        rows = 2 * (own_ref.shape[1] - 16)
         padded = wide.shape[0] // freq_count
         for block in range(freq_count):
             apart = lax.bitwise_xor((freq_rank + block) & (freq_count - 1), freq_rank)
             ref = came_ref if block % 2 else own_ref
-            values = ref[pl.ds(block_place(apart, freq_count), 1)][0]
+            values = decoded(ref[pl.ds(block_place(apart, freq_count), 1)][0])
             at, before = block * padded, (block - 1) % freq_count * padded
             wide[at : at + rows, 0:LANES] = values
             wide[before : before + rows, LANES:] = values
@@ -187,7 +231,7 @@
     planes = len(gathered) == 2
     if planes:
         own = gathered[0]
-        wide_rows = 2 * own.shape[0] * (-(-own.shape[1] // LANES) * LANES)
+        wide_rows = 2 * own.shape[0] * (-(-2 * (own.shape[1] - 16) // LANES) * LANES)
     else:
         wide_rows = REACH + length + 2 * LANES * ((places - 1) // 2)
     return pl.pallas_call(
@@ -254,12 +298,13 @@
     if planes:
         pair_ref, other_ref = refs[:2]
         mz_rank = lax.axis_index("mz")
-        rows = pair_ref.shape[0] // 2
+        coded = pair_ref.shape[0] // 2
+        rows = 2 * (coded - 16)
         skip = bin_count - REACH
         for ref, half in ((pair_ref, mz_rank), (other_ref, 1 - mz_rank)):
             for block in range(2):
                 to = pl.multiple_of((2 * block + half) * rows, 64)
-                window[pl.ds(to, rows), :] = ref[block * rows : (block + 1) * rows, :]
+                window[pl.ds(to, rows), :] = decoded(ref[block * coded : (block + 1) * coded, :])
     else:
         own_ref = refs[0]
         step = own_ref.shape[1]
@@ -453,7 +498,6 @@
     components = loadings.shape[1]
     bin_count = intensity.shape[1]
     axes = ("freq", "mz")
-    mine = pack(elution)
     own = intensity.shape[2] // freq_count
     planes = (
         own == LANES
@@ -466,6 +510,7 @@
         and bin_count >= REACH
     )
     if not planes:
+        mine = pack(elution)
         gathered = lax.all_gather(mine, axes, axis=0).reshape(-1, math.gcd(bin_count, LANES), LANES)
         g = partial_model((gathered,), circulant(bin_weight.reshape(LANES, -1), 0), bin_count, components)
         shifted = elution_terms((gathered,), loadings, shifts, bin_count)
@@ -473,6 +518,7 @@
         gram = lax.psum(gram, "freq")
         owned = lax.psum_scatter(numerator, "freq", scatter_dimension=1, tiled=True)
         return small_call(solve_kernel, (components, own), "solve", gram, owned)[0]
+    mine = encode(elution)
     z_steps = range(4, freq_count, 4)
     held = jnp.stack([mine] + [swap(mine, "freq", freq_count, step) for step in z_steps])
     weights = bin_weight.reshape(LANES, -1)
@@ -484,6 +530,7 @@
     pair = window_pair(mine, came)
     other = swap(pair, "mz", mz_count, 1)
     g = partial_model((held, came), u, bin_count, components)
+    g, other = lax.optimization_barrier((g, other))
     models = (g, swap(g, "mz", mz_count, 1))
     shifted = elution_terms((pair, other), loadings, shifts, bin_count)
     keep, send = product(intensity, models, shifted, loadings, shifts, planes)
@@ -497,7 +544,7 @@
     own_part, *sends = small_call(
         functools.partial(spread_kernel, tail), (components + tail, LANES), "reduce_x", keep, came, across, count=chips
     )
-    parts = [swap(send, "freq", freq_count, step) for send, step in zip(sends, z_steps)]
+    parts = [swap(send, "freq", freq_count, step) for send, step in zip(sends, z_steps)][::-1]
     return small_call(solve_planes_kernel, (components, own), "solve", own_part, *parts)[0]
 
 

time: 51 us -> 48.5 us (0.951)
  waiting for transfers between devices: 19.6 us -> 15.9 us
  starting transfers between devices: 15.6 us -> 16.5 us
    ppermute x12, waiting for transfers between devices: 19.6 us -> 15.9 us  [swap(): return lax.ppermute(x, axes, [(i, i ^ value) for i in range(count)])]
    ppermute x12, starting transfers between devices: 15.6 us -> 16.5 us  [swap(): return lax.ppermute(x, axes, [(i, i ^ value) for i in range(count)])]
  transfers between devices with their start and end apart: 12 -> 12, of which waited for: 10 -> 10; matrix products, arithmetic and copies ran while one was open for 2% -> 2% of each run, Pallas kernels for 12% -> 14%
where the time goes in v6:
time: 48.5 us; the launch traced here: 48.2 us
  starting transfers between devices  16.5 us (34%)
  waiting for transfers between devices  15.9 us (33%)
  Pallas kernels  13.1 us (27%)
  local copies, waits for them, and re-layouts  2.6 us (5%)
    ppermute x12, starting transfers between devices, swap(): return lax.ppermute(x, axes, [(i, i ^ value) for i in range(count)])  16.5 us
    ppermute x12, waiting for transfers between devices, swap(): return lax.ppermute(x, axes, [(i, i ^ value) for i in range(count)])  15.9 us
    pallas_call x1, Pallas kernels, product(): pl.pallas_call(functools.partial(product_kernel, len(models), planes), ou...  3.15 us
    pallas_call x3, Pallas kernels, small_call(): pl.pallas_call(kernel, out_shape=(jax.ShapeDtypeStruct(shape, jnp.float32...  3.09 us
    pallas_call x1, Pallas kernels, elution_terms(): pl.pallas_call(functools.partial(elution_kernel, planes), out_shape=jax.S...  3.04 us
    pallas_call x1, Pallas kernels, partial_model(): pl.pallas_call(functools.partial(model_kernel, places, planes), out_shape...  2.1 us
    unnamed x10, local copies, waits for them, and re-layouts  1.79 us
    pallas_call x1, Pallas kernels, circulant(): pl.pallas_call(functools.partial(circulant_kernel, turn), out_shape=jax.S...  1.53 us
  transfers between devices with their start and end apart: 12, of which 10 were waited for; matrix products, arithmetic and copies ran while one was open for 2% of the time, Pallas kernels for 14%

profile of v6, /device:TPU:0, one launch (start us, length us, event | category | flops | bytes accessed | tf_op | source)
XLA Modules:
  0.0 48.2 jit_solution(11474144198957939608)
XLA Ops:
  0.0 0.0 copy-start
  0.0 0.8 %copy-done = f32[192,64]{0,1:T(8,128)S(1)} copy-done((f32[192,64]{0,1:T(8,128)S(1)}, f32[192,64]{0,1:T(8,128)}, u32[]{:S(2)}) %copy-start) | copy-done | bytes 49176
  0.8 0.0 copy-start.2
  0.8 0.0 copy-start.3
  0.8 0.2 encode_elution.1.mine_ref
  1.1 5.1 %collective-permute-start.2 = (s16[112,128]{1,0:T(8,128)(2,1)S(1)}, s16[112,128]{1,0:T(8,128)(2,1)S(1)}, u32[]{:S(2)}, u32[]{:S(2)}) collective-permute-start(s16[112,128]{1,0:T(8,128)(2,1)S(1)} %encode_elution.1.mine_ref), channel_id=1, source_target_pairs={{0,24},{2,26},{4,28},{6,30},{8,16},{10,18},{12,20},{14,22},{16,8},... | collective-permute-start | bytes 86024 | tf_op jit(solution)/shard_map/ppermute | solution.py:492
  6.2 0.0 collective-permute-start.1
  6.2 0.6 %collective-permute-start = (s16[112,128]{1,0:T(8,128)(2,1)S(1)}, s16[112,128]{1,0:T(8,128)(2,1)S(1)}, u32[]{:S(2)}, u32[]{:S(2)}) collective-permute-start(s16[112,128]{1,0:T(8,128)(2,1)S(1)} %encode_elution.1.mine_ref), channel_id=1, source_target_pairs={{0,8},{2,10},{4,12},{6,14},{8,0},{10,2},{12,4},{14,6},{16,24},{18,... | collective-permute-start | bytes 86024 | tf_op jit(solution)/shard_map/ppermute | solution.py:492
  6.8 0.8 %reshape.3.w_ref = f32[128,48]{1,0:T(8,128)S(1)} reshape(f32[6144]{0:T(1024)} %param.10) | data formatting | bytes 49152 | tf_op jit(solution)/shard_map/reshape | solution.py:524
  7.7 0.0 copy-start.1
  7.7 0.4 collective-permute-done.2
  8.0 2.9 %collective-permute-done.1 = s16[112,128]{1,0:T(8,128)(2,1)S(1)} collective-permute-done((s16[112,128]{1,0:T(8,128)(2,1)S(1)}, s16[112,128]{1,0:T(8,128)(2,1)S(1)}, u32[]{:S(2)}, u32[]{:S(2)}) %collective-permute-start.1) | collective-permute-done | bytes 28704 | tf_op jit(solution)/shard_map/ppermute | solution.py:492
  11.0 0.0 collective-permute-done
  11.0 1.6 %collective-permute-start.3 = (s16[4,112,128]{2,1,0:T(8,128)(2,1)S(1)}, s16[4,112,128]{2,1,0:T(8,128)(2,1)S(1)}, u32[]{:S(2)}, u32[]{:S(2)}) collective-permute-start(s16[4,112,128]{2,1,0:T(8,128)(2,1)S(1)} %pad_add_fusion.1), channel_id=1, source_target_pairs={{0,4},{2,6},{4,0},{6,2},{8,12},{10,14},{12,8},{14,10},{16,20},{18,... | collective-permute-start | bytes 344072 | tf_op jit(solution)/shard_map/ppermute | solution.py:492
  12.5 0.0 copy-start.4
  12.5 0.9 %copy-done.4 = f32[448,128]{1,0:T(8,128)S(1)} copy-done((f32[448,128]{1,0:T(8,128)S(1)}, f32[448,128]{1,0:T(8,128)}, u32[]{:S(2)}) %copy-start.4) | copy-done | bytes 229400
  13.5 1.5 %circulant_block.1.refs_2_ = bf16[256,6144]{1,0:T(8,128)(2,1)S(1)} custom-call(f32[128,48]{1,0:T(8,128)S(1)} %reshape.3.w_ref, f32[448,128]{1,0:T(8,128)S(1)} %copy-done.4), custom_call_target="tpu_custom_call" | custom-call | flops 2000000000 | bytes 4194304 | tf_op jit(solution)/shard_map/circulant_block/pallas_call | solution.py:154
  15.0 0.8 %collective-permute-done.3 = s16[4,112,128]{2,1,0:T(8,128)(2,1)S(1)} collective-permute-done((s16[4,112,128]{2,1,0:T(8,128)(2,1)S(1)}, s16[4,112,128]{2,1,0:T(8,128)(2,1)S(1)}, u32[]{:S(2)}, u32[]{:S(2)}) %collective-permute-start.3) | collective-permute-done | bytes 114720 | tf_op jit(solution)/shard_map/ppermute | solution.py:492
  15.9 0.1 collective-permute-start.4
  15.9 1.5 %collective-permute-done.4.refs_1_.came_ref = s16[8,112,128]{2,1,0:T(8,128)(2,1)S(1)} collective-permute-done((s16[8,112,128]{2,1,0:T(8,128)(2,1)S(1)}, s16[8,112,128]{2,1,0:T(8,128)(2,1)S(1)}, u32[]{:S(2)}, u32[]{:S(2)}) %collective-permute-start.4) | collective-permute-done | bytes 229408 | tf_op jit(solution)/shard_map/ppermute | solution.py:492
  17.4 1.5 %collective-permute-start.5 = (s16[224,128]{1,0:T(8,128)(2,1)S(1)}, s16[224,128]{1,0:T(8,128)(2,1)S(1)}, u32[]{:S(2)}, u32[]{:S(2)}) collective-permute-start(s16[224,128]{1,0:T(8,128)(2,1)S(1)} %window_pair.1.refs_0_), channel_id=1, source_target_pairs={{0,1},{1,0},{2,3},{3,2},{4,5},{5,4},{6,7},{7,6},{8,9},{9,8},{10,11... | collective-permute-start | bytes 172040 | tf_op jit(solution)/shard_map/ppermute | solution.py:492
  18.9 2.1 %partial_model.1.refs_1_ = f32[64,640]{1,0:T(8,128)S(1)} custom-call(s16[8,112,128]{2,1,0:T(8,128)(2,1)S(1)} %pad_add_fusion.refs_0_, s16[8,112,128]{2,1,0:T(8,128)(2,1)S(1)} %collective-permute-done.4.refs_1_.came_ref, bf16[256,6144]{1,0:T(8,128)(2,1)S(1)} %circulant_block.1.refs_2_), custom_call_target="tpu_custom_call" | custom-call | flops 2000000000 | bytes 4194304 | tf_op jit(solution)/shard_map/partial_model/pallas_call | solution.py:237
  21.0 0.6 %collective-permute-done.5.refs_1_ = s16[224,128]{1,0:T(8,128)(2,1)S(1)} collective-permute-done((s16[224,128]{1,0:T(8,128)(2,1)S(1)}, s16[224,128]{1,0:T(8,128)(2,1)S(1)}, u32[]{:S(2)}, u32[]{:S(2)}) %collective-permute-start.5) | collective-permute-done | bytes 57376 | tf_op jit(solution)/shard_map/ppermute | solution.py:492
  21.6 1.5 %collective-permute-start.6 = (f32[64,640]{1,0:T(8,128)S(1)}, f32[64,640]{1,0:T(8,128)S(1)}, u32[]{:S(2)}, u32[]{:S(2)}) collective-permute-start(f32[64,640]{1,0:T(8,128)S(1)} %partial_model.1.refs_1_), channel_id=1, source_target_pairs={{0,1},{1,0},{2,3},{3,2},{4,5},{5,4},{6,7},{7,6},{8,9},{9,8},{10,11... | collective-permute-start | bytes 491528 | tf_op jit(solution)/shard_map/ppermute | solution.py:492
  23.1 0.0 copy-done.2
  23.1 0.0 copy-done.3
  23.1 3.0 %elution_terms.1.refs_3_ = bf16[128,3072]{1,0:T(8,128)(2,1)S(1)} custom-call(s16[224,128]{1,0:T(8,128)(2,1)S(1)} %window_pair.1.refs_0_, s16[224,128]{1,0:T(8,128)(2,1)S(1)} %collective-permute-done.5.refs_1_, f32[8,64]{1,0:T(8,128)S(1)} %copy-done.2, s32[8,64]{1,0:T(8,128)S(1)} %copy-done.3), custom_call_target="tpu_custom_call" | custom-call | flops 1000000000 | bytes 2097152 | tf_op jit(solution)/shard_map/elution_terms/pallas_call | solution.py:327
  26.2 0.9 %collective-permute-done.6.refs_2_ = f32[64,640]{1,0:T(8,128)S(1)} collective-permute-done((f32[64,640]{1,0:T(8,128)S(1)}, f32[64,640]{1,0:T(8,128)S(1)}, u32[]{:S(2)}, u32[]{:S(2)}) %collective-permute-start.6) | collective-permute-done | bytes 163872 | tf_op jit(solution)/shard_map/ppermute | solution.py:492
  27.1 0.0 copy-done.1
  27.1 3.2 %model_products.1 = (f32[544,128]{1,0:T(8,128)S(1)}, f32[544,128]{1,0:T(8,128)S(1)}) custom-call(bf16[8,384,2048]{2,1,0:T(8,128)(2,1)S(1)} %copy-done.1, f32[64,640]{1,0:T(8,128)S(1)} %partial_model.1.refs_1_, f32[64,640]{1,0:T(8,128)S(1)} %collective-permute-done.6.refs_2_, bf16[128,3072]{1,0:T(8,128)(2,1)S(1)} %elution_terms.1.refs_3_, ...), custom_call_target="tpu_custom_call" | custom-call | flops 8000000000 | bytes 12582912 | tf_op jit(solution)/shard_map/model_products/pallas_call | solution.py:390
  30.2 0.1 collective-permute-start.7
  30.3 1.5 %collective-permute-done.7.b_ref = f32[544,128]{1,0:T(8,128)S(1)} collective-permute-done((f32[544,128]{1,0:T(8,128)S(1)}, f32[544,128]{1,0:T(8,128)S(1)}, u32[]{:S(2)}, u32[]{:S(2)}) %collective-permute-start.7) | collective-permute-done | bytes 278560 | tf_op jit(solution)/shard_map/ppermute | solution.py:492
  31.9 1.5 %collective-permute-start.8 = (f32[288,128]{1,0:T(8,128)S(1)}, f32[288,128]{1,0:T(8,128)S(1)}, u32[]{:S(2)}, u32[]{:S(2)}) collective-permute-start(f32[288,128]{1,0:T(8,128)S(1)} %reduce_cores.1), channel_id=1, source_target_pairs={{0,4},{2,6},{4,0},{6,2},{8,12},{10,14},{12,8},{14,10},{16,20},{18,... | collective-permute-start | bytes 442376 | tf_op jit(solution)/shard_map/ppermute | solution.py:492
  33.4 4.4 %collective-permute-done.8.c_ref = f32[288,128]{1,0:T(8,128)S(1)} collective-permute-done((f32[288,128]{1,0:T(8,128)S(1)}, f32[288,128]{1,0:T(8,128)S(1)}, u32[]{:S(2)}, u32[]{:S(2)}) %collective-permute-start.8) | collective-permute-done | bytes 147488 | tf_op jit(solution)/shard_map/ppermute | solution.py:492
  37.9 1.5 %collective-permute-start.9 = (f32[96,128]{1,0:T(8,128)S(1)}, f32[96,128]{1,0:T(8,128)S(1)}, u32[]{:S(2)}, u32[]{:S(2)}) collective-permute-start(f32[96,128]{1,0:T(8,128)S(1)} %get-tuple-element.26), channel_id=1, source_target_pairs={{0,24},{2,26},{4,28},{6,30},{8,16},{10,18},{12,20},{14,22},{16,8},... | collective-permute-start | bytes 147464 | tf_op jit(solution)/shard_map/ppermute | solution.py:492
  39.4 0.6 %collective-permute-start.10 = (f32[96,128]{1,0:T(8,128)S(1)}, f32[96,128]{1,0:T(8,128)S(1)}, u32[]{:S(2)}, u32[]{:S(2)}) collective-permute-start(f32[96,128]{1,0:T(8,128)S(1)} %get-tuple-element.27), channel_id=1, source_target_pairs={{0,16},{2,18},{4,20},{6,22},{8,24},{10,26},{12,28},{14,30},{16,0},... | collective-permute-start | bytes 147464 | tf_op jit(solution)/shard_map/ppermute | solution.py:492
  40.0 2.3 %collective-permute-start.11 = (f32[96,128]{1,0:T(8,128)S(1)}, f32[96,128]{1,0:T(8,128)S(1)}, u32[]{:S(2)}, u32[]{:S(2)}) collective-permute-start(f32[96,128]{1,0:T(8,128)S(1)} %get-tuple-element.28), channel_id=1, source_target_pairs={{0,8},{2,10},{4,12},{6,14},{8,0},{10,2},{12,4},{14,6},{16,24},{18,... | collective-permute-start | bytes 147464 | tf_op jit(solution)/shard_map/ppermute | solution.py:492
  42.3 1.9 %collective-permute-done.9.refs_1_ = f32[96,128]{1,0:T(8,128)S(1)} collective-permute-done((f32[96,128]{1,0:T(8,128)S(1)}, f32[96,128]{1,0:T(8,128)S(1)}, u32[]{:S(2)}, u32[]{:S(2)}) %collective-permute-start.9) | collective-permute-done | bytes 49184 | tf_op jit(solution)/shard_map/ppermute | solution.py:492
  44.2 1.0 %collective-permute-done.10.refs_2_ = f32[96,128]{1,0:T(8,128)S(1)} collective-permute-done((f32[96,128]{1,0:T(8,128)S(1)}, f32[96,128]{1,0:T(8,128)S(1)}, u32[]{:S(2)}, u32[]{:S(2)}) %collective-permute-start.10) | collective-permute-done | bytes 49184 | tf_op jit(solution)/shard_map/ppermute | solution.py:492
  45.2 0.0 collective-permute-done.11.refs_3_
  45.2 3.0 %solve.1 = f32[64,128]{1,0:T(8,128)} custom-call(f32[96,128]{1,0:T(8,128)S(1)} %get-tuple-element.25.refs_0_, f32[96,128]{1,0:T(8,128)S(1)} %collective-permute-done.9.refs_1_, f32[96,128]{1,0:T(8,128)S(1)} %collective-permute-done.10.refs_2_, f32[96,128]{1,0:T(8,128)S(1)} %collective-permute-done.11.refs_3_), custom_call_target="tpu_custom_call" | custom-call | tf_op jit(solution)/shard_map/solve/pallas_call | solution.py:481
  (5 shorter events, 0.1 us)
Async XLA Ops:
  0.0 0.8 %copy-start = (f32[192,64]{0,1:T(8,128)S(1)}, f32[192,64]{0,1:T(8,128)}, u32[]{:S(2)}) copy-start(f32[192,64]{0,1:T(8,128)} %param.7) | copy-start | bytes 147460
  0.8 22.3 %copy-start.2 = (f32[8,64]{1,0:T(8,128)S(1)}, f32[8,64]{1,0:T(8,128)}, u32[]{:S(2)}) copy-start(f32[8,64]{1,0:T(8,128)} %refs_4_.1) | copy-start | bytes 6148
  0.8 22.3 %copy-start.3 = (s32[8,64]{1,0:T(8,128)S(1)}, s32[8,64]{1,0:T(8,128)}, u32[]{:S(2)}) copy-start(s32[8,64]{1,0:T(8,128)} %refs_5_.1) | copy-start | bytes 6148
  1.1 7.0 %collective-permute-start.2 = (s16[112,128]{1,0:T(8,128)(2,1)S(1)}, s16[112,128]{1,0:T(8,128)(2,1)S(1)}, u32[]{:S(2)}, u32[]{:S(2)}) collective-permute-start(s16[112,128]{1,0:T(8,128)(2,1)S(1)} %encode_elution.1.mine_ref), channel_id=1, source_target_pairs={{0,24},{2,26},{4,28},{6,30},{8,16},{10,18},{12,20},{14,22},{16,8},... | collective-permute-start | bytes 86024 | tf_op jit(solution)/shard_map/ppermute | solution.py:492
  6.2 4.8 %collective-permute-start.1 = (s16[112,128]{1,0:T(8,128)(2,1)S(1)}, s16[112,128]{1,0:T(8,128)(2,1)S(1)}, u32[]{:S(2)}, u32[]{:S(2)}) collective-permute-start(s16[112,128]{1,0:T(8,128)(2,1)S(1)} %encode_elution.1.mine_ref), channel_id=1, source_target_pairs={{0,16},{2,18},{4,20},{6,22},{8,24},{10,26},{12,28},{14,30},{16,0},... | collective-permute-start | bytes 86024 | tf_op jit(solution)/shard_map/ppermute | solution.py:492
  6.2 4.8 %collective-permute-start = (s16[112,128]{1,0:T(8,128)(2,1)S(1)}, s16[112,128]{1,0:T(8,128)(2,1)S(1)}, u32[]{:S(2)}, u32[]{:S(2)}) collective-permute-start(s16[112,128]{1,0:T(8,128)(2,1)S(1)} %encode_elution.1.mine_ref), channel_id=1, source_target_pairs={{0,8},{2,10},{4,12},{6,14},{8,0},{10,2},{12,4},{14,6},{16,24},{18,... | collective-permute-start | bytes 86024 | tf_op jit(solution)/shard_map/ppermute | solution.py:492
  7.7 19.4 %copy-start.1 = (bf16[8,384,2048]{2,1,0:T(8,128)(2,1)S(1)}, bf16[8,384,2048]{2,1,0:T(8,128)(2,1)}, u32[]{:S(2)}) copy-start(bf16[8,384,2048]{2,1,0:T(8,128)(2,1)} %refs_0_.1) | copy-start | bytes 37748740
  11.0 4.9 %collective-permute-start.3 = (s16[4,112,128]{2,1,0:T(8,128)(2,1)S(1)}, s16[4,112,128]{2,1,0:T(8,128)(2,1)S(1)}, u32[]{:S(2)}, u32[]{:S(2)}) collective-permute-start(s16[4,112,128]{2,1,0:T(8,128)(2,1)S(1)} %pad_add_fusion.1), channel_id=1, source_target_pairs={{0,4},{2,6},{4,0},{6,2},{8,12},{10,14},{12,8},{14,10},{16,20},{18,... | collective-permute-start | bytes 344072 | tf_op jit(solution)/shard_map/ppermute | solution.py:492
  12.5 0.9 %copy-start.4 = (f32[448,128]{1,0:T(8,128)S(1)}, f32[448,128]{1,0:T(8,128)}, u32[]{:S(2)}) copy-start(f32[448,128]{1,0:T(8,128)} %constant.2.clone.table_ref) | copy-start | bytes 688132
  15.9 1.6 %collective-permute-start.4 = (s16[8,112,128]{2,1,0:T(8,128)(2,1)S(1)}, s16[8,112,128]{2,1,0:T(8,128)(2,1)S(1)}, u32[]{:S(2)}, u32[]{:S(2)}) collective-permute-start(s16[8,112,128]{2,1,0:T(8,128)(2,1)S(1)} %pad_add_fusion.refs_0_), channel_id=1, source_target_pairs={{0,2},{2,0},{4,6},{6,4},{8,10},{10,8},{12,14},{14,12},{16,18},{18,... | collective-permute-start | bytes 688136 | tf_op jit(solution)/shard_map/ppermute | solution.py:492
  17.4 4.2 %collective-permute-start.5 = (s16[224,128]{1,0:T(8,128)(2,1)S(1)}, s16[224,128]{1,0:T(8,128)(2,1)S(1)}, u32[]{:S(2)}, u32[]{:S(2)}) collective-permute-start(s16[224,128]{1,0:T(8,128)(2,1)S(1)} %window_pair.1.refs_0_), channel_id=1, source_target_pairs={{0,1},{1,0},{2,3},{3,2},{4,5},{5,4},{6,7},{7,6},{8,9},{9,8},{10,11... | collective-permute-start | bytes 172040 | tf_op jit(solution)/shard_map/ppermute | solution.py:492
  21.6 5.5 %collective-permute-start.6 = (f32[64,640]{1,0:T(8,128)S(1)}, f32[64,640]{1,0:T(8,128)S(1)}, u32[]{:S(2)}, u32[]{:S(2)}) collective-permute-start(f32[64,640]{1,0:T(8,128)S(1)} %partial_model.1.refs_1_), channel_id=1, source_target_pairs={{0,1},{1,0},{2,3},{3,2},{4,5},{5,4},{6,7},{7,6},{8,9},{9,8},{10,11... | collective-permute-start | bytes 491528 | tf_op jit(solution)/shard_map/ppermute | solution.py:492
  30.2 1.6 %collective-permute-start.7 = (f32[544,128]{1,0:T(8,128)S(1)}, f32[544,128]{1,0:T(8,128)S(1)}, u32[]{:S(2)}, u32[]{:S(2)}) collective-permute-start(f32[544,128]{1,0:T(8,128)S(1)} %get-tuple-element.24), channel_id=1, source_target_pairs={{0,2},{2,0},{4,6},{6,4},{8,10},{10,8},{12,14},{14,12},{16,18},{18,... | collective-permute-start | bytes 835592 | tf_op jit(solution)/shard_map/ppermute | solution.py:492
  31.9 6.0 %collective-permute-start.8 = (f32[288,128]{1,0:T(8,128)S(1)}, f32[288,128]{1,0:T(8,128)S(1)}, u32[]{:S(2)}, u32[]{:S(2)}) collective-permute-start(f32[288,128]{1,0:T(8,128)S(1)} %reduce_cores.1), channel_id=1, source_target_pairs={{0,4},{2,6},{4,0},{6,2},{8,12},{10,14},{12,8},{14,10},{16,20},{18,... | collective-permute-start | bytes 442376 | tf_op jit(solution)/shard_map/ppermute | solution.py:492
  37.9 6.3 %collective-permute-start.9 = (f32[96,128]{1,0:T(8,128)S(1)}, f32[96,128]{1,0:T(8,128)S(1)}, u32[]{:S(2)}, u32[]{:S(2)}) collective-permute-start(f32[96,128]{1,0:T(8,128)S(1)} %get-tuple-element.26), channel_id=1, source_target_pairs={{0,24},{2,26},{4,28},{6,30},{8,16},{10,18},{12,20},{14,22},{16,8},... | collective-permute-start | bytes 147464 | tf_op jit(solution)/shard_map/ppermute | solution.py:492
  39.4 5.8 %collective-permute-start.10 = (f32[96,128]{1,0:T(8,128)S(1)}, f32[96,128]{1,0:T(8,128)S(1)}, u32[]{:S(2)}, u32[]{:S(2)}) collective-permute-start(f32[96,128]{1,0:T(8,128)S(1)} %get-tuple-element.27), channel_id=1, source_target_pairs={{0,16},{2,18},{4,20},{6,22},{8,24},{10,26},{12,28},{14,30},{16,0},... | collective-permute-start | bytes 147464 | tf_op jit(solution)/shard_map/ppermute | solution.py:492
  40.0 5.2 %collective-permute-start.11 = (f32[96,128]{1,0:T(8,128)S(1)}, f32[96,128]{1,0:T(8,128)S(1)}, u32[]{:S(2)}, u32[]{:S(2)}) collective-permute-start(f32[96,128]{1,0:T(8,128)S(1)} %get-tuple-element.28), channel_id=1, source_target_pairs={{0,8},{2,10},{4,12},{6,14},{8,0},{10,2},{12,4},{14,6},{16,24},{18,... | collective-permute-start | bytes 147464 | tf_op jit(solution)/shard_map/ppermute | solution.py:492

commit v7 on v6

--- a/solution.py
+++ b/solution.py
@@ -448,27 +448,88 @@
     return total
 
 
+def fixed_point(x, full):
+    return jnp.clip(jnp.floor(x + 0.5), -full, full)
+
+
+def as_int16(x):
+    return x.astype(jnp.int32).astype(jnp.int16)
+
+
+def row_level(x):
+    peak = jnp.maximum(jnp.max(jnp.abs(x), axis=1, keepdims=True), 1e-30)
+    return jnp.floor(256.0 / math.log(2.0) * jnp.log(peak)) + 1.0
+
+
+def diagonal(x, rows):
+    shape = (rows, LANES)
+    on = lax.broadcasted_iota(jnp.int32, shape, 0) == lax.broadcasted_iota(jnp.int32, shape, 1)
+    return jnp.where(on, jnp.broadcast_to(x, shape), 0.0)
+
+
+def encode_rows(x, gram, o_ref):
+    rows, tail = x.shape[0], gram.shape[0]
+    parts = [x[at : at + LANES] for at in range(0, rows, LANES)]
+    levels = [row_level(part) for part in parts] + [row_level(gram)]
+    at = 0
+    for part, level in zip(parts, levels):
+        o_ref[at : at + part.shape[0], :] = as_int16(fixed_point(part * (FULL / scale_of(level)), FULL))
+        at += part.shape[0]
+    scaled = gram * (FULL / scale_of(levels[-1]))
+    high = fixed_point(scaled, FULL)
+    o_ref[at : at + tail, :] = as_int16(high)
+    o_ref[at + tail : at + 2 * tail, :] = as_int16(fixed_point((scaled - high) * (2 * FULL), FULL))
+    row_id = lax.broadcasted_iota(jnp.int32, (16, LANES), 0)
+    block = jnp.zeros((16, LANES), jnp.float32)
+    for n, level in enumerate(levels):
+        lanes = jnp.sum(diagonal(level, level.shape[0]), axis=0, keepdims=True)
+        block = jnp.where(row_id == n, lanes, block)
+    o_ref[at + 2 * tail :, :] = as_int16(block)
+
+
+def decode_rows(ref, tail):
+    rows = ref.shape[0] - 2 * tail - 16
+    x = ref[...].astype(jnp.int32).astype(jnp.float32)
+
+    def scale(n, count):
+        at = rows + 2 * tail + n
+        return scale_of(jnp.sum(diagonal(x[at : at + 1], count), axis=1, keepdims=True)) * (1.0 / FULL)
+
+    parts = []
+    for n, at in enumerate(range(0, rows, LANES)):
+        count = min(LANES, rows - at)
+        parts.append(x[at : at + count] * scale(n, count))
+    gram = x[rows : rows + tail] + x[rows + tail : rows + 2 * tail] * (0.5 / FULL)
+    return jnp.concatenate(parts, axis=0), gram * scale(len(parts), tail)
+
+
 def halve_kernel(tail, a_ref, b_ref, o_ref):
-    rows = o_ref.shape[0] - tail
-    o_ref[...] = total_of((a_ref, b_ref), rows, rows + tail)
-
-
-def spread_kernel(tail, a_ref, b_ref, c_ref, *outs):
-    rows = outs[0].shape[0] - tail
-    count = len(outs)
-    gram = total_of((a_ref, b_ref), 2 * count * rows, tail) + c_ref[count * rows :, :]
+    rows = o_ref.shape[0] - 2 * tail - 16
+    total = total_of((a_ref, b_ref), rows, rows + tail)
+    encode_rows(total[:rows], total[rows:], o_ref)
+
+
+def spread_kernel(tail, a_ref, b_ref, c_ref, own_ref, *outs):
+    rows = own_ref.shape[0] - tail
+    count = len(outs) + 1
+    total, gram = decode_rows(c_ref, tail)
+    total = total + total_of((a_ref, b_ref), 0, count * rows)
+    gram = gram + total_of((a_ref, b_ref), 2 * count * rows, tail)
+    own_ref[0:rows, :] = total[:rows]
+    own_ref[rows:, :] = gram
     for n, o_ref in enumerate(outs):
-        o_ref[0:rows, :] = total_of((a_ref, b_ref, c_ref), n * rows, rows)
-        o_ref[rows:, :] = gram
-
-
-def solve_planes_kernel(*refs):
+        encode_rows(total[(n + 1) * rows : (n + 2) * rows], gram, o_ref)
+
+
+def solve_planes_kernel(own_ref, *refs):
     o_ref = refs[-1]
     components = o_ref.shape[0]
-    total = total_of(refs[:-1], 0, refs[0].shape[0])
-    gram = total[components:]
+    total, gram = own_ref[:components], own_ref[components:]
+    for ref in refs[:-1]:
+        part, gram_part = decode_rows(ref, gram.shape[0])
+        total, gram = total + part, gram + gram_part
     gram = jnp.concatenate([gram, pltpu.roll(gram, gram.shape[1] // 2, 1)], axis=0)
-    o_ref[...] = eliminate(gram, total[:components])
+    o_ref[...] = eliminate(gram, total)
 
 
 def solve_kernel(g_ref, n_ref, o_ref):
@@ -477,12 +538,12 @@
     o_ref[...] = eliminate(gram, n_ref[...])
 
 
-def small_call(kernel, shape, name, *args, count=1):
+def small_call(kernel, outs, name, *args):
     return pl.pallas_call(
         kernel,
-        out_shape=(jax.ShapeDtypeStruct(shape, jnp.float32),) * count,
+        out_shape=tuple(jax.ShapeDtypeStruct(shape, dtype) for shape, dtype in outs),
         in_specs=vmem(len(args)),
-        out_specs=tuple(vmem(count)),
+        out_specs=tuple(vmem(len(outs))),
         compiler_params=pltpu.CompilerParams(vmem_limit_bytes=8 * MIB),
         name=name,
     )(*args)
@@ -517,7 +578,7 @@
         numerator, gram = product(intensity, (g,), shifted, loadings, shifts, planes)
         gram = lax.psum(gram, "freq")
         owned = lax.psum_scatter(numerator, "freq", scatter_dimension=1, tiled=True)
-        return small_call(solve_kernel, (components, own), "solve", gram, owned)[0]
+        return small_call(solve_kernel, [((components, own), jnp.float32)], "solve", gram, owned)[0]
     mine = encode(elution)
     z_steps = range(4, freq_count, 4)
     held = jnp.stack([mine] + [swap(mine, "freq", freq_count, step) for step in z_steps])
@@ -537,15 +598,27 @@
     tail = components // 2
     chips = freq_count // 4
     came = swap(send, "freq", freq_count, 1)
+    coded = 2 * tail + 16
     (send,) = small_call(
-        functools.partial(halve_kernel, tail), (chips * components + tail, LANES), "reduce_cores", keep, came
+        functools.partial(halve_kernel, tail),
+        [((chips * components + coded, LANES), jnp.int16)],
+        "reduce_cores",
+        keep,
+        came,
     )
     across = swap(send, "freq", freq_count, 2)
     own_part, *sends = small_call(
-        functools.partial(spread_kernel, tail), (components + tail, LANES), "reduce_x", keep, came, across, count=chips
+        functools.partial(spread_kernel, tail),
+        [((components + tail, LANES), jnp.float32)] + [((components + coded, LANES), jnp.int16)] * (chips - 1),
+        "reduce_x",
+        keep,
+        came,
+        across,
     )
     parts = [swap(send, "freq", freq_count, step) for send, step in zip(sends, z_steps)][::-1]
-    return small_call(solve_planes_kernel, (components, own), "solve", own_part, *parts)[0]
+    return small_call(
+        solve_planes_kernel, [((components, own), jnp.float32)], "solve", own_part, *parts
+    )[0]
 
 
 def solution(mesh):

time: 48.5 us -> 47.4 us (0.977)
  waiting for transfers between devices: 15.9 us -> 14.1 us
  Pallas kernels: 13.1 us -> 13.9 us
    ppermute x12, waiting for transfers between devices: 15.9 us -> 14.1 us  [swap(): return lax.ppermute(x, axes, [(i, i ^ value) for i in range(count)])]
    pallas_call x3, Pallas kernels: 3.09 us -> 3.83 us  [small_call(): pl.pallas_call(kernel, out_shape=tuple((jax.ShapeDtypeStruct(shape, dtype...]
  transfers between devices with their start and end apart: 12 -> 12, of which waited for: 10 -> 11; matrix products, arithmetic and copies ran while one was open for 2% -> 2% of each run, Pallas kernels for 14% -> 14%
where the time goes in v7:
time: 47.4 us; the launch traced here: 47.2 us
  starting transfers between devices  16.5 us (35%)
  waiting for transfers between devices  14.1 us (30%)
  Pallas kernels  13.9 us (29%)
  local copies, waits for them, and re-layouts  2.6 us (5%)
    ppermute x12, starting transfers between devices, swap(): return lax.ppermute(x, axes, [(i, i ^ value) for i in range(count)])  16.5 us
    ppermute x12, waiting for transfers between devices, swap(): return lax.ppermute(x, axes, [(i, i ^ value) for i in range(count)])  14.1 us
    pallas_call x3, Pallas kernels, small_call(): pl.pallas_call(kernel, out_shape=tuple((jax.ShapeDtypeStruct(shape, dtype...  3.83 us
    pallas_call x1, Pallas kernels, product(): pl.pallas_call(functools.partial(product_kernel, len(models), planes), ou...  3.15 us
    pallas_call x1, Pallas kernels, elution_terms(): pl.pallas_call(functools.partial(elution_kernel, planes), out_shape=jax.S...  3.04 us
    pallas_call x1, Pallas kernels, partial_model(): pl.pallas_call(functools.partial(model_kernel, places, planes), out_shape...  2.1 us
    unnamed x10, local copies, waits for them, and re-layouts  1.79 us
    pallas_call x1, Pallas kernels, circulant(): pl.pallas_call(functools.partial(circulant_kernel, turn), out_shape=jax.S...  1.53 us
  transfers between devices with their start and end apart: 12, of which 11 were waited for; matrix products, arithmetic and copies ran while one was open for 2% of the time, Pallas kernels for 14%

profile of v7, /device:TPU:0, one launch (start us, length us, event | category | flops | bytes accessed | tf_op | source)
XLA Modules:
  0.0 47.2 jit_solution(14913223668021384457)
XLA Ops:
  0.0 0.0 copy-start
  0.0 0.8 %copy-done = f32[192,64]{0,1:T(8,128)S(1)} copy-done((f32[192,64]{0,1:T(8,128)S(1)}, f32[192,64]{0,1:T(8,128)}, u32[]{:S(2)}) %copy-start) | copy-done | bytes 49176
  0.8 0.0 copy-start.2
  0.8 0.0 copy-start.3
  0.8 0.2 encode_elution.1.mine_ref
  1.1 5.1 %collective-permute-start.2 = (s16[112,128]{1,0:T(8,128)(2,1)S(1)}, s16[112,128]{1,0:T(8,128)(2,1)S(1)}, u32[]{:S(2)}, u32[]{:S(2)}) collective-permute-start(s16[112,128]{1,0:T(8,128)(2,1)S(1)} %encode_elution.1.mine_ref), channel_id=1, source_target_pairs={{0,24},{2,26},{4,28},{6,30},{8,16},{10,18},{12,20},{14,22},{16,8},... | collective-permute-start | bytes 86024 | tf_op jit(solution)/shard_map/ppermute | solution.py:553
  6.2 0.0 collective-permute-start.1
  6.2 0.6 %collective-permute-start = (s16[112,128]{1,0:T(8,128)(2,1)S(1)}, s16[112,128]{1,0:T(8,128)(2,1)S(1)}, u32[]{:S(2)}, u32[]{:S(2)}) collective-permute-start(s16[112,128]{1,0:T(8,128)(2,1)S(1)} %encode_elution.1.mine_ref), channel_id=1, source_target_pairs={{0,8},{2,10},{4,12},{6,14},{8,0},{10,2},{12,4},{14,6},{16,24},{18,... | collective-permute-start | bytes 86024 | tf_op jit(solution)/shard_map/ppermute | solution.py:553
  6.8 0.8 %reshape.3.w_ref = f32[128,48]{1,0:T(8,128)S(1)} reshape(f32[6144]{0:T(1024)} %param.10) | data formatting | bytes 49152 | tf_op jit(solution)/shard_map/reshape | solution.py:585
  7.7 0.0 copy-start.1
  7.7 0.4 collective-permute-done.2
  8.0 2.9 %collective-permute-done.1 = s16[112,128]{1,0:T(8,128)(2,1)S(1)} collective-permute-done((s16[112,128]{1,0:T(8,128)(2,1)S(1)}, s16[112,128]{1,0:T(8,128)(2,1)S(1)}, u32[]{:S(2)}, u32[]{:S(2)}) %collective-permute-start.1) | collective-permute-done | bytes 28704 | tf_op jit(solution)/shard_map/ppermute | solution.py:553
  11.0 0.0 collective-permute-done
  11.0 1.6 %collective-permute-start.3 = (s16[4,112,128]{2,1,0:T(8,128)(2,1)S(1)}, s16[4,112,128]{2,1,0:T(8,128)(2,1)S(1)}, u32[]{:S(2)}, u32[]{:S(2)}) collective-permute-start(s16[4,112,128]{2,1,0:T(8,128)(2,1)S(1)} %pad_add_fusion.1), channel_id=1, source_target_pairs={{0,4},{2,6},{4,0},{6,2},{8,12},{10,14},{12,8},{14,10},{16,20},{18,... | collective-permute-start | bytes 344072 | tf_op jit(solution)/shard_map/ppermute | solution.py:553
  12.5 0.0 copy-start.4
  12.5 0.9 %copy-done.4 = f32[448,128]{1,0:T(8,128)S(1)} copy-done((f32[448,128]{1,0:T(8,128)S(1)}, f32[448,128]{1,0:T(8,128)}, u32[]{:S(2)}) %copy-start.4) | copy-done | bytes 229400
  13.5 1.5 %circulant_block.1.refs_2_ = bf16[256,6144]{1,0:T(8,128)(2,1)S(1)} custom-call(f32[128,48]{1,0:T(8,128)S(1)} %reshape.3.w_ref, f32[448,128]{1,0:T(8,128)S(1)} %copy-done.4), custom_call_target="tpu_custom_call" | custom-call | flops 2000000000 | bytes 4194304 | tf_op jit(solution)/shard_map/circulant_block/pallas_call | solution.py:154
  15.0 0.8 %collective-permute-done.3 = s16[4,112,128]{2,1,0:T(8,128)(2,1)S(1)} collective-permute-done((s16[4,112,128]{2,1,0:T(8,128)(2,1)S(1)}, s16[4,112,128]{2,1,0:T(8,128)(2,1)S(1)}, u32[]{:S(2)}, u32[]{:S(2)}) %collective-permute-start.3) | collective-permute-done | bytes 114720 | tf_op jit(solution)/shard_map/ppermute | solution.py:553
  15.9 0.1 collective-permute-start.4
  15.9 1.5 %collective-permute-done.4.refs_1_.came_ref = s16[8,112,128]{2,1,0:T(8,128)(2,1)S(1)} collective-permute-done((s16[8,112,128]{2,1,0:T(8,128)(2,1)S(1)}, s16[8,112,128]{2,1,0:T(8,128)(2,1)S(1)}, u32[]{:S(2)}, u32[]{:S(2)}) %collective-permute-start.4) | collective-permute-done | bytes 229408 | tf_op jit(solution)/shard_map/ppermute | solution.py:553
  17.4 1.5 %collective-permute-start.5 = (s16[224,128]{1,0:T(8,128)(2,1)S(1)}, s16[224,128]{1,0:T(8,128)(2,1)S(1)}, u32[]{:S(2)}, u32[]{:S(2)}) collective-permute-start(s16[224,128]{1,0:T(8,128)(2,1)S(1)} %window_pair.1.refs_0_), channel_id=1, source_target_pairs={{0,1},{1,0},{2,3},{3,2},{4,5},{5,4},{6,7},{7,6},{8,9},{9,8},{10,11... | collective-permute-start | bytes 172040 | tf_op jit(solution)/shard_map/ppermute | solution.py:553
  18.9 2.1 %partial_model.1.refs_1_ = f32[64,640]{1,0:T(8,128)S(1)} custom-call(s16[8,112,128]{2,1,0:T(8,128)(2,1)S(1)} %pad_add_fusion.refs_0_, s16[8,112,128]{2,1,0:T(8,128)(2,1)S(1)} %collective-permute-done.4.refs_1_.came_ref, bf16[256,6144]{1,0:T(8,128)(2,1)S(1)} %circulant_block.1.refs_2_), custom_call_target="tpu_custom_call" | custom-call | flops 2000000000 | bytes 4194304 | tf_op jit(solution)/shard_map/partial_model/pallas_call | solution.py:237
  21.0 0.6 %collective-permute-done.5.refs_1_ = s16[224,128]{1,0:T(8,128)(2,1)S(1)} collective-permute-done((s16[224,128]{1,0:T(8,128)(2,1)S(1)}, s16[224,128]{1,0:T(8,128)(2,1)S(1)}, u32[]{:S(2)}, u32[]{:S(2)}) %collective-permute-start.5) | collective-permute-done | bytes 57376 | tf_op jit(solution)/shard_map/ppermute | solution.py:553
  21.6 1.5 %collective-permute-start.6 = (f32[64,640]{1,0:T(8,128)S(1)}, f32[64,640]{1,0:T(8,128)S(1)}, u32[]{:S(2)}, u32[]{:S(2)}) collective-permute-start(f32[64,640]{1,0:T(8,128)S(1)} %partial_model.1.refs_1_), channel_id=1, source_target_pairs={{0,1},{1,0},{2,3},{3,2},{4,5},{5,4},{6,7},{7,6},{8,9},{9,8},{10,11... | collective-permute-start | bytes 491528 | tf_op jit(solution)/shard_map/ppermute | solution.py:553
  23.1 0.0 copy-done.2
  23.1 0.0 copy-done.3
  23.1 3.0 %elution_terms.1.refs_3_ = bf16[128,3072]{1,0:T(8,128)(2,1)S(1)} custom-call(s16[224,128]{1,0:T(8,128)(2,1)S(1)} %window_pair.1.refs_0_, s16[224,128]{1,0:T(8,128)(2,1)S(1)} %collective-permute-done.5.refs_1_, f32[8,64]{1,0:T(8,128)S(1)} %copy-done.2, s32[8,64]{1,0:T(8,128)S(1)} %copy-done.3), custom_call_target="tpu_custom_call" | custom-call | flops 1000000000 | bytes 2097152 | tf_op jit(solution)/shard_map/elution_terms/pallas_call | solution.py:327
  26.2 0.9 %collective-permute-done.6.refs_2_ = f32[64,640]{1,0:T(8,128)S(1)} collective-permute-done((f32[64,640]{1,0:T(8,128)S(1)}, f32[64,640]{1,0:T(8,128)S(1)}, u32[]{:S(2)}, u32[]{:S(2)}) %collective-permute-start.6) | collective-permute-done | bytes 163872 | tf_op jit(solution)/shard_map/ppermute | solution.py:553
  27.1 0.0 copy-done.1
  27.1 3.2 %model_products.1 = (f32[544,128]{1,0:T(8,128)S(1)}, f32[544,128]{1,0:T(8,128)S(1)}) custom-call(bf16[8,384,2048]{2,1,0:T(8,128)(2,1)S(1)} %copy-done.1, f32[64,640]{1,0:T(8,128)S(1)} %partial_model.1.refs_1_, f32[64,640]{1,0:T(8,128)S(1)} %collective-permute-done.6.refs_2_, bf16[128,3072]{1,0:T(8,128)(2,1)S(1)} %elution_terms.1.refs_3_, ...), custom_call_target="tpu_custom_call" | custom-call | flops 8000000000 | bytes 12582912 | tf_op jit(solution)/shard_map/model_products/pallas_call | solution.py:390
  30.2 0.1 collective-permute-start.7
  30.3 1.5 %collective-permute-done.7.b_ref = f32[544,128]{1,0:T(8,128)S(1)} collective-permute-done((f32[544,128]{1,0:T(8,128)S(1)}, f32[544,128]{1,0:T(8,128)S(1)}, u32[]{:S(2)}, u32[]{:S(2)}) %collective-permute-start.7) | collective-permute-done | bytes 278560 | tf_op jit(solution)/shard_map/ppermute | solution.py:553
  31.9 0.2 reduce_cores.1
  32.1 1.5 %collective-permute-start.8 = (s16[336,128]{1,0:T(8,128)(2,1)S(1)}, s16[336,128]{1,0:T(8,128)(2,1)S(1)}, u32[]{:S(2)}, u32[]{:S(2)}) collective-permute-start(s16[336,128]{1,0:T(8,128)(2,1)S(1)} %reduce_cores.1), channel_id=1, source_target_pairs={{0,4},{2,6},{4,0},{6,2},{8,12},{10,14},{12,8},{14,10},{16,20},{18,... | collective-permute-start | bytes 258056 | tf_op jit(solution)/shard_map/ppermute | solution.py:553
  33.6 3.1 %collective-permute-done.8.c_ref = s16[336,128]{1,0:T(8,128)(2,1)S(1)} collective-permute-done((s16[336,128]{1,0:T(8,128)(2,1)S(1)}, s16[336,128]{1,0:T(8,128)(2,1)S(1)}, u32[]{:S(2)}, u32[]{:S(2)}) %collective-permute-start.8) | collective-permute-done | bytes 86048 | tf_op jit(solution)/shard_map/ppermute | solution.py:553
  36.7 0.3 reduce_x.1
  37.0 1.5 %collective-permute-start.9 = (s16[144,128]{1,0:T(8,128)(2,1)S(1)}, s16[144,128]{1,0:T(8,128)(2,1)S(1)}, u32[]{:S(2)}, u32[]{:S(2)}) collective-permute-start(s16[144,128]{1,0:T(8,128)(2,1)S(1)} %get-tuple-element.26), channel_id=1, source_target_pairs={{0,24},{2,26},{4,28},{6,30},{8,16},{10,18},{12,20},{14,22},{16,8},... | collective-permute-start | bytes 110600 | tf_op jit(solution)/shard_map/ppermute | solution.py:553
  38.5 0.6 %collective-permute-start.10 = (s16[144,128]{1,0:T(8,128)(2,1)S(1)}, s16[144,128]{1,0:T(8,128)(2,1)S(1)}, u32[]{:S(2)}, u32[]{:S(2)}) collective-permute-start(s16[144,128]{1,0:T(8,128)(2,1)S(1)} %get-tuple-element.27), channel_id=1, source_target_pairs={{0,16},{2,18},{4,20},{6,22},{8,24},{10,26},{12,28},{14,30},{16,0},... | collective-permute-start | bytes 110600 | tf_op jit(solution)/shard_map/ppermute | solution.py:553
  39.2 2.3 %collective-permute-start.11 = (s16[144,128]{1,0:T(8,128)(2,1)S(1)}, s16[144,128]{1,0:T(8,128)(2,1)S(1)}, u32[]{:S(2)}, u32[]{:S(2)}) collective-permute-start(s16[144,128]{1,0:T(8,128)(2,1)S(1)} %get-tuple-element.28), channel_id=1, source_target_pairs={{0,8},{2,10},{4,12},{6,14},{8,0},{10,2},{12,4},{14,6},{16,24},{18,... | collective-permute-start | bytes 110600 | tf_op jit(solution)/shard_map/ppermute | solution.py:553
  41.4 1.6 %collective-permute-done.9.refs_0_ = s16[144,128]{1,0:T(8,128)(2,1)S(1)} collective-permute-done((s16[144,128]{1,0:T(8,128)(2,1)S(1)}, s16[144,128]{1,0:T(8,128)(2,1)S(1)}, u32[]{:S(2)}, u32[]{:S(2)}) %collective-permute-start.9) | collective-permute-done | bytes 36896 | tf_op jit(solution)/shard_map/ppermute | solution.py:553
  43.0 0.4 collective-permute-done.10.refs_1_
  43.5 0.4 collective-permute-done.11.refs_2_
  43.8 3.3 %solve.1 = f32[64,128]{1,0:T(8,128)} custom-call(f32[96,128]{1,0:T(8,128)S(1)} %get-tuple-element.25.own_ref, s16[144,128]{1,0:T(8,128)(2,1)S(1)} %collective-permute-done.9.refs_0_, s16[144,128]{1,0:T(8,128)(2,1)S(1)} %collective-permute-done.10.refs_1_, s16[144,128]{1,0:T(8,128)(2,1)S(1)} %collective-permute-done.11.refs_2_), custom_call_target="tpu_custom_call" | custom-call | tf_op jit(solution)/shard_map/solve/pallas_call | solution.py:542
  (3 shorter events, 0.0 us)
Async XLA Ops:
  0.0 0.8 %copy-start = (f32[192,64]{0,1:T(8,128)S(1)}, f32[192,64]{0,1:T(8,128)}, u32[]{:S(2)}) copy-start(f32[192,64]{0,1:T(8,128)} %param.7) | copy-start | bytes 147460
  0.8 22.3 %copy-start.2 = (f32[8,64]{1,0:T(8,128)S(1)}, f32[8,64]{1,0:T(8,128)}, u32[]{:S(2)}) copy-start(f32[8,64]{1,0:T(8,128)} %refs_4_.1) | copy-start | bytes 6148
  0.8 22.3 %copy-start.3 = (s32[8,64]{1,0:T(8,128)S(1)}, s32[8,64]{1,0:T(8,128)}, u32[]{:S(2)}) copy-start(s32[8,64]{1,0:T(8,128)} %refs_5_.1) | copy-start | bytes 6148
  1.1 7.0 %collective-permute-start.2 = (s16[112,128]{1,0:T(8,128)(2,1)S(1)}, s16[112,128]{1,0:T(8,128)(2,1)S(1)}, u32[]{:S(2)}, u32[]{:S(2)}) collective-permute-start(s16[112,128]{1,0:T(8,128)(2,1)S(1)} %encode_elution.1.mine_ref), channel_id=1, source_target_pairs={{0,24},{2,26},{4,28},{6,30},{8,16},{10,18},{12,20},{14,22},{16,8},... | collective-permute-start | bytes 86024 | tf_op jit(solution)/shard_map/ppermute | solution.py:553
  6.2 4.8 %collective-permute-start.1 = (s16[112,128]{1,0:T(8,128)(2,1)S(1)}, s16[112,128]{1,0:T(8,128)(2,1)S(1)}, u32[]{:S(2)}, u32[]{:S(2)}) collective-permute-start(s16[112,128]{1,0:T(8,128)(2,1)S(1)} %encode_elution.1.mine_ref), channel_id=1, source_target_pairs={{0,16},{2,18},{4,20},{6,22},{8,24},{10,26},{12,28},{14,30},{16,0},... | collective-permute-start | bytes 86024 | tf_op jit(solution)/shard_map/ppermute | solution.py:553
  6.2 4.8 %collective-permute-start = (s16[112,128]{1,0:T(8,128)(2,1)S(1)}, s16[112,128]{1,0:T(8,128)(2,1)S(1)}, u32[]{:S(2)}, u32[]{:S(2)}) collective-permute-start(s16[112,128]{1,0:T(8,128)(2,1)S(1)} %encode_elution.1.mine_ref), channel_id=1, source_target_pairs={{0,8},{2,10},{4,12},{6,14},{8,0},{10,2},{12,4},{14,6},{16,24},{18,... | collective-permute-start | bytes 86024 | tf_op jit(solution)/shard_map/ppermute | solution.py:553
  7.7 19.4 %copy-start.1 = (bf16[8,384,2048]{2,1,0:T(8,128)(2,1)S(1)}, bf16[8,384,2048]{2,1,0:T(8,128)(2,1)}, u32[]{:S(2)}) copy-start(bf16[8,384,2048]{2,1,0:T(8,128)(2,1)} %refs_0_.1) | copy-start | bytes 37748740
  11.0 4.9 %collective-permute-start.3 = (s16[4,112,128]{2,1,0:T(8,128)(2,1)S(1)}, s16[4,112,128]{2,1,0:T(8,128)(2,1)S(1)}, u32[]{:S(2)}, u32[]{:S(2)}) collective-permute-start(s16[4,112,128]{2,1,0:T(8,128)(2,1)S(1)} %pad_add_fusion.1), channel_id=1, source_target_pairs={{0,4},{2,6},{4,0},{6,2},{8,12},{10,14},{12,8},{14,10},{16,20},{18,... | collective-permute-start | bytes 344072 | tf_op jit(solution)/shard_map/ppermute | solution.py:553
  12.5 0.9 %copy-start.4 = (f32[448,128]{1,0:T(8,128)S(1)}, f32[448,128]{1,0:T(8,128)}, u32[]{:S(2)}) copy-start(f32[448,128]{1,0:T(8,128)} %constant.2.clone.table_ref) | copy-start | bytes 688132
  15.9 1.6 %collective-permute-start.4 = (s16[8,112,128]{2,1,0:T(8,128)(2,1)S(1)}, s16[8,112,128]{2,1,0:T(8,128)(2,1)S(1)}, u32[]{:S(2)}, u32[]{:S(2)}) collective-permute-start(s16[8,112,128]{2,1,0:T(8,128)(2,1)S(1)} %pad_add_fusion.refs_0_), channel_id=1, source_target_pairs={{0,2},{2,0},{4,6},{6,4},{8,10},{10,8},{12,14},{14,12},{16,18},{18,... | collective-permute-start | bytes 688136 | tf_op jit(solution)/shard_map/ppermute | solution.py:553
  17.4 4.2 %collective-permute-start.5 = (s16[224,128]{1,0:T(8,128)(2,1)S(1)}, s16[224,128]{1,0:T(8,128)(2,1)S(1)}, u32[]{:S(2)}, u32[]{:S(2)}) collective-permute-start(s16[224,128]{1,0:T(8,128)(2,1)S(1)} %window_pair.1.refs_0_), channel_id=1, source_target_pairs={{0,1},{1,0},{2,3},{3,2},{4,5},{5,4},{6,7},{7,6},{8,9},{9,8},{10,11... | collective-permute-start | bytes 172040 | tf_op jit(solution)/shard_map/ppermute | solution.py:553
  21.6 5.5 %collective-permute-start.6 = (f32[64,640]{1,0:T(8,128)S(1)}, f32[64,640]{1,0:T(8,128)S(1)}, u32[]{:S(2)}, u32[]{:S(2)}) collective-permute-start(f32[64,640]{1,0:T(8,128)S(1)} %partial_model.1.refs_1_), channel_id=1, source_target_pairs={{0,1},{1,0},{2,3},{3,2},{4,5},{5,4},{6,7},{7,6},{8,9},{9,8},{10,11... | collective-permute-start | bytes 491528 | tf_op jit(solution)/shard_map/ppermute | solution.py:553
  30.2 1.6 %collective-permute-start.7 = (f32[544,128]{1,0:T(8,128)S(1)}, f32[544,128]{1,0:T(8,128)S(1)}, u32[]{:S(2)}, u32[]{:S(2)}) collective-permute-start(f32[544,128]{1,0:T(8,128)S(1)} %get-tuple-element.24), channel_id=1, source_target_pairs={{0,2},{2,0},{4,6},{6,4},{8,10},{10,8},{12,14},{14,12},{16,18},{18,... | collective-permute-start | bytes 835592 | tf_op jit(solution)/shard_map/ppermute | solution.py:553
  32.1 4.6 %collective-permute-start.8 = (s16[336,128]{1,0:T(8,128)(2,1)S(1)}, s16[336,128]{1,0:T(8,128)(2,1)S(1)}, u32[]{:S(2)}, u32[]{:S(2)}) collective-permute-start(s16[336,128]{1,0:T(8,128)(2,1)S(1)} %reduce_cores.1), channel_id=1, source_target_pairs={{0,4},{2,6},{4,0},{6,2},{8,12},{10,14},{12,8},{14,10},{16,20},{18,... | collective-permute-start | bytes 258056 | tf_op jit(solution)/shard_map/ppermute | solution.py:553
  37.0 6.0 %collective-permute-start.9 = (s16[144,128]{1,0:T(8,128)(2,1)S(1)}, s16[144,128]{1,0:T(8,128)(2,1)S(1)}, u32[]{:S(2)}, u32[]{:S(2)}) collective-permute-start(s16[144,128]{1,0:T(8,128)(2,1)S(1)} %get-tuple-element.26), channel_id=1, source_target_pairs={{0,24},{2,26},{4,28},{6,30},{8,16},{10,18},{12,20},{14,22},{16,8},... | collective-permute-start | bytes 110600 | tf_op jit(solution)/shard_map/ppermute | solution.py:553
  38.5 4.9 %collective-permute-start.10 = (s16[144,128]{1,0:T(8,128)(2,1)S(1)}, s16[144,128]{1,0:T(8,128)(2,1)S(1)}, u32[]{:S(2)}, u32[]{:S(2)}) collective-permute-start(s16[144,128]{1,0:T(8,128)(2,1)S(1)} %get-tuple-element.27), channel_id=1, source_target_pairs={{0,16},{2,18},{4,20},{6,22},{8,24},{10,26},{12,28},{14,30},{16,0},... | collective-permute-start | bytes 110600 | tf_op jit(solution)/shard_map/ppermute | solution.py:553
  39.2 4.6 %collective-permute-start.11 = (s16[144,128]{1,0:T(8,128)(2,1)S(1)}, s16[144,128]{1,0:T(8,128)(2,1)S(1)}, u32[]{:S(2)}, u32[]{:S(2)}) collective-permute-start(s16[144,128]{1,0:T(8,128)(2,1)S(1)} %get-tuple-element.28), channel_id=1, source_target_pairs={{0,8},{2,10},{4,12},{6,14},{8,0},{10,2},{12,4},{14,6},{16,24},{18,... | collective-permute-start | bytes 110600 | tf_op jit(solution)/shard_map/ppermute | solution.py:553

commit v8 on v7

--- a/solution.py
+++ b/solution.py
@@ -67,6 +67,15 @@
     o_ref[half:, :] = jnp.concatenate([level, level], axis=1)
 
 
+def encode_columns(x, o_ref):
+    rows = x.shape[0]
+    peak = jnp.maximum(jnp.max(jnp.abs(x), axis=0, keepdims=True), 1e-30)
+    level = jnp.floor(256.0 / math.log(2.0) * jnp.log(peak)) + 1.0
+    x = jnp.clip(jnp.floor(x * (FULL / scale_of(level)) + 0.5), -FULL, FULL)
+    o_ref[0:rows, :] = x.astype(jnp.int32).astype(jnp.int16)
+    o_ref[rows:, :] = jnp.broadcast_to(level, (16, x.shape[1])).astype(jnp.int32).astype(jnp.int16)
+
+
 def scale_of(level):
     return jnp.exp(math.log(2.0) / 256.0 * level)
 
@@ -74,7 +83,11 @@
 def decoded(x):
     half = x.shape[0] - 16
     x = x.astype(jnp.int32).astype(jnp.float32)
-    x = x[:half] * (scale_of(x[half : half + 1]) * (1.0 / FULL))
+    return x[:half] * (scale_of(x[half : half + 1]) * (1.0 / FULL))
+
+
+def decoded_terms(x):
+    x = decoded(x)
     high = x.astype(jnp.bfloat16).astype(jnp.float32)
     low = x - high
     left = lax.broadcasted_iota(jnp.int32, x.shape, 1) < LANES // 2
@@ -163,7 +176,10 @@
 
 
 def model_kernel(places, planes, *refs):
-    u_ref, g_ref, wide = refs[-3:]
+    if planes:
+        u_ref, g_ref, coded_ref, wide = refs[-4:]
+    else:
+        u_ref, g_ref, wide = refs[-3:]
     length = u_ref.shape[1]
     components = g_ref.shape[0]
     freq_rank = lax.axis_index("freq")
@@ -175,13 +191,15 @@
         for block in range(freq_count):
             apart = lax.bitwise_xor((freq_rank + block) & (freq_count - 1), freq_rank)
             ref = came_ref if block % 2 else own_ref
-            values = decoded(ref[pl.ds(block_place(apart, freq_count), 1)][0])
+            values = decoded_terms(ref[pl.ds(block_place(apart, freq_count), 1)][0])
             at, before = block * padded, (block - 1) % freq_count * padded
             wide[at : at + rows, 0:LANES] = values
             wide[before : before + rows, LANES:] = values
             wide[at + rows : at + padded, :] = jnp.zeros((padded - rows, 2 * LANES), jnp.bfloat16)
         period = length // freq_count // LANES
-        for a in range(min(period, places)):
+        left = lax.broadcasted_iota(jnp.int32, (LANES, LANES), 1) < components
+        sides = []
+        for a in range(period):
             columns = []
             for block in range(freq_count):
                 first = REACH // LANES + period * block - a
@@ -193,10 +211,18 @@
                 jnp.concatenate(columns, axis=1), wide[:, :width], preferred_element_type=jnp.float32
             )
             made = made[:LANES] + made[LANES:]
+            tiles = []
             for half in range(width // LANES):
-                piece = made[:, half * LANES : (half + 1) * LANES].T
+                tile = made[:, half * LANES : (half + 1) * LANES]
+                tiles.append(tile + pltpu.roll(tile, components, 1))
                 to = (a + half * period) * LANES
-                g_ref[:, to : to + LANES] = piece[:components] + piece[components:]
+                g_ref[:, to : to + LANES] = tiles[-1].T[:components]
+            if len(tiles) == 1:
+                half = LANES // 2
+                sides.append(jnp.where(left[:half], tiles[0][:half], tiles[0][half:]))
+            else:
+                sides.append(jnp.where(left, tiles[0], tiles[1]))
+        encode_columns(jnp.concatenate(sides, axis=0), coded_ref)
         return
     own_ref = refs[0]
     step = own_ref.shape[1]
@@ -234,11 +260,14 @@
         wide_rows = 2 * own.shape[0] * (-(-2 * (own.shape[1] - 16) // LANES) * LANES)
     else:
         wide_rows = REACH + length + 2 * LANES * ((places - 1) // 2)
+    outs = [jax.ShapeDtypeStruct((components, places * LANES), jnp.float32)]
+    if planes:
+        outs.append(jax.ShapeDtypeStruct((places * LANES // 2 + 16, LANES), jnp.int16))
     return pl.pallas_call(
         functools.partial(model_kernel, places, planes),
-        out_shape=jax.ShapeDtypeStruct((components, places * LANES), jnp.float32),
+        out_shape=tuple(outs),
         in_specs=vmem(len(gathered) + 1),
-        out_specs=vmem(1)[0],
+        out_specs=tuple(vmem(len(outs))),
         scratch_shapes=[pltpu.VMEM((wide_rows, 2 * LANES), jnp.bfloat16)],
         compiler_params=pltpu.CompilerParams(vmem_limit_bytes=24 * MIB),
         cost_estimate=pl.CostEstimate(flops=2_000_000_000, bytes_accessed=4 * MIB, transcendentals=0),
@@ -304,7 +333,10 @@
         for ref, half in ((pair_ref, mz_rank), (other_ref, 1 - mz_rank)):
             for block in range(2):
                 to = pl.multiple_of((2 * block + half) * rows, 64)
-                window[pl.ds(to, rows), :] = decoded(ref[block * coded : (block + 1) * coded, :])
+                values = decoded(ref[block * coded : (block + 1) * coded, :])
+                half_rows = rows // 2
+                window[pl.ds(to, half_rows), :] = values
+                window[pl.ds(pl.multiple_of(to + half_rows, 32), half_rows), :] = pltpu.roll(values, LANES // 2, 1)
     else:
         own_ref = refs[0]
         step = own_ref.shape[1]
@@ -316,7 +348,7 @@
     pieces = []
     for at in range(skip, window.shape[0], LANES):
         piece = window[at : at + LANES, :].astype(jnp.float32).T
-        pieces.append(piece[:components] + piece[components:])
+        pieces.append(piece[:components] if planes else piece[:components] + piece[components:])
     shifted_terms(jnp.concatenate(pieces, axis=1), amp_ref[...].T, lag_ref[...].T, bin_count, terms)
 
 
@@ -329,7 +361,11 @@
         out_shape=jax.ShapeDtypeStruct((2 * components, run_count * bin_count), jnp.bfloat16),
         in_specs=vmem(len(elutions) + 2),
         out_specs=vmem(1)[0],
-        scratch_shapes=[pltpu.VMEM((2 * bin_count if planes else places * LANES, LANES), jnp.bfloat16)],
+        scratch_shapes=[
+            pltpu.VMEM((2 * bin_count, LANES), jnp.float32)
+            if planes
+            else pltpu.VMEM((places * LANES, LANES), jnp.bfloat16)
+        ],
         compiler_params=pltpu.CompilerParams(vmem_limit_bytes=12 * MIB),
         cost_estimate=pl.CostEstimate(flops=1_000_000_000, bytes_accessed=2 * MIB, transcendentals=0),
         name="elution_terms",
@@ -345,8 +381,21 @@
     chunk = 2 * LANES
     chunks = local_mz // chunk
     g = g_refs[0][...]
-    for ref in g_refs[1:]:
-        g = g + ref[...]
+    if planes:
+        period = bin_count // LANES
+        x = decoded(g_refs[1][...])
+        first, second, at = [], [], 0
+        for a in range(period):
+            if a + period < g.shape[1] // LANES:
+                tile = x[at : at + LANES].T
+                second.append(tile[components:])
+                at += LANES
+            else:
+                half = x[at : at + LANES // 2]
+                tile = jnp.concatenate([half, pltpu.roll(half, components, 1)], axis=0).T
+                at += LANES // 2
+            first.append(tile[:components])
+        g = g + jnp.concatenate(first + second, axis=1)
     shifted_terms(g, amp_ref[...].T, lag_ref[...].T, bin_count, terms)
     gram = lax.dot_general(
         terms[...], elution_ref[...], (((1,), (1,)), ((), ())), preferred_element_type=jnp.float32
@@ -402,7 +451,10 @@
 
 
 def inverse2(a, b, d):
-    scale = 1.0 / (a * d - b * b)
+    det = a * d - b * b
+    scale = pl.reciprocal(det, approx=True)
+    for _ in range(2):
+        scale = scale * (2.0 - det * scale)
     return d * scale, -b * scale, a * scale
 
 
@@ -573,7 +625,7 @@
     if not planes:
         mine = pack(elution)
         gathered = lax.all_gather(mine, axes, axis=0).reshape(-1, math.gcd(bin_count, LANES), LANES)
-        g = partial_model((gathered,), circulant(bin_weight.reshape(LANES, -1), 0), bin_count, components)
+        (g,) = partial_model((gathered,), circulant(bin_weight.reshape(LANES, -1), 0), bin_count, components)
         shifted = elution_terms((gathered,), loadings, shifts, bin_count)
         numerator, gram = product(intensity, (g,), shifted, loadings, shifts, planes)
         gram = lax.psum(gram, "freq")
@@ -590,9 +642,9 @@
     came = swap(held, "freq", freq_count, 1)
     pair = window_pair(mine, came)
     other = swap(pair, "mz", mz_count, 1)
-    g = partial_model((held, came), u, bin_count, components)
-    g, other = lax.optimization_barrier((g, other))
-    models = (g, swap(g, "mz", mz_count, 1))
+    g, coded = partial_model((held, came), u, bin_count, components)
+    coded, other = lax.optimization_barrier((coded, other))
+    models = (g, swap(coded, "mz", mz_count, 1))
     shifted = elution_terms((pair, other), loadings, shifts, bin_count)
     keep, send = product(intensity, models, shifted, loadings, shifts, planes)
     tail = components // 2

time: 47.4 us -> 47 us (level)
  waiting for transfers between devices: 14.1 us -> 13 us
  Pallas kernels: 13.9 us -> 14.4 us
    ppermute x12, waiting for transfers between devices: 14.1 us -> 13 us  [swap(): return lax.ppermute(x, axes, [(i, i ^ value) for i in range(count)])]
  transfers between devices with their start and end apart: 12 -> 12, of which waited for: 11 -> 10; matrix products, arithmetic and copies ran while one was open for 2% -> 2% of each run, Pallas kernels for 14% -> 15%
where the time goes in v8:
time: 47 us; the launch traced here: 46.7 us
  starting transfers between devices  16.5 us (35%)
  Pallas kernels  14.4 us (31%)
  waiting for transfers between devices  13 us (28%)
  local copies, waits for them, and re-layouts  2.6 us (6%)
    ppermute x12, starting transfers between devices, swap(): return lax.ppermute(x, axes, [(i, i ^ value) for i in range(count)])  16.5 us
    ppermute x12, waiting for transfers between devices, swap(): return lax.ppermute(x, axes, [(i, i ^ value) for i in range(count)])  13 us
    pallas_call x3, Pallas kernels, small_call(): pl.pallas_call(kernel, out_shape=tuple((jax.ShapeDtypeStruct(shape, dtype...  4.08 us
    pallas_call x1, Pallas kernels, product(): pl.pallas_call(functools.partial(product_kernel, len(models), planes), ou...  3.26 us
    pallas_call x1, Pallas kernels, elution_terms(): pl.pallas_call(functools.partial(elution_kernel, planes), out_shape=jax.S...  3.16 us
    pallas_call x1, Pallas kernels, partial_model(): pl.pallas_call(functools.partial(model_kernel, places, planes), out_shape...  2.18 us
    unnamed x10, local copies, waits for them, and re-layouts  1.79 us
    pallas_call x1, Pallas kernels, circulant(): pl.pallas_call(functools.partial(circulant_kernel, turn), out_shape=jax.S...  1.53 us
  transfers between devices with their start and end apart: 12, of which 10 were waited for; matrix products, arithmetic and copies ran while one was open for 2% of the time, Pallas kernels for 15%

profile of v8, /device:TPU:0, one launch (start us, length us, event | category | flops | bytes accessed | tf_op | source)
XLA Modules:
  0.0 46.7 jit_solution(12200288986113641864)
XLA Ops:
  0.0 0.0 copy-start
  0.0 0.8 %copy-done = f32[192,64]{0,1:T(8,128)S(1)} copy-done((f32[192,64]{0,1:T(8,128)S(1)}, f32[192,64]{0,1:T(8,128)}, u32[]{:S(2)}) %copy-start) | copy-done | bytes 49176
  0.8 0.0 copy-start.2
  0.8 0.0 copy-start.3
  0.8 0.2 encode_elution.1.mine_ref
  1.1 5.1 %collective-permute-start.2 = (s16[112,128]{1,0:T(8,128)(2,1)S(1)}, s16[112,128]{1,0:T(8,128)(2,1)S(1)}, u32[]{:S(2)}, u32[]{:S(2)}) collective-permute-start(s16[112,128]{1,0:T(8,128)(2,1)S(1)} %encode_elution.1.mine_ref), channel_id=1, source_target_pairs={{0,24},{2,26},{4,28},{6,30},{8,16},{10,18},{12,20},{14,22},{16,8},... | collective-permute-start | bytes 86024 | tf_op jit(solution)/shard_map/ppermute | solution.py:605
  6.2 0.0 collective-permute-start.1
  6.2 0.6 %collective-permute-start = (s16[112,128]{1,0:T(8,128)(2,1)S(1)}, s16[112,128]{1,0:T(8,128)(2,1)S(1)}, u32[]{:S(2)}, u32[]{:S(2)}) collective-permute-start(s16[112,128]{1,0:T(8,128)(2,1)S(1)} %encode_elution.1.mine_ref), channel_id=1, source_target_pairs={{0,8},{2,10},{4,12},{6,14},{8,0},{10,2},{12,4},{14,6},{16,24},{18,... | collective-permute-start | bytes 86024 | tf_op jit(solution)/shard_map/ppermute | solution.py:605
  6.8 0.8 %reshape.3.w_ref = f32[128,48]{1,0:T(8,128)S(1)} reshape(f32[6144]{0:T(1024)} %param.10) | data formatting | bytes 49152 | tf_op jit(solution)/shard_map/reshape | solution.py:637
  7.7 0.0 copy-start.1
  7.7 0.4 collective-permute-done.2
  8.0 2.9 %collective-permute-done.1 = s16[112,128]{1,0:T(8,128)(2,1)S(1)} collective-permute-done((s16[112,128]{1,0:T(8,128)(2,1)S(1)}, s16[112,128]{1,0:T(8,128)(2,1)S(1)}, u32[]{:S(2)}, u32[]{:S(2)}) %collective-permute-start.1) | collective-permute-done | bytes 28704 | tf_op jit(solution)/shard_map/ppermute | solution.py:605
  11.0 0.0 collective-permute-done
  11.0 1.6 %collective-permute-start.3 = (s16[4,112,128]{2,1,0:T(8,128)(2,1)S(1)}, s16[4,112,128]{2,1,0:T(8,128)(2,1)S(1)}, u32[]{:S(2)}, u32[]{:S(2)}) collective-permute-start(s16[4,112,128]{2,1,0:T(8,128)(2,1)S(1)} %pad_add_fusion.1), channel_id=1, source_target_pairs={{0,4},{2,6},{4,0},{6,2},{8,12},{10,14},{12,8},{14,10},{16,20},{18,... | collective-permute-start | bytes 344072 | tf_op jit(solution)/shard_map/ppermute | solution.py:605
  12.5 0.0 copy-start.4
  12.5 0.9 %copy-done.4 = f32[448,128]{1,0:T(8,128)S(1)} copy-done((f32[448,128]{1,0:T(8,128)S(1)}, f32[448,128]{1,0:T(8,128)}, u32[]{:S(2)}) %copy-start.4) | copy-done | bytes 229400
  13.5 1.5 %circulant_block.1.refs_2_ = bf16[256,6144]{1,0:T(8,128)(2,1)S(1)} custom-call(f32[128,48]{1,0:T(8,128)S(1)} %reshape.3.w_ref, f32[448,128]{1,0:T(8,128)S(1)} %copy-done.4), custom_call_target="tpu_custom_call" | custom-call | flops 2000000000 | bytes 4194304 | tf_op jit(solution)/shard_map/circulant_block/pallas_call | solution.py:167
  15.0 0.8 %collective-permute-done.3 = s16[4,112,128]{2,1,0:T(8,128)(2,1)S(1)} collective-permute-done((s16[4,112,128]{2,1,0:T(8,128)(2,1)S(1)}, s16[4,112,128]{2,1,0:T(8,128)(2,1)S(1)}, u32[]{:S(2)}, u32[]{:S(2)}) %collective-permute-start.3) | collective-permute-done | bytes 114720 | tf_op jit(solution)/shard_map/ppermute | solution.py:605
  15.9 0.1 collective-permute-start.4
  15.9 1.5 %collective-permute-done.4.refs_1_.came_ref = s16[8,112,128]{2,1,0:T(8,128)(2,1)S(1)} collective-permute-done((s16[8,112,128]{2,1,0:T(8,128)(2,1)S(1)}, s16[8,112,128]{2,1,0:T(8,128)(2,1)S(1)}, u32[]{:S(2)}, u32[]{:S(2)}) %collective-permute-start.4) | collective-permute-done | bytes 229408 | tf_op jit(solution)/shard_map/ppermute | solution.py:605
  17.4 1.5 %collective-permute-start.5 = (s16[224,128]{1,0:T(8,128)(2,1)S(1)}, s16[224,128]{1,0:T(8,128)(2,1)S(1)}, u32[]{:S(2)}, u32[]{:S(2)}) collective-permute-start(s16[224,128]{1,0:T(8,128)(2,1)S(1)} %window_pair.1.refs_0_), channel_id=1, source_target_pairs={{0,1},{1,0},{2,3},{3,2},{4,5},{5,4},{6,7},{7,6},{8,9},{9,8},{10,11... | collective-permute-start | bytes 172040 | tf_op jit(solution)/shard_map/ppermute | solution.py:605
  18.9 2.2 %partial_model.1 = (f32[64,640]{1,0:T(8,128)S(1)}, s16[336,128]{1,0:T(8,128)(2,1)S(1)}) custom-call(s16[8,112,128]{2,1,0:T(8,128)(2,1)S(1)} %pad_add_fusion.refs_0_, s16[8,112,128]{2,1,0:T(8,128)(2,1)S(1)} %collective-permute-done.4.refs_1_.came_ref, bf16[256,6144]{1,0:T(8,128)(2,1)S(1)} %circulant_block.1.refs_2_), custom_call_target="tpu_custom_call" | custom-call | flops 2000000000 | bytes 4194304 | tf_op jit(solution)/shard_map/partial_model/pallas_call | solution.py:266
  21.1 0.5 %collective-permute-done.5.refs_1_ = s16[224,128]{1,0:T(8,128)(2,1)S(1)} collective-permute-done((s16[224,128]{1,0:T(8,128)(2,1)S(1)}, s16[224,128]{1,0:T(8,128)(2,1)S(1)}, u32[]{:S(2)}, u32[]{:S(2)}) %collective-permute-start.5) | collective-permute-done | bytes 57376 | tf_op jit(solution)/shard_map/ppermute | solution.py:605
  21.6 1.5 %collective-permute-start.6 = (s16[336,128]{1,0:T(8,128)(2,1)S(1)}, s16[336,128]{1,0:T(8,128)(2,1)S(1)}, u32[]{:S(2)}, u32[]{:S(2)}) collective-permute-start(s16[336,128]{1,0:T(8,128)(2,1)S(1)} %get-tuple-element.25), channel_id=1, source_target_pairs={{0,1},{1,0},{2,3},{3,2},{4,5},{5,4},{6,7},{7,6},{8,9},{9,8},{10,11... | collective-permute-start | bytes 258056 | tf_op jit(solution)/shard_map/ppermute | solution.py:605
  23.1 0.0 copy-done.2
  23.1 0.0 copy-done.3
  23.1 3.2 %elution_terms.1.refs_3_ = bf16[128,3072]{1,0:T(8,128)(2,1)S(1)} custom-call(s16[224,128]{1,0:T(8,128)(2,1)S(1)} %window_pair.1.refs_0_, s16[224,128]{1,0:T(8,128)(2,1)S(1)} %collective-permute-done.5.refs_1_, f32[8,64]{1,0:T(8,128)S(1)} %copy-done.2, s32[8,64]{1,0:T(8,128)S(1)} %copy-done.3), custom_call_target="tpu_custom_call" | custom-call | flops 1000000000 | bytes 2097152 | tf_op jit(solution)/shard_map/elution_terms/pallas_call | solution.py:359
  26.3 0.0 collective-permute-done.6.refs_2_
  26.3 0.0 copy-done.1
  26.3 3.3 %model_products.1 = (f32[544,128]{1,0:T(8,128)S(1)}, f32[544,128]{1,0:T(8,128)S(1)}) custom-call(bf16[8,384,2048]{2,1,0:T(8,128)(2,1)S(1)} %copy-done.1, f32[64,640]{1,0:T(8,128)S(1)} %get-tuple-element.23.refs_1_, s16[336,128]{1,0:T(8,128)(2,1)S(1)} %collective-permute-done.6.refs_2_, bf16[128,3072]{1,0:T(8,128)(2,1)S(1)} %elution_terms.1.refs_3_, ...), custom_call_target="tpu_custom_call" | custom-call | flops 8000000000 | bytes 12582912 | tf_op jit(solution)/shard_map/model_products/pallas_call | solution.py:439
  29.6 0.1 collective-permute-start.7
  29.6 1.5 %collective-permute-done.7.b_ref = f32[544,128]{1,0:T(8,128)S(1)} collective-permute-done((f32[544,128]{1,0:T(8,128)S(1)}, f32[544,128]{1,0:T(8,128)S(1)}, u32[]{:S(2)}, u32[]{:S(2)}) %collective-permute-start.7) | collective-permute-done | bytes 278560 | tf_op jit(solution)/shard_map/ppermute | solution.py:605
  31.2 0.2 reduce_cores.1
  31.4 1.6 %collective-permute-start.8 = (s16[336,128]{1,0:T(8,128)(2,1)S(1)}, s16[336,128]{1,0:T(8,128)(2,1)S(1)}, u32[]{:S(2)}, u32[]{:S(2)}) collective-permute-start(s16[336,128]{1,0:T(8,128)(2,1)S(1)} %reduce_cores.1), channel_id=1, source_target_pairs={{0,4},{2,6},{4,0},{6,2},{8,12},{10,14},{12,8},{14,10},{16,20},{18,... | collective-permute-start | bytes 258056 | tf_op jit(solution)/shard_map/ppermute | solution.py:605
  33.0 3.1 %collective-permute-done.8.c_ref = s16[336,128]{1,0:T(8,128)(2,1)S(1)} collective-permute-done((s16[336,128]{1,0:T(8,128)(2,1)S(1)}, s16[336,128]{1,0:T(8,128)(2,1)S(1)}, u32[]{:S(2)}, u32[]{:S(2)}) %collective-permute-start.8) | collective-permute-done | bytes 86048 | tf_op jit(solution)/shard_map/ppermute | solution.py:605
  36.0 0.3 reduce_x.1
  36.3 1.5 %collective-permute-start.9 = (s16[144,128]{1,0:T(8,128)(2,1)S(1)}, s16[144,128]{1,0:T(8,128)(2,1)S(1)}, u32[]{:S(2)}, u32[]{:S(2)}) collective-permute-start(s16[144,128]{1,0:T(8,128)(2,1)S(1)} %get-tuple-element.30), channel_id=1, source_target_pairs={{0,24},{2,26},{4,28},{6,30},{8,16},{10,18},{12,20},{14,22},{16,8},... | collective-permute-start | bytes 110600 | tf_op jit(solution)/shard_map/ppermute | solution.py:605
  37.9 0.6 %collective-permute-start.10 = (s16[144,128]{1,0:T(8,128)(2,1)S(1)}, s16[144,128]{1,0:T(8,128)(2,1)S(1)}, u32[]{:S(2)}, u32[]{:S(2)}) collective-permute-start(s16[144,128]{1,0:T(8,128)(2,1)S(1)} %get-tuple-element.31), channel_id=1, source_target_pairs={{0,16},{2,18},{4,20},{6,22},{8,24},{10,26},{12,28},{14,30},{16,0},... | collective-permute-start | bytes 110600 | tf_op jit(solution)/shard_map/ppermute | solution.py:605
  38.5 2.3 %collective-permute-start.11 = (s16[144,128]{1,0:T(8,128)(2,1)S(1)}, s16[144,128]{1,0:T(8,128)(2,1)S(1)}, u32[]{:S(2)}, u32[]{:S(2)}) collective-permute-start(s16[144,128]{1,0:T(8,128)(2,1)S(1)} %get-tuple-element.32), channel_id=1, source_target_pairs={{0,8},{2,10},{4,12},{6,14},{8,0},{10,2},{12,4},{14,6},{16,24},{18,... | collective-permute-start | bytes 110600 | tf_op jit(solution)/shard_map/ppermute | solution.py:605
  40.8 1.6 %collective-permute-done.9.refs_0_ = s16[144,128]{1,0:T(8,128)(2,1)S(1)} collective-permute-done((s16[144,128]{1,0:T(8,128)(2,1)S(1)}, s16[144,128]{1,0:T(8,128)(2,1)S(1)}, u32[]{:S(2)}, u32[]{:S(2)}) %collective-permute-start.9) | collective-permute-done | bytes 36896 | tf_op jit(solution)/shard_map/ppermute | solution.py:605
  42.3 0.4 collective-permute-done.10.refs_1_
  42.8 0.4 collective-permute-done.11.refs_2_
  43.1 3.6 %solve.1 = f32[64,128]{1,0:T(8,128)} custom-call(f32[96,128]{1,0:T(8,128)S(1)} %get-tuple-element.29.own_ref, s16[144,128]{1,0:T(8,128)(2,1)S(1)} %collective-permute-done.9.refs_0_, s16[144,128]{1,0:T(8,128)(2,1)S(1)} %collective-permute-done.10.refs_1_, s16[144,128]{1,0:T(8,128)(2,1)S(1)} %collective-permute-done.11.refs_2_), custom_call_target="tpu_custom_call" | custom-call | tf_op jit(solution)/shard_map/solve/pallas_call | solution.py:594
  (3 shorter events, 0.0 us)
Async XLA Ops:
  0.0 0.8 %copy-start = (f32[192,64]{0,1:T(8,128)S(1)}, f32[192,64]{0,1:T(8,128)}, u32[]{:S(2)}) copy-start(f32[192,64]{0,1:T(8,128)} %param.7) | copy-start | bytes 147460
  0.8 22.3 %copy-start.2 = (f32[8,64]{1,0:T(8,128)S(1)}, f32[8,64]{1,0:T(8,128)}, u32[]{:S(2)}) copy-start(f32[8,64]{1,0:T(8,128)} %refs_4_.1) | copy-start | bytes 6148
  0.8 22.3 %copy-start.3 = (s32[8,64]{1,0:T(8,128)S(1)}, s32[8,64]{1,0:T(8,128)}, u32[]{:S(2)}) copy-start(s32[8,64]{1,0:T(8,128)} %refs_5_.1) | copy-start | bytes 6148
  1.1 7.0 %collective-permute-start.2 = (s16[112,128]{1,0:T(8,128)(2,1)S(1)}, s16[112,128]{1,0:T(8,128)(2,1)S(1)}, u32[]{:S(2)}, u32[]{:S(2)}) collective-permute-start(s16[112,128]{1,0:T(8,128)(2,1)S(1)} %encode_elution.1.mine_ref), channel_id=1, source_target_pairs={{0,24},{2,26},{4,28},{6,30},{8,16},{10,18},{12,20},{14,22},{16,8},... | collective-permute-start | bytes 86024 | tf_op jit(solution)/shard_map/ppermute | solution.py:605
  6.2 4.8 %collective-permute-start.1 = (s16[112,128]{1,0:T(8,128)(2,1)S(1)}, s16[112,128]{1,0:T(8,128)(2,1)S(1)}, u32[]{:S(2)}, u32[]{:S(2)}) collective-permute-start(s16[112,128]{1,0:T(8,128)(2,1)S(1)} %encode_elution.1.mine_ref), channel_id=1, source_target_pairs={{0,16},{2,18},{4,20},{6,22},{8,24},{10,26},{12,28},{14,30},{16,0},... | collective-permute-start | bytes 86024 | tf_op jit(solution)/shard_map/ppermute | solution.py:605
  6.2 4.8 %collective-permute-start = (s16[112,128]{1,0:T(8,128)(2,1)S(1)}, s16[112,128]{1,0:T(8,128)(2,1)S(1)}, u32[]{:S(2)}, u32[]{:S(2)}) collective-permute-start(s16[112,128]{1,0:T(8,128)(2,1)S(1)} %encode_elution.1.mine_ref), channel_id=1, source_target_pairs={{0,8},{2,10},{4,12},{6,14},{8,0},{10,2},{12,4},{14,6},{16,24},{18,... | collective-permute-start | bytes 86024 | tf_op jit(solution)/shard_map/ppermute | solution.py:605
  7.7 18.6 %copy-start.1 = (bf16[8,384,2048]{2,1,0:T(8,128)(2,1)S(1)}, bf16[8,384,2048]{2,1,0:T(8,128)(2,1)}, u32[]{:S(2)}) copy-start(bf16[8,384,2048]{2,1,0:T(8,128)(2,1)} %refs_0_.1) | copy-start | bytes 37748740
  11.0 4.9 %collective-permute-start.3 = (s16[4,112,128]{2,1,0:T(8,128)(2,1)S(1)}, s16[4,112,128]{2,1,0:T(8,128)(2,1)S(1)}, u32[]{:S(2)}, u32[]{:S(2)}) collective-permute-start(s16[4,112,128]{2,1,0:T(8,128)(2,1)S(1)} %pad_add_fusion.1), channel_id=1, source_target_pairs={{0,4},{2,6},{4,0},{6,2},{8,12},{10,14},{12,8},{14,10},{16,20},{18,... | collective-permute-start | bytes 344072 | tf_op jit(solution)/shard_map/ppermute | solution.py:605
  12.5 0.9 %copy-start.4 = (f32[448,128]{1,0:T(8,128)S(1)}, f32[448,128]{1,0:T(8,128)}, u32[]{:S(2)}) copy-start(f32[448,128]{1,0:T(8,128)} %constant.2.clone.table_ref) | copy-start | bytes 688132
  15.9 1.6 %collective-permute-start.4 = (s16[8,112,128]{2,1,0:T(8,128)(2,1)S(1)}, s16[8,112,128]{2,1,0:T(8,128)(2,1)S(1)}, u32[]{:S(2)}, u32[]{:S(2)}) collective-permute-start(s16[8,112,128]{2,1,0:T(8,128)(2,1)S(1)} %pad_add_fusion.refs_0_), channel_id=1, source_target_pairs={{0,2},{2,0},{4,6},{6,4},{8,10},{10,8},{12,14},{14,12},{16,18},{18,... | collective-permute-start | bytes 688136 | tf_op jit(solution)/shard_map/ppermute | solution.py:605
  17.4 4.2 %collective-permute-start.5 = (s16[224,128]{1,0:T(8,128)(2,1)S(1)}, s16[224,128]{1,0:T(8,128)(2,1)S(1)}, u32[]{:S(2)}, u32[]{:S(2)}) collective-permute-start(s16[224,128]{1,0:T(8,128)(2,1)S(1)} %window_pair.1.refs_0_), channel_id=1, source_target_pairs={{0,1},{1,0},{2,3},{3,2},{4,5},{5,4},{6,7},{7,6},{8,9},{9,8},{10,11... | collective-permute-start | bytes 172040 | tf_op jit(solution)/shard_map/ppermute | solution.py:605
  21.6 4.7 %collective-permute-start.6 = (s16[336,128]{1,0:T(8,128)(2,1)S(1)}, s16[336,128]{1,0:T(8,128)(2,1)S(1)}, u32[]{:S(2)}, u32[]{:S(2)}) collective-permute-start(s16[336,128]{1,0:T(8,128)(2,1)S(1)} %get-tuple-element.25), channel_id=1, source_target_pairs={{0,1},{1,0},{2,3},{3,2},{4,5},{5,4},{6,7},{7,6},{8,9},{9,8},{10,11... | collective-permute-start | bytes 258056 | tf_op jit(solution)/shard_map/ppermute | solution.py:605
  29.6 1.6 %collective-permute-start.7 = (f32[544,128]{1,0:T(8,128)S(1)}, f32[544,128]{1,0:T(8,128)S(1)}, u32[]{:S(2)}, u32[]{:S(2)}) collective-permute-start(f32[544,128]{1,0:T(8,128)S(1)} %get-tuple-element.28), channel_id=1, source_target_pairs={{0,2},{2,0},{4,6},{6,4},{8,10},{10,8},{12,14},{14,12},{16,18},{18,... | collective-permute-start | bytes 835592 | tf_op jit(solution)/shard_map/ppermute | solution.py:605
  31.4 4.6 %collective-permute-start.8 = (s16[336,128]{1,0:T(8,128)(2,1)S(1)}, s16[336,128]{1,0:T(8,128)(2,1)S(1)}, u32[]{:S(2)}, u32[]{:S(2)}) collective-permute-start(s16[336,128]{1,0:T(8,128)(2,1)S(1)} %reduce_cores.1), channel_id=1, source_target_pairs={{0,4},{2,6},{4,0},{6,2},{8,12},{10,14},{12,8},{14,10},{16,20},{18,... | collective-permute-start | bytes 258056 | tf_op jit(solution)/shard_map/ppermute | solution.py:605
  36.3 6.0 %collective-permute-start.9 = (s16[144,128]{1,0:T(8,128)(2,1)S(1)}, s16[144,128]{1,0:T(8,128)(2,1)S(1)}, u32[]{:S(2)}, u32[]{:S(2)}) collective-permute-start(s16[144,128]{1,0:T(8,128)(2,1)S(1)} %get-tuple-element.30), channel_id=1, source_target_pairs={{0,24},{2,26},{4,28},{6,30},{8,16},{10,18},{12,20},{14,22},{16,8},... | collective-permute-start | bytes 110600 | tf_op jit(solution)/shard_map/ppermute | solution.py:605
  37.9 4.9 %collective-permute-start.10 = (s16[144,128]{1,0:T(8,128)(2,1)S(1)}, s16[144,128]{1,0:T(8,128)(2,1)S(1)}, u32[]{:S(2)}, u32[]{:S(2)}) collective-permute-start(s16[144,128]{1,0:T(8,128)(2,1)S(1)} %get-tuple-element.31), channel_id=1, source_target_pairs={{0,16},{2,18},{4,20},{6,22},{8,24},{10,26},{12,28},{14,30},{16,0},... | collective-permute-start | bytes 110600 | tf_op jit(solution)/shard_map/ppermute | solution.py:605
  38.5 4.6 %collective-permute-start.11 = (s16[144,128]{1,0:T(8,128)(2,1)S(1)}, s16[144,128]{1,0:T(8,128)(2,1)S(1)}, u32[]{:S(2)}, u32[]{:S(2)}) collective-permute-start(s16[144,128]{1,0:T(8,128)(2,1)S(1)} %get-tuple-element.32), channel_id=1, source_target_pairs={{0,8},{2,10},{4,12},{6,14},{8,0},{10,2},{12,4},{14,6},{16,24},{18,... | collective-permute-start | bytes 110600 | tf_op jit(solution)/shard_map/ppermute | solution.py:605

commit v9 on v8

--- a/solution.py
+++ b/solution.py
@@ -286,13 +286,14 @@
         for k in range(amps.shape[1]):
             left = REACH - 1 - jnp.broadcast_to(lags[at : at + height, k : k + 1], lane.shape)
             amp = jnp.broadcast_to(amps[at : at + height, k : k + 1], lane.shape)
-            source = lane + (left & (LANES - 1))
-            index = source & (LANES - 1)
-            far, same = left >= LANES, source < LANES
-            turned = [jnp.take_along_axis(v, index, axis=1, mode="promise_in_bounds") for v in vectors]
-            turned = [jnp.where(far, turned[v + 1], turned[v]) for v in range(out_count + 1)]
+            inside = left & (LANES - 1)
+            index = (lane + inside) & (LANES - 1)
+            far, same = left >= LANES, lane >= inside
+            near = [jnp.where(far, vectors[v + 1], vectors[v]) for v in range(out_count + 1)]
             for v in range(out_count):
-                high, low = two_terms(amp * jnp.where(same, turned[v], turned[v + 1]))
+                joined = jnp.where(same, near[v], near[v + 1])
+                turned = jnp.take_along_axis(joined, index, axis=1, mode="promise_in_bounds")
+                high, low = two_terms(amp * turned)
                 width = min(LANES, bin_count - v * LANES)
                 to = slice(k * bin_count + v * LANES, k * bin_count + v * LANES + width)
                 terms[at : at + height, to] = high[:, :width]
@@ -451,19 +452,22 @@
 
 
 def inverse2(a, b, d):
-    det = a * d - b * b
-    scale = pl.reciprocal(det, approx=True)
-    for _ in range(2):
-        scale = scale * (2.0 - det * scale)
+    scale = 1.0 / (a * d - b * b)
     return d * scale, -b * scale, a * scale
 
 
 def eliminate(gram, right):
     components = gram.shape[0]
-    row_id = lax.broadcasted_iota(jnp.int32, gram.shape, 0)
+    height = 8
+    shape = (height, gram.shape[1])
+    row_id = lax.broadcasted_iota(jnp.int32, shape, 0)
+    starts = range(0, components, height)
+    gram = [gram[at : at + height] for at in starts]
+    right = [right[at : at + height] for at in starts]
     for j in range(0, components, 4):
-        columns = [jnp.broadcast_to(gram[:, j + n : j + n + 1], gram.shape) for n in range(4)]
-        pivot = [[columns[n][j + m : j + m + 1] for n in range(4)] for m in range(4)]
+        here, r = j // height, j % height
+        columns = [[jnp.broadcast_to(tile[:, j + n : j + n + 1], shape) for tile in gram] for n in range(4)]
+        pivot = [[columns[n][here][r + m : r + m + 1] for n in range(4)] for m in range(4)]
         a00, a01, a11 = inverse2(pivot[0][0], pivot[0][1], pivot[1][1])
         b00, b01, b10, b11 = pivot[0][2], pivot[0][3], pivot[1][2], pivot[1][3]
         w00, w01 = a00 * b00 + a01 * b10, a00 * b01 + a01 * b11
@@ -473,24 +477,23 @@
             pivot[2][3] - (b00 * w01 + b10 * w11),
             pivot[3][3] - (b01 * w01 + b11 * w11),
         )
-        away = (row_id < j) | (row_id >= j + 4)
-        c0, c1, c2, c3 = (
-            jnp.where(away, column, jnp.where(row_id == j + n, -1.0, 0.0)) for n, column in enumerate(columns)
-        )
-        t2, t3 = c2 - c0 * w00 - c1 * w10, c3 - c0 * w01 - c1 * w11
-        f2, f3 = t2 * s00 + t3 * s01, t2 * s01 + t3 * s11
-        f0 = c0 * a00 + c1 * a01 - f2 * w00 - f3 * w01
-        f1 = c0 * a01 + c1 * a11 - f2 * w10 - f3 * w11
-        factors = (f0, f1, f2, f3)
-
-        def reduced(x):
-            out = jnp.where(away[:, : x.shape[1]], x, 0.0)
-            for n, factor in enumerate(factors):
-                out = out - factor[:, : x.shape[1]] * x[j + n : j + n + 1]
-            return out
-
-        gram, right = reduced(gram), reduced(right)
-    return right
+        away = (row_id < r) | (row_id >= r + 4)
+        for n in range(4):
+            columns[n][here] = jnp.where(away, columns[n][here], jnp.where(row_id == r + n, -1.0, 0.0))
+        gram_rows = [gram[here][r + n : r + n + 1] for n in range(4)]
+        right_rows = [right[here][r + n : r + n + 1] for n in range(4)]
+        gram[here] = jnp.where(away, gram[here], 0.0)
+        right[here] = jnp.where(away[:, : right[here].shape[1]], right[here], 0.0)
+        for t in range(len(gram)):
+            c0, c1, c2, c3 = (columns[n][t] for n in range(4))
+            t2, t3 = c2 - c0 * w00 - c1 * w10, c3 - c0 * w01 - c1 * w11
+            f2, f3 = t2 * s00 + t3 * s01, t2 * s01 + t3 * s11
+            f0 = c0 * a00 + c1 * a01 - f2 * w00 - f3 * w01
+            f1 = c0 * a01 + c1 * a11 - f2 * w10 - f3 * w11
+            for n, factor in enumerate((f0, f1, f2, f3)):
+                gram[t] = gram[t] - factor * gram_rows[n]
+                right[t] = right[t] - factor[:, : right[t].shape[1]] * right_rows[n]
+    return jnp.concatenate(right, axis=0)
 
 
 def total_of(refs, at, rows):

time: 47 us -> 46.3 us (0.985)
  Pallas kernels: 14.4 us -> 13.7 us
  transfers between devices with their start and end apart: 12 -> 12, of which waited for: 10 -> 11; matrix products, arithmetic and copies ran while one was open for 2% -> 2% of each run, Pallas kernels for 15% -> 14%
where the time goes in v9:
time: 46.3 us; the launch traced here: 46 us
  starting transfers between devices  16.5 us (36%)
  Pallas kernels  13.7 us (30%)
  waiting for transfers between devices  13.1 us (28%)
  local copies, waits for them, and re-layouts  2.6 us (6%)
    ppermute x12, starting transfers between devices, swap(): return lax.ppermute(x, axes, [(i, i ^ value) for i in range(count)])  16.5 us
    ppermute x12, waiting for transfers between devices, swap(): return lax.ppermute(x, axes, [(i, i ^ value) for i in range(count)])  13.1 us
    pallas_call x3, Pallas kernels, small_call(): pl.pallas_call(kernel, out_shape=tuple((jax.ShapeDtypeStruct(shape, dtype...  3.84 us
    pallas_call x1, Pallas kernels, product(): pl.pallas_call(functools.partial(product_kernel, len(models), planes), ou...  3.04 us
    pallas_call x1, Pallas kernels, elution_terms(): pl.pallas_call(functools.partial(elution_kernel, planes), out_shape=jax.S...  2.91 us
    pallas_call x1, Pallas kernels, partial_model(): pl.pallas_call(functools.partial(model_kernel, places, planes), out_shape...  2.18 us
    unnamed x10, local copies, waits for them, and re-layouts  1.79 us
    pallas_call x1, Pallas kernels, circulant(): pl.pallas_call(functools.partial(circulant_kernel, turn), out_shape=jax.S...  1.53 us
  transfers between devices with their start and end apart: 12, of which 11 were waited for; matrix products, arithmetic and copies ran while one was open for 2% of the time, Pallas kernels for 14%

profile of v9, /device:TPU:0, one launch (start us, length us, event | category | flops | bytes accessed | tf_op | source)
XLA Modules:
  0.0 46.0 jit_solution(4560953229618859374)
XLA Ops:
  0.0 0.0 copy-start
  0.0 0.8 %copy-done = f32[192,64]{0,1:T(8,128)S(1)} copy-done((f32[192,64]{0,1:T(8,128)S(1)}, f32[192,64]{0,1:T(8,128)}, u32[]{:S(2)}) %copy-start) | copy-done | bytes 49176
  0.8 0.0 copy-start.2
  0.8 0.0 copy-start.3
  0.8 0.2 encode_elution.1.mine_ref
  1.1 5.1 %collective-permute-start.2 = (s16[112,128]{1,0:T(8,128)(2,1)S(1)}, s16[112,128]{1,0:T(8,128)(2,1)S(1)}, u32[]{:S(2)}, u32[]{:S(2)}) collective-permute-start(s16[112,128]{1,0:T(8,128)(2,1)S(1)} %encode_elution.1.mine_ref), channel_id=1, source_target_pairs={{0,24},{2,26},{4,28},{6,30},{8,16},{10,18},{12,20},{14,22},{16,8},... | collective-permute-start | bytes 86024 | tf_op jit(solution)/shard_map/ppermute | solution.py:608
  6.2 0.0 collective-permute-start.1
  6.2 0.6 %collective-permute-start = (s16[112,128]{1,0:T(8,128)(2,1)S(1)}, s16[112,128]{1,0:T(8,128)(2,1)S(1)}, u32[]{:S(2)}, u32[]{:S(2)}) collective-permute-start(s16[112,128]{1,0:T(8,128)(2,1)S(1)} %encode_elution.1.mine_ref), channel_id=1, source_target_pairs={{0,8},{2,10},{4,12},{6,14},{8,0},{10,2},{12,4},{14,6},{16,24},{18,... | collective-permute-start | bytes 86024 | tf_op jit(solution)/shard_map/ppermute | solution.py:608
  6.8 0.8 %reshape.3.w_ref = f32[128,48]{1,0:T(8,128)S(1)} reshape(f32[6144]{0:T(1024)} %param.10) | data formatting | bytes 49152 | tf_op jit(solution)/shard_map/reshape | solution.py:640
  7.7 0.0 copy-start.1
  7.7 0.4 collective-permute-done.2
  8.0 2.9 %collective-permute-done.1 = s16[112,128]{1,0:T(8,128)(2,1)S(1)} collective-permute-done((s16[112,128]{1,0:T(8,128)(2,1)S(1)}, s16[112,128]{1,0:T(8,128)(2,1)S(1)}, u32[]{:S(2)}, u32[]{:S(2)}) %collective-permute-start.1) | collective-permute-done | bytes 28704 | tf_op jit(solution)/shard_map/ppermute | solution.py:608
  11.0 0.0 collective-permute-done
  11.0 1.6 %collective-permute-start.3 = (s16[4,112,128]{2,1,0:T(8,128)(2,1)S(1)}, s16[4,112,128]{2,1,0:T(8,128)(2,1)S(1)}, u32[]{:S(2)}, u32[]{:S(2)}) collective-permute-start(s16[4,112,128]{2,1,0:T(8,128)(2,1)S(1)} %pad_add_fusion.1), channel_id=1, source_target_pairs={{0,4},{2,6},{4,0},{6,2},{8,12},{10,14},{12,8},{14,10},{16,20},{18,... | collective-permute-start | bytes 344072 | tf_op jit(solution)/shard_map/ppermute | solution.py:608
  12.5 0.0 copy-start.4
  12.5 0.9 %copy-done.4 = f32[448,128]{1,0:T(8,128)S(1)} copy-done((f32[448,128]{1,0:T(8,128)S(1)}, f32[448,128]{1,0:T(8,128)}, u32[]{:S(2)}) %copy-start.4) | copy-done | bytes 229400
  13.5 1.5 %circulant_block.1.refs_2_ = bf16[256,6144]{1,0:T(8,128)(2,1)S(1)} custom-call(f32[128,48]{1,0:T(8,128)S(1)} %reshape.3.w_ref, f32[448,128]{1,0:T(8,128)S(1)} %copy-done.4), custom_call_target="tpu_custom_call" | custom-call | flops 2000000000 | bytes 4194304 | tf_op jit(solution)/shard_map/circulant_block/pallas_call | solution.py:167
  15.0 0.8 %collective-permute-done.3 = s16[4,112,128]{2,1,0:T(8,128)(2,1)S(1)} collective-permute-done((s16[4,112,128]{2,1,0:T(8,128)(2,1)S(1)}, s16[4,112,128]{2,1,0:T(8,128)(2,1)S(1)}, u32[]{:S(2)}, u32[]{:S(2)}) %collective-permute-start.3) | collective-permute-done | bytes 114720 | tf_op jit(solution)/shard_map/ppermute | solution.py:608
  15.9 0.1 collective-permute-start.4
  15.9 1.5 %collective-permute-done.4.refs_1_.came_ref = s16[8,112,128]{2,1,0:T(8,128)(2,1)S(1)} collective-permute-done((s16[8,112,128]{2,1,0:T(8,128)(2,1)S(1)}, s16[8,112,128]{2,1,0:T(8,128)(2,1)S(1)}, u32[]{:S(2)}, u32[]{:S(2)}) %collective-permute-start.4) | collective-permute-done | bytes 229408 | tf_op jit(solution)/shard_map/ppermute | solution.py:608
  17.4 1.5 %collective-permute-start.5 = (s16[224,128]{1,0:T(8,128)(2,1)S(1)}, s16[224,128]{1,0:T(8,128)(2,1)S(1)}, u32[]{:S(2)}, u32[]{:S(2)}) collective-permute-start(s16[224,128]{1,0:T(8,128)(2,1)S(1)} %window_pair.1.refs_0_), channel_id=1, source_target_pairs={{0,1},{1,0},{2,3},{3,2},{4,5},{5,4},{6,7},{7,6},{8,9},{9,8},{10,11... | collective-permute-start | bytes 172040 | tf_op jit(solution)/shard_map/ppermute | solution.py:608
  18.9 2.2 %partial_model.1 = (f32[64,640]{1,0:T(8,128)S(1)}, s16[336,128]{1,0:T(8,128)(2,1)S(1)}) custom-call(s16[8,112,128]{2,1,0:T(8,128)(2,1)S(1)} %pad_add_fusion.refs_0_, s16[8,112,128]{2,1,0:T(8,128)(2,1)S(1)} %collective-permute-done.4.refs_1_.came_ref, bf16[256,6144]{1,0:T(8,128)(2,1)S(1)} %circulant_block.1.refs_2_), custom_call_target="tpu_custom_call" | custom-call | flops 2000000000 | bytes 4194304 | tf_op jit(solution)/shard_map/partial_model/pallas_call | solution.py:266
  21.1 0.5 %collective-permute-done.5.refs_1_ = s16[224,128]{1,0:T(8,128)(2,1)S(1)} collective-permute-done((s16[224,128]{1,0:T(8,128)(2,1)S(1)}, s16[224,128]{1,0:T(8,128)(2,1)S(1)}, u32[]{:S(2)}, u32[]{:S(2)}) %collective-permute-start.5) | collective-permute-done | bytes 57376 | tf_op jit(solution)/shard_map/ppermute | solution.py:608
  21.6 1.5 %collective-permute-start.6 = (s16[336,128]{1,0:T(8,128)(2,1)S(1)}, s16[336,128]{1,0:T(8,128)(2,1)S(1)}, u32[]{:S(2)}, u32[]{:S(2)}) collective-permute-start(s16[336,128]{1,0:T(8,128)(2,1)S(1)} %get-tuple-element.25), channel_id=1, source_target_pairs={{0,1},{1,0},{2,3},{3,2},{4,5},{5,4},{6,7},{7,6},{8,9},{9,8},{10,11... | collective-permute-start | bytes 258056 | tf_op jit(solution)/shard_map/ppermute | solution.py:608
  23.1 0.0 copy-done.2
  23.1 0.0 copy-done.3
  23.1 2.9 %elution_terms.1.refs_3_ = bf16[128,3072]{1,0:T(8,128)(2,1)S(1)} custom-call(s16[224,128]{1,0:T(8,128)(2,1)S(1)} %window_pair.1.refs_0_, s16[224,128]{1,0:T(8,128)(2,1)S(1)} %collective-permute-done.5.refs_1_, f32[8,64]{1,0:T(8,128)S(1)} %copy-done.2, s32[8,64]{1,0:T(8,128)S(1)} %copy-done.3), custom_call_target="tpu_custom_call" | custom-call | flops 1000000000 | bytes 2097152 | tf_op jit(solution)/shard_map/elution_terms/pallas_call | solution.py:360
  26.0 0.1 collective-permute-done.6.refs_2_
  26.1 0.0 copy-done.1
  26.1 3.0 %model_products.1 = (f32[544,128]{1,0:T(8,128)S(1)}, f32[544,128]{1,0:T(8,128)S(1)}) custom-call(bf16[8,384,2048]{2,1,0:T(8,128)(2,1)S(1)} %copy-done.1, f32[64,640]{1,0:T(8,128)S(1)} %get-tuple-element.23.refs_1_, s16[336,128]{1,0:T(8,128)(2,1)S(1)} %collective-permute-done.6.refs_2_, bf16[128,3072]{1,0:T(8,128)(2,1)S(1)} %elution_terms.1.refs_3_, ...), custom_call_target="tpu_custom_call" | custom-call | flops 8000000000 | bytes 12582912 | tf_op jit(solution)/shard_map/model_products/pallas_call | solution.py:440
  29.1 0.1 collective-permute-start.7
  29.2 1.5 %collective-permute-done.7.b_ref = f32[544,128]{1,0:T(8,128)S(1)} collective-permute-done((f32[544,128]{1,0:T(8,128)S(1)}, f32[544,128]{1,0:T(8,128)S(1)}, u32[]{:S(2)}, u32[]{:S(2)}) %collective-permute-start.7) | collective-permute-done | bytes 278560 | tf_op jit(solution)/shard_map/ppermute | solution.py:608
  30.7 0.2 reduce_cores.1
  31.0 1.6 %collective-permute-start.8 = (s16[336,128]{1,0:T(8,128)(2,1)S(1)}, s16[336,128]{1,0:T(8,128)(2,1)S(1)}, u32[]{:S(2)}, u32[]{:S(2)}) collective-permute-start(s16[336,128]{1,0:T(8,128)(2,1)S(1)} %reduce_cores.1), channel_id=1, source_target_pairs={{0,4},{2,6},{4,0},{6,2},{8,12},{10,14},{12,8},{14,10},{16,20},{18,... | collective-permute-start | bytes 258056 | tf_op jit(solution)/shard_map/ppermute | solution.py:608
  32.5 3.1 %collective-permute-done.8.c_ref = s16[336,128]{1,0:T(8,128)(2,1)S(1)} collective-permute-done((s16[336,128]{1,0:T(8,128)(2,1)S(1)}, s16[336,128]{1,0:T(8,128)(2,1)S(1)}, u32[]{:S(2)}, u32[]{:S(2)}) %collective-permute-start.8) | collective-permute-done | bytes 86048 | tf_op jit(solution)/shard_map/ppermute | solution.py:608
  35.6 0.3 reduce_x.1
  35.9 1.5 %collective-permute-start.9 = (s16[144,128]{1,0:T(8,128)(2,1)S(1)}, s16[144,128]{1,0:T(8,128)(2,1)S(1)}, u32[]{:S(2)}, u32[]{:S(2)}) collective-permute-start(s16[144,128]{1,0:T(8,128)(2,1)S(1)} %get-tuple-element.30), channel_id=1, source_target_pairs={{0,24},{2,26},{4,28},{6,30},{8,16},{10,18},{12,20},{14,22},{16,8},... | collective-permute-start | bytes 110600 | tf_op jit(solution)/shard_map/ppermute | solution.py:608
  37.4 0.6 %collective-permute-start.10 = (s16[144,128]{1,0:T(8,128)(2,1)S(1)}, s16[144,128]{1,0:T(8,128)(2,1)S(1)}, u32[]{:S(2)}, u32[]{:S(2)}) collective-permute-start(s16[144,128]{1,0:T(8,128)(2,1)S(1)} %get-tuple-element.31), channel_id=1, source_target_pairs={{0,16},{2,18},{4,20},{6,22},{8,24},{10,26},{12,28},{14,30},{16,0},... | collective-permute-start | bytes 110600 | tf_op jit(solution)/shard_map/ppermute | solution.py:608
  38.1 2.3 %collective-permute-start.11 = (s16[144,128]{1,0:T(8,128)(2,1)S(1)}, s16[144,128]{1,0:T(8,128)(2,1)S(1)}, u32[]{:S(2)}, u32[]{:S(2)}) collective-permute-start(s16[144,128]{1,0:T(8,128)(2,1)S(1)} %get-tuple-element.32), channel_id=1, source_target_pairs={{0,8},{2,10},{4,12},{6,14},{8,0},{10,2},{12,4},{14,6},{16,24},{18,... | collective-permute-start | bytes 110600 | tf_op jit(solution)/shard_map/ppermute | solution.py:608
  40.3 1.6 %collective-permute-done.9.refs_0_ = s16[144,128]{1,0:T(8,128)(2,1)S(1)} collective-permute-done((s16[144,128]{1,0:T(8,128)(2,1)S(1)}, s16[144,128]{1,0:T(8,128)(2,1)S(1)}, u32[]{:S(2)}, u32[]{:S(2)}) %collective-permute-start.9) | collective-permute-done | bytes 36896 | tf_op jit(solution)/shard_map/ppermute | solution.py:608
  41.9 0.4 collective-permute-done.10.refs_1_
  42.4 0.4 collective-permute-done.11.refs_2_
  42.7 3.3 %solve.1 = f32[64,128]{1,0:T(8,128)} custom-call(f32[96,128]{1,0:T(8,128)S(1)} %get-tuple-element.29.own_ref, s16[144,128]{1,0:T(8,128)(2,1)S(1)} %collective-permute-done.9.refs_0_, s16[144,128]{1,0:T(8,128)(2,1)S(1)} %collective-permute-done.10.refs_1_, s16[144,128]{1,0:T(8,128)(2,1)S(1)} %collective-permute-done.11.refs_2_), custom_call_target="tpu_custom_call" | custom-call | tf_op jit(solution)/shard_map/solve/pallas_call | solution.py:597
  (3 shorter events, 0.0 us)
Async XLA Ops:
  0.0 0.8 %copy-start = (f32[192,64]{0,1:T(8,128)S(1)}, f32[192,64]{0,1:T(8,128)}, u32[]{:S(2)}) copy-start(f32[192,64]{0,1:T(8,128)} %param.7) | copy-start | bytes 147460
  0.8 22.3 %copy-start.2 = (f32[8,64]{1,0:T(8,128)S(1)}, f32[8,64]{1,0:T(8,128)}, u32[]{:S(2)}) copy-start(f32[8,64]{1,0:T(8,128)} %refs_4_.1) | copy-start | bytes 6148
  0.8 22.3 %copy-start.3 = (s32[8,64]{1,0:T(8,128)S(1)}, s32[8,64]{1,0:T(8,128)}, u32[]{:S(2)}) copy-start(s32[8,64]{1,0:T(8,128)} %refs_5_.1) | copy-start | bytes 6148
  1.1 7.0 %collective-permute-start.2 = (s16[112,128]{1,0:T(8,128)(2,1)S(1)}, s16[112,128]{1,0:T(8,128)(2,1)S(1)}, u32[]{:S(2)}, u32[]{:S(2)}) collective-permute-start(s16[112,128]{1,0:T(8,128)(2,1)S(1)} %encode_elution.1.mine_ref), channel_id=1, source_target_pairs={{0,24},{2,26},{4,28},{6,30},{8,16},{10,18},{12,20},{14,22},{16,8},... | collective-permute-start | bytes 86024 | tf_op jit(solution)/shard_map/ppermute | solution.py:608
  6.2 4.8 %collective-permute-start.1 = (s16[112,128]{1,0:T(8,128)(2,1)S(1)}, s16[112,128]{1,0:T(8,128)(2,1)S(1)}, u32[]{:S(2)}, u32[]{:S(2)}) collective-permute-start(s16[112,128]{1,0:T(8,128)(2,1)S(1)} %encode_elution.1.mine_ref), channel_id=1, source_target_pairs={{0,16},{2,18},{4,20},{6,22},{8,24},{10,26},{12,28},{14,30},{16,0},... | collective-permute-start | bytes 86024 | tf_op jit(solution)/shard_map/ppermute | solution.py:608
  6.2 4.8 %collective-permute-start = (s16[112,128]{1,0:T(8,128)(2,1)S(1)}, s16[112,128]{1,0:T(8,128)(2,1)S(1)}, u32[]{:S(2)}, u32[]{:S(2)}) collective-permute-start(s16[112,128]{1,0:T(8,128)(2,1)S(1)} %encode_elution.1.mine_ref), channel_id=1, source_target_pairs={{0,8},{2,10},{4,12},{6,14},{8,0},{10,2},{12,4},{14,6},{16,24},{18,... | collective-permute-start | bytes 86024 | tf_op jit(solution)/shard_map/ppermute | solution.py:608
  7.7 18.4 %copy-start.1 = (bf16[8,384,2048]{2,1,0:T(8,128)(2,1)S(1)}, bf16[8,384,2048]{2,1,0:T(8,128)(2,1)}, u32[]{:S(2)}) copy-start(bf16[8,384,2048]{2,1,0:T(8,128)(2,1)} %refs_0_.1) | copy-start | bytes 37748740
  11.0 4.9 %collective-permute-start.3 = (s16[4,112,128]{2,1,0:T(8,128)(2,1)S(1)}, s16[4,112,128]{2,1,0:T(8,128)(2,1)S(1)}, u32[]{:S(2)}, u32[]{:S(2)}) collective-permute-start(s16[4,112,128]{2,1,0:T(8,128)(2,1)S(1)} %pad_add_fusion.1), channel_id=1, source_target_pairs={{0,4},{2,6},{4,0},{6,2},{8,12},{10,14},{12,8},{14,10},{16,20},{18,... | collective-permute-start | bytes 344072 | tf_op jit(solution)/shard_map/ppermute | solution.py:608
  12.5 0.9 %copy-start.4 = (f32[448,128]{1,0:T(8,128)S(1)}, f32[448,128]{1,0:T(8,128)}, u32[]{:S(2)}) copy-start(f32[448,128]{1,0:T(8,128)} %constant.2.clone.table_ref) | copy-start | bytes 688132
  15.9 1.6 %collective-permute-start.4 = (s16[8,112,128]{2,1,0:T(8,128)(2,1)S(1)}, s16[8,112,128]{2,1,0:T(8,128)(2,1)S(1)}, u32[]{:S(2)}, u32[]{:S(2)}) collective-permute-start(s16[8,112,128]{2,1,0:T(8,128)(2,1)S(1)} %pad_add_fusion.refs_0_), channel_id=1, source_target_pairs={{0,2},{2,0},{4,6},{6,4},{8,10},{10,8},{12,14},{14,12},{16,18},{18,... | collective-permute-start | bytes 688136 | tf_op jit(solution)/shard_map/ppermute | solution.py:608
  17.4 4.2 %collective-permute-start.5 = (s16[224,128]{1,0:T(8,128)(2,1)S(1)}, s16[224,128]{1,0:T(8,128)(2,1)S(1)}, u32[]{:S(2)}, u32[]{:S(2)}) collective-permute-start(s16[224,128]{1,0:T(8,128)(2,1)S(1)} %window_pair.1.refs_0_), channel_id=1, source_target_pairs={{0,1},{1,0},{2,3},{3,2},{4,5},{5,4},{6,7},{7,6},{8,9},{9,8},{10,11... | collective-permute-start | bytes 172040 | tf_op jit(solution)/shard_map/ppermute | solution.py:608
  21.6 4.5 %collective-permute-start.6 = (s16[336,128]{1,0:T(8,128)(2,1)S(1)}, s16[336,128]{1,0:T(8,128)(2,1)S(1)}, u32[]{:S(2)}, u32[]{:S(2)}) collective-permute-start(s16[336,128]{1,0:T(8,128)(2,1)S(1)} %get-tuple-element.25), channel_id=1, source_target_pairs={{0,1},{1,0},{2,3},{3,2},{4,5},{5,4},{6,7},{7,6},{8,9},{9,8},{10,11... | collective-permute-start | bytes 258056 | tf_op jit(solution)/shard_map/ppermute | solution.py:608
  29.1 1.6 %collective-permute-start.7 = (f32[544,128]{1,0:T(8,128)S(1)}, f32[544,128]{1,0:T(8,128)S(1)}, u32[]{:S(2)}, u32[]{:S(2)}) collective-permute-start(f32[544,128]{1,0:T(8,128)S(1)} %get-tuple-element.28), channel_id=1, source_target_pairs={{0,2},{2,0},{4,6},{6,4},{8,10},{10,8},{12,14},{14,12},{16,18},{18,... | collective-permute-start | bytes 835592 | tf_op jit(solution)/shard_map/ppermute | solution.py:608
  31.0 4.6 %collective-permute-start.8 = (s16[336,128]{1,0:T(8,128)(2,1)S(1)}, s16[336,128]{1,0:T(8,128)(2,1)S(1)}, u32[]{:S(2)}, u32[]{:S(2)}) collective-permute-start(s16[336,128]{1,0:T(8,128)(2,1)S(1)} %reduce_cores.1), channel_id=1, source_target_pairs={{0,4},{2,6},{4,0},{6,2},{8,12},{10,14},{12,8},{14,10},{16,20},{18,... | collective-permute-start | bytes 258056 | tf_op jit(solution)/shard_map/ppermute | solution.py:608
  35.9 6.0 %collective-permute-start.9 = (s16[144,128]{1,0:T(8,128)(2,1)S(1)}, s16[144,128]{1,0:T(8,128)(2,1)S(1)}, u32[]{:S(2)}, u32[]{:S(2)}) collective-permute-start(s16[144,128]{1,0:T(8,128)(2,1)S(1)} %get-tuple-element.30), channel_id=1, source_target_pairs={{0,24},{2,26},{4,28},{6,30},{8,16},{10,18},{12,20},{14,22},{16,8},... | collective-permute-start | bytes 110600 | tf_op jit(solution)/shard_map/ppermute | solution.py:608
  37.4 4.9 %collective-permute-start.10 = (s16[144,128]{1,0:T(8,128)(2,1)S(1)}, s16[144,128]{1,0:T(8,128)(2,1)S(1)}, u32[]{:S(2)}, u32[]{:S(2)}) collective-permute-start(s16[144,128]{1,0:T(8,128)(2,1)S(1)} %get-tuple-element.31), channel_id=1, source_target_pairs={{0,16},{2,18},{4,20},{6,22},{8,24},{10,26},{12,28},{14,30},{16,0},... | collective-permute-start | bytes 110600 | tf_op jit(solution)/shard_map/ppermute | solution.py:608
  38.1 4.6 %collective-permute-start.11 = (s16[144,128]{1,0:T(8,128)(2,1)S(1)}, s16[144,128]{1,0:T(8,128)(2,1)S(1)}, u32[]{:S(2)}, u32[]{:S(2)}) collective-permute-start(s16[144,128]{1,0:T(8,128)(2,1)S(1)} %get-tuple-element.32), channel_id=1, source_target_pairs={{0,8},{2,10},{4,12},{6,14},{8,0},{10,2},{12,4},{14,6},{16,24},{18,... | collective-permute-start | bytes 110600 | tf_op jit(solution)/shard_map/ppermute | solution.py:608

commit v10 on v9

--- a/solution.py
+++ b/solution.py
@@ -276,28 +276,35 @@
 
 
 def shifted_terms(x, amps, lags, bin_count, terms):
+    for piece in shift_pieces(x, amps, lags, bin_count, terms, range(amps.shape[1])):
+        piece()
+
+
+def shift_pieces(x, amps, lags, bin_count, terms, runs):
     components = x.shape[0]
     out_count = -(-bin_count // LANES)
     x = pltpu.roll(x, x.shape[1] - 1, 1)
     height = 16
     lane = lax.broadcasted_iota(jnp.int32, (height, LANES), 1)
-    for at in range(0, components, height):
+
+    def piece(at, k):
         vectors = [x[at : at + height, v * LANES : (v + 1) * LANES] for v in range(out_count + 2)]
-        for k in range(amps.shape[1]):
-            left = REACH - 1 - jnp.broadcast_to(lags[at : at + height, k : k + 1], lane.shape)
-            amp = jnp.broadcast_to(amps[at : at + height, k : k + 1], lane.shape)
-            inside = left & (LANES - 1)
-            index = (lane + inside) & (LANES - 1)
-            far, same = left >= LANES, lane >= inside
-            near = [jnp.where(far, vectors[v + 1], vectors[v]) for v in range(out_count + 1)]
-            for v in range(out_count):
-                joined = jnp.where(same, near[v], near[v + 1])
-                turned = jnp.take_along_axis(joined, index, axis=1, mode="promise_in_bounds")
-                high, low = two_terms(amp * turned)
-                width = min(LANES, bin_count - v * LANES)
-                to = slice(k * bin_count + v * LANES, k * bin_count + v * LANES + width)
-                terms[at : at + height, to] = high[:, :width]
-                terms[components + at : components + at + height, to] = low[:, :width]
+        left = REACH - 1 - jnp.broadcast_to(lags[at : at + height, k : k + 1], lane.shape)
+        amp = jnp.broadcast_to(amps[at : at + height, k : k + 1], lane.shape)
+        inside = left & (LANES - 1)
+        index = (lane + inside) & (LANES - 1)
+        far, same = left >= LANES, lane >= inside
+        near = [jnp.where(far, vectors[v + 1], vectors[v]) for v in range(out_count + 1)]
+        for v in range(out_count):
+            joined = jnp.where(same, near[v], near[v + 1])
+            turned = jnp.take_along_axis(joined, index, axis=1, mode="promise_in_bounds")
+            high, low = two_terms(amp * turned)
+            width = min(LANES, bin_count - v * LANES)
+            to = slice(k * bin_count + v * LANES, k * bin_count + v * LANES + width)
+            terms[at : at + height, to] = high[:, :width]
+            terms[components + at : components + at + height, to] = low[:, :width]
+
+    return [functools.partial(piece, at, k) for k in runs for at in range(0, components, height)]
 
 
 def pair_kernel(mine_ref, came_ref, o_ref):
@@ -376,7 +383,7 @@
 def product_kernel(parts, planes, *refs):
     i_ref = refs[0]
     g_refs = refs[1 : 1 + parts]
-    elution_ref, amp_ref, lag_ref, num_ref, other_ref, terms = refs[1 + parts :]
+    elution_ref, amp_ref, lag_ref, num_ref, other_ref, terms, partial = refs[1 + parts :]
     run_count, bin_count, local_mz = i_ref.shape
     components = amp_ref.shape[1]
     chunk = 2 * LANES
@@ -397,7 +404,24 @@
                 at += LANES // 2
             first.append(tile[:components])
         g = g + jnp.concatenate(first + second, axis=1)
-    shifted_terms(g, amp_ref[...].T, lag_ref[...].T, bin_count, terms)
+    amps, lags = amp_ref[...].T, lag_ref[...].T
+    middle = run_count // 2
+    for piece in shift_pieces(g, amps, lags, bin_count, terms, range(middle)):
+        piece()
+    waiting = shift_pieces(g, amps, lags, bin_count, terms, range(middle, run_count))
+
+    def multiply(n, first, last):
+        data = i_ref[first:last, :, n * chunk : (n + 1) * chunk].reshape((last - first) * bin_count, chunk)
+        made = jnp.dot(
+            terms[:, first * bin_count : last * bin_count], data, preferred_element_type=jnp.float32
+        )
+        return made[:components] + made[components:]
+
+    share = -(-len(waiting) // chunks)
+    for n in range(chunks):
+        partial[n] = multiply(n, 0, middle)
+        for piece in waiting[n * share : (n + 1) * share]:
+            piece()
     gram = lax.dot_general(
         terms[...], elution_ref[...], (((1,), (1,)), ((), ())), preferred_element_type=jnp.float32
     )
@@ -413,9 +437,7 @@
         other_ref[...] = gram
 
     for n in range(chunks):
-        data = i_ref[:, :, n * chunk : (n + 1) * chunk].reshape(run_count * bin_count, chunk)
-        made = jnp.dot(terms[...], data, preferred_element_type=jnp.float32)
-        made = made[:components] + made[components:]
+        made = partial[n] + multiply(n, middle, run_count)
         if planes:
             freq_rank = lax.axis_index("freq")
             core = freq_rank & 1
@@ -442,7 +464,10 @@
         out_shape=tuple(jax.ShapeDtypeStruct(shape, jnp.float32) for shape in out_shapes),
         in_specs=vmem(len(models) + 4),
         out_specs=tuple(vmem(2)),
-        scratch_shapes=[pltpu.VMEM((2 * components, run_count * bin_count), jnp.bfloat16)],
+        scratch_shapes=[
+            pltpu.VMEM((2 * components, run_count * bin_count), jnp.bfloat16),
+            pltpu.VMEM((chunks, components, chunk), jnp.float32),
+        ],
         compiler_params=pltpu.CompilerParams(vmem_limit_bytes=24 * MIB),
         cost_estimate=pl.CostEstimate(
             flops=8_000_000_000, bytes_accessed=2 * intensity.size, transcendentals=0

time: 46.3 us -> 46 us (level)
  transfers between devices with their start and end apart: 12 -> 12, of which waited for: 11 -> 10; matrix products, arithmetic and copies ran while one was open for 2% -> 2% of each run, Pallas kernels for 14% -> 14%
where the time goes in v10:
time: 46 us; the launch traced here: 45.8 us
  starting transfers between devices  16.5 us (36%)
  Pallas kernels  13.4 us (29%)
  waiting for transfers between devices  13.1 us (28%)
  local copies, waits for them, and re-layouts  2.6 us (6%)
    ppermute x12, starting transfers between devices, swap(): return lax.ppermute(x, axes, [(i, i ^ value) for i in range(count)])  16.5 us
    ppermute x12, waiting for transfers between devices, swap(): return lax.ppermute(x, axes, [(i, i ^ value) for i in range(count)])  13.1 us
    pallas_call x3, Pallas kernels, small_call(): pl.pallas_call(kernel, out_shape=tuple((jax.ShapeDtypeStruct(shape, dtype...  3.84 us
    pallas_call x1, Pallas kernels, elution_terms(): pl.pallas_call(functools.partial(elution_kernel, planes), out_shape=jax.S...  2.92 us
    pallas_call x1, Pallas kernels, product(): pl.pallas_call(functools.partial(product_kernel, len(models), planes), ou...  2.75 us
    pallas_call x1, Pallas kernels, partial_model(): pl.pallas_call(functools.partial(model_kernel, places, planes), out_shape...  2.18 us
    unnamed x10, local copies, waits for them, and re-layouts  1.79 us
    pallas_call x1, Pallas kernels, circulant(): pl.pallas_call(functools.partial(circulant_kernel, turn), out_shape=jax.S...  1.53 us
  transfers between devices with their start and end apart: 12, of which 10 were waited for; matrix products, arithmetic and copies ran while one was open for 2% of the time, Pallas kernels for 14%

profile of v10, /device:TPU:0, one launch (start us, length us, event | category | flops | bytes accessed | tf_op | source)
XLA Modules:
  0.0 45.8 jit_solution(8594365706307655763)
XLA Ops:
  0.0 0.0 copy-start
  0.0 0.8 %copy-done = f32[192,64]{0,1:T(8,128)S(1)} copy-done((f32[192,64]{0,1:T(8,128)S(1)}, f32[192,64]{0,1:T(8,128)}, u32[]{:S(2)}) %copy-start) | copy-done | bytes 49176
  0.8 0.0 copy-start.2
  0.8 0.0 copy-start.3
  0.8 0.2 encode_elution.1.mine_ref
  1.1 5.1 %collective-permute-start.2 = (s16[112,128]{1,0:T(8,128)(2,1)S(1)}, s16[112,128]{1,0:T(8,128)(2,1)S(1)}, u32[]{:S(2)}, u32[]{:S(2)}) collective-permute-start(s16[112,128]{1,0:T(8,128)(2,1)S(1)} %encode_elution.1.mine_ref), channel_id=1, source_target_pairs={{0,24},{2,26},{4,28},{6,30},{8,16},{10,18},{12,20},{14,22},{16,8},... | collective-permute-start | bytes 86024 | tf_op jit(solution)/shard_map/ppermute | solution.py:633
  6.2 0.0 collective-permute-start.1
  6.2 0.6 %collective-permute-start = (s16[112,128]{1,0:T(8,128)(2,1)S(1)}, s16[112,128]{1,0:T(8,128)(2,1)S(1)}, u32[]{:S(2)}, u32[]{:S(2)}) collective-permute-start(s16[112,128]{1,0:T(8,128)(2,1)S(1)} %encode_elution.1.mine_ref), channel_id=1, source_target_pairs={{0,8},{2,10},{4,12},{6,14},{8,0},{10,2},{12,4},{14,6},{16,24},{18,... | collective-permute-start | bytes 86024 | tf_op jit(solution)/shard_map/ppermute | solution.py:633
  6.8 0.8 %reshape.3.w_ref = f32[128,48]{1,0:T(8,128)S(1)} reshape(f32[6144]{0:T(1024)} %param.10) | data formatting | bytes 49152 | tf_op jit(solution)/shard_map/reshape | solution.py:665
  7.7 0.0 copy-start.1
  7.7 0.4 collective-permute-done.2
  8.0 2.9 %collective-permute-done.1 = s16[112,128]{1,0:T(8,128)(2,1)S(1)} collective-permute-done((s16[112,128]{1,0:T(8,128)(2,1)S(1)}, s16[112,128]{1,0:T(8,128)(2,1)S(1)}, u32[]{:S(2)}, u32[]{:S(2)}) %collective-permute-start.1) | collective-permute-done | bytes 28704 | tf_op jit(solution)/shard_map/ppermute | solution.py:633
  11.0 0.0 collective-permute-done
  11.0 1.6 %collective-permute-start.3 = (s16[4,112,128]{2,1,0:T(8,128)(2,1)S(1)}, s16[4,112,128]{2,1,0:T(8,128)(2,1)S(1)}, u32[]{:S(2)}, u32[]{:S(2)}) collective-permute-start(s16[4,112,128]{2,1,0:T(8,128)(2,1)S(1)} %pad_add_fusion.1), channel_id=1, source_target_pairs={{0,4},{2,6},{4,0},{6,2},{8,12},{10,14},{12,8},{14,10},{16,20},{18,... | collective-permute-start | bytes 344072 | tf_op jit(solution)/shard_map/ppermute | solution.py:633
  12.5 0.0 copy-start.4
  12.5 0.9 %copy-done.4 = f32[448,128]{1,0:T(8,128)S(1)} copy-done((f32[448,128]{1,0:T(8,128)S(1)}, f32[448,128]{1,0:T(8,128)}, u32[]{:S(2)}) %copy-start.4) | copy-done | bytes 229400
  13.5 1.5 %circulant_block.1.refs_2_ = bf16[256,6144]{1,0:T(8,128)(2,1)S(1)} custom-call(f32[128,48]{1,0:T(8,128)S(1)} %reshape.3.w_ref, f32[448,128]{1,0:T(8,128)S(1)} %copy-done.4), custom_call_target="tpu_custom_call" | custom-call | flops 2000000000 | bytes 4194304 | tf_op jit(solution)/shard_map/circulant_block/pallas_call | solution.py:167
  15.0 0.8 %collective-permute-done.3 = s16[4,112,128]{2,1,0:T(8,128)(2,1)S(1)} collective-permute-done((s16[4,112,128]{2,1,0:T(8,128)(2,1)S(1)}, s16[4,112,128]{2,1,0:T(8,128)(2,1)S(1)}, u32[]{:S(2)}, u32[]{:S(2)}) %collective-permute-start.3) | collective-permute-done | bytes 114720 | tf_op jit(solution)/shard_map/ppermute | solution.py:633
  15.9 0.1 collective-permute-start.4
  15.9 1.5 %collective-permute-done.4.refs_1_.came_ref = s16[8,112,128]{2,1,0:T(8,128)(2,1)S(1)} collective-permute-done((s16[8,112,128]{2,1,0:T(8,128)(2,1)S(1)}, s16[8,112,128]{2,1,0:T(8,128)(2,1)S(1)}, u32[]{:S(2)}, u32[]{:S(2)}) %collective-permute-start.4) | collective-permute-done | bytes 229408 | tf_op jit(solution)/shard_map/ppermute | solution.py:633
  17.4 1.5 %collective-permute-start.5 = (s16[224,128]{1,0:T(8,128)(2,1)S(1)}, s16[224,128]{1,0:T(8,128)(2,1)S(1)}, u32[]{:S(2)}, u32[]{:S(2)}) collective-permute-start(s16[224,128]{1,0:T(8,128)(2,1)S(1)} %window_pair.1.refs_0_), channel_id=1, source_target_pairs={{0,1},{1,0},{2,3},{3,2},{4,5},{5,4},{6,7},{7,6},{8,9},{9,8},{10,11... | collective-permute-start | bytes 172040 | tf_op jit(solution)/shard_map/ppermute | solution.py:633
  18.9 2.2 %partial_model.1 = (f32[64,640]{1,0:T(8,128)S(1)}, s16[336,128]{1,0:T(8,128)(2,1)S(1)}) custom-call(s16[8,112,128]{2,1,0:T(8,128)(2,1)S(1)} %pad_add_fusion.refs_0_, s16[8,112,128]{2,1,0:T(8,128)(2,1)S(1)} %collective-permute-done.4.refs_1_.came_ref, bf16[256,6144]{1,0:T(8,128)(2,1)S(1)} %circulant_block.1.refs_2_), custom_call_target="tpu_custom_call" | custom-call | flops 2000000000 | bytes 4194304 | tf_op jit(solution)/shard_map/partial_model/pallas_call | solution.py:266
  21.1 0.5 %collective-permute-done.5.refs_1_ = s16[224,128]{1,0:T(8,128)(2,1)S(1)} collective-permute-done((s16[224,128]{1,0:T(8,128)(2,1)S(1)}, s16[224,128]{1,0:T(8,128)(2,1)S(1)}, u32[]{:S(2)}, u32[]{:S(2)}) %collective-permute-start.5) | collective-permute-done | bytes 57376 | tf_op jit(solution)/shard_map/ppermute | solution.py:633
  21.6 1.5 %collective-permute-start.6 = (s16[336,128]{1,0:T(8,128)(2,1)S(1)}, s16[336,128]{1,0:T(8,128)(2,1)S(1)}, u32[]{:S(2)}, u32[]{:S(2)}) collective-permute-start(s16[336,128]{1,0:T(8,128)(2,1)S(1)} %get-tuple-element.25), channel_id=1, source_target_pairs={{0,1},{1,0},{2,3},{3,2},{4,5},{5,4},{6,7},{7,6},{8,9},{9,8},{10,11... | collective-permute-start | bytes 258056 | tf_op jit(solution)/shard_map/ppermute | solution.py:633
  23.1 0.0 copy-done.2
  23.1 0.0 copy-done.3
  23.1 2.9 %elution_terms.1.refs_3_ = bf16[128,3072]{1,0:T(8,128)(2,1)S(1)} custom-call(s16[224,128]{1,0:T(8,128)(2,1)S(1)} %window_pair.1.refs_0_, s16[224,128]{1,0:T(8,128)(2,1)S(1)} %collective-permute-done.5.refs_1_, f32[8,64]{1,0:T(8,128)S(1)} %copy-done.2, s32[8,64]{1,0:T(8,128)S(1)} %copy-done.3), custom_call_target="tpu_custom_call" | custom-call | flops 1000000000 | bytes 2097152 | tf_op jit(solution)/shard_map/elution_terms/pallas_call | solution.py:367
  26.0 0.0 collective-permute-done.6.refs_2_
  26.1 0.0 copy-done.1
  26.1 2.8 %model_products.1 = (f32[544,128]{1,0:T(8,128)S(1)}, f32[544,128]{1,0:T(8,128)S(1)}) custom-call(bf16[8,384,2048]{2,1,0:T(8,128)(2,1)S(1)} %copy-done.1, f32[64,640]{1,0:T(8,128)S(1)} %get-tuple-element.23.refs_1_, s16[336,128]{1,0:T(8,128)(2,1)S(1)} %collective-permute-done.6.refs_2_, bf16[128,3072]{1,0:T(8,128)(2,1)S(1)} %elution_terms.1.refs_3_, ...), custom_call_target="tpu_custom_call" | custom-call | flops 8000000000 | bytes 12582912 | tf_op jit(solution)/shard_map/model_products/pallas_call | solution.py:462
  28.8 0.1 collective-permute-start.7
  28.9 1.5 %collective-permute-done.7.b_ref = f32[544,128]{1,0:T(8,128)S(1)} collective-permute-done((f32[544,128]{1,0:T(8,128)S(1)}, f32[544,128]{1,0:T(8,128)S(1)}, u32[]{:S(2)}, u32[]{:S(2)}) %collective-permute-start.7) | collective-permute-done | bytes 278560 | tf_op jit(solution)/shard_map/ppermute | solution.py:633
  30.5 0.2 reduce_cores.1
  30.7 1.6 %collective-permute-start.8 = (s16[336,128]{1,0:T(8,128)(2,1)S(1)}, s16[336,128]{1,0:T(8,128)(2,1)S(1)}, u32[]{:S(2)}, u32[]{:S(2)}) collective-permute-start(s16[336,128]{1,0:T(8,128)(2,1)S(1)} %reduce_cores.1), channel_id=1, source_target_pairs={{0,4},{2,6},{4,0},{6,2},{8,12},{10,14},{12,8},{14,10},{16,20},{18,... | collective-permute-start | bytes 258056 | tf_op jit(solution)/shard_map/ppermute | solution.py:633
  32.2 3.1 %collective-permute-done.8.c_ref = s16[336,128]{1,0:T(8,128)(2,1)S(1)} collective-permute-done((s16[336,128]{1,0:T(8,128)(2,1)S(1)}, s16[336,128]{1,0:T(8,128)(2,1)S(1)}, u32[]{:S(2)}, u32[]{:S(2)}) %collective-permute-start.8) | collective-permute-done | bytes 86048 | tf_op jit(solution)/shard_map/ppermute | solution.py:633
  35.3 0.3 reduce_x.1
  35.6 1.5 %collective-permute-start.9 = (s16[144,128]{1,0:T(8,128)(2,1)S(1)}, s16[144,128]{1,0:T(8,128)(2,1)S(1)}, u32[]{:S(2)}, u32[]{:S(2)}) collective-permute-start(s16[144,128]{1,0:T(8,128)(2,1)S(1)} %get-tuple-element.30), channel_id=1, source_target_pairs={{0,24},{2,26},{4,28},{6,30},{8,16},{10,18},{12,20},{14,22},{16,8},... | collective-permute-start | bytes 110600 | tf_op jit(solution)/shard_map/ppermute | solution.py:633
  37.1 0.6 %collective-permute-start.10 = (s16[144,128]{1,0:T(8,128)(2,1)S(1)}, s16[144,128]{1,0:T(8,128)(2,1)S(1)}, u32[]{:S(2)}, u32[]{:S(2)}) collective-permute-start(s16[144,128]{1,0:T(8,128)(2,1)S(1)} %get-tuple-element.31), channel_id=1, source_target_pairs={{0,16},{2,18},{4,20},{6,22},{8,24},{10,26},{12,28},{14,30},{16,0},... | collective-permute-start | bytes 110600 | tf_op jit(solution)/shard_map/ppermute | solution.py:633
  37.8 2.3 %collective-permute-start.11 = (s16[144,128]{1,0:T(8,128)(2,1)S(1)}, s16[144,128]{1,0:T(8,128)(2,1)S(1)}, u32[]{:S(2)}, u32[]{:S(2)}) collective-permute-start(s16[144,128]{1,0:T(8,128)(2,1)S(1)} %get-tuple-element.32), channel_id=1, source_target_pairs={{0,8},{2,10},{4,12},{6,14},{8,0},{10,2},{12,4},{14,6},{16,24},{18,... | collective-permute-start | bytes 110600 | tf_op jit(solution)/shard_map/ppermute | solution.py:633
  40.1 1.6 %collective-permute-done.9.refs_0_ = s16[144,128]{1,0:T(8,128)(2,1)S(1)} collective-permute-done((s16[144,128]{1,0:T(8,128)(2,1)S(1)}, s16[144,128]{1,0:T(8,128)(2,1)S(1)}, u32[]{:S(2)}, u32[]{:S(2)}) %collective-permute-start.9) | collective-permute-done | bytes 36896 | tf_op jit(solution)/shard_map/ppermute | solution.py:633
  41.6 0.4 collective-permute-done.10.refs_1_
  42.1 0.4 collective-permute-done.11.refs_2_
  42.4 3.3 %solve.1 = f32[64,128]{1,0:T(8,128)} custom-call(f32[96,128]{1,0:T(8,128)S(1)} %get-tuple-element.29.own_ref, s16[144,128]{1,0:T(8,128)(2,1)S(1)} %collective-permute-done.9.refs_0_, s16[144,128]{1,0:T(8,128)(2,1)S(1)} %collective-permute-done.10.refs_1_, s16[144,128]{1,0:T(8,128)(2,1)S(1)} %collective-permute-done.11.refs_2_), custom_call_target="tpu_custom_call" | custom-call | tf_op jit(solution)/shard_map/solve/pallas_call | solution.py:622
  (3 shorter events, 0.0 us)
Async XLA Ops:
  0.0 0.8 %copy-start = (f32[192,64]{0,1:T(8,128)S(1)}, f32[192,64]{0,1:T(8,128)}, u32[]{:S(2)}) copy-start(f32[192,64]{0,1:T(8,128)} %param.7) | copy-start | bytes 147460
  0.8 22.3 %copy-start.2 = (f32[8,64]{1,0:T(8,128)S(1)}, f32[8,64]{1,0:T(8,128)}, u32[]{:S(2)}) copy-start(f32[8,64]{1,0:T(8,128)} %refs_4_.1) | copy-start | bytes 6148
  0.8 22.3 %copy-start.3 = (s32[8,64]{1,0:T(8,128)S(1)}, s32[8,64]{1,0:T(8,128)}, u32[]{:S(2)}) copy-start(s32[8,64]{1,0:T(8,128)} %refs_5_.1) | copy-start | bytes 6148
  1.1 7.0 %collective-permute-start.2 = (s16[112,128]{1,0:T(8,128)(2,1)S(1)}, s16[112,128]{1,0:T(8,128)(2,1)S(1)}, u32[]{:S(2)}, u32[]{:S(2)}) collective-permute-start(s16[112,128]{1,0:T(8,128)(2,1)S(1)} %encode_elution.1.mine_ref), channel_id=1, source_target_pairs={{0,24},{2,26},{4,28},{6,30},{8,16},{10,18},{12,20},{14,22},{16,8},... | collective-permute-start | bytes 86024 | tf_op jit(solution)/shard_map/ppermute | solution.py:633
  6.2 4.8 %collective-permute-start.1 = (s16[112,128]{1,0:T(8,128)(2,1)S(1)}, s16[112,128]{1,0:T(8,128)(2,1)S(1)}, u32[]{:S(2)}, u32[]{:S(2)}) collective-permute-start(s16[112,128]{1,0:T(8,128)(2,1)S(1)} %encode_elution.1.mine_ref), channel_id=1, source_target_pairs={{0,16},{2,18},{4,20},{6,22},{8,24},{10,26},{12,28},{14,30},{16,0},... | collective-permute-start | bytes 86024 | tf_op jit(solution)/shard_map/ppermute | solution.py:633
  6.2 4.8 %collective-permute-start = (s16[112,128]{1,0:T(8,128)(2,1)S(1)}, s16[112,128]{1,0:T(8,128)(2,1)S(1)}, u32[]{:S(2)}, u32[]{:S(2)}) collective-permute-start(s16[112,128]{1,0:T(8,128)(2,1)S(1)} %encode_elution.1.mine_ref), channel_id=1, source_target_pairs={{0,8},{2,10},{4,12},{6,14},{8,0},{10,2},{12,4},{14,6},{16,24},{18,... | collective-permute-start | bytes 86024 | tf_op jit(solution)/shard_map/ppermute | solution.py:633
  7.7 18.4 %copy-start.1 = (bf16[8,384,2048]{2,1,0:T(8,128)(2,1)S(1)}, bf16[8,384,2048]{2,1,0:T(8,128)(2,1)}, u32[]{:S(2)}) copy-start(bf16[8,384,2048]{2,1,0:T(8,128)(2,1)} %refs_0_.1) | copy-start | bytes 37748740
  11.0 4.9 %collective-permute-start.3 = (s16[4,112,128]{2,1,0:T(8,128)(2,1)S(1)}, s16[4,112,128]{2,1,0:T(8,128)(2,1)S(1)}, u32[]{:S(2)}, u32[]{:S(2)}) collective-permute-start(s16[4,112,128]{2,1,0:T(8,128)(2,1)S(1)} %pad_add_fusion.1), channel_id=1, source_target_pairs={{0,4},{2,6},{4,0},{6,2},{8,12},{10,14},{12,8},{14,10},{16,20},{18,... | collective-permute-start | bytes 344072 | tf_op jit(solution)/shard_map/ppermute | solution.py:633
  12.5 0.9 %copy-start.4 = (f32[448,128]{1,0:T(8,128)S(1)}, f32[448,128]{1,0:T(8,128)}, u32[]{:S(2)}) copy-start(f32[448,128]{1,0:T(8,128)} %constant.2.clone.table_ref) | copy-start | bytes 688132
  15.9 1.6 %collective-permute-start.4 = (s16[8,112,128]{2,1,0:T(8,128)(2,1)S(1)}, s16[8,112,128]{2,1,0:T(8,128)(2,1)S(1)}, u32[]{:S(2)}, u32[]{:S(2)}) collective-permute-start(s16[8,112,128]{2,1,0:T(8,128)(2,1)S(1)} %pad_add_fusion.refs_0_), channel_id=1, source_target_pairs={{0,2},{2,0},{4,6},{6,4},{8,10},{10,8},{12,14},{14,12},{16,18},{18,... | collective-permute-start | bytes 688136 | tf_op jit(solution)/shard_map/ppermute | solution.py:633
  17.4 4.2 %collective-permute-start.5 = (s16[224,128]{1,0:T(8,128)(2,1)S(1)}, s16[224,128]{1,0:T(8,128)(2,1)S(1)}, u32[]{:S(2)}, u32[]{:S(2)}) collective-permute-start(s16[224,128]{1,0:T(8,128)(2,1)S(1)} %window_pair.1.refs_0_), channel_id=1, source_target_pairs={{0,1},{1,0},{2,3},{3,2},{4,5},{5,4},{6,7},{7,6},{8,9},{9,8},{10,11... | collective-permute-start | bytes 172040 | tf_op jit(solution)/shard_map/ppermute | solution.py:633
  21.6 4.5 %collective-permute-start.6 = (s16[336,128]{1,0:T(8,128)(2,1)S(1)}, s16[336,128]{1,0:T(8,128)(2,1)S(1)}, u32[]{:S(2)}, u32[]{:S(2)}) collective-permute-start(s16[336,128]{1,0:T(8,128)(2,1)S(1)} %get-tuple-element.25), channel_id=1, source_target_pairs={{0,1},{1,0},{2,3},{3,2},{4,5},{5,4},{6,7},{7,6},{8,9},{9,8},{10,11... | collective-permute-start | bytes 258056 | tf_op jit(solution)/shard_map/ppermute | solution.py:633
  28.8 1.6 %collective-permute-start.7 = (f32[544,128]{1,0:T(8,128)S(1)}, f32[544,128]{1,0:T(8,128)S(1)}, u32[]{:S(2)}, u32[]{:S(2)}) collective-permute-start(f32[544,128]{1,0:T(8,128)S(1)} %get-tuple-element.28), channel_id=1, source_target_pairs={{0,2},{2,0},{4,6},{6,4},{8,10},{10,8},{12,14},{14,12},{16,18},{18,... | collective-permute-start | bytes 835592 | tf_op jit(solution)/shard_map/ppermute | solution.py:633
  30.7 4.6 %collective-permute-start.8 = (s16[336,128]{1,0:T(8,128)(2,1)S(1)}, s16[336,128]{1,0:T(8,128)(2,1)S(1)}, u32[]{:S(2)}, u32[]{:S(2)}) collective-permute-start(s16[336,128]{1,0:T(8,128)(2,1)S(1)} %reduce_cores.1), channel_id=1, source_target_pairs={{0,4},{2,6},{4,0},{6,2},{8,12},{10,14},{12,8},{14,10},{16,20},{18,... | collective-permute-start | bytes 258056 | tf_op jit(solution)/shard_map/ppermute | solution.py:633
  35.6 6.0 %collective-permute-start.9 = (s16[144,128]{1,0:T(8,128)(2,1)S(1)}, s16[144,128]{1,0:T(8,128)(2,1)S(1)}, u32[]{:S(2)}, u32[]{:S(2)}) collective-permute-start(s16[144,128]{1,0:T(8,128)(2,1)S(1)} %get-tuple-element.30), channel_id=1, source_target_pairs={{0,24},{2,26},{4,28},{6,30},{8,16},{10,18},{12,20},{14,22},{16,8},... | collective-permute-start | bytes 110600 | tf_op jit(solution)/shard_map/ppermute | solution.py:633
  37.1 4.9 %collective-permute-start.10 = (s16[144,128]{1,0:T(8,128)(2,1)S(1)}, s16[144,128]{1,0:T(8,128)(2,1)S(1)}, u32[]{:S(2)}, u32[]{:S(2)}) collective-permute-start(s16[144,128]{1,0:T(8,128)(2,1)S(1)} %get-tuple-element.31), channel_id=1, source_target_pairs={{0,16},{2,18},{4,20},{6,22},{8,24},{10,26},{12,28},{14,30},{16,0},... | collective-permute-start | bytes 110600 | tf_op jit(solution)/shard_map/ppermute | solution.py:633
  37.8 4.6 %collective-permute-start.11 = (s16[144,128]{1,0:T(8,128)(2,1)S(1)}, s16[144,128]{1,0:T(8,128)(2,1)S(1)}, u32[]{:S(2)}, u32[]{:S(2)}) collective-permute-start(s16[144,128]{1,0:T(8,128)(2,1)S(1)} %get-tuple-element.32), channel_id=1, source_target_pairs={{0,8},{2,10},{4,12},{6,14},{8,0},{10,2},{12,4},{14,6},{16,24},{18,... | collective-permute-start | bytes 110600 | tf_op jit(solution)/shard_map/ppermute | solution.py:633

commit v11 on v10

--- a/solution.py
+++ b/solution.py
@@ -405,10 +405,14 @@
             first.append(tile[:components])
         g = g + jnp.concatenate(first + second, axis=1)
     amps, lags = amp_ref[...].T, lag_ref[...].T
-    middle = run_count // 2
-    for piece in shift_pieces(g, amps, lags, bin_count, terms, range(middle)):
+    group = max(run_count // 4, 1)
+    firsts = range(0, run_count, group)
+
+    def shifts(first):
+        return shift_pieces(g, amps, lags, bin_count, terms, range(first, first + group))
+
+    for piece in shifts(0):
         piece()
-    waiting = shift_pieces(g, amps, lags, bin_count, terms, range(middle, run_count))
 
     def multiply(n, first, last):
         data = i_ref[first:last, :, n * chunk : (n + 1) * chunk].reshape((last - first) * bin_count, chunk)
@@ -417,11 +421,14 @@
         )
         return made[:components] + made[components:]
 
-    share = -(-len(waiting) // chunks)
-    for n in range(chunks):
-        partial[n] = multiply(n, 0, middle)
-        for piece in waiting[n * share : (n + 1) * share]:
-            piece()
+    for first in firsts[:-1]:
+        waiting = shifts(first + group)
+        share = -(-len(waiting) // chunks)
+        for n in range(chunks):
+            made = multiply(n, first, first + group)
+            partial[n] = made if first == 0 else partial[n] + made
+            for piece in waiting[n * share : (n + 1) * share]:
+                piece()
     gram = lax.dot_general(
         terms[...], elution_ref[...], (((1,), (1,)), ((), ())), preferred_element_type=jnp.float32
     )
@@ -437,7 +444,7 @@
         other_ref[...] = gram
 
     for n in range(chunks):
-        made = partial[n] + multiply(n, middle, run_count)
+        made = partial[n] + multiply(n, firsts[-1], run_count)
         if planes:
             freq_rank = lax.axis_index("freq")
             core = freq_rank & 1

time: 46 us -> 46 us (level)
  no operation moved by 1% of the time
where the time goes in v11:
time: 46 us; the launch traced here: 45.8 us
  starting transfers between devices  16.5 us (36%)
  Pallas kernels  13.5 us (29%)
  waiting for transfers between devices  13.1 us (28%)
  local copies, waits for them, and re-layouts  2.6 us (6%)
    ppermute x12, starting transfers between devices, swap(): return lax.ppermute(x, axes, [(i, i ^ value) for i in range(count)])  16.5 us
    ppermute x12, waiting for transfers between devices, swap(): return lax.ppermute(x, axes, [(i, i ^ value) for i in range(count)])  13.1 us
    pallas_call x3, Pallas kernels, small_call(): pl.pallas_call(kernel, out_shape=tuple((jax.ShapeDtypeStruct(shape, dtype...  3.84 us
    pallas_call x1, Pallas kernels, elution_terms(): pl.pallas_call(functools.partial(elution_kernel, planes), out_shape=jax.S...  2.92 us
    pallas_call x1, Pallas kernels, product(): pl.pallas_call(functools.partial(product_kernel, len(models), planes), ou...  2.76 us
    pallas_call x1, Pallas kernels, partial_model(): pl.pallas_call(functools.partial(model_kernel, places, planes), out_shape...  2.18 us
    unnamed x10, local copies, waits for them, and re-layouts  1.79 us
    pallas_call x1, Pallas kernels, circulant(): pl.pallas_call(functools.partial(circulant_kernel, turn), out_shape=jax.S...  1.53 us
  transfers between devices with their start and end apart: 12, of which 10 were waited for; matrix products, arithmetic and copies ran while one was open for 2% of the time, Pallas kernels for 14%

profile of v11, /device:TPU:0, one launch (start us, length us, event | category | flops | bytes accessed | tf_op | source)
XLA Modules:
  0.0 45.8 jit_solution(15212251483234204674)
XLA Ops:
  0.0 0.0 copy-start
  0.0 0.8 %copy-done = f32[192,64]{0,1:T(8,128)S(1)} copy-done((f32[192,64]{0,1:T(8,128)S(1)}, f32[192,64]{0,1:T(8,128)}, u32[]{:S(2)}) %copy-start) | copy-done | bytes 49176
  0.8 0.0 copy-start.2
  0.8 0.0 copy-start.3
  0.8 0.2 encode_elution.1.mine_ref
  1.1 5.1 %collective-permute-start.2 = (s16[112,128]{1,0:T(8,128)(2,1)S(1)}, s16[112,128]{1,0:T(8,128)(2,1)S(1)}, u32[]{:S(2)}, u32[]{:S(2)}) collective-permute-start(s16[112,128]{1,0:T(8,128)(2,1)S(1)} %encode_elution.1.mine_ref), channel_id=1, source_target_pairs={{0,24},{2,26},{4,28},{6,30},{8,16},{10,18},{12,20},{14,22},{16,8},... | collective-permute-start | bytes 86024 | tf_op jit(solution)/shard_map/ppermute | solution.py:640
  6.2 0.0 collective-permute-start.1
  6.2 0.6 %collective-permute-start = (s16[112,128]{1,0:T(8,128)(2,1)S(1)}, s16[112,128]{1,0:T(8,128)(2,1)S(1)}, u32[]{:S(2)}, u32[]{:S(2)}) collective-permute-start(s16[112,128]{1,0:T(8,128)(2,1)S(1)} %encode_elution.1.mine_ref), channel_id=1, source_target_pairs={{0,8},{2,10},{4,12},{6,14},{8,0},{10,2},{12,4},{14,6},{16,24},{18,... | collective-permute-start | bytes 86024 | tf_op jit(solution)/shard_map/ppermute | solution.py:640
  6.8 0.8 %reshape.3.w_ref = f32[128,48]{1,0:T(8,128)S(1)} reshape(f32[6144]{0:T(1024)} %param.10) | data formatting | bytes 49152 | tf_op jit(solution)/shard_map/reshape | solution.py:672
  7.7 0.0 copy-start.1
  7.7 0.4 collective-permute-done.2
  8.0 2.9 %collective-permute-done.1 = s16[112,128]{1,0:T(8,128)(2,1)S(1)} collective-permute-done((s16[112,128]{1,0:T(8,128)(2,1)S(1)}, s16[112,128]{1,0:T(8,128)(2,1)S(1)}, u32[]{:S(2)}, u32[]{:S(2)}) %collective-permute-start.1) | collective-permute-done | bytes 28704 | tf_op jit(solution)/shard_map/ppermute | solution.py:640
  11.0 0.0 collective-permute-done
  11.0 1.6 %collective-permute-start.3 = (s16[4,112,128]{2,1,0:T(8,128)(2,1)S(1)}, s16[4,112,128]{2,1,0:T(8,128)(2,1)S(1)}, u32[]{:S(2)}, u32[]{:S(2)}) collective-permute-start(s16[4,112,128]{2,1,0:T(8,128)(2,1)S(1)} %pad_add_fusion.1), channel_id=1, source_target_pairs={{0,4},{2,6},{4,0},{6,2},{8,12},{10,14},{12,8},{14,10},{16,20},{18,... | collective-permute-start | bytes 344072 | tf_op jit(solution)/shard_map/ppermute | solution.py:640
  12.5 0.0 copy-start.4
  12.5 0.9 %copy-done.4 = f32[448,128]{1,0:T(8,128)S(1)} copy-done((f32[448,128]{1,0:T(8,128)S(1)}, f32[448,128]{1,0:T(8,128)}, u32[]{:S(2)}) %copy-start.4) | copy-done | bytes 229400
  13.5 1.5 %circulant_block.1.refs_2_ = bf16[256,6144]{1,0:T(8,128)(2,1)S(1)} custom-call(f32[128,48]{1,0:T(8,128)S(1)} %reshape.3.w_ref, f32[448,128]{1,0:T(8,128)S(1)} %copy-done.4), custom_call_target="tpu_custom_call" | custom-call | flops 2000000000 | bytes 4194304 | tf_op jit(solution)/shard_map/circulant_block/pallas_call | solution.py:167
  15.0 0.8 %collective-permute-done.3 = s16[4,112,128]{2,1,0:T(8,128)(2,1)S(1)} collective-permute-done((s16[4,112,128]{2,1,0:T(8,128)(2,1)S(1)}, s16[4,112,128]{2,1,0:T(8,128)(2,1)S(1)}, u32[]{:S(2)}, u32[]{:S(2)}) %collective-permute-start.3) | collective-permute-done | bytes 114720 | tf_op jit(solution)/shard_map/ppermute | solution.py:640
  15.9 0.1 collective-permute-start.4
  15.9 1.5 %collective-permute-done.4.refs_1_.came_ref = s16[8,112,128]{2,1,0:T(8,128)(2,1)S(1)} collective-permute-done((s16[8,112,128]{2,1,0:T(8,128)(2,1)S(1)}, s16[8,112,128]{2,1,0:T(8,128)(2,1)S(1)}, u32[]{:S(2)}, u32[]{:S(2)}) %collective-permute-start.4) | collective-permute-done | bytes 229408 | tf_op jit(solution)/shard_map/ppermute | solution.py:640
  17.4 1.5 %collective-permute-start.5 = (s16[224,128]{1,0:T(8,128)(2,1)S(1)}, s16[224,128]{1,0:T(8,128)(2,1)S(1)}, u32[]{:S(2)}, u32[]{:S(2)}) collective-permute-start(s16[224,128]{1,0:T(8,128)(2,1)S(1)} %window_pair.1.refs_0_), channel_id=1, source_target_pairs={{0,1},{1,0},{2,3},{3,2},{4,5},{5,4},{6,7},{7,6},{8,9},{9,8},{10,11... | collective-permute-start | bytes 172040 | tf_op jit(solution)/shard_map/ppermute | solution.py:640
  18.9 2.2 %partial_model.1 = (f32[64,640]{1,0:T(8,128)S(1)}, s16[336,128]{1,0:T(8,128)(2,1)S(1)}) custom-call(s16[8,112,128]{2,1,0:T(8,128)(2,1)S(1)} %pad_add_fusion.refs_0_, s16[8,112,128]{2,1,0:T(8,128)(2,1)S(1)} %collective-permute-done.4.refs_1_.came_ref, bf16[256,6144]{1,0:T(8,128)(2,1)S(1)} %circulant_block.1.refs_2_), custom_call_target="tpu_custom_call" | custom-call | flops 2000000000 | bytes 4194304 | tf_op jit(solution)/shard_map/partial_model/pallas_call | solution.py:266
  21.1 0.5 %collective-permute-done.5.refs_1_ = s16[224,128]{1,0:T(8,128)(2,1)S(1)} collective-permute-done((s16[224,128]{1,0:T(8,128)(2,1)S(1)}, s16[224,128]{1,0:T(8,128)(2,1)S(1)}, u32[]{:S(2)}, u32[]{:S(2)}) %collective-permute-start.5) | collective-permute-done | bytes 57376 | tf_op jit(solution)/shard_map/ppermute | solution.py:640
  21.6 1.5 %collective-permute-start.6 = (s16[336,128]{1,0:T(8,128)(2,1)S(1)}, s16[336,128]{1,0:T(8,128)(2,1)S(1)}, u32[]{:S(2)}, u32[]{:S(2)}) collective-permute-start(s16[336,128]{1,0:T(8,128)(2,1)S(1)} %get-tuple-element.25), channel_id=1, source_target_pairs={{0,1},{1,0},{2,3},{3,2},{4,5},{5,4},{6,7},{7,6},{8,9},{9,8},{10,11... | collective-permute-start | bytes 258056 | tf_op jit(solution)/shard_map/ppermute | solution.py:640
  23.1 0.0 copy-done.2
  23.1 0.0 copy-done.3
  23.1 2.9 %elution_terms.1.refs_3_ = bf16[128,3072]{1,0:T(8,128)(2,1)S(1)} custom-call(s16[224,128]{1,0:T(8,128)(2,1)S(1)} %window_pair.1.refs_0_, s16[224,128]{1,0:T(8,128)(2,1)S(1)} %collective-permute-done.5.refs_1_, f32[8,64]{1,0:T(8,128)S(1)} %copy-done.2, s32[8,64]{1,0:T(8,128)S(1)} %copy-done.3), custom_call_target="tpu_custom_call" | custom-call | flops 1000000000 | bytes 2097152 | tf_op jit(solution)/shard_map/elution_terms/pallas_call | solution.py:367
  26.0 0.0 collective-permute-done.6.refs_2_
  26.1 0.0 copy-done.1
  26.1 2.8 %model_products.1 = (f32[544,128]{1,0:T(8,128)S(1)}, f32[544,128]{1,0:T(8,128)S(1)}) custom-call(bf16[8,384,2048]{2,1,0:T(8,128)(2,1)S(1)} %copy-done.1, f32[64,640]{1,0:T(8,128)S(1)} %get-tuple-element.23.refs_1_, s16[336,128]{1,0:T(8,128)(2,1)S(1)} %collective-permute-done.6.refs_2_, bf16[128,3072]{1,0:T(8,128)(2,1)S(1)} %elution_terms.1.refs_3_, ...), custom_call_target="tpu_custom_call" | custom-call | flops 8000000000 | bytes 12582912 | tf_op jit(solution)/shard_map/model_products/pallas_call | solution.py:469
  28.9 0.1 collective-permute-start.7
  28.9 1.5 %collective-permute-done.7.b_ref = f32[544,128]{1,0:T(8,128)S(1)} collective-permute-done((f32[544,128]{1,0:T(8,128)S(1)}, f32[544,128]{1,0:T(8,128)S(1)}, u32[]{:S(2)}, u32[]{:S(2)}) %collective-permute-start.7) | collective-permute-done | bytes 278560 | tf_op jit(solution)/shard_map/ppermute | solution.py:640
  30.5 0.2 reduce_cores.1
  30.7 1.6 %collective-permute-start.8 = (s16[336,128]{1,0:T(8,128)(2,1)S(1)}, s16[336,128]{1,0:T(8,128)(2,1)S(1)}, u32[]{:S(2)}, u32[]{:S(2)}) collective-permute-start(s16[336,128]{1,0:T(8,128)(2,1)S(1)} %reduce_cores.1), channel_id=1, source_target_pairs={{0,4},{2,6},{4,0},{6,2},{8,12},{10,14},{12,8},{14,10},{16,20},{18,... | collective-permute-start | bytes 258056 | tf_op jit(solution)/shard_map/ppermute | solution.py:640
  32.3 3.1 %collective-permute-done.8.c_ref = s16[336,128]{1,0:T(8,128)(2,1)S(1)} collective-permute-done((s16[336,128]{1,0:T(8,128)(2,1)S(1)}, s16[336,128]{1,0:T(8,128)(2,1)S(1)}, u32[]{:S(2)}, u32[]{:S(2)}) %collective-permute-start.8) | collective-permute-done | bytes 86048 | tf_op jit(solution)/shard_map/ppermute | solution.py:640
  35.3 0.3 reduce_x.1
  35.6 1.5 %collective-permute-start.9 = (s16[144,128]{1,0:T(8,128)(2,1)S(1)}, s16[144,128]{1,0:T(8,128)(2,1)S(1)}, u32[]{:S(2)}, u32[]{:S(2)}) collective-permute-start(s16[144,128]{1,0:T(8,128)(2,1)S(1)} %get-tuple-element.30), channel_id=1, source_target_pairs={{0,24},{2,26},{4,28},{6,30},{8,16},{10,18},{12,20},{14,22},{16,8},... | collective-permute-start | bytes 110600 | tf_op jit(solution)/shard_map/ppermute | solution.py:640
  37.1 0.6 %collective-permute-start.10 = (s16[144,128]{1,0:T(8,128)(2,1)S(1)}, s16[144,128]{1,0:T(8,128)(2,1)S(1)}, u32[]{:S(2)}, u32[]{:S(2)}) collective-permute-start(s16[144,128]{1,0:T(8,128)(2,1)S(1)} %get-tuple-element.31), channel_id=1, source_target_pairs={{0,16},{2,18},{4,20},{6,22},{8,24},{10,26},{12,28},{14,30},{16,0},... | collective-permute-start | bytes 110600 | tf_op jit(solution)/shard_map/ppermute | solution.py:640
  37.8 2.3 %collective-permute-start.11 = (s16[144,128]{1,0:T(8,128)(2,1)S(1)}, s16[144,128]{1,0:T(8,128)(2,1)S(1)}, u32[]{:S(2)}, u32[]{:S(2)}) collective-permute-start(s16[144,128]{1,0:T(8,128)(2,1)S(1)} %get-tuple-element.32), channel_id=1, source_target_pairs={{0,8},{2,10},{4,12},{6,14},{8,0},{10,2},{12,4},{14,6},{16,24},{18,... | collective-permute-start | bytes 110600 | tf_op jit(solution)/shard_map/ppermute | solution.py:640
  40.1 1.6 %collective-permute-done.9.refs_0_ = s16[144,128]{1,0:T(8,128)(2,1)S(1)} collective-permute-done((s16[144,128]{1,0:T(8,128)(2,1)S(1)}, s16[144,128]{1,0:T(8,128)(2,1)S(1)}, u32[]{:S(2)}, u32[]{:S(2)}) %collective-permute-start.9) | collective-permute-done | bytes 36896 | tf_op jit(solution)/shard_map/ppermute | solution.py:640
  41.6 0.4 collective-permute-done.10.refs_1_
  42.1 0.4 collective-permute-done.11.refs_2_
  42.4 3.3 %solve.1 = f32[64,128]{1,0:T(8,128)} custom-call(f32[96,128]{1,0:T(8,128)S(1)} %get-tuple-element.29.own_ref, s16[144,128]{1,0:T(8,128)(2,1)S(1)} %collective-permute-done.9.refs_0_, s16[144,128]{1,0:T(8,128)(2,1)S(1)} %collective-permute-done.10.refs_1_, s16[144,128]{1,0:T(8,128)(2,1)S(1)} %collective-permute-done.11.refs_2_), custom_call_target="tpu_custom_call" | custom-call | tf_op jit(solution)/shard_map/solve/pallas_call | solution.py:629
  (3 shorter events, 0.0 us)
Async XLA Ops:
  0.0 0.8 %copy-start = (f32[192,64]{0,1:T(8,128)S(1)}, f32[192,64]{0,1:T(8,128)}, u32[]{:S(2)}) copy-start(f32[192,64]{0,1:T(8,128)} %param.7) | copy-start | bytes 147460
  0.8 22.3 %copy-start.2 = (f32[8,64]{1,0:T(8,128)S(1)}, f32[8,64]{1,0:T(8,128)}, u32[]{:S(2)}) copy-start(f32[8,64]{1,0:T(8,128)} %refs_4_.1) | copy-start | bytes 6148
  0.8 22.3 %copy-start.3 = (s32[8,64]{1,0:T(8,128)S(1)}, s32[8,64]{1,0:T(8,128)}, u32[]{:S(2)}) copy-start(s32[8,64]{1,0:T(8,128)} %refs_5_.1) | copy-start | bytes 6148
  1.1 7.0 %collective-permute-start.2 = (s16[112,128]{1,0:T(8,128)(2,1)S(1)}, s16[112,128]{1,0:T(8,128)(2,1)S(1)}, u32[]{:S(2)}, u32[]{:S(2)}) collective-permute-start(s16[112,128]{1,0:T(8,128)(2,1)S(1)} %encode_elution.1.mine_ref), channel_id=1, source_target_pairs={{0,24},{2,26},{4,28},{6,30},{8,16},{10,18},{12,20},{14,22},{16,8},... | collective-permute-start | bytes 86024 | tf_op jit(solution)/shard_map/ppermute | solution.py:640
  6.2 4.8 %collective-permute-start.1 = (s16[112,128]{1,0:T(8,128)(2,1)S(1)}, s16[112,128]{1,0:T(8,128)(2,1)S(1)}, u32[]{:S(2)}, u32[]{:S(2)}) collective-permute-start(s16[112,128]{1,0:T(8,128)(2,1)S(1)} %encode_elution.1.mine_ref), channel_id=1, source_target_pairs={{0,16},{2,18},{4,20},{6,22},{8,24},{10,26},{12,28},{14,30},{16,0},... | collective-permute-start | bytes 86024 | tf_op jit(solution)/shard_map/ppermute | solution.py:640
  6.2 4.8 %collective-permute-start = (s16[112,128]{1,0:T(8,128)(2,1)S(1)}, s16[112,128]{1,0:T(8,128)(2,1)S(1)}, u32[]{:S(2)}, u32[]{:S(2)}) collective-permute-start(s16[112,128]{1,0:T(8,128)(2,1)S(1)} %encode_elution.1.mine_ref), channel_id=1, source_target_pairs={{0,8},{2,10},{4,12},{6,14},{8,0},{10,2},{12,4},{14,6},{16,24},{18,... | collective-permute-start | bytes 86024 | tf_op jit(solution)/shard_map/ppermute | solution.py:640
  7.7 18.4 %copy-start.1 = (bf16[8,384,2048]{2,1,0:T(8,128)(2,1)S(1)}, bf16[8,384,2048]{2,1,0:T(8,128)(2,1)}, u32[]{:S(2)}) copy-start(bf16[8,384,2048]{2,1,0:T(8,128)(2,1)} %refs_0_.1) | copy-start | bytes 37748740
  11.0 4.9 %collective-permute-start.3 = (s16[4,112,128]{2,1,0:T(8,128)(2,1)S(1)}, s16[4,112,128]{2,1,0:T(8,128)(2,1)S(1)}, u32[]{:S(2)}, u32[]{:S(2)}) collective-permute-start(s16[4,112,128]{2,1,0:T(8,128)(2,1)S(1)} %pad_add_fusion.1), channel_id=1, source_target_pairs={{0,4},{2,6},{4,0},{6,2},{8,12},{10,14},{12,8},{14,10},{16,20},{18,... | collective-permute-start | bytes 344072 | tf_op jit(solution)/shard_map/ppermute | solution.py:640
  12.5 0.9 %copy-start.4 = (f32[448,128]{1,0:T(8,128)S(1)}, f32[448,128]{1,0:T(8,128)}, u32[]{:S(2)}) copy-start(f32[448,128]{1,0:T(8,128)} %constant.2.clone.table_ref) | copy-start | bytes 688132
  15.9 1.6 %collective-permute-start.4 = (s16[8,112,128]{2,1,0:T(8,128)(2,1)S(1)}, s16[8,112,128]{2,1,0:T(8,128)(2,1)S(1)}, u32[]{:S(2)}, u32[]{:S(2)}) collective-permute-start(s16[8,112,128]{2,1,0:T(8,128)(2,1)S(1)} %pad_add_fusion.refs_0_), channel_id=1, source_target_pairs={{0,2},{2,0},{4,6},{6,4},{8,10},{10,8},{12,14},{14,12},{16,18},{18,... | collective-permute-start | bytes 688136 | tf_op jit(solution)/shard_map/ppermute | solution.py:640
  17.4 4.2 %collective-permute-start.5 = (s16[224,128]{1,0:T(8,128)(2,1)S(1)}, s16[224,128]{1,0:T(8,128)(2,1)S(1)}, u32[]{:S(2)}, u32[]{:S(2)}) collective-permute-start(s16[224,128]{1,0:T(8,128)(2,1)S(1)} %window_pair.1.refs_0_), channel_id=1, source_target_pairs={{0,1},{1,0},{2,3},{3,2},{4,5},{5,4},{6,7},{7,6},{8,9},{9,8},{10,11... | collective-permute-start | bytes 172040 | tf_op jit(solution)/shard_map/ppermute | solution.py:640
  21.6 4.5 %collective-permute-start.6 = (s16[336,128]{1,0:T(8,128)(2,1)S(1)}, s16[336,128]{1,0:T(8,128)(2,1)S(1)}, u32[]{:S(2)}, u32[]{:S(2)}) collective-permute-start(s16[336,128]{1,0:T(8,128)(2,1)S(1)} %get-tuple-element.25), channel_id=1, source_target_pairs={{0,1},{1,0},{2,3},{3,2},{4,5},{5,4},{6,7},{7,6},{8,9},{9,8},{10,11... | collective-permute-start | bytes 258056 | tf_op jit(solution)/shard_map/ppermute | solution.py:640
  28.9 1.6 %collective-permute-start.7 = (f32[544,128]{1,0:T(8,128)S(1)}, f32[544,128]{1,0:T(8,128)S(1)}, u32[]{:S(2)}, u32[]{:S(2)}) collective-permute-start(f32[544,128]{1,0:T(8,128)S(1)} %get-tuple-element.28), channel_id=1, source_target_pairs={{0,2},{2,0},{4,6},{6,4},{8,10},{10,8},{12,14},{14,12},{16,18},{18,... | collective-permute-start | bytes 835592 | tf_op jit(solution)/shard_map/ppermute | solution.py:640
  30.7 4.6 %collective-permute-start.8 = (s16[336,128]{1,0:T(8,128)(2,1)S(1)}, s16[336,128]{1,0:T(8,128)(2,1)S(1)}, u32[]{:S(2)}, u32[]{:S(2)}) collective-permute-start(s16[336,128]{1,0:T(8,128)(2,1)S(1)} %reduce_cores.1), channel_id=1, source_target_pairs={{0,4},{2,6},{4,0},{6,2},{8,12},{10,14},{12,8},{14,10},{16,20},{18,... | collective-permute-start | bytes 258056 | tf_op jit(solution)/shard_map/ppermute | solution.py:640
  35.6 6.0 %collective-permute-start.9 = (s16[144,128]{1,0:T(8,128)(2,1)S(1)}, s16[144,128]{1,0:T(8,128)(2,1)S(1)}, u32[]{:S(2)}, u32[]{:S(2)}) collective-permute-start(s16[144,128]{1,0:T(8,128)(2,1)S(1)} %get-tuple-element.30), channel_id=1, source_target_pairs={{0,24},{2,26},{4,28},{6,30},{8,16},{10,18},{12,20},{14,22},{16,8},... | collective-permute-start | bytes 110600 | tf_op jit(solution)/shard_map/ppermute | solution.py:640
  37.1 4.9 %collective-permute-start.10 = (s16[144,128]{1,0:T(8,128)(2,1)S(1)}, s16[144,128]{1,0:T(8,128)(2,1)S(1)}, u32[]{:S(2)}, u32[]{:S(2)}) collective-permute-start(s16[144,128]{1,0:T(8,128)(2,1)S(1)} %get-tuple-element.31), channel_id=1, source_target_pairs={{0,16},{2,18},{4,20},{6,22},{8,24},{10,26},{12,28},{14,30},{16,0},... | collective-permute-start | bytes 110600 | tf_op jit(solution)/shard_map/ppermute | solution.py:640
  37.8 4.6 %collective-permute-start.11 = (s16[144,128]{1,0:T(8,128)(2,1)S(1)}, s16[144,128]{1,0:T(8,128)(2,1)S(1)}, u32[]{:S(2)}, u32[]{:S(2)}) collective-permute-start(s16[144,128]{1,0:T(8,128)(2,1)S(1)} %get-tuple-element.32), channel_id=1, source_target_pairs={{0,8},{2,10},{4,12},{6,14},{8,0},{10,2},{12,4},{14,6},{16,24},{18,... | collective-permute-start | bytes 110600 | tf_op jit(solution)/shard_map/ppermute | solution.py:640

commit v12 on v10

--- a/solution.py
+++ b/solution.py
@@ -338,13 +338,15 @@
         coded = pair_ref.shape[0] // 2
         rows = 2 * (coded - 16)
         skip = bin_count - REACH
-        for ref, half in ((pair_ref, mz_rank), (other_ref, 1 - mz_rank)):
-            for block in range(2):
-                to = pl.multiple_of((2 * block + half) * rows, 64)
-                values = decoded(ref[block * coded : (block + 1) * coded, :])
-                half_rows = rows // 2
-                window[pl.ds(to, half_rows), :] = values
-                window[pl.ds(pl.multiple_of(to + half_rows, 32), half_rows), :] = pltpu.roll(values, LANES // 2, 1)
+        for block in range(2):
+            part = slice(block * coded, (block + 1) * coded)
+            pair, other = decoded(pair_ref[part, :]), decoded(other_ref[part, :])
+            for half, values in enumerate(
+                (jnp.where(mz_rank == 0, pair, other), jnp.where(mz_rank == 0, other, pair))
+            ):
+                to = (2 * block + half) * rows
+                window[to : to + rows // 2, :] = values
+                window[to + rows // 2 : to + rows, :] = pltpu.roll(values, LANES // 2, 1)
     else:
         own_ref = refs[0]
         step = own_ref.shape[1]

time: 46 us -> 46 us (level)
  transfers between devices with their start and end apart: 12 -> 12, of which waited for: 10 -> 11; matrix products, arithmetic and copies ran while one was open for 2% -> 2% of each run, Pallas kernels for 14% -> 14%
where the time goes in v12:
time: 46 us; the launch traced here: 45.8 us
  starting transfers between devices  16.5 us (36%)
  Pallas kernels  13.4 us (29%)
  waiting for transfers between devices  13.1 us (28%)
  local copies, waits for them, and re-layouts  2.6 us (6%)
    ppermute x12, starting transfers between devices, swap(): return lax.ppermute(x, axes, [(i, i ^ value) for i in range(count)])  16.5 us
    ppermute x12, waiting for transfers between devices, swap(): return lax.ppermute(x, axes, [(i, i ^ value) for i in range(count)])  13.1 us
    pallas_call x3, Pallas kernels, small_call(): pl.pallas_call(kernel, out_shape=tuple((jax.ShapeDtypeStruct(shape, dtype...  3.84 us
    pallas_call x1, Pallas kernels, elution_terms(): pl.pallas_call(functools.partial(elution_kernel, planes), out_shape=jax.S...  2.88 us
    pallas_call x1, Pallas kernels, product(): pl.pallas_call(functools.partial(product_kernel, len(models), planes), ou...  2.75 us
    pallas_call x1, Pallas kernels, partial_model(): pl.pallas_call(functools.partial(model_kernel, places, planes), out_shape...  2.18 us
    unnamed x10, local copies, waits for them, and re-layouts  1.79 us
    pallas_call x1, Pallas kernels, circulant(): pl.pallas_call(functools.partial(circulant_kernel, turn), out_shape=jax.S...  1.53 us
  transfers between devices with their start and end apart: 12, of which 11 were waited for; matrix products, arithmetic and copies ran while one was open for 2% of the time, Pallas kernels for 14%

profile of v12, /device:TPU:0, one launch (start us, length us, event | category | flops | bytes accessed | tf_op | source)
XLA Modules:
  0.0 45.8 jit_solution(9768936071582729586)
XLA Ops:
  0.0 0.0 copy-start
  0.0 0.8 %copy-done = f32[192,64]{0,1:T(8,128)S(1)} copy-done((f32[192,64]{0,1:T(8,128)S(1)}, f32[192,64]{0,1:T(8,128)}, u32[]{:S(2)}) %copy-start) | copy-done | bytes 49176
  0.8 0.0 copy-start.2
  0.8 0.0 copy-start.3
  0.8 0.2 encode_elution.1.mine_ref
  1.1 5.1 %collective-permute-start.2 = (s16[112,128]{1,0:T(8,128)(2,1)S(1)}, s16[112,128]{1,0:T(8,128)(2,1)S(1)}, u32[]{:S(2)}, u32[]{:S(2)}) collective-permute-start(s16[112,128]{1,0:T(8,128)(2,1)S(1)} %encode_elution.1.mine_ref), channel_id=1, source_target_pairs={{0,24},{2,26},{4,28},{6,30},{8,16},{10,18},{12,20},{14,22},{16,8},... | collective-permute-start | bytes 86024 | tf_op jit(solution)/shard_map/ppermute | solution.py:635
  6.2 0.0 collective-permute-start.1
  6.2 0.6 %collective-permute-start = (s16[112,128]{1,0:T(8,128)(2,1)S(1)}, s16[112,128]{1,0:T(8,128)(2,1)S(1)}, u32[]{:S(2)}, u32[]{:S(2)}) collective-permute-start(s16[112,128]{1,0:T(8,128)(2,1)S(1)} %encode_elution.1.mine_ref), channel_id=1, source_target_pairs={{0,8},{2,10},{4,12},{6,14},{8,0},{10,2},{12,4},{14,6},{16,24},{18,... | collective-permute-start | bytes 86024 | tf_op jit(solution)/shard_map/ppermute | solution.py:635
  6.8 0.8 %reshape.3.w_ref = f32[128,48]{1,0:T(8,128)S(1)} reshape(f32[6144]{0:T(1024)} %param.10) | data formatting | bytes 49152 | tf_op jit(solution)/shard_map/reshape | solution.py:667
  7.7 0.0 copy-start.1
  7.7 0.4 collective-permute-done.2
  8.0 2.9 %collective-permute-done.1 = s16[112,128]{1,0:T(8,128)(2,1)S(1)} collective-permute-done((s16[112,128]{1,0:T(8,128)(2,1)S(1)}, s16[112,128]{1,0:T(8,128)(2,1)S(1)}, u32[]{:S(2)}, u32[]{:S(2)}) %collective-permute-start.1) | collective-permute-done | bytes 28704 | tf_op jit(solution)/shard_map/ppermute | solution.py:635
  11.0 0.0 collective-permute-done
  11.0 1.6 %collective-permute-start.3 = (s16[4,112,128]{2,1,0:T(8,128)(2,1)S(1)}, s16[4,112,128]{2,1,0:T(8,128)(2,1)S(1)}, u32[]{:S(2)}, u32[]{:S(2)}) collective-permute-start(s16[4,112,128]{2,1,0:T(8,128)(2,1)S(1)} %pad_add_fusion.1), channel_id=1, source_target_pairs={{0,4},{2,6},{4,0},{6,2},{8,12},{10,14},{12,8},{14,10},{16,20},{18,... | collective-permute-start | bytes 344072 | tf_op jit(solution)/shard_map/ppermute | solution.py:635
  12.5 0.0 copy-start.4
  12.5 0.9 %copy-done.4 = f32[448,128]{1,0:T(8,128)S(1)} copy-done((f32[448,128]{1,0:T(8,128)S(1)}, f32[448,128]{1,0:T(8,128)}, u32[]{:S(2)}) %copy-start.4) | copy-done | bytes 229400
  13.5 1.5 %circulant_block.1.refs_2_ = bf16[256,6144]{1,0:T(8,128)(2,1)S(1)} custom-call(f32[128,48]{1,0:T(8,128)S(1)} %reshape.3.w_ref, f32[448,128]{1,0:T(8,128)S(1)} %copy-done.4), custom_call_target="tpu_custom_call" | custom-call | flops 2000000000 | bytes 4194304 | tf_op jit(solution)/shard_map/circulant_block/pallas_call | solution.py:167
  15.0 0.8 %collective-permute-done.3 = s16[4,112,128]{2,1,0:T(8,128)(2,1)S(1)} collective-permute-done((s16[4,112,128]{2,1,0:T(8,128)(2,1)S(1)}, s16[4,112,128]{2,1,0:T(8,128)(2,1)S(1)}, u32[]{:S(2)}, u32[]{:S(2)}) %collective-permute-start.3) | collective-permute-done | bytes 114720 | tf_op jit(solution)/shard_map/ppermute | solution.py:635
  15.9 0.1 collective-permute-start.4
  15.9 1.5 %collective-permute-done.4.refs_1_.came_ref = s16[8,112,128]{2,1,0:T(8,128)(2,1)S(1)} collective-permute-done((s16[8,112,128]{2,1,0:T(8,128)(2,1)S(1)}, s16[8,112,128]{2,1,0:T(8,128)(2,1)S(1)}, u32[]{:S(2)}, u32[]{:S(2)}) %collective-permute-start.4) | collective-permute-done | bytes 229408 | tf_op jit(solution)/shard_map/ppermute | solution.py:635
  17.4 1.5 %collective-permute-start.5 = (s16[224,128]{1,0:T(8,128)(2,1)S(1)}, s16[224,128]{1,0:T(8,128)(2,1)S(1)}, u32[]{:S(2)}, u32[]{:S(2)}) collective-permute-start(s16[224,128]{1,0:T(8,128)(2,1)S(1)} %window_pair.1.refs_0_), channel_id=1, source_target_pairs={{0,1},{1,0},{2,3},{3,2},{4,5},{5,4},{6,7},{7,6},{8,9},{9,8},{10,11... | collective-permute-start | bytes 172040 | tf_op jit(solution)/shard_map/ppermute | solution.py:635
  18.9 2.2 %partial_model.1 = (f32[64,640]{1,0:T(8,128)S(1)}, s16[336,128]{1,0:T(8,128)(2,1)S(1)}) custom-call(s16[8,112,128]{2,1,0:T(8,128)(2,1)S(1)} %pad_add_fusion.refs_0_, s16[8,112,128]{2,1,0:T(8,128)(2,1)S(1)} %collective-permute-done.4.refs_1_.came_ref, bf16[256,6144]{1,0:T(8,128)(2,1)S(1)} %circulant_block.1.refs_2_), custom_call_target="tpu_custom_call" | custom-call | flops 2000000000 | bytes 4194304 | tf_op jit(solution)/shard_map/partial_model/pallas_call | solution.py:266
  21.1 0.5 %collective-permute-done.5.refs_1_ = s16[224,128]{1,0:T(8,128)(2,1)S(1)} collective-permute-done((s16[224,128]{1,0:T(8,128)(2,1)S(1)}, s16[224,128]{1,0:T(8,128)(2,1)S(1)}, u32[]{:S(2)}, u32[]{:S(2)}) %collective-permute-start.5) | collective-permute-done | bytes 57376 | tf_op jit(solution)/shard_map/ppermute | solution.py:635
  21.6 1.5 %collective-permute-start.6 = (s16[336,128]{1,0:T(8,128)(2,1)S(1)}, s16[336,128]{1,0:T(8,128)(2,1)S(1)}, u32[]{:S(2)}, u32[]{:S(2)}) collective-permute-start(s16[336,128]{1,0:T(8,128)(2,1)S(1)} %get-tuple-element.25), channel_id=1, source_target_pairs={{0,1},{1,0},{2,3},{3,2},{4,5},{5,4},{6,7},{7,6},{8,9},{9,8},{10,11... | collective-permute-start | bytes 258056 | tf_op jit(solution)/shard_map/ppermute | solution.py:635
  23.1 0.0 copy-done.2
  23.1 0.0 copy-done.3
  23.1 2.9 %elution_terms.1.refs_3_ = bf16[128,3072]{1,0:T(8,128)(2,1)S(1)} custom-call(s16[224,128]{1,0:T(8,128)(2,1)S(1)} %window_pair.1.refs_0_, s16[224,128]{1,0:T(8,128)(2,1)S(1)} %collective-permute-done.5.refs_1_, f32[8,64]{1,0:T(8,128)S(1)} %copy-done.2, s32[8,64]{1,0:T(8,128)S(1)} %copy-done.3), custom_call_target="tpu_custom_call" | custom-call | flops 1000000000 | bytes 2097152 | tf_op jit(solution)/shard_map/elution_terms/pallas_call | solution.py:369
  26.0 0.1 collective-permute-done.6.refs_2_
  26.1 0.0 copy-done.1
  26.1 2.8 %model_products.1 = (f32[544,128]{1,0:T(8,128)S(1)}, f32[544,128]{1,0:T(8,128)S(1)}) custom-call(bf16[8,384,2048]{2,1,0:T(8,128)(2,1)S(1)} %copy-done.1, f32[64,640]{1,0:T(8,128)S(1)} %get-tuple-element.23.refs_1_, s16[336,128]{1,0:T(8,128)(2,1)S(1)} %collective-permute-done.6.refs_2_, bf16[128,3072]{1,0:T(8,128)(2,1)S(1)} %elution_terms.1.refs_3_, ...), custom_call_target="tpu_custom_call" | custom-call | flops 8000000000 | bytes 12582912 | tf_op jit(solution)/shard_map/model_products/pallas_call | solution.py:464
  28.8 0.1 collective-permute-start.7
  28.9 1.5 %collective-permute-done.7.b_ref = f32[544,128]{1,0:T(8,128)S(1)} collective-permute-done((f32[544,128]{1,0:T(8,128)S(1)}, f32[544,128]{1,0:T(8,128)S(1)}, u32[]{:S(2)}, u32[]{:S(2)}) %collective-permute-start.7) | collective-permute-done | bytes 278560 | tf_op jit(solution)/shard_map/ppermute | solution.py:635
  30.5 0.2 reduce_cores.1
  30.7 1.6 %collective-permute-start.8 = (s16[336,128]{1,0:T(8,128)(2,1)S(1)}, s16[336,128]{1,0:T(8,128)(2,1)S(1)}, u32[]{:S(2)}, u32[]{:S(2)}) collective-permute-start(s16[336,128]{1,0:T(8,128)(2,1)S(1)} %reduce_cores.1), channel_id=1, source_target_pairs={{0,4},{2,6},{4,0},{6,2},{8,12},{10,14},{12,8},{14,10},{16,20},{18,... | collective-permute-start | bytes 258056 | tf_op jit(solution)/shard_map/ppermute | solution.py:635
  32.2 3.1 %collective-permute-done.8.c_ref = s16[336,128]{1,0:T(8,128)(2,1)S(1)} collective-permute-done((s16[336,128]{1,0:T(8,128)(2,1)S(1)}, s16[336,128]{1,0:T(8,128)(2,1)S(1)}, u32[]{:S(2)}, u32[]{:S(2)}) %collective-permute-start.8) | collective-permute-done | bytes 86048 | tf_op jit(solution)/shard_map/ppermute | solution.py:635
  35.3 0.3 reduce_x.1
  35.6 1.5 %collective-permute-start.9 = (s16[144,128]{1,0:T(8,128)(2,1)S(1)}, s16[144,128]{1,0:T(8,128)(2,1)S(1)}, u32[]{:S(2)}, u32[]{:S(2)}) collective-permute-start(s16[144,128]{1,0:T(8,128)(2,1)S(1)} %get-tuple-element.30), channel_id=1, source_target_pairs={{0,24},{2,26},{4,28},{6,30},{8,16},{10,18},{12,20},{14,22},{16,8},... | collective-permute-start | bytes 110600 | tf_op jit(solution)/shard_map/ppermute | solution.py:635
  37.1 0.6 %collective-permute-start.10 = (s16[144,128]{1,0:T(8,128)(2,1)S(1)}, s16[144,128]{1,0:T(8,128)(2,1)S(1)}, u32[]{:S(2)}, u32[]{:S(2)}) collective-permute-start(s16[144,128]{1,0:T(8,128)(2,1)S(1)} %get-tuple-element.31), channel_id=1, source_target_pairs={{0,16},{2,18},{4,20},{6,22},{8,24},{10,26},{12,28},{14,30},{16,0},... | collective-permute-start | bytes 110600 | tf_op jit(solution)/shard_map/ppermute | solution.py:635
  37.8 2.3 %collective-permute-start.11 = (s16[144,128]{1,0:T(8,128)(2,1)S(1)}, s16[144,128]{1,0:T(8,128)(2,1)S(1)}, u32[]{:S(2)}, u32[]{:S(2)}) collective-permute-start(s16[144,128]{1,0:T(8,128)(2,1)S(1)} %get-tuple-element.32), channel_id=1, source_target_pairs={{0,8},{2,10},{4,12},{6,14},{8,0},{10,2},{12,4},{14,6},{16,24},{18,... | collective-permute-start | bytes 110600 | tf_op jit(solution)/shard_map/ppermute | solution.py:635
  40.1 1.6 %collective-permute-done.9.refs_0_ = s16[144,128]{1,0:T(8,128)(2,1)S(1)} collective-permute-done((s16[144,128]{1,0:T(8,128)(2,1)S(1)}, s16[144,128]{1,0:T(8,128)(2,1)S(1)}, u32[]{:S(2)}, u32[]{:S(2)}) %collective-permute-start.9) | collective-permute-done | bytes 36896 | tf_op jit(solution)/shard_map/ppermute | solution.py:635
  41.6 0.4 collective-permute-done.10.refs_1_
  42.1 0.4 collective-permute-done.11.refs_2_
  42.4 3.3 %solve.1 = f32[64,128]{1,0:T(8,128)} custom-call(f32[96,128]{1,0:T(8,128)S(1)} %get-tuple-element.29.own_ref, s16[144,128]{1,0:T(8,128)(2,1)S(1)} %collective-permute-done.9.refs_0_, s16[144,128]{1,0:T(8,128)(2,1)S(1)} %collective-permute-done.10.refs_1_, s16[144,128]{1,0:T(8,128)(2,1)S(1)} %collective-permute-done.11.refs_2_), custom_call_target="tpu_custom_call" | custom-call | tf_op jit(solution)/shard_map/solve/pallas_call | solution.py:624
  (3 shorter events, 0.0 us)
Async XLA Ops:
  0.0 0.8 %copy-start = (f32[192,64]{0,1:T(8,128)S(1)}, f32[192,64]{0,1:T(8,128)}, u32[]{:S(2)}) copy-start(f32[192,64]{0,1:T(8,128)} %param.7) | copy-start | bytes 147460
  0.8 22.3 %copy-start.2 = (f32[8,64]{1,0:T(8,128)S(1)}, f32[8,64]{1,0:T(8,128)}, u32[]{:S(2)}) copy-start(f32[8,64]{1,0:T(8,128)} %refs_4_.1) | copy-start | bytes 6148
  0.8 22.3 %copy-start.3 = (s32[8,64]{1,0:T(8,128)S(1)}, s32[8,64]{1,0:T(8,128)}, u32[]{:S(2)}) copy-start(s32[8,64]{1,0:T(8,128)} %refs_5_.1) | copy-start | bytes 6148
  1.1 7.0 %collective-permute-start.2 = (s16[112,128]{1,0:T(8,128)(2,1)S(1)}, s16[112,128]{1,0:T(8,128)(2,1)S(1)}, u32[]{:S(2)}, u32[]{:S(2)}) collective-permute-start(s16[112,128]{1,0:T(8,128)(2,1)S(1)} %encode_elution.1.mine_ref), channel_id=1, source_target_pairs={{0,24},{2,26},{4,28},{6,30},{8,16},{10,18},{12,20},{14,22},{16,8},... | collective-permute-start | bytes 86024 | tf_op jit(solution)/shard_map/ppermute | solution.py:635
  6.2 4.8 %collective-permute-start.1 = (s16[112,128]{1,0:T(8,128)(2,1)S(1)}, s16[112,128]{1,0:T(8,128)(2,1)S(1)}, u32[]{:S(2)}, u32[]{:S(2)}) collective-permute-start(s16[112,128]{1,0:T(8,128)(2,1)S(1)} %encode_elution.1.mine_ref), channel_id=1, source_target_pairs={{0,16},{2,18},{4,20},{6,22},{8,24},{10,26},{12,28},{14,30},{16,0},... | collective-permute-start | bytes 86024 | tf_op jit(solution)/shard_map/ppermute | solution.py:635
  6.2 4.8 %collective-permute-start = (s16[112,128]{1,0:T(8,128)(2,1)S(1)}, s16[112,128]{1,0:T(8,128)(2,1)S(1)}, u32[]{:S(2)}, u32[]{:S(2)}) collective-permute-start(s16[112,128]{1,0:T(8,128)(2,1)S(1)} %encode_elution.1.mine_ref), channel_id=1, source_target_pairs={{0,8},{2,10},{4,12},{6,14},{8,0},{10,2},{12,4},{14,6},{16,24},{18,... | collective-permute-start | bytes 86024 | tf_op jit(solution)/shard_map/ppermute | solution.py:635
  7.7 18.4 %copy-start.1 = (bf16[8,384,2048]{2,1,0:T(8,128)(2,1)S(1)}, bf16[8,384,2048]{2,1,0:T(8,128)(2,1)}, u32[]{:S(2)}) copy-start(bf16[8,384,2048]{2,1,0:T(8,128)(2,1)} %refs_0_.1) | copy-start | bytes 37748740
  11.0 4.9 %collective-permute-start.3 = (s16[4,112,128]{2,1,0:T(8,128)(2,1)S(1)}, s16[4,112,128]{2,1,0:T(8,128)(2,1)S(1)}, u32[]{:S(2)}, u32[]{:S(2)}) collective-permute-start(s16[4,112,128]{2,1,0:T(8,128)(2,1)S(1)} %pad_add_fusion.1), channel_id=1, source_target_pairs={{0,4},{2,6},{4,0},{6,2},{8,12},{10,14},{12,8},{14,10},{16,20},{18,... | collective-permute-start | bytes 344072 | tf_op jit(solution)/shard_map/ppermute | solution.py:635
  12.5 0.9 %copy-start.4 = (f32[448,128]{1,0:T(8,128)S(1)}, f32[448,128]{1,0:T(8,128)}, u32[]{:S(2)}) copy-start(f32[448,128]{1,0:T(8,128)} %constant.2.clone.table_ref) | copy-start | bytes 688132
  15.9 1.6 %collective-permute-start.4 = (s16[8,112,128]{2,1,0:T(8,128)(2,1)S(1)}, s16[8,112,128]{2,1,0:T(8,128)(2,1)S(1)}, u32[]{:S(2)}, u32[]{:S(2)}) collective-permute-start(s16[8,112,128]{2,1,0:T(8,128)(2,1)S(1)} %pad_add_fusion.refs_0_), channel_id=1, source_target_pairs={{0,2},{2,0},{4,6},{6,4},{8,10},{10,8},{12,14},{14,12},{16,18},{18,... | collective-permute-start | bytes 688136 | tf_op jit(solution)/shard_map/ppermute | solution.py:635
  17.4 4.2 %collective-permute-start.5 = (s16[224,128]{1,0:T(8,128)(2,1)S(1)}, s16[224,128]{1,0:T(8,128)(2,1)S(1)}, u32[]{:S(2)}, u32[]{:S(2)}) collective-permute-start(s16[224,128]{1,0:T(8,128)(2,1)S(1)} %window_pair.1.refs_0_), channel_id=1, source_target_pairs={{0,1},{1,0},{2,3},{3,2},{4,5},{5,4},{6,7},{7,6},{8,9},{9,8},{10,11... | collective-permute-start | bytes 172040 | tf_op jit(solution)/shard_map/ppermute | solution.py:635
  21.6 4.5 %collective-permute-start.6 = (s16[336,128]{1,0:T(8,128)(2,1)S(1)}, s16[336,128]{1,0:T(8,128)(2,1)S(1)}, u32[]{:S(2)}, u32[]{:S(2)}) collective-permute-start(s16[336,128]{1,0:T(8,128)(2,1)S(1)} %get-tuple-element.25), channel_id=1, source_target_pairs={{0,1},{1,0},{2,3},{3,2},{4,5},{5,4},{6,7},{7,6},{8,9},{9,8},{10,11... | collective-permute-start | bytes 258056 | tf_op jit(solution)/shard_map/ppermute | solution.py:635
  28.8 1.6 %collective-permute-start.7 = (f32[544,128]{1,0:T(8,128)S(1)}, f32[544,128]{1,0:T(8,128)S(1)}, u32[]{:S(2)}, u32[]{:S(2)}) collective-permute-start(f32[544,128]{1,0:T(8,128)S(1)} %get-tuple-element.28), channel_id=1, source_target_pairs={{0,2},{2,0},{4,6},{6,4},{8,10},{10,8},{12,14},{14,12},{16,18},{18,... | collective-permute-start | bytes 835592 | tf_op jit(solution)/shard_map/ppermute | solution.py:635
  30.7 4.6 %collective-permute-start.8 = (s16[336,128]{1,0:T(8,128)(2,1)S(1)}, s16[336,128]{1,0:T(8,128)(2,1)S(1)}, u32[]{:S(2)}, u32[]{:S(2)}) collective-permute-start(s16[336,128]{1,0:T(8,128)(2,1)S(1)} %reduce_cores.1), channel_id=1, source_target_pairs={{0,4},{2,6},{4,0},{6,2},{8,12},{10,14},{12,8},{14,10},{16,20},{18,... | collective-permute-start | bytes 258056 | tf_op jit(solution)/shard_map/ppermute | solution.py:635
  35.6 6.0 %collective-permute-start.9 = (s16[144,128]{1,0:T(8,128)(2,1)S(1)}, s16[144,128]{1,0:T(8,128)(2,1)S(1)}, u32[]{:S(2)}, u32[]{:S(2)}) collective-permute-start(s16[144,128]{1,0:T(8,128)(2,1)S(1)} %get-tuple-element.30), channel_id=1, source_target_pairs={{0,24},{2,26},{4,28},{6,30},{8,16},{10,18},{12,20},{14,22},{16,8},... | collective-permute-start | bytes 110600 | tf_op jit(solution)/shard_map/ppermute | solution.py:635
  37.1 4.9 %collective-permute-start.10 = (s16[144,128]{1,0:T(8,128)(2,1)S(1)}, s16[144,128]{1,0:T(8,128)(2,1)S(1)}, u32[]{:S(2)}, u32[]{:S(2)}) collective-permute-start(s16[144,128]{1,0:T(8,128)(2,1)S(1)} %get-tuple-element.31), channel_id=1, source_target_pairs={{0,16},{2,18},{4,20},{6,22},{8,24},{10,26},{12,28},{14,30},{16,0},... | collective-permute-start | bytes 110600 | tf_op jit(solution)/shard_map/ppermute | solution.py:635
  37.8 4.6 %collective-permute-start.11 = (s16[144,128]{1,0:T(8,128)(2,1)S(1)}, s16[144,128]{1,0:T(8,128)(2,1)S(1)}, u32[]{:S(2)}, u32[]{:S(2)}) collective-permute-start(s16[144,128]{1,0:T(8,128)(2,1)S(1)} %get-tuple-element.32), channel_id=1, source_target_pairs={{0,8},{2,10},{4,12},{6,14},{8,0},{10,2},{12,4},{14,6},{16,24},{18,... | collective-permute-start | bytes 110600 | tf_op jit(solution)/shard_map/ppermute | solution.py:635

commit v13 on v10

--- a/solution.py
+++ b/solution.py
@@ -695,7 +695,8 @@
         came,
         across,
     )
-    parts = [swap(send, "freq", freq_count, step) for send, step in zip(sends, z_steps)][::-1]
+    parts = [swap(send, "freq", freq_count, step) for send, step in zip(sends, z_steps)]
+    parts = parts[1:] + parts[:1]
     return small_call(
         solve_planes_kernel, [((components, own), jnp.float32)], "solve", own_part, *parts
     )[0]

time: 46 us -> 47.1 us (1.024)
  waiting for transfers between devices: 13.1 us -> 15 us
  starting transfers between devices: 16.5 us -> 15.6 us
    ppermute x12, waiting for transfers between devices: 13.1 us -> 15 us  [swap(): return lax.ppermute(x, axes, [(i, i ^ value) for i in range(count)])]
    ppermute x12, starting transfers between devices: 16.5 us -> 15.6 us  [swap(): return lax.ppermute(x, axes, [(i, i ^ value) for i in range(count)])]
  transfers between devices with their start and end apart: 12 -> 12, of which waited for: 10 -> 9; matrix products, arithmetic and copies ran while one was open for 2% -> 2% of each run, Pallas kernels for 14% -> 14%
where the time goes in v13:
time: 47.1 us; the launch traced here: 46.8 us
  starting transfers between devices  15.6 us (33%)
  waiting for transfers between devices  15 us (32%)
  Pallas kernels  13.4 us (28%)
  local copies, waits for them, and re-layouts  2.6 us (6%)
    ppermute x12, starting transfers between devices, swap(): return lax.ppermute(x, axes, [(i, i ^ value) for i in range(count)])  15.6 us
    ppermute x12, waiting for transfers between devices, swap(): return lax.ppermute(x, axes, [(i, i ^ value) for i in range(count)])  15 us
    pallas_call x3, Pallas kernels, small_call(): pl.pallas_call(kernel, out_shape=tuple((jax.ShapeDtypeStruct(shape, dtype...  3.84 us
    pallas_call x1, Pallas kernels, elution_terms(): pl.pallas_call(functools.partial(elution_kernel, planes), out_shape=jax.S...  2.92 us
    pallas_call x1, Pallas kernels, product(): pl.pallas_call(functools.partial(product_kernel, len(models), planes), ou...  2.75 us
    pallas_call x1, Pallas kernels, partial_model(): pl.pallas_call(functools.partial(model_kernel, places, planes), out_shape...  2.18 us
    unnamed x10, local copies, waits for them, and re-layouts  1.79 us
    pallas_call x1, Pallas kernels, circulant(): pl.pallas_call(functools.partial(circulant_kernel, turn), out_shape=jax.S...  1.53 us
  transfers between devices with their start and end apart: 12, of which 9 were waited for; matrix products, arithmetic and copies ran while one was open for 2% of the time, Pallas kernels for 14%

profile of v13, /device:TPU:0, one launch (start us, length us, event | category | flops | bytes accessed | tf_op | source)
XLA Modules:
  0.0 46.8 jit_solution(1349507465558720083)
XLA Ops:
  0.0 0.0 copy-start
  0.0 0.8 %copy-done = f32[192,64]{0,1:T(8,128)S(1)} copy-done((f32[192,64]{0,1:T(8,128)S(1)}, f32[192,64]{0,1:T(8,128)}, u32[]{:S(2)}) %copy-start) | copy-done | bytes 49176
  0.8 0.0 copy-start.2
  0.8 0.0 copy-start.3
  0.8 0.2 encode_elution.1.mine_ref
  1.1 5.1 %collective-permute-start.2 = (s16[112,128]{1,0:T(8,128)(2,1)S(1)}, s16[112,128]{1,0:T(8,128)(2,1)S(1)}, u32[]{:S(2)}, u32[]{:S(2)}) collective-permute-start(s16[112,128]{1,0:T(8,128)(2,1)S(1)} %encode_elution.1.mine_ref), channel_id=1, source_target_pairs={{0,24},{2,26},{4,28},{6,30},{8,16},{10,18},{12,20},{14,22},{16,8},... | collective-permute-start | bytes 86024 | tf_op jit(solution)/shard_map/ppermute | solution.py:633
  6.2 0.0 collective-permute-start.1
  6.2 0.6 %collective-permute-start = (s16[112,128]{1,0:T(8,128)(2,1)S(1)}, s16[112,128]{1,0:T(8,128)(2,1)S(1)}, u32[]{:S(2)}, u32[]{:S(2)}) collective-permute-start(s16[112,128]{1,0:T(8,128)(2,1)S(1)} %encode_elution.1.mine_ref), channel_id=1, source_target_pairs={{0,8},{2,10},{4,12},{6,14},{8,0},{10,2},{12,4},{14,6},{16,24},{18,... | collective-permute-start | bytes 86024 | tf_op jit(solution)/shard_map/ppermute | solution.py:633
  6.8 0.8 %reshape.3.w_ref = f32[128,48]{1,0:T(8,128)S(1)} reshape(f32[6144]{0:T(1024)} %param.10) | data formatting | bytes 49152 | tf_op jit(solution)/shard_map/reshape | solution.py:665
  7.7 0.0 copy-start.1
  7.7 0.4 collective-permute-done.2
  8.0 2.9 %collective-permute-done.1 = s16[112,128]{1,0:T(8,128)(2,1)S(1)} collective-permute-done((s16[112,128]{1,0:T(8,128)(2,1)S(1)}, s16[112,128]{1,0:T(8,128)(2,1)S(1)}, u32[]{:S(2)}, u32[]{:S(2)}) %collective-permute-start.1) | collective-permute-done | bytes 28704 | tf_op jit(solution)/shard_map/ppermute | solution.py:633
  11.0 0.0 collective-permute-done
  11.0 1.6 %collective-permute-start.3 = (s16[4,112,128]{2,1,0:T(8,128)(2,1)S(1)}, s16[4,112,128]{2,1,0:T(8,128)(2,1)S(1)}, u32[]{:S(2)}, u32[]{:S(2)}) collective-permute-start(s16[4,112,128]{2,1,0:T(8,128)(2,1)S(1)} %pad_add_fusion.1), channel_id=1, source_target_pairs={{0,4},{2,6},{4,0},{6,2},{8,12},{10,14},{12,8},{14,10},{16,20},{18,... | collective-permute-start | bytes 344072 | tf_op jit(solution)/shard_map/ppermute | solution.py:633
  12.5 0.0 copy-start.4
  12.5 0.9 %copy-done.4 = f32[448,128]{1,0:T(8,128)S(1)} copy-done((f32[448,128]{1,0:T(8,128)S(1)}, f32[448,128]{1,0:T(8,128)}, u32[]{:S(2)}) %copy-start.4) | copy-done | bytes 229400
  13.5 1.5 %circulant_block.1.refs_2_ = bf16[256,6144]{1,0:T(8,128)(2,1)S(1)} custom-call(f32[128,48]{1,0:T(8,128)S(1)} %reshape.3.w_ref, f32[448,128]{1,0:T(8,128)S(1)} %copy-done.4), custom_call_target="tpu_custom_call" | custom-call | flops 2000000000 | bytes 4194304 | tf_op jit(solution)/shard_map/circulant_block/pallas_call | solution.py:167
  15.0 0.8 %collective-permute-done.3 = s16[4,112,128]{2,1,0:T(8,128)(2,1)S(1)} collective-permute-done((s16[4,112,128]{2,1,0:T(8,128)(2,1)S(1)}, s16[4,112,128]{2,1,0:T(8,128)(2,1)S(1)}, u32[]{:S(2)}, u32[]{:S(2)}) %collective-permute-start.3) | collective-permute-done | bytes 114720 | tf_op jit(solution)/shard_map/ppermute | solution.py:633
  15.9 0.1 collective-permute-start.4
  15.9 1.5 %collective-permute-done.4.refs_1_.came_ref = s16[8,112,128]{2,1,0:T(8,128)(2,1)S(1)} collective-permute-done((s16[8,112,128]{2,1,0:T(8,128)(2,1)S(1)}, s16[8,112,128]{2,1,0:T(8,128)(2,1)S(1)}, u32[]{:S(2)}, u32[]{:S(2)}) %collective-permute-start.4) | collective-permute-done | bytes 229408 | tf_op jit(solution)/shard_map/ppermute | solution.py:633
  17.4 1.5 %collective-permute-start.5 = (s16[224,128]{1,0:T(8,128)(2,1)S(1)}, s16[224,128]{1,0:T(8,128)(2,1)S(1)}, u32[]{:S(2)}, u32[]{:S(2)}) collective-permute-start(s16[224,128]{1,0:T(8,128)(2,1)S(1)} %window_pair.1.refs_0_), channel_id=1, source_target_pairs={{0,1},{1,0},{2,3},{3,2},{4,5},{5,4},{6,7},{7,6},{8,9},{9,8},{10,11... | collective-permute-start | bytes 172040 | tf_op jit(solution)/shard_map/ppermute | solution.py:633
  18.9 2.2 %partial_model.1 = (f32[64,640]{1,0:T(8,128)S(1)}, s16[336,128]{1,0:T(8,128)(2,1)S(1)}) custom-call(s16[8,112,128]{2,1,0:T(8,128)(2,1)S(1)} %pad_add_fusion.refs_0_, s16[8,112,128]{2,1,0:T(8,128)(2,1)S(1)} %collective-permute-done.4.refs_1_.came_ref, bf16[256,6144]{1,0:T(8,128)(2,1)S(1)} %circulant_block.1.refs_2_), custom_call_target="tpu_custom_call" | custom-call | flops 2000000000 | bytes 4194304 | tf_op jit(solution)/shard_map/partial_model/pallas_call | solution.py:266
  21.1 0.5 %collective-permute-done.5.refs_1_ = s16[224,128]{1,0:T(8,128)(2,1)S(1)} collective-permute-done((s16[224,128]{1,0:T(8,128)(2,1)S(1)}, s16[224,128]{1,0:T(8,128)(2,1)S(1)}, u32[]{:S(2)}, u32[]{:S(2)}) %collective-permute-start.5) | collective-permute-done | bytes 57376 | tf_op jit(solution)/shard_map/ppermute | solution.py:633
  21.6 1.5 %collective-permute-start.6 = (s16[336,128]{1,0:T(8,128)(2,1)S(1)}, s16[336,128]{1,0:T(8,128)(2,1)S(1)}, u32[]{:S(2)}, u32[]{:S(2)}) collective-permute-start(s16[336,128]{1,0:T(8,128)(2,1)S(1)} %get-tuple-element.25), channel_id=1, source_target_pairs={{0,1},{1,0},{2,3},{3,2},{4,5},{5,4},{6,7},{7,6},{8,9},{9,8},{10,11... | collective-permute-start | bytes 258056 | tf_op jit(solution)/shard_map/ppermute | solution.py:633
  23.1 0.0 copy-done.2
  23.1 0.0 copy-done.3
  23.1 2.9 %elution_terms.1.refs_3_ = bf16[128,3072]{1,0:T(8,128)(2,1)S(1)} custom-call(s16[224,128]{1,0:T(8,128)(2,1)S(1)} %window_pair.1.refs_0_, s16[224,128]{1,0:T(8,128)(2,1)S(1)} %collective-permute-done.5.refs_1_, f32[8,64]{1,0:T(8,128)S(1)} %copy-done.2, s32[8,64]{1,0:T(8,128)S(1)} %copy-done.3), custom_call_target="tpu_custom_call" | custom-call | flops 1000000000 | bytes 2097152 | tf_op jit(solution)/shard_map/elution_terms/pallas_call | solution.py:367
  26.0 0.0 collective-permute-done.6.refs_2_
  26.1 0.0 copy-done.1
  26.1 2.8 %model_products.1 = (f32[544,128]{1,0:T(8,128)S(1)}, f32[544,128]{1,0:T(8,128)S(1)}) custom-call(bf16[8,384,2048]{2,1,0:T(8,128)(2,1)S(1)} %copy-done.1, f32[64,640]{1,0:T(8,128)S(1)} %get-tuple-element.23.refs_1_, s16[336,128]{1,0:T(8,128)(2,1)S(1)} %collective-permute-done.6.refs_2_, bf16[128,3072]{1,0:T(8,128)(2,1)S(1)} %elution_terms.1.refs_3_, ...), custom_call_target="tpu_custom_call" | custom-call | flops 8000000000 | bytes 12582912 | tf_op jit(solution)/shard_map/model_products/pallas_call | solution.py:462
  28.8 0.1 collective-permute-start.7
  28.9 1.5 %collective-permute-done.7.b_ref = f32[544,128]{1,0:T(8,128)S(1)} collective-permute-done((f32[544,128]{1,0:T(8,128)S(1)}, f32[544,128]{1,0:T(8,128)S(1)}, u32[]{:S(2)}, u32[]{:S(2)}) %collective-permute-start.7) | collective-permute-done | bytes 278560 | tf_op jit(solution)/shard_map/ppermute | solution.py:633
  30.5 0.2 reduce_cores.1
  30.7 1.6 %collective-permute-start.8 = (s16[336,128]{1,0:T(8,128)(2,1)S(1)}, s16[336,128]{1,0:T(8,128)(2,1)S(1)}, u32[]{:S(2)}, u32[]{:S(2)}) collective-permute-start(s16[336,128]{1,0:T(8,128)(2,1)S(1)} %reduce_cores.1), channel_id=1, source_target_pairs={{0,4},{2,6},{4,0},{6,2},{8,12},{10,14},{12,8},{14,10},{16,20},{18,... | collective-permute-start | bytes 258056 | tf_op jit(solution)/shard_map/ppermute | solution.py:633
  32.2 3.1 %collective-permute-done.8.c_ref = s16[336,128]{1,0:T(8,128)(2,1)S(1)} collective-permute-done((s16[336,128]{1,0:T(8,128)(2,1)S(1)}, s16[336,128]{1,0:T(8,128)(2,1)S(1)}, u32[]{:S(2)}, u32[]{:S(2)}) %collective-permute-start.8) | collective-permute-done | bytes 86048 | tf_op jit(solution)/shard_map/ppermute | solution.py:633
  35.3 0.3 reduce_x.1
  35.6 2.1 %collective-permute-start.9 = (s16[144,128]{1,0:T(8,128)(2,1)S(1)}, s16[144,128]{1,0:T(8,128)(2,1)S(1)}, u32[]{:S(2)}, u32[]{:S(2)}) collective-permute-start(s16[144,128]{1,0:T(8,128)(2,1)S(1)} %get-tuple-element.30), channel_id=1, source_target_pairs={{0,16},{2,18},{4,20},{6,22},{8,24},{10,26},{12,28},{14,30},{16,0},... | collective-permute-start | bytes 110600 | tf_op jit(solution)/shard_map/ppermute | solution.py:633
  37.7 0.2 collective-permute-start.10
  37.9 1.3 %collective-permute-start.11 = (s16[144,128]{1,0:T(8,128)(2,1)S(1)}, s16[144,128]{1,0:T(8,128)(2,1)S(1)}, u32[]{:S(2)}, u32[]{:S(2)}) collective-permute-start(s16[144,128]{1,0:T(8,128)(2,1)S(1)} %get-tuple-element.32), channel_id=1, source_target_pairs={{0,8},{2,10},{4,12},{6,14},{8,0},{10,2},{12,4},{14,6},{16,24},{18,... | collective-permute-start | bytes 110600 | tf_op jit(solution)/shard_map/ppermute | solution.py:633
  39.2 1.4 %collective-permute-done.9.refs_0_ = s16[144,128]{1,0:T(8,128)(2,1)S(1)} collective-permute-done((s16[144,128]{1,0:T(8,128)(2,1)S(1)}, s16[144,128]{1,0:T(8,128)(2,1)S(1)}, u32[]{:S(2)}, u32[]{:S(2)}) %collective-permute-start.9) | collective-permute-done | bytes 36896 | tf_op jit(solution)/shard_map/ppermute | solution.py:633
  40.5 2.9 %collective-permute-done.10.refs_1_ = s16[144,128]{1,0:T(8,128)(2,1)S(1)} collective-permute-done((s16[144,128]{1,0:T(8,128)(2,1)S(1)}, s16[144,128]{1,0:T(8,128)(2,1)S(1)}, u32[]{:S(2)}, u32[]{:S(2)}) %collective-permute-start.10) | collective-permute-done | bytes 36896 | tf_op jit(solution)/shard_map/ppermute | solution.py:633
  43.5 0.0 collective-permute-done.11.refs_2_
  43.5 3.3 %solve.1 = f32[64,128]{1,0:T(8,128)} custom-call(f32[96,128]{1,0:T(8,128)S(1)} %get-tuple-element.29.own_ref, s16[144,128]{1,0:T(8,128)(2,1)S(1)} %collective-permute-done.9.refs_0_, s16[144,128]{1,0:T(8,128)(2,1)S(1)} %collective-permute-done.10.refs_1_, s16[144,128]{1,0:T(8,128)(2,1)S(1)} %collective-permute-done.11.refs_2_), custom_call_target="tpu_custom_call" | custom-call | tf_op jit(solution)/shard_map/solve/pallas_call | solution.py:622
  (3 shorter events, 0.0 us)
Async XLA Ops:
  0.0 0.8 %copy-start = (f32[192,64]{0,1:T(8,128)S(1)}, f32[192,64]{0,1:T(8,128)}, u32[]{:S(2)}) copy-start(f32[192,64]{0,1:T(8,128)} %param.7) | copy-start | bytes 147460
  0.8 22.3 %copy-start.2 = (f32[8,64]{1,0:T(8,128)S(1)}, f32[8,64]{1,0:T(8,128)}, u32[]{:S(2)}) copy-start(f32[8,64]{1,0:T(8,128)} %refs_4_.1) | copy-start | bytes 6148
  0.8 22.3 %copy-start.3 = (s32[8,64]{1,0:T(8,128)S(1)}, s32[8,64]{1,0:T(8,128)}, u32[]{:S(2)}) copy-start(s32[8,64]{1,0:T(8,128)} %refs_5_.1) | copy-start | bytes 6148
  1.1 7.0 %collective-permute-start.2 = (s16[112,128]{1,0:T(8,128)(2,1)S(1)}, s16[112,128]{1,0:T(8,128)(2,1)S(1)}, u32[]{:S(2)}, u32[]{:S(2)}) collective-permute-start(s16[112,128]{1,0:T(8,128)(2,1)S(1)} %encode_elution.1.mine_ref), channel_id=1, source_target_pairs={{0,24},{2,26},{4,28},{6,30},{8,16},{10,18},{12,20},{14,22},{16,8},... | collective-permute-start | bytes 86024 | tf_op jit(solution)/shard_map/ppermute | solution.py:633
  6.2 4.8 %collective-permute-start.1 = (s16[112,128]{1,0:T(8,128)(2,1)S(1)}, s16[112,128]{1,0:T(8,128)(2,1)S(1)}, u32[]{:S(2)}, u32[]{:S(2)}) collective-permute-start(s16[112,128]{1,0:T(8,128)(2,1)S(1)} %encode_elution.1.mine_ref), channel_id=1, source_target_pairs={{0,16},{2,18},{4,20},{6,22},{8,24},{10,26},{12,28},{14,30},{16,0},... | collective-permute-start | bytes 86024 | tf_op jit(solution)/shard_map/ppermute | solution.py:633
  6.2 4.8 %collective-permute-start = (s16[112,128]{1,0:T(8,128)(2,1)S(1)}, s16[112,128]{1,0:T(8,128)(2,1)S(1)}, u32[]{:S(2)}, u32[]{:S(2)}) collective-permute-start(s16[112,128]{1,0:T(8,128)(2,1)S(1)} %encode_elution.1.mine_ref), channel_id=1, source_target_pairs={{0,8},{2,10},{4,12},{6,14},{8,0},{10,2},{12,4},{14,6},{16,24},{18,... | collective-permute-start | bytes 86024 | tf_op jit(solution)/shard_map/ppermute | solution.py:633
  7.7 18.4 %copy-start.1 = (bf16[8,384,2048]{2,1,0:T(8,128)(2,1)S(1)}, bf16[8,384,2048]{2,1,0:T(8,128)(2,1)}, u32[]{:S(2)}) copy-start(bf16[8,384,2048]{2,1,0:T(8,128)(2,1)} %refs_0_.1) | copy-start | bytes 37748740
  11.0 4.9 %collective-permute-start.3 = (s16[4,112,128]{2,1,0:T(8,128)(2,1)S(1)}, s16[4,112,128]{2,1,0:T(8,128)(2,1)S(1)}, u32[]{:S(2)}, u32[]{:S(2)}) collective-permute-start(s16[4,112,128]{2,1,0:T(8,128)(2,1)S(1)} %pad_add_fusion.1), channel_id=1, source_target_pairs={{0,4},{2,6},{4,0},{6,2},{8,12},{10,14},{12,8},{14,10},{16,20},{18,... | collective-permute-start | bytes 344072 | tf_op jit(solution)/shard_map/ppermute | solution.py:633
  12.5 0.9 %copy-start.4 = (f32[448,128]{1,0:T(8,128)S(1)}, f32[448,128]{1,0:T(8,128)}, u32[]{:S(2)}) copy-start(f32[448,128]{1,0:T(8,128)} %constant.2.clone.table_ref) | copy-start | bytes 688132
  15.9 1.6 %collective-permute-start.4 = (s16[8,112,128]{2,1,0:T(8,128)(2,1)S(1)}, s16[8,112,128]{2,1,0:T(8,128)(2,1)S(1)}, u32[]{:S(2)}, u32[]{:S(2)}) collective-permute-start(s16[8,112,128]{2,1,0:T(8,128)(2,1)S(1)} %pad_add_fusion.refs_0_), channel_id=1, source_target_pairs={{0,2},{2,0},{4,6},{6,4},{8,10},{10,8},{12,14},{14,12},{16,18},{18,... | collective-permute-start | bytes 688136 | tf_op jit(solution)/shard_map/ppermute | solution.py:633
  17.4 4.2 %collective-permute-start.5 = (s16[224,128]{1,0:T(8,128)(2,1)S(1)}, s16[224,128]{1,0:T(8,128)(2,1)S(1)}, u32[]{:S(2)}, u32[]{:S(2)}) collective-permute-start(s16[224,128]{1,0:T(8,128)(2,1)S(1)} %window_pair.1.refs_0_), channel_id=1, source_target_pairs={{0,1},{1,0},{2,3},{3,2},{4,5},{5,4},{6,7},{7,6},{8,9},{9,8},{10,11... | collective-permute-start | bytes 172040 | tf_op jit(solution)/shard_map/ppermute | solution.py:633
  21.6 4.5 %collective-permute-start.6 = (s16[336,128]{1,0:T(8,128)(2,1)S(1)}, s16[336,128]{1,0:T(8,128)(2,1)S(1)}, u32[]{:S(2)}, u32[]{:S(2)}) collective-permute-start(s16[336,128]{1,0:T(8,128)(2,1)S(1)} %get-tuple-element.25), channel_id=1, source_target_pairs={{0,1},{1,0},{2,3},{3,2},{4,5},{5,4},{6,7},{7,6},{8,9},{9,8},{10,11... | collective-permute-start | bytes 258056 | tf_op jit(solution)/shard_map/ppermute | solution.py:633
  28.8 1.6 %collective-permute-start.7 = (f32[544,128]{1,0:T(8,128)S(1)}, f32[544,128]{1,0:T(8,128)S(1)}, u32[]{:S(2)}, u32[]{:S(2)}) collective-permute-start(f32[544,128]{1,0:T(8,128)S(1)} %get-tuple-element.28), channel_id=1, source_target_pairs={{0,2},{2,0},{4,6},{6,4},{8,10},{10,8},{12,14},{14,12},{16,18},{18,... | collective-permute-start | bytes 835592 | tf_op jit(solution)/shard_map/ppermute | solution.py:633
  30.7 4.6 %collective-permute-start.8 = (s16[336,128]{1,0:T(8,128)(2,1)S(1)}, s16[336,128]{1,0:T(8,128)(2,1)S(1)}, u32[]{:S(2)}, u32[]{:S(2)}) collective-permute-start(s16[336,128]{1,0:T(8,128)(2,1)S(1)} %reduce_cores.1), channel_id=1, source_target_pairs={{0,4},{2,6},{4,0},{6,2},{8,12},{10,14},{12,8},{14,10},{16,20},{18,... | collective-permute-start | bytes 258056 | tf_op jit(solution)/shard_map/ppermute | solution.py:633
  35.6 4.9 %collective-permute-start.9 = (s16[144,128]{1,0:T(8,128)(2,1)S(1)}, s16[144,128]{1,0:T(8,128)(2,1)S(1)}, u32[]{:S(2)}, u32[]{:S(2)}) collective-permute-start(s16[144,128]{1,0:T(8,128)(2,1)S(1)} %get-tuple-element.30), channel_id=1, source_target_pairs={{0,16},{2,18},{4,20},{6,22},{8,24},{10,26},{12,28},{14,30},{16,0},... | collective-permute-start | bytes 110600 | tf_op jit(solution)/shard_map/ppermute | solution.py:633
  37.7 5.8 %collective-permute-start.10 = (s16[144,128]{1,0:T(8,128)(2,1)S(1)}, s16[144,128]{1,0:T(8,128)(2,1)S(1)}, u32[]{:S(2)}, u32[]{:S(2)}) collective-permute-start(s16[144,128]{1,0:T(8,128)(2,1)S(1)} %get-tuple-element.31), channel_id=1, source_target_pairs={{0,24},{2,26},{4,28},{6,30},{8,16},{10,18},{12,20},{14,22},{16,8},... | collective-permute-start | bytes 110600 | tf_op jit(solution)/shard_map/ppermute | solution.py:633
  37.9 5.6 %collective-permute-start.11 = (s16[144,128]{1,0:T(8,128)(2,1)S(1)}, s16[144,128]{1,0:T(8,128)(2,1)S(1)}, u32[]{:S(2)}, u32[]{:S(2)}) collective-permute-start(s16[144,128]{1,0:T(8,128)(2,1)S(1)} %get-tuple-element.32), channel_id=1, source_target_pairs={{0,8},{2,10},{4,12},{6,14},{8,0},{10,2},{12,4},{14,6},{16,24},{18,... | collective-permute-start | bytes 110600 | tf_op jit(solution)/shard_map/ppermute | solution.py:633
